TPU v7x, 32 devices: a whole 2x2x4 slice. The times are simulated.
32 devices in a mesh: ctx: 32 (over z, y, x, core), grp: 1.
Axes of the slice: x: 2, y: 2, z: 4, core: 2. Of those that a mesh axis runs over, the one named last changes fastest.
Arguments:
- query_in: bfloat16 [4096, 8192], P('ctx', 'grp'), may hold values from -6 to 6
- key_in: bfloat16 [4096, 8192], P('ctx', 'grp'), may hold values from -6 to 6
- value_in: bfloat16 [4096, 8192], P('ctx', 'grp'), may hold values from -6 to 6
- short_taps: float32 [3, 3, 8192], P(None, None, 'grp'), may hold values from -3 to 3
- decay_rate: float32 [16, 8192], P(None, 'grp'), may hold values from 0 to 1, as said below
- residues: float32 [16, 8192], P(None, 'grp'), may hold values from -2.5 to 2.5
- doc_lengths: int32 [16], replicated, may hold values from 1 to 1024, 4096 in all
- residual: bfloat16 [4096, 8192], P('ctx', 'grp'), may hold values from -6 to 6
- norm_gain: float32 [8192], P('grp'), may hold values from 0.5 to 1.5
Outputs:
- hidden_out: bfloat16 [4096, 8192], P('ctx', 'grp')
- normed: bfloat16 [4096, 8192], P('ctx', 'grp')
Inputs may be any that keep to these rules, and one draw needn't show every extreme that they name: `doc_lengths`: the lengths are positive, sum to 4096, and the largest is exactly 1024. `decay_rate`: positive decay rates.
All inputs are finite; a program needn't handle non-finite values.
Results may differ from a plain program's by a relative error of at most 0.0045.
Values may be sent and summed in bfloat16 or wider, within the bound.
No kernel may reach another device: no remote copies, remote signals or barrier semaphores. Data moves between devices by JAX's collectives and lax.ppermute only.
A program may use at most 128 MiB of HBM per device.

v0:
```python
import math

import jax
import jax.numpy as jnp
from jax import lax
from jax.sharding import PartitionSpec as P

D = 8192


highest = lax.Precision.HIGHEST


def from_behind(shard, axis, by):
    count = lax.axis_size(axis)
    pairs = [(i, i + by) for i in range(count) if 0 <= i + by < count]
    return lax.ppermute(shard, axis, pairs)


def combine_maps(earlier, later):
    return (earlier[0] * later[0], later[0] * earlier[1] + later[1])


def doc_starts(doc_lengths, positions):
    starts = jnp.cumsum(doc_lengths) - doc_lengths
    return jnp.max(jnp.where(starts[None, :] <= positions[:, None], starts[None, :], 0), axis=1)


def shift_mats(row_start, positions, tok_rows):
    row_ids = jnp.arange(tok_rows, dtype=jnp.int32)
    rim_ids = jnp.arange(2, dtype=jnp.int32)
    keep_one = (row_start < positions)[:, None]
    keep_two = (row_start <= positions - 2)[:, None]
    lag_one = ((row_ids[None, :] == row_ids[:, None] - 1) & keep_one).astype(jnp.bfloat16)
    lag_two = ((row_ids[None, :] == row_ids[:, None] - 2) & keep_two).astype(jnp.bfloat16)
    rim_one = ((rim_ids[None, :] == 1) & (row_ids[:, None] == 0) & keep_one).astype(jnp.bfloat16)
    rim_two = ((rim_ids[None, :] == row_ids[:, None]) & keep_two).astype(jnp.bfloat16)
    unit = (row_ids[:, None] == row_ids[None, :]).astype(jnp.bfloat16)
    return (unit, lag_one, lag_two, rim_one, rim_two)


def rows_conv(signal, rim, taps, mats):
    unit, lag_one, lag_two, rim_one, rim_two = mats
    first = jnp.dot(lag_one, signal, preferred_element_type=jnp.float32) + jnp.dot(
        rim_one, rim, preferred_element_type=jnp.float32
    )
    second = jnp.dot(lag_two, signal, preferred_element_type=jnp.float32) + jnp.dot(
        rim_two, rim, preferred_element_type=jnp.float32
    )
    return (
        taps[0][None, :] * signal.astype(jnp.float32)
        + taps[1][None, :] * first
        + taps[2][None, :] * second
    )


def cols_conv(signal, rim, taps, mats):
    unit, lag_one, lag_two, rim_one, rim_two = mats
    own = jnp.einsum("sc,ts->ct", signal, unit, preferred_element_type=jnp.float32)
    first = jnp.einsum(
        "sc,ts->ct", signal, lag_one, preferred_element_type=jnp.float32
    ) + jnp.einsum("rc,tr->ct", rim, rim_one, preferred_element_type=jnp.float32)
    second = jnp.einsum(
        "sc,ts->ct", signal, lag_two, preferred_element_type=jnp.float32
    ) + jnp.einsum("rc,tr->ct", rim, rim_two, preferred_element_type=jnp.float32)
    return taps[0][:, None] * own + taps[1][:, None] * first + taps[2][:, None] * second


def channel_conv(gate_vals, row_start, row_pos, rate, weight):
    span_rows = 128
    channels, length = gate_vals.shape
    block_count = length // span_rows
    lag_ids = jnp.arange(span_rows, dtype=jnp.float32)
    decay_table = jnp.exp(-lag_ids[None, None, :] * rate[:, :, None])
    step_table = jnp.exp(-(lag_ids[None, None, :] + 1.0) * rate[:, :, None]) * weight[:, :, None]
    lag_grid = jnp.maximum(lag_ids[:, None] - lag_ids[None, :], 0.0)
    lower = (lag_ids[:, None] >= lag_ids[None, :]).astype(jnp.float32)
    toeplitz = jnp.zeros((channels, span_rows, span_rows), jnp.float32)
    for mode in range(rate.shape[1]):
        toeplitz = toeplitz + weight[:, mode, None, None] * jnp.exp(
            -rate[:, mode, None, None] * lag_grid[None]
        )
    toeplitz = toeplitz * lower[None]
    blocked = gate_vals.reshape(channels, block_count, span_rows)
    start_blk = row_start.reshape(block_count, span_rows)
    pos_blk = row_pos.reshape(block_count, span_rows)
    inside = (start_blk < pos_blk[:, :1]).astype(jnp.float32)
    group_size = math.gcd(block_count, 8)
    group_count = block_count // group_size

    def intra_group(index):
        gate_grp = lax.dynamic_slice_in_dim(blocked, index * group_size, group_size, 1)
        start_grp = lax.dynamic_slice_in_dim(start_blk, index * group_size, group_size, 0)
        pos_grp = lax.dynamic_slice_in_dim(pos_blk, index * group_size, group_size, 0)
        same_doc = (pos_grp[:, None, :] >= start_grp[:, :, None]).astype(jnp.float32)
        return jnp.sum(toeplitz[:, None] * same_doc[None] * gate_grp[:, :, None, :], axis=3)

    intra = lax.map(intra_group, jnp.arange(group_count, dtype=jnp.int32))
    intra = intra.transpose(1, 0, 2, 3).reshape(channels, block_count, span_rows)
    end_mask = (pos_blk >= start_blk[:, span_rows - 1 :]).astype(jnp.float32)
    block_ends = jnp.einsum(
        "cnj,cbj->cnb", decay_table[:, :, ::-1], blocked * end_mask[None], precision=highest
    )
    carried = jnp.exp(-float(span_rows) * rate)[:, :, None] * inside[None, None, :, span_rows - 1]
    prefix_maps = lax.associative_scan(combine_maps, (carried, block_ends), axis=2)
    entering = jnp.concatenate(
        [jnp.zeros((channels, rate.shape[1], 1), jnp.float32), prefix_maps[1][:, :, :-1]], axis=2
    )
    from_state = jnp.einsum("cni,cnb->cbi", step_table, entering, precision=highest)
    result = intra + from_state * inside[None]
    return result.reshape(channels, length)


def shards(
    query_in, key_in, value_in, short_taps, decay_rate, residues, doc_lengths, residual, norm_gain
):
    tok_rows = query_in.shape[0]
    ctx_index = lax.axis_index("ctx")
    tails = jnp.stack([query_in[tok_rows - 2 :], key_in[tok_rows - 2 :], value_in[tok_rows - 2 :]])
    rim_rows = from_behind(tails, "ctx", 1)
    positions = ctx_index * tok_rows + jnp.arange(tok_rows, dtype=jnp.int32)
    row_start = doc_starts(doc_lengths, positions)
    mats = shift_mats(row_start, positions, tok_rows)
    q_short = rows_conv(query_in, rim_rows[0], short_taps[0], mats)
    weight = residues * jnp.sqrt(-jnp.expm1(-2.0 * decay_rate))
    k_cols = cols_conv(key_in, rim_rows[1], short_taps[1], mats)
    v_cols = cols_conv(value_in, rim_rows[2], short_taps[2], mats)
    gate_cols = (k_cols * v_cols).astype(jnp.bfloat16)
    moved = lax.all_to_all(gate_cols, "ctx", split_axis=0, concat_axis=1, tiled=True)
    few_chans = moved.shape[0]
    all_rows = moved.shape[1]
    all_pos = jnp.arange(all_rows, dtype=jnp.int32)
    all_start = doc_starts(doc_lengths, all_pos)
    rate_few = lax.dynamic_slice_in_dim(decay_rate, ctx_index * few_chans, few_chans, 1).T
    weight_few = lax.dynamic_slice_in_dim(weight, ctx_index * few_chans, few_chans, 1).T
    conv_few = channel_conv(moved.astype(jnp.float32), all_start, all_pos, rate_few, weight_few)
    returned = lax.all_to_all(
        conv_few.astype(jnp.bfloat16), "ctx", split_axis=1, concat_axis=0, tiled=True
    )
    conv_out = returned.T
    hidden = residual.astype(jnp.float32) + q_short * conv_out.astype(jnp.float32)
    square_sum = lax.psum(jnp.sum(hidden * hidden, axis=1), "grp")
    inverse_rms = lax.rsqrt(square_sum / D + 1e-06)
    normed = (hidden * inverse_rms[:, None] * norm_gain[None, :]).astype(jnp.bfloat16)
    return (hidden.astype(jnp.bfloat16), normed)


def solution(mesh):
    return jax.shard_map(
        shards,
        mesh=mesh,
        in_specs=(
            P("ctx", "grp"),
            P("ctx", "grp"),
            P("ctx", "grp"),
            P(None, None, "grp"),
            P(None, "grp"),
            P(None, "grp"),
            P(),
            P("ctx", "grp"),
            P("grp"),
        ),
        out_specs=(P("ctx", "grp"), P("ctx", "grp")),
        check_vma=False,
    )
```

profile of v0, /device:TPU:9, one launch (start us, length us, event | category | flops | bytes accessed | tf_op | source)
XLA Modules:
  0.0 619.3 jit_solution(546161510502391606)
XLA Ops:
  0.6 1.1 slice_bitcast_fusion.5
  1.7 1.0 slice_bitcast_fusion.3
  2.9 3.7 collective-permute-start
  8.4 2.3 convolution_bitcast_fusion.3
  10.7 0.8 convolution_bitcast_fusion.1
  11.5 0.8 copy-done
  14.1 0.8 fusion.78
  16.4 0.8 fusion.11
  17.2 0.8 fusion.9
  18.0 0.9 fusion.6
  18.9 1.1 fusion.19
  20.0 2.5 copy.146
  22.4 5.1 all-to-all-start
  29.3 1.4 slice.341
  30.7 1.4 slice.336
  32.2 1.7 multiply_exponential_fusion
  33.9 4.1 rev.3
  38.0 0.8 fusion.75
  38.8 0.8 copy.138
  42.4 32.3 %all-to-all-done = bf16[32,256,128]{2,1,0:T(8,128)(2,1)S(1)} async-done(((bf16[32,256,128]{2,1,0:T(8,128)(2,1)}), bf16[32,256,128]{2,1,0:T(8,128)(2,1)S(1)}, u32[]{:S(2)}, u32[]{:S(2)}) %all-to-all-start) | async-done | bytes 2097184 | tf_op jit(solution)/shard_map/all_to_all | solution.py:129
  74.6 1.3 copy-done.3
  76.5 1.1 copy-done.5
  77.6 8.5 %fusion.21 = f32[256,16,32]{2,1,0:T(8,128)S(1)} fusion(f32[256,16,128]{2,1,0:T(8,128)S(1)} %copy-done.5, f32[256,32,128]{2,0,1:T(8,128)S(1)} %broadcast_multiply_fusion), kind=kOutput, calls=%fused_computation.40 | convolution fusion | flops 201326592 | bytes 6815744 | tf_op jit(solution)/shard_map/cnj,cbj->cnb/dot_general | solution.py:101
  86.0 11.7 %slice.338 = f32[256,16,16]{2,1,0:T(8,128)} slice(f32[256,16,32]{2,1,0:T(8,128)S(1)} %fusion.21), slice={[0:256:1], [0:16:1], [0:31:2]} | slice | bytes 524288 | tf_op jit(solution)/shard_map/slice | solution.py:105
  97.7 12.1 %slice.339 = f32[256,16,16]{2,1,0:T(8,128)} slice(f32[256,16,32]{2,1,0:T(8,128)S(1)} %fusion.21), slice={[0:256:1], [0:16:1], [1:32:2]} | slice | bytes 524288 | tf_op jit(solution)/shard_map/slice | solution.py:105
  109.9 2.5 copy.150
  112.4 2.5 copy.151
  114.8 1.0 fusion.79
  118.0 11.7 %slice.369 = f32[256,16,15]{2,1,0:T(8,128)} slice(f32[256,16,32]{2,1,0:T(8,128)S(1)} %fusion.21), slice={[0:256:1], [0:16:1], [2:32:2]} | slice | bytes 491520 | tf_op jit(solution)/shard_map/slice | solution.py:105
  131.1 2.6 copy.152
  133.7 1.0 copy.149
  134.7 1.2 fusion.30
  135.9 5.7 pad.54
  141.7 1.1 slice_add_fusion.2
  143.1 2.5 copy.153
  145.5 2.5 convert_bitcast_fusion
  148.3 385.7 %while.11 = (s32[]{:T(128)}, f32[4,256,8,128]{3,2,1,0:T(8,128)}, s32[4]{0:T(128)S(1)}, s32[32,128]{1,0:T(8,128)S(1)}, s32[32,128]{1,0:T(8,128)S(1)}, /*index=5*/...) while((s32[]{:T(128)}, f32[4,256,8,128]{3,2,1,0:T(8,128)}, ...), condition=%wide.region_5.6_spmd.clone, body=%wide.region_3.5_spmd.clone.sunk | while | flops 301989888 | bytes 43180984 | solution.py:98
  149.8 53.4 %add_multiply_fusion.5 = f32[256,128,128]{2,1,0:T(8,128)} fusion(f32[128,128]{1,0:T(8,128)S(1)} %get-tuple-element.834, f32[256]{0:T(256)S(1)} %get-tuple-element.832, f32[256]{0:T(256)S(1)} %get-tuple-element.833, f32[256]{0:T(256)S(1)} %get-tuple-element.829, f32[256]{0:T(256)S(1)} %get-tuple-element.830, f32[256]{0:T(256)S(1)} %get-tuple-element.827, ...), kind=kLoop, calls=%fused_computation.2.clone.1 | loop fusion | flops 201326592 | bytes 16941056 | tf_op jit(solution)/shard_map/mul | solution.py:83
  203.2 1.3 constant_dynamic-slice_fusion.5
  205.1 38.6 %multiply_reduce_fusion.3 = f32[256,8,128]{2,1,0:T(8,128)S(1)} fusion(f32[256,8,128]{2,1,0:T(8,128)S(1)} %copy.158, f32[8,128,128]{2,1,0:T(8,128)S(1)} %compare_convert_fusion.4, f32[256,128,128]{2,1,0:T(8,128)} %add_multiply_fusion.5), kind=kLoop, calls=%fused_computation.1.clone.1 | loop fusion | flops 100401152 | bytes 19398656 | tf_op jit(solution)/shard_map/while/body/eval_jaxpr/reduce_sum | solution.py:96
  243.7 1.1 bitcast_dynamic-update-slice_fusion.2
  246.2 53.4 %add_multiply_fusion.5 = f32[256,128,128]{2,1,0:T(8,128)} fusion(f32[128,128]{1,0:T(8,128)S(1)} %get-tuple-element.834, f32[256]{0:T(256)S(1)} %get-tuple-element.832, f32[256]{0:T(256)S(1)} %get-tuple-element.833, f32[256]{0:T(256)S(1)} %get-tuple-element.829, f32[256]{0:T(256)S(1)} %get-tuple-element.830, f32[256]{0:T(256)S(1)} %get-tuple-element.827, ...), kind=kLoop, calls=%fused_computation.2.clone.1 | loop fusion | flops 201326592 | bytes 16941056 | tf_op jit(solution)/shard_map/mul | solution.py:83
  299.6 1.3 constant_dynamic-slice_fusion.5
  301.6 38.6 %multiply_reduce_fusion.3 = f32[256,8,128]{2,1,0:T(8,128)S(1)} fusion(f32[256,8,128]{2,1,0:T(8,128)S(1)} %copy.158, f32[8,128,128]{2,1,0:T(8,128)S(1)} %compare_convert_fusion.4, f32[256,128,128]{2,1,0:T(8,128)} %add_multiply_fusion.5), kind=kLoop, calls=%fused_computation.1.clone.1 | loop fusion | flops 100401152 | bytes 19398656 | tf_op jit(solution)/shard_map/while/body/eval_jaxpr/reduce_sum | solution.py:96
  340.1 1.1 bitcast_dynamic-update-slice_fusion.2
  342.7 53.4 %add_multiply_fusion.5 = f32[256,128,128]{2,1,0:T(8,128)} fusion(f32[128,128]{1,0:T(8,128)S(1)} %get-tuple-element.834, f32[256]{0:T(256)S(1)} %get-tuple-element.832, f32[256]{0:T(256)S(1)} %get-tuple-element.833, f32[256]{0:T(256)S(1)} %get-tuple-element.829, f32[256]{0:T(256)S(1)} %get-tuple-element.830, f32[256]{0:T(256)S(1)} %get-tuple-element.827, ...), kind=kLoop, calls=%fused_computation.2.clone.1 | loop fusion | flops 201326592 | bytes 16941056 | tf_op jit(solution)/shard_map/mul | solution.py:83
  396.1 1.3 constant_dynamic-slice_fusion.5
  398.0 38.6 %multiply_reduce_fusion.3 = f32[256,8,128]{2,1,0:T(8,128)S(1)} fusion(f32[256,8,128]{2,1,0:T(8,128)S(1)} %copy.158, f32[8,128,128]{2,1,0:T(8,128)S(1)} %compare_convert_fusion.4, f32[256,128,128]{2,1,0:T(8,128)} %add_multiply_fusion.5), kind=kLoop, calls=%fused_computation.1.clone.1 | loop fusion | flops 100401152 | bytes 19398656 | tf_op jit(solution)/shard_map/while/body/eval_jaxpr/reduce_sum | solution.py:96
  436.5 1.0 bitcast_dynamic-update-slice_fusion.2
  439.0 53.4 %add_multiply_fusion.5 = f32[256,128,128]{2,1,0:T(8,128)} fusion(f32[128,128]{1,0:T(8,128)S(1)} %get-tuple-element.834, f32[256]{0:T(256)S(1)} %get-tuple-element.832, f32[256]{0:T(256)S(1)} %get-tuple-element.833, f32[256]{0:T(256)S(1)} %get-tuple-element.829, f32[256]{0:T(256)S(1)} %get-tuple-element.830, f32[256]{0:T(256)S(1)} %get-tuple-element.827, ...), kind=kLoop, calls=%fused_computation.2.clone.1 | loop fusion | flops 201326592 | bytes 16941056 | tf_op jit(solution)/shard_map/mul | solution.py:83
  492.5 1.3 constant_dynamic-slice_fusion.5
  494.4 38.6 %multiply_reduce_fusion.3 = f32[256,8,128]{2,1,0:T(8,128)S(1)} fusion(f32[256,8,128]{2,1,0:T(8,128)S(1)} %copy.158, f32[8,128,128]{2,1,0:T(8,128)S(1)} %compare_convert_fusion.4, f32[256,128,128]{2,1,0:T(8,128)} %add_multiply_fusion.5), kind=kLoop, calls=%fused_computation.1.clone.1 | loop fusion | flops 100401152 | bytes 19398656 | tf_op jit(solution)/shard_map/while/body/eval_jaxpr/reduce_sum | solution.py:96
  532.9 1.1 bitcast_dynamic-update-slice_fusion.2
  534.0 10.8 %fusion.20 = bf16[256,32,128]{2,1,0:T(8,128)(2,1)S(1)} fusion(f32[256,16,31]{2,1,0:T(8,128)} %copy.153, f32[32,128]{1,0:T(8,128)S(1)} %copy-done.14, f32[256,16]{1,0:T(8,128)S(1)} %copy-done.9, f32[128]{0:T(128)S(1)} %copy-done.56, f32[256,16]{1,0:T(8,128)S(1)} %copy-done.8, f32[4,256,8,128]{3,2,1,0:T(8,128)} %get-tuple-element.39), kind=kOutput, calls=%fused_computation.39 | convolution fusion | flops 205520896 | bytes 6849024 | tf_op jit(solution)/shard_map/cni,cnb->cbi/dot_general | solution.py:109
  544.9 2.1 copy.140
  547.0 5.8 all-to-all-start.1
  552.9 0.8 fusion.36
  553.7 2.7 fusion.41
  556.4 3.0 fusion.17
  559.5 40.6 %all-to-all-done.1 = bf16[256,32,128]{2,0,1:T(8,128)(2,1)} async-done(((bf16[256,32,128]{2,0,1:T(8,128)(2,1)}), bf16[256,32,128]{2,0,1:T(8,128)(2,1)}, u32[]{:S(2)}, u32[]{:S(2)}) %all-to-all-start.1) | async-done | bytes 2097184 | tf_op jit(solution)/shard_map/all_to_all | solution.py:137
  600.0 4.0 convert_element_type.89
  604.0 5.8 copy.147
  609.8 6.3 %multiply_reduce_fusion.1 = (f32[128]{0:T(128)S(1)}, f32[128,8192]{1,0:T(8,128)S(1)}) fusion(f32[8192,128]{0,1:T(8,128)} %copy.147, f32[128,8192]{1,0:T(8,128)} %fusion.17, f32[128,8192]{1,0:T(8,128)} %fusion.41, bf16[3,2,8192]{2,1,0:T(2,128)(2,1)S(1)} %copy-done.11, pred[128]{0:T(512)(128)(4,1)S(1)} %copy-done.21, f32[8192]{0:T(1024)S(1)} %bitcast.141, ...), kind=kOutput, calls=%fused_computation.44 | convolution fusion | flops 12583296 | bytes 18940928 | tf_op jit(solution)/shard_map/dot_general | solution.py:47
  616.1 2.7 multiply_convert_fusion
  (204 shorter events, 19.3 us)
Async XLA Ops:
  0.6 10.1 %copy-start.1 = (bf16[128,8192]{1,0:T(8,128)(2,1)S(1)}, bf16[128,8192]{1,0:T(8,128)(2,1)}, u32[]{:S(2)}) copy-start(bf16[128,8192]{1,0:T(8,128)(2,1)} %param.13) | copy-start | bytes 6291460
  2.9 13.4 %collective-permute-start = (bf16[3,2,8192]{2,1,0:T(2,128)(2,1)S(1)}, bf16[3,2,8192]{2,1,0:T(2,128)(2,1)S(1)}, u32[]{:S(2)}, u32[]{:S(2)}) collective-permute-start(bf16[3,2,8192]{2,1,0:T(2,128)(2,1)S(1)} %pad_maximum_fusion.2), channel_id=1, source_target_pairs={{0,1},{1,2},{2,3},{3,4},{4,5},{5,6},{6,7},{7,8},{8,9},{9,10},{10,1... | collective-permute-start | bytes 294920 | tf_op jit(solution)/shard_map/ppermute | solution.py:17
  6.6 4.9 copy-start.30
  6.7 6.4 %copy-start.28 = (s32[128]{0:T(128)}, s32[128]{0:T(128)S(1)}, u32[]{:S(2)}) copy-start(s32[128]{0:T(128)S(1)} %iota_add_fusion) | copy-start | bytes 1540
  8.3 9.6 %copy-start.22 = (pred[128]{0:T(512)(128)(4,1)}, pred[128]{0:T(512)(128)(4,1)S(1)}, u32[]{:S(2)}) copy-start(pred[128]{0:T(512)(128)(4,1)S(1)} %get-tuple-element.454) | copy-start | bytes 388
  8.4 9.6 %copy-start.24 = (pred[128]{0:T(512)(128)(4,1)}, pred[128]{0:T(512)(128)(4,1)S(1)}, u32[]{:S(2)}) copy-start(pred[128]{0:T(512)(128)(4,1)S(1)} %get-tuple-element.459) | copy-start | bytes 388
  8.4 10.5 %copy-start.20 = (pred[128]{0:T(512)(128)(4,1)}, pred[128]{0:T(512)(128)(4,1)S(1)}, u32[]{:S(2)}) copy-start(pred[128]{0:T(512)(128)(4,1)S(1)} %get-tuple-element.453) | copy-start | bytes 388
  10.7 1.6 copy-start
  13.1 1.0 copy-start.12
  16.4 1.6 copy-start.26
  16.4 2.5 copy-start.10
  22.4 52.2 %all-to-all-start = ((bf16[32,256,128]{2,1,0:T(8,128)(2,1)}), bf16[32,256,128]{2,1,0:T(8,128)(2,1)S(1)}, u32[]{:S(2)}, u32[]{:S(2)}) async-start(bf16[32,256,128]{2,1,0:T(8,128)(2,1)} %bitcast.127), calls=%async_computation | async-start | bytes 4194304 | tf_op jit(solution)/shard_map/all_to_all | solution.py:129
  27.9 0.9 copy-start.13
  32.2 44.3 %copy-start.7 = (f32[256,16]{1,0:T(8,128)}, f32[256,16]{1,0:T(8,128)S(1)}, u32[]{:S(2)}) copy-start(f32[256,16]{1,0:T(8,128)S(1)} %copy.132) | copy-start | bytes 49156
  74.6 1.3 copy-start.3
  76.0 1.6 copy-start.5
  134.7 10.8 %copy-start.4 = (bf16[32,256,128]{2,1,0:T(8,128)(2,1)S(1)}, bf16[32,256,128]{2,1,0:T(8,128)(2,1)}, u32[]{:S(2)}) copy-start(bf16[32,256,128]{2,1,0:T(8,128)(2,1)} %copy-done.3) | copy-start | bytes 6291460
  142.8 5.2 copy-start.18
  142.8 5.2 copy-start.32
  142.8 5.2 copy-start.33
  142.8 5.2 copy-start.34
  142.8 5.2 copy-start.35
  142.9 5.2 copy-start.36
  142.9 5.2 copy-start.37
  142.9 5.2 copy-start.38
  142.9 5.2 copy-start.39
  142.9 5.2 copy-start.40
  142.9 5.2 copy-start.41
  142.9 5.2 copy-start.42
  142.9 5.2 copy-start.43
  142.9 5.2 copy-start.44
  142.9 5.2 copy-start.45
  143.0 5.2 copy-start.46
  143.0 5.2 copy-start.47
  143.0 5.2 copy-start.48
  143.0 5.2 copy-start.49
  143.0 5.2 copy-start.50
  143.0 5.2 copy-start.51
  143.0 5.2 copy-start.52
  143.0 5.2 copy-start.53
  143.0 5.2 copy-start.54
  143.0 5.2 copy-start.55
  148.3 385.7 %copy-start.8 = (f32[256,16]{1,0:T(8,128)S(1)}, f32[256,16]{1,0:T(8,128)}, u32[]{:S(2)}) copy-start(f32[256,16]{1,0:T(8,128)} %copy-done.7) | copy-start | bytes 49156
  148.3 385.7 %copy-start.9 = (f32[256,16]{1,0:T(8,128)S(1)}, f32[256,16]{1,0:T(8,128)}, u32[]{:S(2)}) copy-start(f32[256,16]{1,0:T(8,128)} %copy.138) | copy-start | bytes 49156
  148.3 385.7 %copy-start.14 = (f32[32,128]{1,0:T(8,128)S(1)}, f32[32,128]{1,0:T(8,128)}, u32[]{:S(2)}) copy-start(f32[32,128]{1,0:T(8,128)} %copy-done.13) | copy-start | bytes 49156
  148.3 385.7 %copy-start.56 = (f32[128]{0:T(128)S(1)}, f32[128]{0:T(128)}, u32[]{:S(2)}) copy-start(f32[128]{0:T(128)} %add_negate_fusion) | copy-start | bytes 1540
  544.9 8.0 %copy-start.2 = (bf16[128,8192]{1,0:T(8,128)(2,1)S(1)}, bf16[128,8192]{1,0:T(8,128)(2,1)}, u32[]{:S(2)}) copy-start(bf16[128,8192]{1,0:T(8,128)(2,1)} %param.11) | copy-start | bytes 6291460
  544.9 8.0 %copy-start.23 = (pred[128]{0:T(512)(128)(4,1)S(1)}, pred[128]{0:T(512)(128)(4,1)}, u32[]{:S(2)}) copy-start(pred[128]{0:T(512)(128)(4,1)} %copy-done.22) | copy-start | bytes 388
  544.9 8.0 %copy-start.31 = (s32[128]{0:T(128)S(1)}, s32[128]{0:T(128)}, u32[]{:S(2)}) copy-start(s32[128]{0:T(128)} %copy-done.30) | copy-start | bytes 1540
  547.0 53.0 %all-to-all-start.1 = ((bf16[256,32,128]{2,0,1:T(8,128)(2,1)}), bf16[256,32,128]{2,0,1:T(8,128)(2,1)}, u32[]{:S(2)}, u32[]{:S(2)}) async-start(bf16[256,32,128]{2,0,1:T(8,128)(2,1)} %copy.140), calls=%async_computation.1 | async-start | bytes 4194304 | tf_op jit(solution)/shard_map/all_to_all | solution.py:137
  552.8 0.8 copy-start.21
  552.9 0.8 copy-start.29
  553.6 2.8 copy-start.11
  553.7 2.8 copy-start.16
  553.7 2.7 copy-start.17
  553.7 2.7 copy-start.25
  553.7 2.7 copy-start.27
  604.0 5.8 copy-start.6
  604.0 5.8 copy-start.15
  609.8 6.3 %copy-start.19 = (f32[8192]{0:T(1024)S(1)}, f32[8192]{0:T(1024)}, u32[]{:S(2)}) copy-start(f32[8192]{0:T(1024)} %param.19) | copy-start | bytes 98308
where the time goes:
time: 629 us; the launch traced here: 619 us
  other arithmetic  389 us (62%)
  local copies, waits for them, and re-layouts  96.4 us (15%)
  waiting for transfers between devices  72.8 us (12%)
  matrix products  41.5 us (7%)
  starting transfers between devices  14.6 us (2%)
    mul x4, other arithmetic, channel_conv(): toeplitz = toeplitz * lower[None]  214 us
    reduce_sum x4, other arithmetic, intra_group(): jnp.sum(toeplitz[:, None] * same_doc[None] * gate_grp[:, :, None, :], axi...  154 us
    all_to_all x1, waiting for transfers between devices, shards(): lax.all_to_all(conv_few.astype(jnp.bfloat16), 'ctx', split_axis=1, concat...  40.6 us
    slice x24, local copies, waits for them, and re-layouts, channel_conv(): lax.associative_scan(combine_maps, (carried, block_ends), axis=2)  40.4 us
    all_to_all x1, waiting for transfers between devices, shards(): lax.all_to_all(gate_cols, 'ctx', split_axis=0, concat_axis=1, tiled=True)  32.3 us
    unnamed x120, local copies, waits for them, and re-layouts  14.9 us
  transfers between devices with their start and end apart: 3, of which 2 were waited for; matrix products, arithmetic and copies ran while one was open for 5% of the time, Pallas kernels for 0%

commit v1 on v0

v1 whole, which is shorter than its diff:
```python
import functools

import jax
import jax.numpy as jnp
from jax import lax
from jax.experimental import pallas as pl
from jax.experimental.pallas import tpu as pltpu
from jax.sharding import PartitionSpec as P

SUBS = 8
LANES = 128
VMEM_LIMIT = 48 * 1024 * 1024
f32 = jnp.float32
bf16 = jnp.bfloat16


def from_behind(shard, axis, by):
    count = lax.axis_size(axis)
    pairs = [(i, i + by) for i in range(count) if 0 <= i + by < count]
    return lax.ppermute(shard, axis, pairs)


def doc_start_rows(len_ref, base, span):
    rows = lax.broadcasted_iota(jnp.int32, (SUBS, LANES), 0) * span + base
    starts = [jnp.int32(0)]
    for d in range(len_ref.shape[0] - 1):
        starts.append(starts[-1] + len_ref[d])
    out = []
    for j in range(span):
        pos = rows + j
        best = jnp.zeros((SUBS, LANES), jnp.int32)
        for start in starts[1:]:
            best = jnp.where(pos >= start, start, best)
        out.append(best)
    return rows, out


def flag(cond):
    return jnp.where(cond, 1.0, 0.0).astype(f32)


def row_of(ref, index):
    return jnp.broadcast_to(ref[pl.ds(index, 1), :], (SUBS, LANES))


def spread(x, scratch, span):
    scratch[...] = x.astype(f32)
    return [scratch[pl.ds(j, SUBS, stride=span), :] for j in range(span)]


def short_conv(steps, rim, taps, keep_one, keep_two):
    top = lax.broadcasted_iota(jnp.int32, (SUBS, LANES), 0) == 0
    rim = rim.astype(f32)
    behind_one = jnp.where(top, jnp.broadcast_to(rim[1:2], (SUBS, LANES)), pltpu.roll(steps[-1], 1, 0))
    behind_two = jnp.where(top, jnp.broadcast_to(rim[0:1], (SUBS, LANES)), pltpu.roll(steps[-2], 1, 0))
    padded = [behind_two, behind_one] + steps
    taps = [jnp.broadcast_to(taps[m : m + 1], (SUBS, LANES)) for m in range(3)]
    return [
        taps[0] * padded[j + 2]
        + (taps[1] * padded[j + 1]) * keep_one[j]
        + (taps[2] * padded[j]) * keep_two[j]
        for j in range(len(steps))
    ]


def state_kernel(
    base_ref, len_ref, key_ref, value_ref, rim_ref, taps_ref, rate_ref, weight_ref,
    gate_ref, state_ref, end_ref,
    masks, wide_k, wide_v, tables, ends,
    *, span, modes, width,
):
    @pl.when(pl.program_id(0) == 0)
    def _():
        rows, starts = doc_start_rows(len_ref, base_ref[0], span)
        for j in range(span):
            masks[0, j] = flag(starts[j] < rows + j)
            masks[1, j] = flag(starts[j] < rows + (j - 1))
            masks[2, j] = flag(starts[span - 1] <= rows + j)
        sub = lax.broadcasted_iota(jnp.int32, (SUBS, LANES), 0)
        through = flag(starts[span - 1] < rows)
        one = through * flag(sub >= 1)
        two = one * pltpu.roll(one, 1, 0) * flag(sub >= 2)
        four = two * pltpu.roll(two, 2, 0) * flag(sub >= 4)
        masks[3, 0] = one
        masks[3, 1] = two
        masks[3, 2] = four
        masks[3, 3] = flag(sub >= 1)

    def tile(i, carry):
        lane = pl.multiple_of(i * LANES, LANES)
        cols = pl.ds(lane, LANES)
        keep_one = [masks[0, j] for j in range(span)]
        keep_two = [masks[1, j] for j in range(span)]
        k_steps = spread(key_ref[:, cols], wide_k, span)
        v_steps = spread(value_ref[:, cols], wide_v, span)
        k_short = short_conv(k_steps, rim_ref[1, :, cols], taps_ref[1, :, cols], keep_one, keep_two)
        v_short = short_conv(v_steps, rim_ref[2, :, cols], taps_ref[2, :, cols], keep_one, keep_two)
        gates = []
        for j in range(0, span, 2):
            pair = jnp.concatenate([k_short[j] * v_short[j], k_short[j + 1] * v_short[j + 1]], axis=0).astype(bf16)
            gate_ref[pl.ds(j * SUBS, 2 * SUBS), cols] = pair
            pair = pair.astype(f32)
            gates += [pair[:SUBS] * masks[2, j], pair[SUBS:] * masks[2, j + 1]]
        rate = rate_ref[:, cols]
        tables[0] = jnp.exp(-rate)
        tables[1] = jnp.exp(-float(span) * rate)
        tables[2] = jnp.exp(-float(2 * span) * rate)
        tables[3] = jnp.exp(-float(4 * span) * rate)
        tables[4] = weight_ref[:, cols]
        decay = [row_of(tables.at[0], n) for n in range(modes)]
        state = [gates[0]] * modes
        for j in range(1, span):
            state = [decay[n] * state[n] + gates[j] for n in range(modes)]
        for n in range(modes):
            x = state[n]
            x = x + (row_of(tables.at[1], n) * masks[3, 0]) * pltpu.roll(x, 1, 0)
            x = x + (row_of(tables.at[2], n) * masks[3, 1]) * pltpu.roll(x, 2, 0)
            x = x + (row_of(tables.at[3], n) * masks[3, 2]) * pltpu.roll(x, 4, 0)
            ends[pl.ds(n, 1), :] = x[SUBS - 1 :]
            state_ref[pl.ds(n * SUBS, SUBS), cols] = (row_of(tables.at[4], n) * masks[3, 3]) * pltpu.roll(x, 1, 0)
        if width:
            end_ref[lax.div(lane, width), :, pl.ds(pl.multiple_of(lax.rem(lane, width), LANES), LANES)] = ends[...].astype(bf16)
        else:
            end_ref[:, cols] = ends[...].astype(bf16)
        return carry

    lax.fori_loop(0, key_ref.shape[1] // LANES, tile, 0)


def local_kernel(
    base_ref, len_ref, gate_ref, query_ref, rim_ref, taps_ref, rate_ref, weight_ref,
    near_ref, short_ref,
    masks, wide_q,
    *, span, modes,
):
    @pl.when(pl.program_id(0) == 0)
    def _():
        rows, starts = doc_start_rows(len_ref, base_ref[0], span)
        for j in range(span):
            masks[0, j] = flag(starts[j] < rows + j)
            masks[1, j] = flag(starts[j] < rows + (j - 1))

    def tile(i, carry):
        cols = pl.ds(pl.multiple_of(i * LANES, LANES), LANES)
        keep_one = [masks[0, j] for j in range(span)]
        keep_two = [masks[1, j] for j in range(span)]
        q_steps = spread(query_ref[:, cols], wide_q, span)
        q_short = short_conv(q_steps, rim_ref[0, :, cols], taps_ref[0, :, cols], keep_one, keep_two)
        for j in range(span):
            short_ref[pl.ds(j * SUBS, SUBS), cols] = q_short[j]
        decay = jnp.exp(-rate_ref[:, cols])
        term = weight_ref[:, cols]
        taps = []
        for lag in range(span):
            part = term[:SUBS]
            for n in range(SUBS, modes, SUBS):
                part = part + term[n : n + SUBS]
            for shift in (1, 2, 4):
                part = part + pltpu.roll(part, shift, 0)
            taps.append(part)
            term = term * decay
        live = []
        for j in range(span):
            if j % 2 == 0:
                pair = gate_ref[pl.ds(j * SUBS, 2 * SUBS), cols].astype(f32)
            live = [g * keep_one[j] for g in live]
            live.append(pair[(j % 2) * SUBS : (j % 2 + 1) * SUBS])
            total = taps[0] * live[j]
            for lag in range(1, j + 1):
                total = total + taps[lag] * live[j - lag]
            near_ref[pl.ds(j * SUBS, SUBS), cols] = total
        return carry

    lax.fori_loop(0, gate_ref.shape[1] // LANES, tile, 0)


def prefix_kernel(len_ref, end_ref, rate_ref, enter_ref, through, *, span):
    blocks = end_ref.shape[0]
    for i in range(blocks):
        through[i] = jnp.float32(1.0)
    start = jnp.int32(0)
    through[0] = jnp.float32(0.0)
    for d in range(len_ref.shape[0] - 1):
        start = start + len_ref[d]
        through[lax.div(start, jnp.int32(span))] = jnp.float32(0.0)
    decay = jnp.exp(-float(span) * rate_ref[...])
    state = jnp.zeros(decay.shape, f32)
    for i in range(blocks):
        enter_ref[i] = state.astype(bf16)
        state = end_ref[i].astype(f32) + (decay * through[i]) * state


def final_kernel(
    base_ref, len_ref, state_ref, enter_ref, near_ref, short_ref, resid_ref, rate_ref, weight_ref, gain_ref,
    *refs,
    span, modes, width, channels,
):
    if channels:
        hidden_ref, normed_ref, masks, tables, sums, whole = refs
    else:
        hidden_ref, wide_ref, sum_ref, masks, tables, sums, whole = refs
    step = pl.program_id(0)
    tiles = resid_ref.shape[1] // LANES

    @pl.when(step == 0)
    def _():
        rows, starts = doc_start_rows(len_ref, base_ref[0], span)
        for j in range(span):
            masks[0, j] = flag(starts[j] < rows)
        masks[1, 0] = flag(starts[0] < base_ref[0])
        sums[...] = jnp.zeros(sums.shape, f32)

    def tile(i, carry):
        lane = pl.multiple_of(i * LANES, LANES)
        cols = pl.ds(lane, LANES)
        if width:
            enter = enter_ref[lax.div(lane, width), :, pl.ds(pl.multiple_of(lax.rem(lane, width), LANES), LANES)]
        else:
            enter = enter_ref[:, cols]
        rate = rate_ref[:, cols]
        tables[0] = jnp.exp(-rate)
        tables[1] = weight_ref[:, cols] * enter.astype(f32)
        tables[2] = rate
        sub = lax.broadcasted_iota(jnp.int32, (SUBS, LANES), 0).astype(f32) * (-float(span))
        through = masks[1, 0]
        decay = [row_of(tables.at[0], n) for n in range(modes)]
        part = [
            state_ref[pl.ds(n * SUBS, SUBS), cols]
            + (row_of(tables.at[1], n) * through) * jnp.exp(row_of(tables.at[2], n) * sub)
            for n in range(modes)
        ]
        tile_at = step * tiles + i
        for j in range(span):
            part = [part[n] * decay[n] for n in range(modes)]
            total = part
            while len(total) > 1:
                total = [total[m] + total[m + 1] for m in range(0, len(total), 2)]
            conv = near_ref[pl.ds(j * SUBS, SUBS), cols] + total[0] * masks[0, j]
            conv = conv.astype(bf16).astype(f32)
            whole[tile_at, pl.ds(j, SUBS, stride=span), :] = short_ref[pl.ds(j * SUBS, SUBS), cols] * conv
        hidden = whole[tile_at] + resid_ref[:, cols].astype(f32)
        whole[tile_at] = hidden
        hidden_ref[:, cols] = hidden.astype(bf16)
        if not channels:
            wide_ref[:, cols] = hidden
        sums[...] = sums[...] + hidden * hidden
        return carry

    lax.fori_loop(0, tiles, tile, 0)

    @pl.when(step == pl.num_programs(0) - 1)
    def _():
        if channels:
            inverse = lax.rsqrt(jnp.sum(sums[...], axis=1, keepdims=True) / channels + 1e-06)
            inverse = jnp.broadcast_to(inverse, sums.shape)
            sums[...] = inverse

            def scale(i, carry):
                cols = pl.ds(pl.multiple_of(i * LANES, LANES), LANES)
                normed_ref[:, cols] = (whole[i] * sums[...] * gain_ref[:, cols]).astype(bf16)
                return carry

            lax.fori_loop(0, normed_ref.shape[1] // LANES, scale, 0)
        else:
            sum_ref[...] = sums[...]


def shards(
    query_in, key_in, value_in, short_taps, decay_rate, residues, doc_lengths, residual, norm_gain
):
    tok_rows, chans = query_in.shape
    modes = decay_rate.shape[0]
    span = tok_rows // SUBS
    blocks = lax.axis_size("ctx")
    grp = lax.axis_size("grp")
    few = chans // blocks
    width = few if few % LANES == 0 else 0
    chunk = min(chans, max(1024, width))
    steps = chans // chunk
    ctx_index = lax.axis_index("ctx")
    base = (ctx_index * tok_rows).astype(jnp.int32).reshape(1)
    tails = jnp.stack([query_in[tok_rows - 2 :], key_in[tok_rows - 2 :], value_in[tok_rows - 2 :]])
    rim_rows = from_behind(tails, "ctx", 1)
    weight = residues * jnp.sqrt(-jnp.expm1(-2.0 * decay_rate))

    smem = pl.BlockSpec(memory_space=pltpu.SMEM)

    def rows_spec(rows):
        return pl.BlockSpec((rows, chunk), lambda i: (0, i))

    rim_spec = pl.BlockSpec((3, 2, chunk), lambda i: (0, 0, i))
    taps_spec = pl.BlockSpec((3, 3, chunk), lambda i: (0, 0, i))
    if width:
        end_spec = pl.BlockSpec((chunk // width, modes, width), lambda i: (i, 0, 0))
        end_shape = (blocks, modes, width)
    else:
        end_spec = rows_spec(modes)
        end_shape = (modes, chans)
    params = pltpu.CompilerParams(vmem_limit_bytes=VMEM_LIMIT)
    tile_shape = (SUBS, LANES)

    def cost(per_tile, moved):
        return pl.CostEstimate(flops=per_tile * (chans // LANES) * SUBS * LANES, bytes_accessed=moved, transcendentals=0)

    gates, states, ends = pl.pallas_call(
        functools.partial(state_kernel, span=span, modes=modes, width=width),
        grid=(steps,),
        in_specs=[smem, smem, rows_spec(tok_rows), rows_spec(tok_rows), rim_spec, taps_spec, rows_spec(modes), rows_spec(modes)],
        out_specs=[rows_spec(tok_rows), rows_spec(modes * SUBS), end_spec],
        out_shape=[
            jax.ShapeDtypeStruct((tok_rows, chans), bf16),
            jax.ShapeDtypeStruct((modes * SUBS, chans), f32),
            jax.ShapeDtypeStruct(end_shape, bf16),
        ],
        scratch_shapes=[
            pltpu.VMEM((4, span) + tile_shape, f32),
            pltpu.VMEM((tok_rows, LANES), f32),
            pltpu.VMEM((tok_rows, LANES), f32),
            pltpu.VMEM((5, modes, LANES), f32),
            pltpu.VMEM((modes, LANES), f32),
        ],
        compiler_params=params,
        cost_estimate=cost(1000, 12 * tok_rows * chans),
        name="block_states",
    )(base, doc_lengths, key_in, value_in, rim_rows, short_taps, decay_rate, weight)

    near, q_short = pl.pallas_call(
        functools.partial(local_kernel, span=span, modes=modes),
        grid=(steps,),
        in_specs=[smem, smem, rows_spec(tok_rows), rows_spec(tok_rows), rim_spec, taps_spec, rows_spec(modes), rows_spec(modes)],
        out_specs=[rows_spec(tok_rows), rows_spec(tok_rows)],
        out_shape=[jax.ShapeDtypeStruct((tok_rows, chans), f32), jax.ShapeDtypeStruct((tok_rows, chans), f32)],
        scratch_shapes=[pltpu.VMEM((2, span) + tile_shape, f32), pltpu.VMEM((tok_rows, LANES), f32)],
        compiler_params=params,
        cost_estimate=cost(700, 12 * tok_rows * chans),
        name="near_part",
    )(base, doc_lengths, gates, query_in, rim_rows, short_taps, decay_rate, weight)

    if not width:
        ends = ends.reshape(modes, blocks, few).transpose(1, 0, 2)
    moved = lax.all_to_all(ends, "ctx", split_axis=0, concat_axis=0, tiled=True)
    rate_few = lax.dynamic_slice_in_dim(decay_rate, ctx_index * few, few, 1)
    enter_few = pl.pallas_call(
        functools.partial(prefix_kernel, span=tok_rows),
        in_specs=[smem, pl.BlockSpec(memory_space=pltpu.VMEM), pl.BlockSpec(memory_space=pltpu.VMEM)],
        out_specs=pl.BlockSpec(memory_space=pltpu.VMEM),
        out_shape=jax.ShapeDtypeStruct((blocks, modes, few), bf16),
        scratch_shapes=[pltpu.SMEM((blocks,), f32)],
        name="block_prefix",
    )(doc_lengths, moved, rate_few)
    enter = lax.all_to_all(enter_few, "ctx", split_axis=0, concat_axis=0, tiled=True)
    if not width:
        enter = enter.transpose(1, 0, 2).reshape(modes, chans)

    alone = grp == 1
    out_specs = [rows_spec(tok_rows)]
    out_shape = [jax.ShapeDtypeStruct((tok_rows, chans), bf16)]
    if alone:
        out_specs.append(pl.BlockSpec((tok_rows, chans), lambda i: (0, 0)))
        out_shape.append(jax.ShapeDtypeStruct((tok_rows, chans), bf16))
    else:
        out_specs += [rows_spec(tok_rows), pl.BlockSpec((tok_rows, LANES), lambda i: (0, 0))]
        out_shape += [jax.ShapeDtypeStruct((tok_rows, chans), f32), jax.ShapeDtypeStruct((tok_rows, LANES), f32)]
    outs = pl.pallas_call(
        functools.partial(final_kernel, span=span, modes=modes, width=width, channels=chans if alone else 0),
        grid=(steps,),
        in_specs=[
            smem, smem, rows_spec(modes * SUBS), end_spec, rows_spec(tok_rows), rows_spec(tok_rows), rows_spec(tok_rows),
            rows_spec(modes), rows_spec(modes), pl.BlockSpec((1, chans), lambda i: (0, 0)),
        ],
        out_specs=out_specs,
        out_shape=out_shape,
        scratch_shapes=[
            pltpu.VMEM((2, span) + tile_shape, f32),
            pltpu.VMEM((3, modes, LANES), f32),
            pltpu.VMEM((tok_rows, LANES), f32),
            pltpu.VMEM((chans // LANES, tok_rows, LANES), f32),
        ],
        compiler_params=params,
        cost_estimate=cost(900, 18 * tok_rows * chans),
        name="far_part",
    )(base, doc_lengths, states, enter, near, q_short, residual, decay_rate, weight, norm_gain.reshape(1, chans))
    if alone:
        return tuple(outs)
    hidden_out, hidden, sums = outs
    square_sum = lax.psum(jnp.sum(sums, axis=1), "grp")
    inverse_rms = lax.rsqrt(square_sum / (chans * grp) + 1e-06)
    normed = (hidden * inverse_rms[:, None] * norm_gain[None, :]).astype(bf16)
    return (hidden_out, normed)


def solution(mesh):
    return jax.shard_map(
        shards,
        mesh=mesh,
        in_specs=(
            P("ctx", "grp"),
            P("ctx", "grp"),
            P("ctx", "grp"),
            P(None, None, "grp"),
            P(None, "grp"),
            P(None, "grp"),
            P(),
            P("ctx", "grp"),
            P("grp"),
        ),
        out_specs=(P("ctx", "grp"), P("ctx", "grp")),
        check_vma=False,
    )
```

time: 629 us -> 84.9 us (0.13)
  the two profiles are of different devices: /device:TPU:9 before, /device:TPU:0 now
where the time goes in v1:
time: 84.9 us; the launch traced here: 84.1 us
  Pallas kernels  43.3 us (51%)
  starting transfers between devices  15.1 us (18%)
  local copies, waits for them, and re-layouts  13.3 us (16%)
  waiting for transfers between devices  9.97 us (12%)
  other arithmetic  1.68 us (2%)
    pallas_call x1, Pallas kernels, shards(): pl.pallas_call(functools.partial(state_kernel, span=span, modes=modes, wi...  16.3 us
    pallas_call x1, Pallas kernels, shards(): pl.pallas_call(functools.partial(final_kernel, span=span, modes=modes, wi...  14.3 us
    pallas_call x1, Pallas kernels, shards(): pl.pallas_call(functools.partial(local_kernel, span=span, modes=modes), g...  10.9 us
    unnamed x28, local copies, waits for them, and re-layouts  10.6 us
    all_to_all x1, waiting for transfers between devices, shards(): moved = lax.all_to_all(ends, 'ctx', split_axis=0, concat_axis=0, tiled=True)  9.96 us
    all_to_all x1, starting transfers between devices, shards(): moved = lax.all_to_all(ends, 'ctx', split_axis=0, concat_axis=0, tiled=True)  9.46 us
    all_to_all x1, starting transfers between devices, shards(): lax.all_to_all(enter_few, 'ctx', split_axis=0, concat_axis=0, tiled=True)  3.31 us
    ppermute x1, starting transfers between devices, from_behind(): return lax.ppermute(shard, axis, pairs)  2.36 us
  transfers between devices with their start and end apart: 3, of which 1 were waited for; matrix products, arithmetic and copies ran while one was open for 3% of the time, Pallas kernels for 13%

profile of v1, /device:TPU:0, one launch (start us, length us, event | category | flops | bytes accessed | tf_op | source)
XLA Modules:
  0.0 84.1 jit_solution(15719692929886004282)
XLA Ops:
  0.6 0.0 copy-start
  0.6 0.0 copy-start.6
  0.7 1.0 %slice_bitcast_fusion.2 = bf16[1,2,8192]{2,1,0:T(2,128)(2,1)S(1)} fusion(bf16[128,8192]{1,0:T(8,128)(2,1)} %query_ref.1), kind=kLoop, calls=%fused_computation.4 | loop fusion | bytes 65536 | tf_op jit(solution)/shard_map/stack | solution.py:282
  1.7 1.0 %slice_bitcast_fusion = (bf16[1,2,8192]{2,1,0:T(2,128)(2,1)S(1)}, bf16[1,2,8192]{2,1,0:T(2,128)(2,1)S(1)}) fusion(bf16[128,8192]{1,0:T(8,128)(2,1)} %value_ref.1, bf16[128,8192]{1,0:T(8,128)(2,1)} %key_ref.1), kind=kLoop, calls=%fused_computation.2 | loop fusion | bytes 131072 | tf_op jit(solution)/shard_map/stack | solution.py:282
  2.7 0.2 pad_maximum_fusion
  2.9 2.4 %collective-permute-start = (bf16[3,2,8192]{2,1,0:T(2,128)(2,1)S(1)}, bf16[3,2,8192]{2,1,0:T(2,128)(2,1)S(1)}, u32[]{:S(2)}, u32[]{:S(2)}) collective-permute-start(bf16[3,2,8192]{2,1,0:T(2,128)(2,1)S(1)} %pad_maximum_fusion), channel_id=1, source_target_pairs={{0,1},{1,2},{2,3},{3,4},{4,5},{5,6},{6,7},{7,8},{8,9},{9,10},{10,1... | collective-permute-start | bytes 294920 | tf_op jit(solution)/shard_map/ppermute | solution.py:20
  5.3 1.5 %sqrt_multiply_fusion.weight_ref = f32[16,8192]{1,0:T(8,128)S(1)} fusion(f32[16,8192]{1,0:T(8,128)} %param.14, f32[16,8192]{1,0:T(8,128)} %rate_ref.5), kind=kLoop, calls=%fused_computation | loop fusion | flops 393216 | bytes 1572864 | tf_op jit(solution)/shard_map/mul | solution.py:284
  6.8 0.0 collective-permute-done.rim_ref
  6.8 0.0 copy-start.7
  6.8 0.6 copy-done.7
  7.4 0.0 copy-done
  7.4 0.0 copy-done.6
  7.4 0.0 copy-start.1
  7.4 1.6 %copy-done.1 = bf16[128,8192]{1,0:T(8,128)(2,1)S(1)} copy-done((bf16[128,8192]{1,0:T(8,128)(2,1)S(1)}, bf16[128,8192]{1,0:T(8,128)(2,1)}, u32[]{:S(2)}) %copy-start.1) | copy-done | bytes 2097176
  9.0 0.0 copy-start.8
  9.0 0.9 %copy-done.8 = bf16[3,2,8192]{2,1,0:T(2,128)(2,1)S(1)} copy-done((bf16[3,2,8192]{2,1,0:T(2,128)(2,1)S(1)}, bf16[3,2,8192]{2,1,0:T(2,128)(2,1)}, u32[]{:S(2)}) %copy-start.8) | copy-done | bytes 98328
  9.9 0.0 copy-start.12
  9.9 0.7 copy-done.12
  10.6 0.0 copy-start.2
  10.6 0.0 copy-start.13
  10.6 16.3 %block_states.1 = (bf16[128,8192]{1,0:T(8,128)(2,1)S(1)}, f32[128,8192]{1,0:T(8,128)}, bf16[32,16,256]{2,1,0:T(8,128)(2,1)S(1)}) custom-call(s32[1]{0:T(128)} %bitcast.base_ref, s32[16]{0:T(128)S(1)} %copy-done.12, bf16[128,8192]{1,0:T(8,128)(2,1)S(1)} %copy-done.1, bf16[128,8192]{1,0:T(8,128)(2,1)} %value_ref.1, bf16[3,2,8192]{2,1,0:T(2,128)(2,1)S(1)} %copy-done.8, ...), custom_call_target="tpu_custom_call" | custom-call | flops 65536000 | bytes 12582912 | tf_op jit(solution)/shard_map/block_states/pallas_call | solution.py:305
  26.8 0.0 copy-start.4
  26.8 1.3 %copy-done.4 = bf16[128,8192]{1,0:T(8,128)(2,1)} copy-done((bf16[128,8192]{1,0:T(8,128)(2,1)}, bf16[128,8192]{1,0:T(8,128)(2,1)S(1)}, u32[]{:S(2)}) %copy-start.4) | copy-done | bytes 2097176
  28.2 0.0 copy-start.10
  28.2 0.7 copy-done.10
  28.9 9.5 %all-to-all-start = ((bf16[32,16,256]{2,1,0:T(8,128)(2,1)}), bf16[32,16,256]{2,1,0:T(8,128)(2,1)}, u32[]{:S(2)}, u32[]{:S(2)}) async-start(bf16[32,16,256]{2,1,0:T(8,128)(2,1)} %copy-done.10), calls=%async_computation | async-start | bytes 524288 | tf_op jit(solution)/shard_map/all_to_all | solution.py:341
  38.3 0.6 constant_dynamic-slice_fusion.rate_ref
  38.9 10.0 %all-to-all-done.end_ref = bf16[32,16,256]{2,1,0:T(8,128)(2,1)} async-done(((bf16[32,16,256]{2,1,0:T(8,128)(2,1)}), bf16[32,16,256]{2,1,0:T(8,128)(2,1)}, u32[]{:S(2)}, u32[]{:S(2)}) %all-to-all-start) | async-done | bytes 262176 | tf_op jit(solution)/shard_map/all_to_all | solution.py:341
  48.9 1.8 %block_prefix.1 = bf16[32,16,256]{2,1,0:T(8,128)(2,1)} custom-call(s32[16]{0:T(128)} %len_ref.7, bf16[32,16,256]{2,1,0:T(8,128)(2,1)} %all-to-all-done.end_ref, f32[16,256]{1,0:T(8,128)} %constant_dynamic-slice_fusion.rate_ref), custom_call_target="tpu_custom_call" | custom-call | tf_op jit(solution)/shard_map/block_prefix/pallas_call | solution.py:343
  50.7 3.3 %all-to-all-start.1 = ((bf16[32,16,256]{2,1,0:T(8,128)(2,1)}), bf16[32,16,256]{2,1,0:T(8,128)(2,1)}, u32[]{:S(2)}, u32[]{:S(2)}) async-start(bf16[32,16,256]{2,1,0:T(8,128)(2,1)} %block_prefix.1), calls=%async_computation.1 | async-start | bytes 524288 | tf_op jit(solution)/shard_map/all_to_all | solution.py:351
  54.0 0.0 copy-done.2
  54.0 0.0 copy-done.13
  54.0 0.0 copy-start.5
  54.0 1.6 %copy-done.5 = bf16[128,8192]{1,0:T(8,128)(2,1)S(1)} copy-done((bf16[128,8192]{1,0:T(8,128)(2,1)S(1)}, bf16[128,8192]{1,0:T(8,128)(2,1)}, u32[]{:S(2)}) %copy-start.5) | copy-done | bytes 2097176
  55.6 0.0 copy-start.9
  55.6 0.9 %copy-done.9 = bf16[3,2,8192]{2,1,0:T(2,128)(2,1)S(1)} copy-done((bf16[3,2,8192]{2,1,0:T(2,128)(2,1)S(1)}, bf16[3,2,8192]{2,1,0:T(2,128)(2,1)}, u32[]{:S(2)}) %copy-start.9) | copy-done | bytes 98328
  56.5 10.9 %near_part.1 = (f32[128,8192]{1,0:T(8,128)}, f32[128,8192]{1,0:T(8,128)}) custom-call(s32[1]{0:T(128)} %bitcast.base_ref, s32[16]{0:T(128)S(1)} %copy-done.13, bf16[128,8192]{1,0:T(8,128)(2,1)S(1)} %copy-done.5, bf16[128,8192]{1,0:T(8,128)(2,1)S(1)} %copy-done.2, bf16[3,2,8192]{2,1,0:T(2,128)(2,1)S(1)} %copy-done.9, f32[3,3,8192]{2,1,0:T(4,128)S(1)} %copy-done.6, ...), custom_call_target="tpu_custom_call" | custom-call | flops 45875200 | bytes 12582912 | tf_op jit(solution)/shard_map/near_part/pallas_call | solution.py:327
  67.4 0.0 all-to-all-done.1.enter_ref
  67.4 0.0 copy-start.3
  67.4 1.6 %copy-done.3 = bf16[128,8192]{1,0:T(8,128)(2,1)S(1)} copy-done((bf16[128,8192]{1,0:T(8,128)(2,1)S(1)}, bf16[128,8192]{1,0:T(8,128)(2,1)}, u32[]{:S(2)}) %copy-start.3) | copy-done | bytes 2097176
  69.0 0.0 copy-start.11
  69.0 0.8 copy-done.11
  69.8 14.3 %far_part.1 = (bf16[128,8192]{1,0:T(8,128)(2,1)}, bf16[128,8192]{1,0:T(8,128)(2,1)}) custom-call(s32[1]{0:T(128)} %bitcast.base_ref, s32[16]{0:T(128)S(1)} %copy-done.13, f32[128,8192]{1,0:T(8,128)} %get-tuple-element.7.state_ref, bf16[32,16,256]{2,1,0:T(8,128)(2,1)} %all-to-all-done.1.enter_ref, f32[128,8192]{1,0:T(8,128)} %get-tuple-element.10.near_ref, ...), custom_call_target="tpu_custom_call" | custom-call | flops 58982400 | bytes 18874368 | tf_op jit(solution)/shard_map/far_part/pallas_call | solution.py:364
Async XLA Ops:
  0.6 6.8 %copy-start = (f32[16,8192]{1,0:T(8,128)S(1)}, f32[16,8192]{1,0:T(8,128)}, u32[]{:S(2)}) copy-start(f32[16,8192]{1,0:T(8,128)} %rate_ref.5) | copy-start | bytes 1572868
  0.6 6.8 %copy-start.6 = (f32[3,3,8192]{2,1,0:T(4,128)S(1)}, f32[3,3,8192]{2,1,0:T(4,128)}, u32[]{:S(2)}) copy-start(f32[3,3,8192]{2,1,0:T(4,128)} %taps_ref.3) | copy-start | bytes 884740
  2.9 3.9 %collective-permute-start = (bf16[3,2,8192]{2,1,0:T(2,128)(2,1)S(1)}, bf16[3,2,8192]{2,1,0:T(2,128)(2,1)S(1)}, u32[]{:S(2)}, u32[]{:S(2)}) collective-permute-start(bf16[3,2,8192]{2,1,0:T(2,128)(2,1)S(1)} %pad_maximum_fusion), channel_id=1, source_target_pairs={{0,1},{1,2},{2,3},{3,4},{4,5},{5,6},{6,7},{7,8},{8,9},{9,10},{10,1... | collective-permute-start | bytes 294920 | tf_op jit(solution)/shard_map/ppermute | solution.py:20
  6.8 0.6 copy-start.7
  7.4 1.6 %copy-start.1 = (bf16[128,8192]{1,0:T(8,128)(2,1)S(1)}, bf16[128,8192]{1,0:T(8,128)(2,1)}, u32[]{:S(2)}) copy-start(bf16[128,8192]{1,0:T(8,128)(2,1)} %key_ref.1) | copy-start | bytes 6291460
  9.0 0.9 %copy-start.8 = (bf16[3,2,8192]{2,1,0:T(2,128)(2,1)S(1)}, bf16[3,2,8192]{2,1,0:T(2,128)(2,1)}, u32[]{:S(2)}) copy-start(bf16[3,2,8192]{2,1,0:T(2,128)(2,1)} %copy-done.7) | copy-start | bytes 294916
  9.9 0.7 copy-start.12
  10.6 43.4 %copy-start.2 = (bf16[128,8192]{1,0:T(8,128)(2,1)S(1)}, bf16[128,8192]{1,0:T(8,128)(2,1)}, u32[]{:S(2)}) copy-start(bf16[128,8192]{1,0:T(8,128)(2,1)} %query_ref.1) | copy-start | bytes 6291460
  10.6 43.5 %copy-start.13 = (s32[16]{0:T(128)S(1)}, s32[16]{0:T(128)}, u32[]{:S(2)}) copy-start(s32[16]{0:T(128)} %len_ref.7) | copy-start | bytes 196
  26.8 1.3 %copy-start.4 = (bf16[128,8192]{1,0:T(8,128)(2,1)}, bf16[128,8192]{1,0:T(8,128)(2,1)S(1)}, u32[]{:S(2)}) copy-start(bf16[128,8192]{1,0:T(8,128)(2,1)S(1)} %get-tuple-element.9.gate_ref) | copy-start | bytes 6291460
  28.2 0.7 copy-start.10
  28.9 20.0 %all-to-all-start = ((bf16[32,16,256]{2,1,0:T(8,128)(2,1)}), bf16[32,16,256]{2,1,0:T(8,128)(2,1)}, u32[]{:S(2)}, u32[]{:S(2)}) async-start(bf16[32,16,256]{2,1,0:T(8,128)(2,1)} %copy-done.10), calls=%async_computation | async-start | bytes 524288 | tf_op jit(solution)/shard_map/all_to_all | solution.py:341
  50.7 16.7 %all-to-all-start.1 = ((bf16[32,16,256]{2,1,0:T(8,128)(2,1)}), bf16[32,16,256]{2,1,0:T(8,128)(2,1)}, u32[]{:S(2)}, u32[]{:S(2)}) async-start(bf16[32,16,256]{2,1,0:T(8,128)(2,1)} %block_prefix.1), calls=%async_computation.1 | async-start | bytes 524288 | tf_op jit(solution)/shard_map/all_to_all | solution.py:351
  54.0 1.6 %copy-start.5 = (bf16[128,8192]{1,0:T(8,128)(2,1)S(1)}, bf16[128,8192]{1,0:T(8,128)(2,1)}, u32[]{:S(2)}) copy-start(bf16[128,8192]{1,0:T(8,128)(2,1)} %copy-done.4) | copy-start | bytes 6291460
  55.6 0.9 %copy-start.9 = (bf16[3,2,8192]{2,1,0:T(2,128)(2,1)S(1)}, bf16[3,2,8192]{2,1,0:T(2,128)(2,1)}, u32[]{:S(2)}) copy-start(bf16[3,2,8192]{2,1,0:T(2,128)(2,1)} %copy-done.7) | copy-start | bytes 294916
  67.4 1.6 %copy-start.3 = (bf16[128,8192]{1,0:T(8,128)(2,1)S(1)}, bf16[128,8192]{1,0:T(8,128)(2,1)}, u32[]{:S(2)}) copy-start(bf16[128,8192]{1,0:T(8,128)(2,1)} %resid_ref.1) | copy-start | bytes 6291460
  69.0 0.8 copy-start.11

commit v2 on v1

--- a/solution.py
+++ b/solution.py
@@ -9,7 +9,8 @@
 
 SUBS = 8
 LANES = 128
-VMEM_LIMIT = 48 * 1024 * 1024
+VMEM_LIMIT = 60 * 1024 * 1024
+UNROLL = 2
 f32 = jnp.float32
 bf16 = jnp.bfloat16
 
@@ -39,6 +40,15 @@
     return jnp.where(cond, 1.0, 0.0).astype(f32)
 
 
+def each_tile(count, tile):
+    def group(i, carry):
+        for slot in range(UNROLL):
+            tile(i * UNROLL + slot, slot)
+        return carry
+
+    lax.fori_loop(0, count // UNROLL, group, 0)
+
+
 def row_of(ref, index):
     return jnp.broadcast_to(ref[pl.ds(index, 1), :], (SUBS, LANES))
 
@@ -66,7 +76,7 @@
 def state_kernel(
     base_ref, len_ref, key_ref, value_ref, rim_ref, taps_ref, rate_ref, weight_ref,
     gate_ref, state_ref, end_ref,
-    masks, wide_k, wide_v, tables, ends,
+    masks, wide_k, wide_v, all_tables, all_ends,
     *, span, modes, width,
 ):
     @pl.when(pl.program_id(0) == 0)
@@ -86,13 +96,14 @@
         masks[3, 2] = four
         masks[3, 3] = flag(sub >= 1)
 
-    def tile(i, carry):
+    def tile(i, slot):
         lane = pl.multiple_of(i * LANES, LANES)
         cols = pl.ds(lane, LANES)
+        tables, ends = all_tables.at[slot], all_ends.at[slot]
         keep_one = [masks[0, j] for j in range(span)]
         keep_two = [masks[1, j] for j in range(span)]
-        k_steps = spread(key_ref[:, cols], wide_k, span)
-        v_steps = spread(value_ref[:, cols], wide_v, span)
+        k_steps = spread(key_ref[:, cols], wide_k.at[slot], span)
+        v_steps = spread(value_ref[:, cols], wide_v.at[slot], span)
         k_short = short_conv(k_steps, rim_ref[1, :, cols], taps_ref[1, :, cols], keep_one, keep_two)
         v_short = short_conv(v_steps, rim_ref[2, :, cols], taps_ref[2, :, cols], keep_one, keep_two)
         gates = []
@@ -122,32 +133,24 @@
             end_ref[lax.div(lane, width), :, pl.ds(pl.multiple_of(lax.rem(lane, width), LANES), LANES)] = ends[...].astype(bf16)
         else:
             end_ref[:, cols] = ends[...].astype(bf16)
-        return carry
-
-    lax.fori_loop(0, key_ref.shape[1] // LANES, tile, 0)
-
-
-def local_kernel(
-    base_ref, len_ref, gate_ref, query_ref, rim_ref, taps_ref, rate_ref, weight_ref,
-    near_ref, short_ref,
-    masks, wide_q,
-    *, span, modes,
-):
+
+    each_tile(key_ref.shape[1] // LANES, tile)
+
+
+def keep_masks(base_ref, len_ref, masks, span):
+    rows, starts = doc_start_rows(len_ref, base_ref[0], span)
+    for j in range(span):
+        masks[0, j] = flag(starts[j] < rows + j)
+        masks[1, j] = flag(starts[j] < rows + (j - 1))
+
+
+def near_kernel(base_ref, len_ref, gate_ref, rate_ref, weight_ref, near_ref, masks, *, span, modes):
     @pl.when(pl.program_id(0) == 0)
     def _():
-        rows, starts = doc_start_rows(len_ref, base_ref[0], span)
-        for j in range(span):
-            masks[0, j] = flag(starts[j] < rows + j)
-            masks[1, j] = flag(starts[j] < rows + (j - 1))
-
-    def tile(i, carry):
+        keep_masks(base_ref, len_ref, masks, span)
+
+    def tile(i, slot):
         cols = pl.ds(pl.multiple_of(i * LANES, LANES), LANES)
-        keep_one = [masks[0, j] for j in range(span)]
-        keep_two = [masks[1, j] for j in range(span)]
-        q_steps = spread(query_ref[:, cols], wide_q, span)
-        q_short = short_conv(q_steps, rim_ref[0, :, cols], taps_ref[0, :, cols], keep_one, keep_two)
-        for j in range(span):
-            short_ref[pl.ds(j * SUBS, SUBS), cols] = q_short[j]
         decay = jnp.exp(-rate_ref[:, cols])
         term = weight_ref[:, cols]
         taps = []
@@ -163,15 +166,32 @@
         for j in range(span):
             if j % 2 == 0:
                 pair = gate_ref[pl.ds(j * SUBS, 2 * SUBS), cols].astype(f32)
-            live = [g * keep_one[j] for g in live]
+            keep = masks[0, j]
+            live = [g * keep for g in live]
             live.append(pair[(j % 2) * SUBS : (j % 2 + 1) * SUBS])
             total = taps[0] * live[j]
             for lag in range(1, j + 1):
                 total = total + taps[lag] * live[j - lag]
             near_ref[pl.ds(j * SUBS, SUBS), cols] = total
-        return carry
-
-    lax.fori_loop(0, gate_ref.shape[1] // LANES, tile, 0)
+
+    each_tile(gate_ref.shape[1] // LANES, tile)
+
+
+def query_kernel(base_ref, len_ref, query_ref, rim_ref, taps_ref, short_ref, masks, wide_q, *, span):
+    @pl.when(pl.program_id(0) == 0)
+    def _():
+        keep_masks(base_ref, len_ref, masks, span)
+
+    def tile(i, slot):
+        cols = pl.ds(pl.multiple_of(i * LANES, LANES), LANES)
+        keep_one = [masks[0, j] for j in range(span)]
+        keep_two = [masks[1, j] for j in range(span)]
+        q_steps = spread(query_ref[:, cols], wide_q.at[slot], span)
+        q_short = short_conv(q_steps, rim_ref[0, :, cols], taps_ref[0, :, cols], keep_one, keep_two)
+        for j in range(span):
+            short_ref[pl.ds(j * SUBS, SUBS), cols] = q_short[j]
+
+    each_tile(query_ref.shape[1] // LANES, tile)
 
 
 def prefix_kernel(len_ref, end_ref, rate_ref, enter_ref, through, *, span):
@@ -196,9 +216,9 @@
     span, modes, width, channels,
 ):
     if channels:
-        hidden_ref, normed_ref, masks, tables, sums, whole = refs
+        hidden_ref, normed_ref, masks, all_tables, sums, whole = refs
     else:
-        hidden_ref, wide_ref, sum_ref, masks, tables, sums, whole = refs
+        hidden_ref, wide_ref, sum_ref, masks, all_tables, sums, whole = refs
     step = pl.program_id(0)
     tiles = resid_ref.shape[1] // LANES
 
@@ -210,9 +230,10 @@
         masks[1, 0] = flag(starts[0] < base_ref[0])
         sums[...] = jnp.zeros(sums.shape, f32)
 
-    def tile(i, carry):
+    def tile(i, slot):
         lane = pl.multiple_of(i * LANES, LANES)
         cols = pl.ds(lane, LANES)
+        tables = all_tables.at[slot]
         if width:
             enter = enter_ref[lax.div(lane, width), :, pl.ds(pl.multiple_of(lax.rem(lane, width), LANES), LANES)]
         else:
@@ -244,9 +265,8 @@
         if not channels:
             wide_ref[:, cols] = hidden
         sums[...] = sums[...] + hidden * hidden
-        return carry
-
-    lax.fori_loop(0, tiles, tile, 0)
+
+    each_tile(tiles, tile)
 
     @pl.when(step == pl.num_programs(0) - 1)
     def _():
@@ -314,31 +334,44 @@
         ],
         scratch_shapes=[
             pltpu.VMEM((4, span) + tile_shape, f32),
-            pltpu.VMEM((tok_rows, LANES), f32),
-            pltpu.VMEM((tok_rows, LANES), f32),
-            pltpu.VMEM((5, modes, LANES), f32),
-            pltpu.VMEM((modes, LANES), f32),
+            pltpu.VMEM((UNROLL, tok_rows, LANES), f32),
+            pltpu.VMEM((UNROLL, tok_rows, LANES), f32),
+            pltpu.VMEM((UNROLL, 5, modes, LANES), f32),
+            pltpu.VMEM((UNROLL, modes, LANES), f32),
         ],
         compiler_params=params,
         cost_estimate=cost(1000, 12 * tok_rows * chans),
         name="block_states",
     )(base, doc_lengths, key_in, value_in, rim_rows, short_taps, decay_rate, weight)
 
-    near, q_short = pl.pallas_call(
-        functools.partial(local_kernel, span=span, modes=modes),
+    near = pl.pallas_call(
+        functools.partial(near_kernel, span=span, modes=modes),
         grid=(steps,),
-        in_specs=[smem, smem, rows_spec(tok_rows), rows_spec(tok_rows), rim_spec, taps_spec, rows_spec(modes), rows_spec(modes)],
-        out_specs=[rows_spec(tok_rows), rows_spec(tok_rows)],
-        out_shape=[jax.ShapeDtypeStruct((tok_rows, chans), f32), jax.ShapeDtypeStruct((tok_rows, chans), f32)],
-        scratch_shapes=[pltpu.VMEM((2, span) + tile_shape, f32), pltpu.VMEM((tok_rows, LANES), f32)],
+        in_specs=[smem, smem, rows_spec(tok_rows), rows_spec(modes), rows_spec(modes)],
+        out_specs=rows_spec(tok_rows),
+        out_shape=jax.ShapeDtypeStruct((tok_rows, chans), f32),
+        scratch_shapes=[pltpu.VMEM((2, span) + tile_shape, f32)],
         compiler_params=params,
-        cost_estimate=cost(700, 12 * tok_rows * chans),
+        cost_estimate=cost(600, 7 * tok_rows * chans),
         name="near_part",
-    )(base, doc_lengths, gates, query_in, rim_rows, short_taps, decay_rate, weight)
+    )(base, doc_lengths, gates, decay_rate, weight)
+
+    q_short = pl.pallas_call(
+        functools.partial(query_kernel, span=span),
+        grid=(steps,),
+        in_specs=[smem, smem, rows_spec(tok_rows), rim_spec, taps_spec],
+        out_specs=rows_spec(tok_rows),
+        out_shape=jax.ShapeDtypeStruct((tok_rows, chans), f32),
+        scratch_shapes=[pltpu.VMEM((2, span) + tile_shape, f32), pltpu.VMEM((UNROLL, tok_rows, LANES), f32)],
+        compiler_params=params,
+        cost_estimate=cost(200, 6 * tok_rows * chans),
+        name="query_part",
+    )(base, doc_lengths, query_in, rim_rows, short_taps)
 
     if not width:
         ends = ends.reshape(modes, blocks, few).transpose(1, 0, 2)
     moved = lax.all_to_all(ends, "ctx", split_axis=0, concat_axis=0, tiled=True)
+    moved, near = lax.optimization_barrier((moved, near))
     rate_few = lax.dynamic_slice_in_dim(decay_rate, ctx_index * few, few, 1)
     enter_few = pl.pallas_call(
         functools.partial(prefix_kernel, span=tok_rows),
@@ -372,7 +405,7 @@
         out_shape=out_shape,
         scratch_shapes=[
             pltpu.VMEM((2, span) + tile_shape, f32),
-            pltpu.VMEM((3, modes, LANES), f32),
+            pltpu.VMEM((UNROLL, 3, modes, LANES), f32),
             pltpu.VMEM((tok_rows, LANES), f32),
             pltpu.VMEM((chans // LANES, tok_rows, LANES), f32),
         ],

time: 84.9 us -> 76.6 us (0.902)
  local copies, waits for them, and re-layouts: 13.3 us -> 5.37 us
  waiting for transfers between devices: 9.97 us -> 3.6 us
  Pallas kernels: 43.3 us -> 47.1 us
  starting transfers between devices: 15.1 us -> 16.4 us
    all_to_all x1, waiting for transfers between devices: 9.96 us -> 0.32 us  [shards(): moved = lax.all_to_all(ends, 'ctx', split_axis=0, concat_axis=0, tiled=True)]
    unnamed x28 -> x6, local copies, waits for them, and re-layouts: 10.6 us -> 2.06 us
    pallas_call x1 -> x2, Pallas kernels: 10.9 us -> 16.3 us  [the longest x1 8.95 us: shards(): pl.pallas_call(functools.partial(near_kernel, span=span, modes=modes), gr...]
    all_to_all x1, waiting for transfers between devices: 0.01 us -> 3.27 us  [shards(): lax.all_to_all(enter_few, 'ctx', split_axis=0, concat_axis=0, tiled=True)]
    all_to_all x1, starting transfers between devices: 3.31 us -> 5.51 us  [shards(): lax.all_to_all(enter_few, 'ctx', split_axis=0, concat_axis=0, tiled=True)]
    pallas_call x1, Pallas kernels: 16.3 us -> 14.9 us  [shards(): pl.pallas_call(functools.partial(state_kernel, span=span, modes=modes, wi...]
    all_to_all x1, starting transfers between devices: 9.46 us -> 8.53 us  [shards(): moved = lax.all_to_all(ends, 'ctx', split_axis=0, concat_axis=0, tiled=True)]
  transfers between devices with their start and end apart: 3 -> 3, of which waited for: 1 -> 2; matrix products, arithmetic and copies ran while one was open for 3% -> 5% of each run, Pallas kernels for 13% -> 21%
where the time goes in v2:
time: 76.6 us; the launch traced here: 75.7 us
  Pallas kernels  47.1 us (61%)
  starting transfers between devices  16.4 us (21%)
  local copies, waits for them, and re-layouts  5.37 us (7%)
  waiting for transfers between devices  3.6 us (5%)
  other arithmetic  2.49 us (3%)
    pallas_call x1, Pallas kernels, shards(): pl.pallas_call(functools.partial(state_kernel, span=span, modes=modes, wi...  14.9 us
    pallas_call x1, Pallas kernels, shards(): pl.pallas_call(functools.partial(final_kernel, span=span, modes=modes, wi...  14.2 us
    pallas_call x1, Pallas kernels, shards(): pl.pallas_call(functools.partial(near_kernel, span=span, modes=modes), gr...  8.95 us
    all_to_all x1, starting transfers between devices, shards(): moved = lax.all_to_all(ends, 'ctx', split_axis=0, concat_axis=0, tiled=True)  8.53 us
    pallas_call x1, Pallas kernels, shards(): pl.pallas_call(functools.partial(query_kernel, span=span), grid=(steps,),...  7.32 us
    all_to_all x1, starting transfers between devices, shards(): lax.all_to_all(enter_few, 'ctx', split_axis=0, concat_axis=0, tiled=True)  5.51 us
    all_to_all x1, waiting for transfers between devices, shards(): lax.all_to_all(enter_few, 'ctx', split_axis=0, concat_axis=0, tiled=True)  3.27 us
    ppermute x1, starting transfers between devices, from_behind(): return lax.ppermute(shard, axis, pairs)  2.36 us
  transfers between devices with their start and end apart: 3, of which 2 were waited for; matrix products, arithmetic and copies ran while one was open for 5% of the time, Pallas kernels for 21%

profile of v2, /device:TPU:0, one launch (start us, length us, event | category | flops | bytes accessed | tf_op | source)
XLA Modules:
  0.0 75.7 jit_solution(13886073054186551637)
XLA Ops:
  0.6 0.9 %slice_bitcast_fusion.2 = bf16[1,2,8192]{2,1,0:T(2,128)(2,1)S(1)} fusion(bf16[128,8192]{1,0:T(8,128)(2,1)} %query_ref.1), kind=kLoop, calls=%fused_computation.4 | loop fusion | bytes 65536 | tf_op jit(solution)/shard_map/stack | solution.py:302
  1.6 1.0 %slice_bitcast_fusion = (bf16[1,2,8192]{2,1,0:T(2,128)(2,1)S(1)}, bf16[1,2,8192]{2,1,0:T(2,128)(2,1)S(1)}) fusion(bf16[128,8192]{1,0:T(8,128)(2,1)} %value_ref.1, bf16[128,8192]{1,0:T(8,128)(2,1)} %key_ref.1), kind=kLoop, calls=%fused_computation.2 | loop fusion | bytes 131072 | tf_op jit(solution)/shard_map/stack | solution.py:302
  2.6 0.2 pad_maximum_fusion
  2.8 2.4 %collective-permute-start = (bf16[3,2,8192]{2,1,0:T(2,128)(2,1)S(1)}, bf16[3,2,8192]{2,1,0:T(2,128)(2,1)S(1)}, u32[]{:S(2)}, u32[]{:S(2)}) collective-permute-start(bf16[3,2,8192]{2,1,0:T(2,128)(2,1)S(1)} %pad_maximum_fusion), channel_id=1, source_target_pairs={{0,1},{1,2},{2,3},{3,4},{4,5},{5,6},{6,7},{7,8},{8,9},{9,10},{10,1... | collective-permute-start | bytes 294920 | tf_op jit(solution)/shard_map/ppermute | solution.py:21
  5.2 2.3 %sqrt_multiply_fusion.weight_ref = f32[16,8192]{1,0:T(8,128)} fusion(f32[16,8192]{1,0:T(8,128)} %param.14, f32[16,8192]{1,0:T(8,128)} %rate_ref.5), kind=kLoop, calls=%fused_computation | loop fusion | flops 393216 | bytes 1572864 | tf_op jit(solution)/shard_map/mul | solution.py:304
  7.5 0.0 collective-permute-done.rim_ref
  7.5 0.0 copy-start.2
  7.5 0.6 copy-done.2
  8.1 14.9 %block_states.1 = (bf16[128,8192]{1,0:T(8,128)(2,1)}, f32[128,8192]{1,0:T(8,128)}, bf16[32,16,256]{2,1,0:T(8,128)(2,1)}) custom-call(s32[1]{0:T(128)} %bitcast.base_ref, s32[16]{0:T(128)} %len_ref.9, bf16[128,8192]{1,0:T(8,128)(2,1)} %key_ref.1, bf16[128,8192]{1,0:T(8,128)(2,1)} %value_ref.1, bf16[3,2,8192]{2,1,0:T(2,128)(2,1)} %copy-done.2, ...), custom_call_target="tpu_custom_call" | custom-call | flops 65536000 | bytes 12582912 | tf_op jit(solution)/shard_map/block_states/pallas_call | solution.py:325
  23.0 8.5 %all-to-all-start = ((bf16[32,16,256]{2,1,0:T(8,128)(2,1)}), bf16[32,16,256]{2,1,0:T(8,128)(2,1)S(1)}, u32[]{:S(2)}, u32[]{:S(2)}) async-start(bf16[32,16,256]{2,1,0:T(8,128)(2,1)} %get-tuple-element.8), calls=%async_computation | async-start | bytes 524288 | tf_op jit(solution)/shard_map/all_to_all | solution.py:373
  31.6 1.3 %constant_dynamic-slice_fusion.rate_ref = f32[16,256]{1,0:T(8,128)} fusion(f32[16,8192]{1,0:T(8,128)} %rate_ref.5, s32[]{:T(128)S(6)} %select_n.3), kind=kLoop, calls=%fused_computation.5 | loop fusion | bytes 32772 | tf_op jit(solution)/shard_map/dynamic_slice | solution.py:375
  32.9 8.9 %near_part.1.near_ref = f32[128,8192]{1,0:T(8,128)} custom-call(s32[1]{0:T(128)} %bitcast.base_ref, s32[16]{0:T(128)} %len_ref.9, bf16[128,8192]{1,0:T(8,128)(2,1)} %get-tuple-element.9.gate_ref, f32[16,8192]{1,0:T(8,128)} %rate_ref.5, f32[16,8192]{1,0:T(8,128)} %sqrt_multiply_fusion.weight_ref), custom_call_target="tpu_custom_call" | custom-call | flops 39321600 | bytes 7340032 | tf_op jit(solution)/shard_map/near_part/pallas_call | solution.py:347
  41.9 0.3 all-to-all-done.end_ref
  42.2 0.0 copy-start.1
  42.2 0.7 copy-done.1
  42.9 1.8 %block_prefix.1 = bf16[32,16,256]{2,1,0:T(8,128)(2,1)} custom-call(s32[16]{0:T(128)} %len_ref.9, bf16[32,16,256]{2,1,0:T(8,128)(2,1)} %copy-done.1, f32[16,256]{1,0:T(8,128)} %constant_dynamic-slice_fusion.rate_ref), custom_call_target="tpu_custom_call" | custom-call | tf_op jit(solution)/shard_map/block_prefix/pallas_call | solution.py:376
  44.7 5.5 %all-to-all-start.1 = ((bf16[32,16,256]{2,1,0:T(8,128)(2,1)}), bf16[32,16,256]{2,1,0:T(8,128)(2,1)S(1)}, u32[]{:S(2)}, u32[]{:S(2)}) async-start(bf16[32,16,256]{2,1,0:T(8,128)(2,1)} %block_prefix.1), calls=%async_computation.1 | async-start | bytes 524288 | tf_op jit(solution)/shard_map/all_to_all | solution.py:384
  50.2 7.3 %query_part.1.short_ref = f32[128,8192]{1,0:T(8,128)} custom-call(s32[1]{0:T(128)} %bitcast.base_ref, s32[16]{0:T(128)} %len_ref.9, bf16[128,8192]{1,0:T(8,128)(2,1)} %query_ref.1, bf16[3,2,8192]{2,1,0:T(2,128)(2,1)} %copy-done.2, f32[3,3,8192]{2,1,0:T(4,128)} %taps_ref.3), custom_call_target="tpu_custom_call" | custom-call | flops 13107200 | bytes 6291456 | tf_op jit(solution)/shard_map/query_part/pallas_call | solution.py:359
  57.5 3.3 %all-to-all-done.1.enter_ref = bf16[32,16,256]{2,1,0:T(8,128)(2,1)S(1)} async-done(((bf16[32,16,256]{2,1,0:T(8,128)(2,1)}), bf16[32,16,256]{2,1,0:T(8,128)(2,1)S(1)}, u32[]{:S(2)}, u32[]{:S(2)}) %all-to-all-start.1) | async-done | bytes 262176 | tf_op jit(solution)/shard_map/all_to_all | solution.py:384
  60.8 0.0 copy-start
  60.8 0.7 copy-done
  61.5 14.2 %far_part.1 = (bf16[128,8192]{1,0:T(8,128)(2,1)}, bf16[128,8192]{1,0:T(8,128)(2,1)}) custom-call(s32[1]{0:T(128)} %bitcast.base_ref, s32[16]{0:T(128)} %len_ref.9, f32[128,8192]{1,0:T(8,128)} %get-tuple-element.7.state_ref, bf16[32,16,256]{2,1,0:T(8,128)(2,1)} %copy-done, f32[128,8192]{1,0:T(8,128)} %near_part.1.near_ref, f32[128,8192]{1,0:T(8,128)} %query_part.1.short_ref, ...), custom_call_target="tpu_custom_call" | custom-call | flops 58982400 | bytes 18874368 | tf_op jit(solution)/shard_map/far_part/pallas_call | solution.py:397
Async XLA Ops:
  2.8 4.7 %collective-permute-start = (bf16[3,2,8192]{2,1,0:T(2,128)(2,1)S(1)}, bf16[3,2,8192]{2,1,0:T(2,128)(2,1)S(1)}, u32[]{:S(2)}, u32[]{:S(2)}) collective-permute-start(bf16[3,2,8192]{2,1,0:T(2,128)(2,1)S(1)} %pad_maximum_fusion), channel_id=1, source_target_pairs={{0,1},{1,2},{2,3},{3,4},{4,5},{5,6},{6,7},{7,8},{8,9},{9,10},{10,1... | collective-permute-start | bytes 294920 | tf_op jit(solution)/shard_map/ppermute | solution.py:21
  7.5 0.6 copy-start.2
  23.0 19.1 %all-to-all-start = ((bf16[32,16,256]{2,1,0:T(8,128)(2,1)}), bf16[32,16,256]{2,1,0:T(8,128)(2,1)S(1)}, u32[]{:S(2)}, u32[]{:S(2)}) async-start(bf16[32,16,256]{2,1,0:T(8,128)(2,1)} %get-tuple-element.8), calls=%async_computation | async-start | bytes 524288 | tf_op jit(solution)/shard_map/all_to_all | solution.py:373
  42.2 0.7 copy-start.1
  44.7 16.1 %all-to-all-start.1 = ((bf16[32,16,256]{2,1,0:T(8,128)(2,1)}), bf16[32,16,256]{2,1,0:T(8,128)(2,1)S(1)}, u32[]{:S(2)}, u32[]{:S(2)}) async-start(bf16[32,16,256]{2,1,0:T(8,128)(2,1)} %block_prefix.1), calls=%async_computation.1 | async-start | bytes 524288 | tf_op jit(solution)/shard_map/all_to_all | solution.py:384
  60.8 0.7 copy-start

commit v3 on v2

--- a/solution.py
+++ b/solution.py
@@ -9,8 +9,8 @@
 
 SUBS = 8
 LANES = 128
-VMEM_LIMIT = 60 * 1024 * 1024
-UNROLL = 2
+VMEM_LIMIT = 63 * 1024 * 1024
+PAIR = 2
 f32 = jnp.float32
 bf16 = jnp.bfloat16
 
@@ -40,22 +40,32 @@
     return jnp.where(cond, 1.0, 0.0).astype(f32)
 
 
-def each_tile(count, tile):
+def each_pair(count, pair):
     def group(i, carry):
-        for slot in range(UNROLL):
-            tile(i * UNROLL + slot, slot)
+        pair(i)
         return carry
 
-    lax.fori_loop(0, count // UNROLL, group, 0)
+    lax.fori_loop(0, count // PAIR, group, 0)
+
+
+def order_matrix(span, back):
+    size = SUBS * span
+    rows = lax.broadcasted_iota(jnp.int32, (size, size), 1 if back else 0)
+    cols = lax.broadcasted_iota(jnp.int32, (size, size), 0 if back else 1)
+    source = (rows % SUBS) * span + rows // SUBS
+    return flag(cols == source).astype(bf16)
+
+
+def reorder(order, x):
+    return jnp.dot(order[...], x, preferred_element_type=f32)
+
+
+def step_rows(x, slot, span):
+    return [x[j * SUBS : (j + 1) * SUBS, slot * LANES : (slot + 1) * LANES] for j in range(span)]
 
 
 def row_of(ref, index):
     return jnp.broadcast_to(ref[pl.ds(index, 1), :], (SUBS, LANES))
-
-
-def spread(x, scratch, span):
-    scratch[...] = x.astype(f32)
-    return [scratch[pl.ds(j, SUBS, stride=span), :] for j in range(span)]
 
 
 def short_conv(steps, rim, taps, keep_one, keep_two):
@@ -76,11 +86,12 @@
 def state_kernel(
     base_ref, len_ref, key_ref, value_ref, rim_ref, taps_ref, rate_ref, weight_ref,
     gate_ref, state_ref, end_ref,
-    masks, wide_k, wide_v, all_tables, all_ends,
+    masks, order, all_tables, all_ends,
     *, span, modes, width,
 ):
     @pl.when(pl.program_id(0) == 0)
     def _():
+        order[...] = order_matrix(span, False)
         rows, starts = doc_start_rows(len_ref, base_ref[0], span)
         for j in range(span):
             masks[0, j] = flag(starts[j] < rows + j)
@@ -96,14 +107,21 @@
         masks[3, 2] = four
         masks[3, 3] = flag(sub >= 1)
 
-    def tile(i, slot):
+    def pair(i):
+        both = pl.ds(pl.multiple_of(i * (PAIR * LANES), PAIR * LANES), PAIR * LANES)
+        k_rows = reorder(order, key_ref[:, both])
+        v_rows = reorder(order, value_ref[:, both])
+        for slot in range(PAIR):
+            tile(i * PAIR + slot, slot, k_rows, v_rows)
+
+    def tile(i, slot, k_rows, v_rows):
         lane = pl.multiple_of(i * LANES, LANES)
         cols = pl.ds(lane, LANES)
         tables, ends = all_tables.at[slot], all_ends.at[slot]
         keep_one = [masks[0, j] for j in range(span)]
         keep_two = [masks[1, j] for j in range(span)]
-        k_steps = spread(key_ref[:, cols], wide_k.at[slot], span)
-        v_steps = spread(value_ref[:, cols], wide_v.at[slot], span)
+        k_steps = step_rows(k_rows, slot, span)
+        v_steps = step_rows(v_rows, slot, span)
         k_short = short_conv(k_steps, rim_ref[1, :, cols], taps_ref[1, :, cols], keep_one, keep_two)
         v_short = short_conv(v_steps, rim_ref[2, :, cols], taps_ref[2, :, cols], keep_one, keep_two)
         gates = []
@@ -134,7 +152,13 @@
         else:
             end_ref[:, cols] = ends[...].astype(bf16)
 
-    each_tile(key_ref.shape[1] // LANES, tile)
+    each_pair(key_ref.shape[1] // LANES, pair)
+
+
+def tail_kernel(query_ref, key_ref, value_ref, tail_ref):
+    for i, ref in enumerate((query_ref, key_ref, value_ref)):
+        rows = ref[...].astype(f32)
+        tail_ref[i] = rows[rows.shape[0] - 2 :].astype(bf16)
 
 
 def keep_masks(base_ref, len_ref, masks, span):
@@ -149,7 +173,7 @@
     def _():
         keep_masks(base_ref, len_ref, masks, span)
 
-    def tile(i, slot):
+    def tile(i):
         cols = pl.ds(pl.multiple_of(i * LANES, LANES), LANES)
         decay = jnp.exp(-rate_ref[:, cols])
         term = weight_ref[:, cols]
@@ -174,24 +198,35 @@
                 total = total + taps[lag] * live[j - lag]
             near_ref[pl.ds(j * SUBS, SUBS), cols] = total
 
-    each_tile(gate_ref.shape[1] // LANES, tile)
-
-
-def query_kernel(base_ref, len_ref, query_ref, rim_ref, taps_ref, short_ref, masks, wide_q, *, span):
+    def pair(i):
+        for slot in range(PAIR):
+            tile(i * PAIR + slot)
+
+    each_pair(gate_ref.shape[1] // LANES, pair)
+
+
+def query_kernel(base_ref, len_ref, query_ref, rim_ref, taps_ref, short_ref, masks, order, *, span):
     @pl.when(pl.program_id(0) == 0)
     def _():
+        order[...] = order_matrix(span, False)
         keep_masks(base_ref, len_ref, masks, span)
 
-    def tile(i, slot):
+    def pair(i):
+        both = pl.ds(pl.multiple_of(i * (PAIR * LANES), PAIR * LANES), PAIR * LANES)
+        q_rows = reorder(order, query_ref[:, both])
+        for slot in range(PAIR):
+            tile(i * PAIR + slot, slot, q_rows)
+
+    def tile(i, slot, q_rows):
         cols = pl.ds(pl.multiple_of(i * LANES, LANES), LANES)
         keep_one = [masks[0, j] for j in range(span)]
         keep_two = [masks[1, j] for j in range(span)]
-        q_steps = spread(query_ref[:, cols], wide_q.at[slot], span)
+        q_steps = step_rows(q_rows, slot, span)
         q_short = short_conv(q_steps, rim_ref[0, :, cols], taps_ref[0, :, cols], keep_one, keep_two)
         for j in range(span):
             short_ref[pl.ds(j * SUBS, SUBS), cols] = q_short[j]
 
-    each_tile(query_ref.shape[1] // LANES, tile)
+    each_pair(query_ref.shape[1] // LANES, pair)
 
 
 def prefix_kernel(len_ref, end_ref, rate_ref, enter_ref, through, *, span):
@@ -216,24 +251,37 @@
     span, modes, width, channels,
 ):
     if channels:
-        hidden_ref, normed_ref, masks, all_tables, sums, whole = refs
+        hidden_ref, normed_ref, masks, order, order_back, rounded, all_tables, sums, whole = refs
     else:
-        hidden_ref, wide_ref, sum_ref, masks, all_tables, sums, whole = refs
+        hidden_ref, wide_ref, sum_ref, masks, order, order_back, rounded, all_tables, sums, whole = refs
     step = pl.program_id(0)
     tiles = resid_ref.shape[1] // LANES
 
     @pl.when(step == 0)
     def _():
+        order[...] = order_matrix(span, False)
+        order_back[...] = order_matrix(span, True)
         rows, starts = doc_start_rows(len_ref, base_ref[0], span)
         for j in range(span):
             masks[0, j] = flag(starts[j] < rows)
         masks[1, 0] = flag(starts[0] < base_ref[0])
         sums[...] = jnp.zeros(sums.shape, f32)
 
-    def tile(i, slot):
+    def pair(i):
+        both = pl.ds(pl.multiple_of(i * (PAIR * LANES), PAIR * LANES), PAIR * LANES)
+        resid_rows = reorder(order, resid_ref[:, both])
+        squares = [None] * span
+        for slot in range(PAIR):
+            squares = tile(i * PAIR + slot, slot, resid_rows, squares)
+        for j in range(span):
+            sums[pl.ds(j * SUBS, SUBS), :] += squares[j]
+        hidden_ref[:, both] = reorder(order_back, rounded[...]).astype(bf16)
+
+    def tile(i, slot, resid_rows, squares):
         lane = pl.multiple_of(i * LANES, LANES)
         cols = pl.ds(lane, LANES)
         tables = all_tables.at[slot]
+        resid_steps = step_rows(resid_rows, slot, span)
         if width:
             enter = enter_ref[lax.div(lane, width), :, pl.ds(pl.multiple_of(lax.rem(lane, width), LANES), LANES)]
         else:
@@ -258,29 +306,35 @@
                 total = [total[m] + total[m + 1] for m in range(0, len(total), 2)]
             conv = near_ref[pl.ds(j * SUBS, SUBS), cols] + total[0] * masks[0, j]
             conv = conv.astype(bf16).astype(f32)
-            whole[tile_at, pl.ds(j, SUBS, stride=span), :] = short_ref[pl.ds(j * SUBS, SUBS), cols] * conv
-        hidden = whole[tile_at] + resid_ref[:, cols].astype(f32)
-        whole[tile_at] = hidden
-        hidden_ref[:, cols] = hidden.astype(bf16)
-        if not channels:
-            wide_ref[:, cols] = hidden
-        sums[...] = sums[...] + hidden * hidden
-
-    each_tile(tiles, tile)
+            hidden = resid_steps[j] + short_ref[pl.ds(j * SUBS, SUBS), cols] * conv
+            if channels:
+                whole[tile_at, pl.ds(j * SUBS, SUBS), :] = hidden
+            else:
+                wide_ref[pl.ds(j * SUBS, SUBS), cols] = hidden
+            squares[j] = hidden * hidden if slot == 0 else squares[j] + hidden * hidden
+            if j % 2 == 1:
+                couple = jnp.concatenate([last, hidden], axis=0).astype(bf16)
+                rounded[pl.ds((j - 1) * SUBS, 2 * SUBS), pl.ds(slot * LANES, LANES)] = couple
+            last = hidden
+        return squares
+
+    each_pair(tiles, pair)
 
     @pl.when(step == pl.num_programs(0) - 1)
     def _():
         if channels:
             inverse = lax.rsqrt(jnp.sum(sums[...], axis=1, keepdims=True) / channels + 1e-06)
-            inverse = jnp.broadcast_to(inverse, sums.shape)
-            sums[...] = inverse
-
-            def scale(i, carry):
-                cols = pl.ds(pl.multiple_of(i * LANES, LANES), LANES)
-                normed_ref[:, cols] = (whole[i] * sums[...] * gain_ref[:, cols]).astype(bf16)
-                return carry
-
-            lax.fori_loop(0, normed_ref.shape[1] // LANES, scale, 0)
+            sums[...] = jnp.broadcast_to(inverse, sums.shape)
+
+            def scale(i):
+                both = pl.ds(pl.multiple_of(i * (PAIR * LANES), PAIR * LANES), PAIR * LANES)
+                for slot in range(PAIR):
+                    cols = pl.ds(pl.multiple_of((i * PAIR + slot) * LANES, LANES), LANES)
+                    normed = whole[i * PAIR + slot] * sums[...] * gain_ref[:, cols]
+                    rounded[:, pl.ds(slot * LANES, LANES)] = normed.astype(bf16)
+                normed_ref[:, both] = reorder(order_back, rounded[...]).astype(bf16)
+
+            each_pair(normed_ref.shape[1] // LANES, scale)
         else:
             sum_ref[...] = sums[...]
 
@@ -299,7 +353,17 @@
     steps = chans // chunk
     ctx_index = lax.axis_index("ctx")
     base = (ctx_index * tok_rows).astype(jnp.int32).reshape(1)
-    tails = jnp.stack([query_in[tok_rows - 2 :], key_in[tok_rows - 2 :], value_in[tok_rows - 2 :]])
+    params = pltpu.CompilerParams(vmem_limit_bytes=VMEM_LIMIT)
+    last_rows = pl.BlockSpec((16, chans), lambda i: (tok_rows // 16 - 1, 0))
+    tails = pl.pallas_call(
+        tail_kernel,
+        grid=(1,),
+        in_specs=[last_rows] * 3,
+        out_specs=pl.BlockSpec((3, 2, chans), lambda i: (0, 0, 0)),
+        out_shape=jax.ShapeDtypeStruct((3, 2, chans), bf16),
+        compiler_params=params,
+        name="tails",
+    )(query_in, key_in, value_in)
     rim_rows = from_behind(tails, "ctx", 1)
     weight = residues * jnp.sqrt(-jnp.expm1(-2.0 * decay_rate))
 
@@ -334,10 +398,9 @@
         ],
         scratch_shapes=[
             pltpu.VMEM((4, span) + tile_shape, f32),
-            pltpu.VMEM((UNROLL, tok_rows, LANES), f32),
-            pltpu.VMEM((UNROLL, tok_rows, LANES), f32),
-            pltpu.VMEM((UNROLL, 5, modes, LANES), f32),
-            pltpu.VMEM((UNROLL, modes, LANES), f32),
+            pltpu.VMEM((tok_rows, tok_rows), bf16),
+            pltpu.VMEM((PAIR, 5, modes, LANES), f32),
+            pltpu.VMEM((PAIR, modes, LANES), f32),
         ],
         compiler_params=params,
         cost_estimate=cost(1000, 12 * tok_rows * chans),
@@ -362,7 +425,7 @@
         in_specs=[smem, smem, rows_spec(tok_rows), rim_spec, taps_spec],
         out_specs=rows_spec(tok_rows),
         out_shape=jax.ShapeDtypeStruct((tok_rows, chans), f32),
-        scratch_shapes=[pltpu.VMEM((2, span) + tile_shape, f32), pltpu.VMEM((UNROLL, tok_rows, LANES), f32)],
+        scratch_shapes=[pltpu.VMEM((2, span) + tile_shape, f32), pltpu.VMEM((tok_rows, tok_rows), bf16)],
         compiler_params=params,
         cost_estimate=cost(200, 6 * tok_rows * chans),
         name="query_part",
@@ -379,6 +442,7 @@
         out_specs=pl.BlockSpec(memory_space=pltpu.VMEM),
         out_shape=jax.ShapeDtypeStruct((blocks, modes, few), bf16),
         scratch_shapes=[pltpu.SMEM((blocks,), f32)],
+        compiler_params=params,
         name="block_prefix",
     )(doc_lengths, moved, rate_few)
     enter = lax.all_to_all(enter_few, "ctx", split_axis=0, concat_axis=0, tiled=True)
@@ -405,7 +469,10 @@
         out_shape=out_shape,
         scratch_shapes=[
             pltpu.VMEM((2, span) + tile_shape, f32),
-            pltpu.VMEM((UNROLL, 3, modes, LANES), f32),
+            pltpu.VMEM((tok_rows, tok_rows), bf16),
+            pltpu.VMEM((tok_rows, tok_rows), bf16),
+            pltpu.VMEM((tok_rows, PAIR * LANES), bf16),
+            pltpu.VMEM((PAIR, 3, modes, LANES), f32),
             pltpu.VMEM((tok_rows, LANES), f32),
             pltpu.VMEM((chans // LANES, tok_rows, LANES), f32),
         ],
@@ -419,6 +486,7 @@
     square_sum = lax.psum(jnp.sum(sums, axis=1), "grp")
     inverse_rms = lax.rsqrt(square_sum / (chans * grp) + 1e-06)
     normed = (hidden * inverse_rms[:, None] * norm_gain[None, :]).astype(bf16)
+    normed = normed.reshape(span, SUBS, chans).transpose(1, 0, 2).reshape(tok_rows, chans)
     return (hidden_out, normed)
 
 

time: 76.6 us -> 86.5 us (1.13)
  Pallas kernels: 47.1 us -> 60.9 us
  local copies, waits for them, and re-layouts: 5.37 us -> 3.39 us
  waiting for transfers between devices: 3.6 us -> 1.85 us
    pallas_call x1, Pallas kernels: 14.2 us -> 23 us  [shards(): pl.pallas_call(functools.partial(final_kernel, span=span, modes=modes, wi...]
    another operation x2 -> x0, local copies, waits for them, and re-layouts: 1.99 us -> none  [shards(): jnp.stack([query_in[tok_rows - 2:], key_in[tok_rows - 2:], value_in[tok_r...]
    pallas_call x0 -> x1, Pallas kernels: none -> 1.84 us  [shards(): pl.pallas_call(tail_kernel, grid=(1,), in_specs=[last_rows] * 3, out_spec...]
    pallas_call x1, Pallas kernels: 7.32 us -> 9.07 us  [shards(): pl.pallas_call(functools.partial(query_kernel, span=span), grid=(steps,),...]
    all_to_all x1, waiting for transfers between devices: 3.27 us -> 1.53 us  [shards(): lax.all_to_all(enter_few, 'ctx', split_axis=0, concat_axis=0, tiled=True)]
    pallas_call x1, Pallas kernels: 14.9 us -> 16.2 us  [shards(): pl.pallas_call(functools.partial(state_kernel, span=span, modes=modes, wi...]
    unnamed x6 -> x8, local copies, waits for them, and re-layouts: 2.06 us -> 2.07 us
  transfers between devices with their start and end apart: 3 -> 3, of which waited for: 2 -> 2; matrix products, arithmetic and copies ran while one was open for 5% -> 4% of each run, Pallas kernels for 21% -> 21%
where the time goes in v3:
time: 86.5 us; the launch traced here: 85.7 us
  Pallas kernels  60.9 us (70%)
  starting transfers between devices  16.8 us (19%)
  local copies, waits for them, and re-layouts  3.39 us (4%)
  other arithmetic  2.17 us (3%)
  waiting for transfers between devices  1.85 us (2%)
    pallas_call x1, Pallas kernels, shards(): pl.pallas_call(functools.partial(final_kernel, span=span, modes=modes, wi...  23 us
    pallas_call x1, Pallas kernels, shards(): pl.pallas_call(functools.partial(state_kernel, span=span, modes=modes, wi...  16.2 us
    pallas_call x1, Pallas kernels, shards(): pl.pallas_call(functools.partial(query_kernel, span=span), grid=(steps,),...  9.07 us
    pallas_call x1, Pallas kernels, shards(): pl.pallas_call(functools.partial(near_kernel, span=span, modes=modes), gr...  8.95 us
    all_to_all x1, starting transfers between devices, shards(): moved = lax.all_to_all(ends, 'ctx', split_axis=0, concat_axis=0, tiled=True)  8.89 us
    all_to_all x1, starting transfers between devices, shards(): lax.all_to_all(enter_few, 'ctx', split_axis=0, concat_axis=0, tiled=True)  5.51 us
    ppermute x1, starting transfers between devices, from_behind(): return lax.ppermute(shard, axis, pairs)  2.35 us
    mul x1, other arithmetic, shards(): weight = residues * jnp.sqrt(-jnp.expm1(-2.0 * decay_rate))  2.17 us
  transfers between devices with their start and end apart: 3, of which 2 were waited for; matrix products, arithmetic and copies ran while one was open for 4% of the time, Pallas kernels for 21%

profile of v3, /device:TPU:0, one launch (start us, length us, event | category | flops | bytes accessed | tf_op | source)
XLA Modules:
  0.0 85.7 jit_solution(1872667951562264442)
XLA Ops:
  0.6 0.0 copy-start
  0.6 1.8 %tails.1 = bf16[3,2,8192]{2,1,0:T(2,128)(2,1)} custom-call(bf16[128,8192]{1,0:T(8,128)(2,1)} %query_ref.3, bf16[128,8192]{1,0:T(8,128)(2,1)} %key_ref.3, bf16[128,8192]{1,0:T(8,128)(2,1)} %value_ref.3), custom_call_target="tpu_custom_call" | custom-call | tf_op jit(solution)/shard_map/tails/pallas_call | solution.py:358
  2.5 2.3 %collective-permute-start = (bf16[3,2,8192]{2,1,0:T(2,128)(2,1)}, bf16[3,2,8192]{2,1,0:T(2,128)(2,1)S(1)}, u32[]{:S(2)}, u32[]{:S(2)}) collective-permute-start(bf16[3,2,8192]{2,1,0:T(2,128)(2,1)} %tails.1), channel_id=1, source_target_pairs={{0,1},{1,2},{2,3},{3,4},{4,5},{5,6},{6,7},{7,8},{8,9},{9,10},{10,1... | collective-permute-start | bytes 294920 | tf_op jit(solution)/shard_map/ppermute | solution.py:21
  4.8 0.0 copy-done
  4.9 2.2 %sqrt_multiply_fusion.weight_ref = f32[16,8192]{1,0:T(8,128)} fusion(f32[16,8192]{1,0:T(8,128)} %param.14, f32[16,8192]{1,0:T(8,128)S(1)} %copy-done), kind=kLoop, calls=%fused_computation | loop fusion | flops 393216 | bytes 1572864 | tf_op jit(solution)/shard_map/mul | solution.py:368
  7.0 0.0 collective-permute-done.rim_ref
  7.0 0.0 copy-start.3
  7.0 0.6 copy-done.3
  7.7 16.2 %block_states.1 = (bf16[128,8192]{1,0:T(8,128)(2,1)}, f32[128,8192]{1,0:T(8,128)}, bf16[32,16,256]{2,1,0:T(8,128)(2,1)}) custom-call(s32[1]{0:T(128)} %bitcast.base_ref, s32[16]{0:T(128)} %len_ref.9, bf16[128,8192]{1,0:T(8,128)(2,1)} %key_ref.3, bf16[128,8192]{1,0:T(8,128)(2,1)} %value_ref.3, bf16[3,2,8192]{2,1,0:T(2,128)(2,1)} %copy-done.3, ...), custom_call_target="tpu_custom_call" | custom-call | flops 65536000 | bytes 12582912 | tf_op jit(solution)/shard_map/block_states/pallas_call | solution.py:389
  23.9 8.9 %all-to-all-start = ((bf16[32,16,256]{2,1,0:T(8,128)(2,1)}), bf16[32,16,256]{2,1,0:T(8,128)(2,1)S(1)}, u32[]{:S(2)}, u32[]{:S(2)}) async-start(bf16[32,16,256]{2,1,0:T(8,128)(2,1)} %get-tuple-element.8), calls=%async_computation | async-start | bytes 524288 | tf_op jit(solution)/shard_map/all_to_all | solution.py:436
  32.8 1.3 %constant_dynamic-slice_fusion.rate_ref = f32[16,256]{1,0:T(8,128)} fusion(f32[16,8192]{1,0:T(8,128)} %rate_ref.5, s32[]{:T(128)S(6)} %select_n.3), kind=kLoop, calls=%fused_computation.1 | loop fusion | bytes 32772 | tf_op jit(solution)/shard_map/dynamic_slice | solution.py:438
  34.1 8.9 %near_part.1.near_ref = f32[128,8192]{1,0:T(8,128)} custom-call(s32[1]{0:T(128)} %bitcast.base_ref, s32[16]{0:T(128)} %len_ref.9, bf16[128,8192]{1,0:T(8,128)(2,1)} %get-tuple-element.9.gate_ref, f32[16,8192]{1,0:T(8,128)} %rate_ref.5, f32[16,8192]{1,0:T(8,128)} %sqrt_multiply_fusion.weight_ref), custom_call_target="tpu_custom_call" | custom-call | flops 39321600 | bytes 7340032 | tf_op jit(solution)/shard_map/near_part/pallas_call | solution.py:410
  43.1 0.3 all-to-all-done.end_ref
  43.4 0.0 copy-start.2
  43.4 0.7 copy-done.2
  44.1 1.8 %block_prefix.1 = bf16[32,16,256]{2,1,0:T(8,128)(2,1)} custom-call(s32[16]{0:T(128)} %len_ref.9, bf16[32,16,256]{2,1,0:T(8,128)(2,1)} %copy-done.2, f32[16,256]{1,0:T(8,128)} %constant_dynamic-slice_fusion.rate_ref), custom_call_target="tpu_custom_call" | custom-call | tf_op jit(solution)/shard_map/block_prefix/pallas_call | solution.py:439
  45.9 5.5 %all-to-all-start.1 = ((bf16[32,16,256]{2,1,0:T(8,128)(2,1)}), bf16[32,16,256]{2,1,0:T(8,128)(2,1)S(1)}, u32[]{:S(2)}, u32[]{:S(2)}) async-start(bf16[32,16,256]{2,1,0:T(8,128)(2,1)} %block_prefix.1), calls=%async_computation.1 | async-start | bytes 524288 | tf_op jit(solution)/shard_map/all_to_all | solution.py:448
  51.4 9.1 %query_part.1.short_ref = f32[128,8192]{1,0:T(8,128)} custom-call(s32[1]{0:T(128)} %bitcast.base_ref, s32[16]{0:T(128)} %len_ref.9, bf16[128,8192]{1,0:T(8,128)(2,1)} %query_ref.3, bf16[3,2,8192]{2,1,0:T(2,128)(2,1)} %copy-done.3, f32[3,3,8192]{2,1,0:T(4,128)} %taps_ref.3), custom_call_target="tpu_custom_call" | custom-call | flops 13107200 | bytes 6291456 | tf_op jit(solution)/shard_map/query_part/pallas_call | solution.py:422
  60.5 1.5 %all-to-all-done.1.enter_ref = bf16[32,16,256]{2,1,0:T(8,128)(2,1)S(1)} async-done(((bf16[32,16,256]{2,1,0:T(8,128)(2,1)}), bf16[32,16,256]{2,1,0:T(8,128)(2,1)S(1)}, u32[]{:S(2)}, u32[]{:S(2)}) %all-to-all-start.1) | async-done | bytes 262176 | tf_op jit(solution)/shard_map/all_to_all | solution.py:448
  62.0 0.0 copy-start.1
  62.0 0.7 copy-done.1
  62.7 23.0 %far_part.1 = (bf16[128,8192]{1,0:T(8,128)(2,1)}, bf16[128,8192]{1,0:T(8,128)(2,1)}) custom-call(s32[1]{0:T(128)} %bitcast.base_ref, s32[16]{0:T(128)} %len_ref.9, f32[128,8192]{1,0:T(8,128)} %get-tuple-element.7.state_ref, bf16[32,16,256]{2,1,0:T(8,128)(2,1)} %copy-done.1, f32[128,8192]{1,0:T(8,128)} %near_part.1.near_ref, ...), custom_call_target="tpu_custom_call" | custom-call | flops 58982400 | bytes 18874368 | tf_op jit(solution)/shard_map/far_part/pallas_call | solution.py:461
Async XLA Ops:
  0.6 4.2 %copy-start = (f32[16,8192]{1,0:T(8,128)S(1)}, f32[16,8192]{1,0:T(8,128)}, u32[]{:S(2)}) copy-start(f32[16,8192]{1,0:T(8,128)} %rate_ref.5) | copy-start | bytes 1572868
  2.5 4.5 %collective-permute-start = (bf16[3,2,8192]{2,1,0:T(2,128)(2,1)}, bf16[3,2,8192]{2,1,0:T(2,128)(2,1)S(1)}, u32[]{:S(2)}, u32[]{:S(2)}) collective-permute-start(bf16[3,2,8192]{2,1,0:T(2,128)(2,1)} %tails.1), channel_id=1, source_target_pairs={{0,1},{1,2},{2,3},{3,4},{4,5},{5,6},{6,7},{7,8},{8,9},{9,10},{10,1... | collective-permute-start | bytes 294920 | tf_op jit(solution)/shard_map/ppermute | solution.py:21
  7.0 0.6 copy-start.3
  23.9 19.5 %all-to-all-start = ((bf16[32,16,256]{2,1,0:T(8,128)(2,1)}), bf16[32,16,256]{2,1,0:T(8,128)(2,1)S(1)}, u32[]{:S(2)}, u32[]{:S(2)}) async-start(bf16[32,16,256]{2,1,0:T(8,128)(2,1)} %get-tuple-element.8), calls=%async_computation | async-start | bytes 524288 | tf_op jit(solution)/shard_map/all_to_all | solution.py:436
  43.4 0.7 copy-start.2
  45.9 16.1 %all-to-all-start.1 = ((bf16[32,16,256]{2,1,0:T(8,128)(2,1)}), bf16[32,16,256]{2,1,0:T(8,128)(2,1)S(1)}, u32[]{:S(2)}, u32[]{:S(2)}) async-start(bf16[32,16,256]{2,1,0:T(8,128)(2,1)} %block_prefix.1), calls=%async_computation.1 | async-start | bytes 524288 | tf_op jit(solution)/shard_map/all_to_all | solution.py:448
  62.0 0.7 copy-start.1

commit v4 on v2

v4 whole, which is shorter than its diff:
```python
import functools
import math

import jax
import jax.numpy as jnp
from jax import lax
from jax.experimental import pallas as pl
from jax.experimental.pallas import tpu as pltpu
from jax.sharding import PartitionSpec as P

SUBS = 8
LANES = 128
VMEM_LIMIT = 63 * 1024 * 1024
f32 = jnp.float32
bf16 = jnp.bfloat16


def from_behind(shard, axis, by):
    count = lax.axis_size(axis)
    pairs = [(i, i + by) for i in range(count) if 0 <= i + by < count]
    return lax.ppermute(shard, axis, pairs)


def doc_start_rows(len_ref, base, span):
    rows = lax.broadcasted_iota(jnp.int32, (SUBS, LANES), 0) * span + base
    starts = [jnp.int32(0)]
    for d in range(len_ref.shape[0] - 1):
        starts.append(starts[-1] + len_ref[d])
    out = []
    for j in range(span):
        pos = rows + j
        best = jnp.zeros((SUBS, LANES), jnp.int32)
        for start in starts[1:]:
            best = jnp.where(pos >= start, start, best)
        out.append(best)
    return rows, out


def flag(cond):
    return jnp.where(cond, 1.0, 0.0).astype(f32)


def each_group(count, most, group):
    size = math.gcd(count, most)

    def step(i, carry):
        group([pl.multiple_of((i * size + m) * LANES, LANES) for m in range(size)])
        return carry

    lax.fori_loop(0, count // size, step, 0)


def cols_of(lane):
    return pl.ds(lane, LANES)


def row_of(ref, index):
    return jnp.broadcast_to(ref[pl.ds(index, 1), :], (SUBS, LANES))


def spread(x, wide, span):
    x = x.astype(f32)
    for b in range(SUBS):
        wide[pl.ds(b * (span + 1), span), :] = x[b * span : (b + 1) * span]


def steps_of(wide, span):
    return [wide[pl.ds(j, SUBS, stride=span + 1), :] for j in range(span)]


def short_conv(steps, rim, taps, keep_one, keep_two):
    top = lax.broadcasted_iota(jnp.int32, (SUBS, LANES), 0) == 0
    rim = rim.astype(f32)
    behind_one = jnp.where(top, jnp.broadcast_to(rim[1:2], (SUBS, LANES)), pltpu.roll(steps[-1], 1, 0))
    behind_two = jnp.where(top, jnp.broadcast_to(rim[0:1], (SUBS, LANES)), pltpu.roll(steps[-2], 1, 0))
    padded = [behind_two, behind_one] + steps
    taps = [jnp.broadcast_to(taps[m : m + 1], (SUBS, LANES)) for m in range(3)]
    return [
        taps[0] * padded[j + 2]
        + (taps[1] * padded[j + 1]) * keep_one[j]
        + (taps[2] * padded[j]) * keep_two[j]
        for j in range(len(steps))
    ]


def state_kernel(
    base_ref, len_ref, key_ref, value_ref, rim_ref, taps_ref, rate_ref, weight_ref,
    gate_ref, state_ref, end_ref,
    masks, wide_k, wide_v, tables, ends, held,
    *, span, modes, width, most,
):
    @pl.when(pl.program_id(0) == 0)
    def _():
        rows, starts = doc_start_rows(len_ref, base_ref[0], span)
        for j in range(span):
            masks[0, j] = flag(starts[j] < rows + j)
            masks[1, j] = flag(starts[j] < rows + (j - 1))
            masks[2, j] = flag(starts[span - 1] <= rows + j)
        sub = lax.broadcasted_iota(jnp.int32, (SUBS, LANES), 0)
        through = flag(starts[span - 1] < rows)
        one = through * flag(sub >= 1)
        two = one * pltpu.roll(one, 1, 0) * flag(sub >= 2)
        four = two * pltpu.roll(two, 2, 0) * flag(sub >= 4)
        masks[3, 0] = one
        masks[3, 1] = two
        masks[3, 2] = four
        masks[3, 3] = flag(sub >= 1)

    def group(lanes):
        for slot, lane in enumerate(lanes):
            spread(key_ref[:, cols_of(lane)], wide_k.at[slot], span)
            spread(value_ref[:, cols_of(lane)], wide_v.at[slot], span)
            rate = rate_ref[:, cols_of(lane)]
            for m, by in enumerate((1, span, 2 * span, 4 * span)):
                tables[slot, m] = jnp.exp(-float(by) * rate)
            tables[slot, 4] = weight_ref[:, cols_of(lane)]
        for slot, lane in enumerate(lanes):
            cols = cols_of(lane)
            keep_one = [masks[0, j] for j in range(span)]
            keep_two = [masks[1, j] for j in range(span)]
            k_short = short_conv(steps_of(wide_k.at[slot], span), rim_ref[1, :, cols], taps_ref[1, :, cols], keep_one, keep_two)
            v_short = short_conv(steps_of(wide_v.at[slot], span), rim_ref[2, :, cols], taps_ref[2, :, cols], keep_one, keep_two)
            for j in range(0, span, 2):
                pair = jnp.concatenate([k_short[j] * v_short[j], k_short[j + 1] * v_short[j + 1]], axis=0).astype(bf16)
                gate_ref[pl.ds(j * SUBS, 2 * SUBS), cols] = pair
                pair = pair.astype(f32)
                held[slot, j] = pair[:SUBS] * masks[2, j]
                held[slot, j + 1] = pair[SUBS:] * masks[2, j + 1]
        states = []
        for slot, lane in enumerate(lanes):
            decay = [row_of(tables.at[slot, 0], n) for n in range(modes)]
            state = [held[slot, 0]] * modes
            for j in range(1, span):
                gate = held[slot, j]
                state = [decay[n] * state[n] + gate for n in range(modes)]
            states.append(state)
        for m, shift in enumerate((1, 2, 4)):
            for slot in range(len(lanes)):
                states[slot] = [
                    x + (row_of(tables.at[slot, m + 1], n) * masks[3, m]) * pltpu.roll(x, shift, 0)
                    for n, x in enumerate(states[slot])
                ]
        for slot, lane in enumerate(lanes):
            for n, x in enumerate(states[slot]):
                ends[slot, pl.ds(n, 1), :] = x[SUBS - 1 :]
                state_ref[pl.ds(n * SUBS, SUBS), cols_of(lane)] = (
                    row_of(tables.at[slot, 4], n) * masks[3, 3]
                ) * pltpu.roll(x, 1, 0)
        for slot, lane in enumerate(lanes):
            end = ends[slot].astype(bf16)
            if width:
                end_ref[lax.div(lane, width), :, cols_of(pl.multiple_of(lax.rem(lane, width), LANES))] = end
            else:
                end_ref[:, cols_of(lane)] = end

    each_group(key_ref.shape[1] // LANES, most, group)


def keep_masks(base_ref, len_ref, masks, span):
    rows, starts = doc_start_rows(len_ref, base_ref[0], span)
    for j in range(span):
        masks[0, j] = flag(starts[j] < rows + j)
        masks[1, j] = flag(starts[j] < rows + (j - 1))


def near_kernel(base_ref, len_ref, gate_ref, rate_ref, weight_ref, near_ref, masks, *, span, modes, most):
    @pl.when(pl.program_id(0) == 0)
    def _():
        keep_masks(base_ref, len_ref, masks, span)

    def group(lanes):
        taps = []
        for lane in lanes:
            decay = jnp.exp(-rate_ref[:, cols_of(lane)])
            term = weight_ref[:, cols_of(lane)]
            parts = []
            for lag in range(span):
                part = term[:SUBS]
                for n in range(SUBS, modes, SUBS):
                    part = part + term[n : n + SUBS]
                parts.append(part)
                term = term * decay
            taps.append(parts)
        for shift in (1, 2, 4):
            taps = [[part + pltpu.roll(part, shift, 0) for part in parts] for parts in taps]
        for parts, lane in zip(taps, lanes):
            live = []
            for j in range(span):
                if j % 2 == 0:
                    pair = gate_ref[pl.ds(j * SUBS, 2 * SUBS), cols_of(lane)].astype(f32)
                keep = masks[0, j]
                live = [g * keep for g in live]
                live.append(pair[(j % 2) * SUBS : (j % 2 + 1) * SUBS])
                total = parts[0] * live[j]
                for lag in range(1, j + 1):
                    total = total + parts[lag] * live[j - lag]
                near_ref[pl.ds(j * SUBS, SUBS), cols_of(lane)] = total

    each_group(gate_ref.shape[1] // LANES, most, group)


def query_kernel(base_ref, len_ref, query_ref, rim_ref, taps_ref, short_ref, masks, wide_q, *, span, most):
    @pl.when(pl.program_id(0) == 0)
    def _():
        keep_masks(base_ref, len_ref, masks, span)

    def group(lanes):
        for slot, lane in enumerate(lanes):
            spread(query_ref[:, cols_of(lane)], wide_q.at[slot], span)
        for slot, lane in enumerate(lanes):
            cols = cols_of(lane)
            keep_one = [masks[0, j] for j in range(span)]
            keep_two = [masks[1, j] for j in range(span)]
            q_short = short_conv(steps_of(wide_q.at[slot], span), rim_ref[0, :, cols], taps_ref[0, :, cols], keep_one, keep_two)
            for j in range(span):
                short_ref[pl.ds(j * SUBS, SUBS), cols] = q_short[j]

    each_group(query_ref.shape[1] // LANES, most, group)


def prefix_kernel(len_ref, end_ref, rate_ref, enter_ref, through, *, span):
    blocks = end_ref.shape[0]
    for i in range(blocks):
        through[i] = jnp.float32(1.0)
    start = jnp.int32(0)
    through[0] = jnp.float32(0.0)
    for d in range(len_ref.shape[0] - 1):
        start = start + len_ref[d]
        through[lax.div(start, jnp.int32(span))] = jnp.float32(0.0)
    decay = jnp.exp(-float(span) * rate_ref[...])
    state = jnp.zeros(decay.shape, f32)
    for i in range(blocks):
        enter_ref[i] = state.astype(bf16)
        state = end_ref[i].astype(f32) + (decay * through[i]) * state


def final_kernel(
    base_ref, len_ref, state_ref, enter_ref, near_ref, short_ref, resid_ref, rate_ref, weight_ref, gain_ref,
    *refs,
    span, modes, width, channels, most,
):
    if channels:
        hidden_ref, normed_ref, masks, wide, tables, sums, whole = refs
    else:
        hidden_ref, wide_ref, sum_ref, masks, wide, tables, sums, whole = refs
    step = pl.program_id(0)
    tiles = resid_ref.shape[1] // LANES

    @pl.when(step == 0)
    def _():
        rows, starts = doc_start_rows(len_ref, base_ref[0], span)
        for j in range(span):
            masks[0, j] = flag(starts[j] < rows)
        masks[1, 0] = flag(starts[0] < base_ref[0])
        sums[...] = jnp.zeros(sums.shape, f32)

    def group(lanes):
        sub = lax.broadcasted_iota(jnp.int32, (SUBS, LANES), 0).astype(f32) * (-float(span))
        through = masks[1, 0]
        for slot, lane in enumerate(lanes):
            if width:
                enter = enter_ref[lax.div(lane, width), :, cols_of(pl.multiple_of(lax.rem(lane, width), LANES))]
            else:
                enter = enter_ref[:, cols_of(lane)]
            rate = rate_ref[:, cols_of(lane)]
            tables[slot, 0] = jnp.exp(-rate)
            tables[slot, 1] = weight_ref[:, cols_of(lane)] * enter.astype(f32)
            tables[slot, 2] = rate
        parts = [
            [
                state_ref[pl.ds(n * SUBS, SUBS), cols_of(lane)]
                + (row_of(tables.at[slot, 1], n) * through) * jnp.exp(row_of(tables.at[slot, 2], n) * sub)
                for n in range(modes)
            ]
            for slot, lane in enumerate(lanes)
        ]
        for slot, lane in enumerate(lanes):
            part = parts[slot]
            decay = [row_of(tables.at[slot, 0], n) for n in range(modes)]
            for j in range(span):
                part = [part[n] * decay[n] for n in range(modes)]
                total = part
                while len(total) > 1:
                    total = [total[m] + total[m + 1] for m in range(0, len(total), 2)]
                conv = near_ref[pl.ds(j * SUBS, SUBS), cols_of(lane)] + total[0] * masks[0, j]
                conv = conv.astype(bf16).astype(f32)
                wide[slot, pl.ds(j, SUBS, stride=span + 1), :] = short_ref[pl.ds(j * SUBS, SUBS), cols_of(lane)] * conv
        for b in range(SUBS):
            rows = pl.ds(b * span, span)
            squares = sums[rows, :]
            for slot, lane in enumerate(lanes):
                hidden = wide[slot, pl.ds(b * (span + 1), span), :] + resid_ref[rows, cols_of(lane)].astype(f32)
                if channels:
                    whole[lax.div(lane, LANES) + step * tiles, rows, :] = hidden
                else:
                    wide_ref[rows, cols_of(lane)] = hidden
                hidden_ref[rows, cols_of(lane)] = hidden.astype(bf16)
                squares = squares + hidden * hidden
            sums[rows, :] = squares

    each_group(tiles, most, group)

    @pl.when(step == pl.num_programs(0) - 1)
    def _():
        if channels:
            inverse = lax.rsqrt(jnp.sum(sums[...], axis=1, keepdims=True) / channels + 1e-06)
            sums[...] = jnp.broadcast_to(inverse, sums.shape)

            def scale(lanes):
                for lane in lanes:
                    normed = whole[lax.div(lane, LANES)] * sums[...] * gain_ref[:, cols_of(lane)]
                    normed_ref[:, cols_of(lane)] = normed.astype(bf16)

            each_group(normed_ref.shape[1] // LANES, 4, scale)
        else:
            sum_ref[...] = sums[...]


def shards(
    query_in, key_in, value_in, short_taps, decay_rate, residues, doc_lengths, residual, norm_gain
):
    tok_rows, chans = query_in.shape
    modes = decay_rate.shape[0]
    span = tok_rows // SUBS
    blocks = lax.axis_size("ctx")
    grp = lax.axis_size("grp")
    few = chans // blocks
    width = few if few % LANES == 0 else 0
    chunk = min(chans, max(1024, width))
    steps = chans // chunk
    ctx_index = lax.axis_index("ctx")
    base = (ctx_index * tok_rows).astype(jnp.int32).reshape(1)
    tails = jnp.stack([query_in[tok_rows - 2 :], key_in[tok_rows - 2 :], value_in[tok_rows - 2 :]])
    rim_rows = from_behind(tails, "ctx", 1)
    weight = residues * jnp.sqrt(-jnp.expm1(-2.0 * decay_rate))

    smem = pl.BlockSpec(memory_space=pltpu.SMEM)

    def rows_spec(rows):
        return pl.BlockSpec((rows, chunk), lambda i: (0, i))

    rim_spec = pl.BlockSpec((3, 2, chunk), lambda i: (0, 0, i))
    taps_spec = pl.BlockSpec((3, 3, chunk), lambda i: (0, 0, i))
    if width:
        end_spec = pl.BlockSpec((chunk // width, modes, width), lambda i: (i, 0, 0))
        end_shape = (blocks, modes, width)
    else:
        end_spec = rows_spec(modes)
        end_shape = (modes, chans)
    params = pltpu.CompilerParams(vmem_limit_bytes=VMEM_LIMIT)
    tile_shape = (SUBS, LANES)
    wide_rows = SUBS * (span + 1)

    def cost(per_tile, moved):
        return pl.CostEstimate(flops=per_tile * (chans // LANES) * SUBS * LANES, bytes_accessed=moved, transcendentals=0)

    gates, states, ends = pl.pallas_call(
        functools.partial(state_kernel, span=span, modes=modes, width=width, most=2),
        grid=(steps,),
        in_specs=[smem, smem, rows_spec(tok_rows), rows_spec(tok_rows), rim_spec, taps_spec, rows_spec(modes), rows_spec(modes)],
        out_specs=[rows_spec(tok_rows), rows_spec(modes * SUBS), end_spec],
        out_shape=[
            jax.ShapeDtypeStruct((tok_rows, chans), bf16),
            jax.ShapeDtypeStruct((modes * SUBS, chans), f32),
            jax.ShapeDtypeStruct(end_shape, bf16),
        ],
        scratch_shapes=[
            pltpu.VMEM((4, span) + tile_shape, f32),
            pltpu.VMEM((2, wide_rows, LANES), f32),
            pltpu.VMEM((2, wide_rows, LANES), f32),
            pltpu.VMEM((2, 5, modes, LANES), f32),
            pltpu.VMEM((2, modes, LANES), f32),
            pltpu.VMEM((2, span) + tile_shape, f32),
        ],
        compiler_params=params,
        cost_estimate=cost(1000, 12 * tok_rows * chans),
        name="block_states",
    )(base, doc_lengths, key_in, value_in, rim_rows, short_taps, decay_rate, weight)

    near = pl.pallas_call(
        functools.partial(near_kernel, span=span, modes=modes, most=4),
        grid=(steps,),
        in_specs=[smem, smem, rows_spec(tok_rows), rows_spec(modes), rows_spec(modes)],
        out_specs=rows_spec(tok_rows),
        out_shape=jax.ShapeDtypeStruct((tok_rows, chans), f32),
        scratch_shapes=[pltpu.VMEM((2, span) + tile_shape, f32)],
        compiler_params=params,
        cost_estimate=cost(600, 7 * tok_rows * chans),
        name="near_part",
    )(base, doc_lengths, gates, decay_rate, weight)

    q_short = pl.pallas_call(
        functools.partial(query_kernel, span=span, most=4),
        grid=(steps,),
        in_specs=[smem, smem, rows_spec(tok_rows), rim_spec, taps_spec],
        out_specs=rows_spec(tok_rows),
        out_shape=jax.ShapeDtypeStruct((tok_rows, chans), f32),
        scratch_shapes=[pltpu.VMEM((2, span) + tile_shape, f32), pltpu.VMEM((4, wide_rows, LANES), f32)],
        compiler_params=params,
        cost_estimate=cost(200, 6 * tok_rows * chans),
        name="query_part",
    )(base, doc_lengths, query_in, rim_rows, short_taps)

    if not width:
        ends = ends.reshape(modes, blocks, few).transpose(1, 0, 2)
    moved = lax.all_to_all(ends, "ctx", split_axis=0, concat_axis=0, tiled=True)
    moved, near = lax.optimization_barrier((moved, near))
    rate_few = lax.dynamic_slice_in_dim(decay_rate, ctx_index * few, few, 1)
    enter_few = pl.pallas_call(
        functools.partial(prefix_kernel, span=tok_rows),
        in_specs=[smem, pl.BlockSpec(memory_space=pltpu.VMEM), pl.BlockSpec(memory_space=pltpu.VMEM)],
        out_specs=pl.BlockSpec(memory_space=pltpu.VMEM),
        out_shape=jax.ShapeDtypeStruct((blocks, modes, few), bf16),
        scratch_shapes=[pltpu.SMEM((blocks,), f32)],
        compiler_params=params,
        name="block_prefix",
    )(doc_lengths, moved, rate_few)
    enter = lax.all_to_all(enter_few, "ctx", split_axis=0, concat_axis=0, tiled=True)
    if not width:
        enter = enter.transpose(1, 0, 2).reshape(modes, chans)

    alone = grp == 1
    out_specs = [rows_spec(tok_rows)]
    out_shape = [jax.ShapeDtypeStruct((tok_rows, chans), bf16)]
    if alone:
        out_specs.append(pl.BlockSpec((tok_rows, chans), lambda i: (0, 0)))
        out_shape.append(jax.ShapeDtypeStruct((tok_rows, chans), bf16))
    else:
        out_specs += [rows_spec(tok_rows), pl.BlockSpec((tok_rows, LANES), lambda i: (0, 0))]
        out_shape += [jax.ShapeDtypeStruct((tok_rows, chans), f32), jax.ShapeDtypeStruct((tok_rows, LANES), f32)]
    outs = pl.pallas_call(
        functools.partial(final_kernel, span=span, modes=modes, width=width, channels=chans if alone else 0, most=2),
        grid=(steps,),
        in_specs=[
            smem, smem, rows_spec(modes * SUBS), end_spec, rows_spec(tok_rows), rows_spec(tok_rows), rows_spec(tok_rows),
            rows_spec(modes), rows_spec(modes), pl.BlockSpec((1, chans), lambda i: (0, 0)),
        ],
        out_specs=out_specs,
        out_shape=out_shape,
        scratch_shapes=[
            pltpu.VMEM((2, span) + tile_shape, f32),
            pltpu.VMEM((2, wide_rows, LANES), f32),
            pltpu.VMEM((2, 3, modes, LANES), f32),
            pltpu.VMEM((tok_rows, LANES), f32),
            pltpu.VMEM((chans // LANES, tok_rows, LANES), f32),
        ],
        compiler_params=params,
        cost_estimate=cost(900, 18 * tok_rows * chans),
        name="far_part",
    )(base, doc_lengths, states, enter, near, q_short, residual, decay_rate, weight, norm_gain.reshape(1, chans))
    if alone:
        return tuple(outs)
    hidden_out, hidden, sums = outs
    square_sum = lax.psum(jnp.sum(sums, axis=1), "grp")
    inverse_rms = lax.rsqrt(square_sum / (chans * grp) + 1e-06)
    normed = (hidden * inverse_rms[:, None] * norm_gain[None, :]).astype(bf16)
    return (hidden_out, normed)


def solution(mesh):
    return jax.shard_map(
        shards,
        mesh=mesh,
        in_specs=(
            P("ctx", "grp"),
            P("ctx", "grp"),
            P("ctx", "grp"),
            P(None, None, "grp"),
            P(None, "grp"),
            P(None, "grp"),
            P(),
            P("ctx", "grp"),
            P("grp"),
        ),
        out_specs=(P("ctx", "grp"), P("ctx", "grp")),
        check_vma=False,
    )
```

time: 76.6 us -> 74.4 us (0.971)
  Pallas kernels: 47.1 us -> 44.4 us
    pallas_call x1, Pallas kernels: 14.9 us -> 12.9 us  [shards(): pl.pallas_call(functools.partial(state_kernel, span=span, modes=modes, wi...]
  transfers between devices with their start and end apart: 3 -> 3, of which waited for: 2 -> 2; matrix products, arithmetic and copies ran while one was open for 5% -> 5% of each run, Pallas kernels for 21% -> 22%
where the time goes in v4:
time: 74.4 us; the launch traced here: 73.3 us
  Pallas kernels  44.4 us (60%)
  starting transfers between devices  16.5 us (22%)
  local copies, waits for them, and re-layouts  5.37 us (7%)
  waiting for transfers between devices  3.87 us (5%)
  other arithmetic  2.49 us (3%)
    pallas_call x1, Pallas kernels, shards(): pl.pallas_call(functools.partial(final_kernel, span=span, modes=modes, wi...  13.8 us
    pallas_call x1, Pallas kernels, shards(): pl.pallas_call(functools.partial(state_kernel, span=span, modes=modes, wi...  12.9 us
    pallas_call x1, Pallas kernels, shards(): pl.pallas_call(functools.partial(near_kernel, span=span, modes=modes, mos...  9.04 us
    all_to_all x1, starting transfers between devices, shards(): moved = lax.all_to_all(ends, 'ctx', split_axis=0, concat_axis=0, tiled=True)  8.53 us
    pallas_call x1, Pallas kernels, shards(): pl.pallas_call(functools.partial(query_kernel, span=span, most=4), grid=(...  6.96 us
    all_to_all x1, starting transfers between devices, shards(): lax.all_to_all(enter_few, 'ctx', split_axis=0, concat_axis=0, tiled=True)  5.6 us
    all_to_all x1, waiting for transfers between devices, shards(): lax.all_to_all(enter_few, 'ctx', split_axis=0, concat_axis=0, tiled=True)  3.64 us
    ppermute x1, starting transfers between devices, from_behind(): return lax.ppermute(shard, axis, pairs)  2.36 us
  transfers between devices with their start and end apart: 3, of which 2 were waited for; matrix products, arithmetic and copies ran while one was open for 5% of the time, Pallas kernels for 22%

profile of v4, /device:TPU:0, one launch (start us, length us, event | category | flops | bytes accessed | tf_op | source)
XLA Modules:
  0.0 73.3 jit_solution(7005474907192594524)
XLA Ops:
  0.6 0.9 %slice_bitcast_fusion.2 = bf16[1,2,8192]{2,1,0:T(2,128)(2,1)S(1)} fusion(bf16[128,8192]{1,0:T(8,128)(2,1)} %query_ref.1), kind=kLoop, calls=%fused_computation.4 | loop fusion | bytes 65536 | tf_op jit(solution)/shard_map/stack | solution.py:333
  1.6 1.0 %slice_bitcast_fusion = (bf16[1,2,8192]{2,1,0:T(2,128)(2,1)S(1)}, bf16[1,2,8192]{2,1,0:T(2,128)(2,1)S(1)}) fusion(bf16[128,8192]{1,0:T(8,128)(2,1)} %value_ref.1, bf16[128,8192]{1,0:T(8,128)(2,1)} %key_ref.1), kind=kLoop, calls=%fused_computation.2 | loop fusion | bytes 131072 | tf_op jit(solution)/shard_map/stack | solution.py:333
  2.6 0.2 pad_maximum_fusion
  2.8 2.4 %collective-permute-start = (bf16[3,2,8192]{2,1,0:T(2,128)(2,1)S(1)}, bf16[3,2,8192]{2,1,0:T(2,128)(2,1)S(1)}, u32[]{:S(2)}, u32[]{:S(2)}) collective-permute-start(bf16[3,2,8192]{2,1,0:T(2,128)(2,1)S(1)} %pad_maximum_fusion), channel_id=1, source_target_pairs={{0,1},{1,2},{2,3},{3,4},{4,5},{5,6},{6,7},{7,8},{8,9},{9,10},{10,1... | collective-permute-start | bytes 294920 | tf_op jit(solution)/shard_map/ppermute | solution.py:21
  5.2 2.3 %sqrt_multiply_fusion.weight_ref = f32[16,8192]{1,0:T(8,128)} fusion(f32[16,8192]{1,0:T(8,128)} %param.14, f32[16,8192]{1,0:T(8,128)} %rate_ref.5), kind=kLoop, calls=%fused_computation | loop fusion | flops 393216 | bytes 1572864 | tf_op jit(solution)/shard_map/mul | solution.py:335
  7.5 0.0 collective-permute-done.rim_ref
  7.5 0.0 copy-start.2
  7.5 0.6 copy-done.2
  8.1 12.9 %block_states.1 = (bf16[128,8192]{1,0:T(8,128)(2,1)}, f32[128,8192]{1,0:T(8,128)}, bf16[32,16,256]{2,1,0:T(8,128)(2,1)}) custom-call(s32[1]{0:T(128)} %bitcast.base_ref, s32[16]{0:T(128)} %len_ref.9, bf16[128,8192]{1,0:T(8,128)(2,1)} %key_ref.1, bf16[128,8192]{1,0:T(8,128)(2,1)} %value_ref.1, bf16[3,2,8192]{2,1,0:T(2,128)(2,1)} %copy-done.2, ...), custom_call_target="tpu_custom_call" | custom-call | flops 65536000 | bytes 12582912 | tf_op jit(solution)/shard_map/block_states/pallas_call | solution.py:357
  21.0 8.5 %all-to-all-start = ((bf16[32,16,256]{2,1,0:T(8,128)(2,1)}), bf16[32,16,256]{2,1,0:T(8,128)(2,1)S(1)}, u32[]{:S(2)}, u32[]{:S(2)}) async-start(bf16[32,16,256]{2,1,0:T(8,128)(2,1)} %get-tuple-element.8), calls=%async_computation | async-start | bytes 524288 | tf_op jit(solution)/shard_map/all_to_all | solution.py:406
  29.6 1.3 %constant_dynamic-slice_fusion.rate_ref = f32[16,256]{1,0:T(8,128)} fusion(f32[16,8192]{1,0:T(8,128)} %rate_ref.5, s32[]{:T(128)S(6)} %select_n.3), kind=kLoop, calls=%fused_computation.5 | loop fusion | bytes 32772 | tf_op jit(solution)/shard_map/dynamic_slice | solution.py:408
  30.9 9.0 %near_part.1.near_ref = f32[128,8192]{1,0:T(8,128)} custom-call(s32[1]{0:T(128)} %bitcast.base_ref, s32[16]{0:T(128)} %len_ref.9, bf16[128,8192]{1,0:T(8,128)(2,1)} %get-tuple-element.9.gate_ref, f32[16,8192]{1,0:T(8,128)} %rate_ref.5, f32[16,8192]{1,0:T(8,128)} %sqrt_multiply_fusion.weight_ref), custom_call_target="tpu_custom_call" | custom-call | flops 39321600 | bytes 7340032 | tf_op jit(solution)/shard_map/near_part/pallas_call | solution.py:380
  39.9 0.2 all-to-all-done.end_ref
  40.1 0.0 copy-start.1
  40.1 0.7 copy-done.1
  40.8 1.8 %block_prefix.1 = bf16[32,16,256]{2,1,0:T(8,128)(2,1)} custom-call(s32[16]{0:T(128)} %len_ref.9, bf16[32,16,256]{2,1,0:T(8,128)(2,1)} %copy-done.1, f32[16,256]{1,0:T(8,128)} %constant_dynamic-slice_fusion.rate_ref), custom_call_target="tpu_custom_call" | custom-call | tf_op jit(solution)/shard_map/block_prefix/pallas_call | solution.py:409
  42.6 5.6 %all-to-all-start.1 = ((bf16[32,16,256]{2,1,0:T(8,128)(2,1)}), bf16[32,16,256]{2,1,0:T(8,128)(2,1)S(1)}, u32[]{:S(2)}, u32[]{:S(2)}) async-start(bf16[32,16,256]{2,1,0:T(8,128)(2,1)} %block_prefix.1), calls=%async_computation.1 | async-start | bytes 524288 | tf_op jit(solution)/shard_map/all_to_all | solution.py:418
  48.3 7.0 %query_part.1.short_ref = f32[128,8192]{1,0:T(8,128)} custom-call(s32[1]{0:T(128)} %bitcast.base_ref, s32[16]{0:T(128)} %len_ref.9, bf16[128,8192]{1,0:T(8,128)(2,1)} %query_ref.1, bf16[3,2,8192]{2,1,0:T(2,128)(2,1)} %copy-done.2, f32[3,3,8192]{2,1,0:T(4,128)} %taps_ref.3), custom_call_target="tpu_custom_call" | custom-call | flops 13107200 | bytes 6291456 | tf_op jit(solution)/shard_map/query_part/pallas_call | solution.py:392
  55.2 3.6 %all-to-all-done.1.enter_ref = bf16[32,16,256]{2,1,0:T(8,128)(2,1)S(1)} async-done(((bf16[32,16,256]{2,1,0:T(8,128)(2,1)}), bf16[32,16,256]{2,1,0:T(8,128)(2,1)S(1)}, u32[]{:S(2)}, u32[]{:S(2)}) %all-to-all-start.1) | async-done | bytes 262176 | tf_op jit(solution)/shard_map/all_to_all | solution.py:418
  58.9 0.0 copy-start
  58.9 0.7 copy-done
  59.6 13.8 %far_part.1 = (bf16[128,8192]{1,0:T(8,128)(2,1)}, bf16[128,8192]{1,0:T(8,128)(2,1)}) custom-call(s32[1]{0:T(128)} %bitcast.base_ref, s32[16]{0:T(128)} %len_ref.9, f32[128,8192]{1,0:T(8,128)} %get-tuple-element.7.state_ref, bf16[32,16,256]{2,1,0:T(8,128)(2,1)} %copy-done, f32[128,8192]{1,0:T(8,128)} %near_part.1.near_ref, f32[128,8192]{1,0:T(8,128)} %query_part.1.short_ref, ...), custom_call_target="tpu_custom_call" | custom-call | flops 58982400 | bytes 18874368 | tf_op jit(solution)/shard_map/far_part/pallas_call | solution.py:431
Async XLA Ops:
  2.8 4.7 %collective-permute-start = (bf16[3,2,8192]{2,1,0:T(2,128)(2,1)S(1)}, bf16[3,2,8192]{2,1,0:T(2,128)(2,1)S(1)}, u32[]{:S(2)}, u32[]{:S(2)}) collective-permute-start(bf16[3,2,8192]{2,1,0:T(2,128)(2,1)S(1)} %pad_maximum_fusion), channel_id=1, source_target_pairs={{0,1},{1,2},{2,3},{3,4},{4,5},{5,6},{6,7},{7,8},{8,9},{9,10},{10,1... | collective-permute-start | bytes 294920 | tf_op jit(solution)/shard_map/ppermute | solution.py:21
  7.5 0.6 copy-start.2
  21.0 19.1 %all-to-all-start = ((bf16[32,16,256]{2,1,0:T(8,128)(2,1)}), bf16[32,16,256]{2,1,0:T(8,128)(2,1)S(1)}, u32[]{:S(2)}, u32[]{:S(2)}) async-start(bf16[32,16,256]{2,1,0:T(8,128)(2,1)} %get-tuple-element.8), calls=%async_computation | async-start | bytes 524288 | tf_op jit(solution)/shard_map/all_to_all | solution.py:406
  40.1 0.7 copy-start.1
  42.6 16.2 %all-to-all-start.1 = ((bf16[32,16,256]{2,1,0:T(8,128)(2,1)}), bf16[32,16,256]{2,1,0:T(8,128)(2,1)S(1)}, u32[]{:S(2)}, u32[]{:S(2)}) async-start(bf16[32,16,256]{2,1,0:T(8,128)(2,1)} %block_prefix.1), calls=%async_computation.1 | async-start | bytes 524288 | tf_op jit(solution)/shard_map/all_to_all | solution.py:418
  58.9 0.7 copy-start

commit v5 on v4

--- a/solution.py
+++ b/solution.py
@@ -10,7 +10,7 @@
 
 SUBS = 8
 LANES = 128
-VMEM_LIMIT = 63 * 1024 * 1024
+MIB = 1024 * 1024
 f32 = jnp.float32
 bf16 = jnp.bfloat16
 
@@ -50,6 +50,32 @@
     lax.fori_loop(0, count // size, step, 0)
 
 
+def each_chunk(chans, chunk, before, group, after, most):
+    def step(c, carry):
+        before(c)
+
+        def inner(lanes):
+            group([pl.multiple_of(c * chunk + lane, LANES) for lane in lanes])
+
+        each_group(chunk // LANES, most, inner)
+        after(c)
+        return carry
+
+    lax.fori_loop(0, chans // chunk, step, 0)
+
+
+def cols_copy(src, dst, sem, c, chunk):
+    cols = pl.ds(pl.multiple_of(c * chunk, chunk), chunk)
+    return pltpu.make_async_copy(src.at[:, cols], dst.at[:, cols], sem.at[c])
+
+
+def end_copy(src, dst, sem, c, chunk, width):
+    if not width:
+        return cols_copy(src, dst, sem, c, chunk)
+    rows = pl.ds(c * (chunk // width), chunk // width)
+    return pltpu.make_async_copy(src.at[rows], dst.at[rows], sem.at[c])
+
+
 def cols_of(lane):
     return pl.ds(lane, LANES)
 
@@ -85,12 +111,23 @@
 
 def state_kernel(
     base_ref, len_ref, key_ref, value_ref, rim_ref, taps_ref, rate_ref, weight_ref,
-    gate_ref, state_ref, end_ref,
-    masks, wide_k, wide_v, tables, ends, held,
-    *, span, modes, width, most,
+    gate_ref, state_ref, end_out,
+    key_buf, value_buf, end_ref, sems, masks, wide_k, wide_v, tables, ends, held,
+    *, span, modes, width, most, chunk,
 ):
-    @pl.when(pl.program_id(0) == 0)
-    def _():
+    chans = key_buf.shape[1]
+
+    def fetches(c):
+        return [cols_copy(key_ref, key_buf, sems.at[0], c, chunk), cols_copy(value_ref, value_buf, sems.at[1], c, chunk)]
+
+    def store(c):
+        return end_copy(end_ref, end_out, sems.at[2], c, chunk, width)
+
+    for c in range(chans // chunk):
+        for copy in fetches(c):
+            copy.start()
+
+    def prepare():
         rows, starts = doc_start_rows(len_ref, base_ref[0], span)
         for j in range(span):
             masks[0, j] = flag(starts[j] < rows + j)
@@ -106,10 +143,12 @@
         masks[3, 2] = four
         masks[3, 3] = flag(sub >= 1)
 
+    prepare()
+
     def group(lanes):
         for slot, lane in enumerate(lanes):
-            spread(key_ref[:, cols_of(lane)], wide_k.at[slot], span)
-            spread(value_ref[:, cols_of(lane)], wide_v.at[slot], span)
+            spread(key_buf[:, cols_of(lane)], wide_k.at[slot], span)
+            spread(value_buf[:, cols_of(lane)], wide_v.at[slot], span)
             rate = rate_ref[:, cols_of(lane)]
             for m, by in enumerate((1, span, 2 * span, 4 * span)):
                 tables[slot, m] = jnp.exp(-float(by) * rate)
@@ -153,7 +192,13 @@
             else:
                 end_ref[:, cols_of(lane)] = end
 
-    each_group(key_ref.shape[1] // LANES, most, group)
+    def before(c):
+        for copy in fetches(c):
+            copy.wait()
+
+    each_chunk(chans, chunk, before, group, lambda c: store(c).start(), most)
+    for c in range(chans // chunk):
+        store(c).wait()
 
 
 def keep_masks(base_ref, len_ref, masks, span):
@@ -164,9 +209,7 @@
 
 
 def near_kernel(base_ref, len_ref, gate_ref, rate_ref, weight_ref, near_ref, masks, *, span, modes, most):
-    @pl.when(pl.program_id(0) == 0)
-    def _():
-        keep_masks(base_ref, len_ref, masks, span)
+    keep_masks(base_ref, len_ref, masks, span)
 
     def group(lanes):
         taps = []
@@ -199,14 +242,19 @@
     each_group(gate_ref.shape[1] // LANES, most, group)
 
 
-def query_kernel(base_ref, len_ref, query_ref, rim_ref, taps_ref, short_ref, masks, wide_q, *, span, most):
-    @pl.when(pl.program_id(0) == 0)
-    def _():
-        keep_masks(base_ref, len_ref, masks, span)
+def query_kernel(base_ref, len_ref, query_ref, rim_ref, taps_ref, short_ref, query_buf, sems, masks, wide_q, *, span, most, chunk):
+    chans = query_buf.shape[1]
+
+    def fetch(c):
+        return cols_copy(query_ref, query_buf, sems, c, chunk)
+
+    for c in range(chans // chunk):
+        fetch(c).start()
+    keep_masks(base_ref, len_ref, masks, span)
 
     def group(lanes):
         for slot, lane in enumerate(lanes):
-            spread(query_ref[:, cols_of(lane)], wide_q.at[slot], span)
+            spread(query_buf[:, cols_of(lane)], wide_q.at[slot], span)
         for slot, lane in enumerate(lanes):
             cols = cols_of(lane)
             keep_one = [masks[0, j] for j in range(span)]
@@ -215,11 +263,13 @@
             for j in range(span):
                 short_ref[pl.ds(j * SUBS, SUBS), cols] = q_short[j]
 
-    each_group(query_ref.shape[1] // LANES, most, group)
-
-
-def prefix_kernel(len_ref, end_ref, rate_ref, enter_ref, through, *, span):
+    each_chunk(chans, chunk, lambda c: fetch(c).wait(), group, lambda c: None, most)
+
+
+def prefix_kernel(len_ref, end_in, rate_ref, enter_out, end_ref, enter_ref, sems, through, *, span):
     blocks = end_ref.shape[0]
+    fetch = pltpu.make_async_copy(end_in, end_ref, sems.at[0])
+    fetch.start()
     for i in range(blocks):
         through[i] = jnp.float32(1.0)
     start = jnp.int32(0)
@@ -229,30 +279,43 @@
         through[lax.div(start, jnp.int32(span))] = jnp.float32(0.0)
     decay = jnp.exp(-float(span) * rate_ref[...])
     state = jnp.zeros(decay.shape, f32)
+    fetch.wait()
     for i in range(blocks):
         enter_ref[i] = state.astype(bf16)
         state = end_ref[i].astype(f32) + (decay * through[i]) * state
+    store = pltpu.make_async_copy(enter_ref, enter_out, sems.at[1])
+    store.start()
+    store.wait()
 
 
 def final_kernel(
-    base_ref, len_ref, state_ref, enter_ref, near_ref, short_ref, resid_ref, rate_ref, weight_ref, gain_ref,
+    base_ref, len_ref, state_ref, enter_in, near_ref, short_ref, resid_in, rate_ref, weight_ref, gain_ref,
     *refs,
-    span, modes, width, channels, most,
+    span, modes, width, channels, most, chunk,
 ):
     if channels:
-        hidden_ref, normed_ref, masks, wide, tables, sums, whole = refs
+        hidden_out, normed_out, enter_ref, resid_ref, hidden_ref, sems, masks, wide, tables, sums, whole, normed_ref = refs
     else:
-        hidden_ref, wide_ref, sum_ref, masks, wide, tables, sums, whole = refs
-    step = pl.program_id(0)
-    tiles = resid_ref.shape[1] // LANES
-
-    @pl.when(step == 0)
-    def _():
-        rows, starts = doc_start_rows(len_ref, base_ref[0], span)
-        for j in range(span):
-            masks[0, j] = flag(starts[j] < rows)
-        masks[1, 0] = flag(starts[0] < base_ref[0])
-        sums[...] = jnp.zeros(sums.shape, f32)
+        hidden_out, wide_ref, sum_ref, enter_ref, resid_ref, hidden_ref, sems, masks, wide, tables, sums = refs
+    chans = resid_ref.shape[1]
+
+    def fetches(c):
+        return [end_copy(enter_in, enter_ref, sems.at[0], c, chunk, width), cols_copy(resid_in, resid_ref, sems.at[1], c, chunk)]
+
+    def store(c):
+        return cols_copy(hidden_ref, hidden_out, sems.at[2], c, chunk)
+
+    def store_normed(c):
+        return cols_copy(normed_ref, normed_out, sems.at[3], c, chunk)
+
+    for c in range(chans // chunk):
+        for copy in fetches(c):
+            copy.start()
+    rows, starts = doc_start_rows(len_ref, base_ref[0], span)
+    for j in range(span):
+        masks[0, j] = flag(starts[j] < rows)
+    masks[1, 0] = flag(starts[0] < base_ref[0])
+    sums[...] = jnp.zeros(sums.shape, f32)
 
     def group(lanes):
         sub = lax.broadcasted_iota(jnp.int32, (SUBS, LANES), 0).astype(f32) * (-float(span))
@@ -291,29 +354,34 @@
             for slot, lane in enumerate(lanes):
                 hidden = wide[slot, pl.ds(b * (span + 1), span), :] + resid_ref[rows, cols_of(lane)].astype(f32)
                 if channels:
-                    whole[lax.div(lane, LANES) + step * tiles, rows, :] = hidden
+                    whole[lax.div(lane, LANES), rows, :] = hidden
                 else:
                     wide_ref[rows, cols_of(lane)] = hidden
                 hidden_ref[rows, cols_of(lane)] = hidden.astype(bf16)
                 squares = squares + hidden * hidden
             sums[rows, :] = squares
 
-    each_group(tiles, most, group)
-
-    @pl.when(step == pl.num_programs(0) - 1)
-    def _():
-        if channels:
-            inverse = lax.rsqrt(jnp.sum(sums[...], axis=1, keepdims=True) / channels + 1e-06)
-            sums[...] = jnp.broadcast_to(inverse, sums.shape)
-
-            def scale(lanes):
-                for lane in lanes:
-                    normed = whole[lax.div(lane, LANES)] * sums[...] * gain_ref[:, cols_of(lane)]
-                    normed_ref[:, cols_of(lane)] = normed.astype(bf16)
-
-            each_group(normed_ref.shape[1] // LANES, 4, scale)
-        else:
-            sum_ref[...] = sums[...]
+    def before(c):
+        for copy in fetches(c):
+            copy.wait()
+
+    each_chunk(chans, chunk, before, group, lambda c: store(c).start(), most)
+    if channels:
+        inverse = lax.rsqrt(jnp.sum(sums[...], axis=1, keepdims=True) / channels + 1e-06)
+        sums[...] = jnp.broadcast_to(inverse, sums.shape)
+
+        def scale(lanes):
+            for lane in lanes:
+                normed = whole[lax.div(lane, LANES)] * sums[...] * gain_ref[:, cols_of(lane)]
+                normed_ref[:, cols_of(lane)] = normed.astype(bf16)
+
+        each_chunk(chans, chunk, lambda c: None, scale, lambda c: store_normed(c).start(), 4)
+        for c in range(chans // chunk):
+            store_normed(c).wait()
+    else:
+        sum_ref[...] = sums[...]
+    for c in range(chans // chunk):
+        store(c).wait()
 
 
 def shards(
@@ -327,7 +395,7 @@
     few = chans // blocks
     width = few if few % LANES == 0 else 0
     chunk = min(chans, max(1024, width))
-    steps = chans // chunk
+    pieces = chans // chunk
     ctx_index = lax.axis_index("ctx")
     base = (ctx_index * tok_rows).astype(jnp.int32).reshape(1)
     tails = jnp.stack([query_in[tok_rows - 2 :], key_in[tok_rows - 2 :], value_in[tok_rows - 2 :]])
@@ -335,36 +403,40 @@
     weight = residues * jnp.sqrt(-jnp.expm1(-2.0 * decay_rate))
 
     smem = pl.BlockSpec(memory_space=pltpu.SMEM)
-
-    def rows_spec(rows):
-        return pl.BlockSpec((rows, chunk), lambda i: (0, i))
-
-    rim_spec = pl.BlockSpec((3, 2, chunk), lambda i: (0, 0, i))
-    taps_spec = pl.BlockSpec((3, 3, chunk), lambda i: (0, 0, i))
-    if width:
-        end_spec = pl.BlockSpec((chunk // width, modes, width), lambda i: (i, 0, 0))
-        end_shape = (blocks, modes, width)
-    else:
-        end_spec = rows_spec(modes)
-        end_shape = (modes, chans)
-    params = pltpu.CompilerParams(vmem_limit_bytes=VMEM_LIMIT)
+    vmem = pl.BlockSpec(memory_space=pltpu.VMEM)
+    hbm = pl.BlockSpec(memory_space=pltpu.HBM)
+    end_shape = (blocks, modes, few) if width else (modes, chans)
     tile_shape = (SUBS, LANES)
     wide_rows = SUBS * (span + 1)
+    params = pltpu.CompilerParams(vmem_limit_bytes=16 * MIB)
+
+    def near_by(x):
+        return pltpu.with_memory_space_constraint(x, pltpu.VMEM)
+
+    def far_off(x):
+        return pltpu.with_memory_space_constraint(x, pltpu.HBM)
+
+    def copies(kinds):
+        return pltpu.SemaphoreType.DMA((kinds, pieces))
 
     def cost(per_tile, moved):
         return pl.CostEstimate(flops=per_tile * (chans // LANES) * SUBS * LANES, bytes_accessed=moved, transcendentals=0)
 
+    rates, weights, taps, rims = near_by(decay_rate), near_by(weight), near_by(short_taps), near_by(rim_rows)
     gates, states, ends = pl.pallas_call(
-        functools.partial(state_kernel, span=span, modes=modes, width=width, most=2),
-        grid=(steps,),
-        in_specs=[smem, smem, rows_spec(tok_rows), rows_spec(tok_rows), rim_spec, taps_spec, rows_spec(modes), rows_spec(modes)],
-        out_specs=[rows_spec(tok_rows), rows_spec(modes * SUBS), end_spec],
+        functools.partial(state_kernel, span=span, modes=modes, width=width, most=2, chunk=chunk),
+        in_specs=[smem, smem, hbm, hbm, vmem, vmem, vmem, vmem],
+        out_specs=[vmem, vmem, hbm],
         out_shape=[
-            jax.ShapeDtypeStruct((tok_rows, chans), bf16),
-            jax.ShapeDtypeStruct((modes * SUBS, chans), f32),
+            pltpu.VMEM((tok_rows, chans), bf16),
+            pltpu.VMEM((modes * SUBS, chans), f32),
             jax.ShapeDtypeStruct(end_shape, bf16),
         ],
         scratch_shapes=[
+            pltpu.VMEM((tok_rows, chans), bf16),
+            pltpu.VMEM((tok_rows, chans), bf16),
+            pltpu.VMEM(end_shape, bf16),
+            copies(3),
             pltpu.VMEM((4, span) + tile_shape, f32),
             pltpu.VMEM((2, wide_rows, LANES), f32),
             pltpu.VMEM((2, wide_rows, LANES), f32),
@@ -375,31 +447,34 @@
         compiler_params=params,
         cost_estimate=cost(1000, 12 * tok_rows * chans),
         name="block_states",
-    )(base, doc_lengths, key_in, value_in, rim_rows, short_taps, decay_rate, weight)
+    )(base, doc_lengths, far_off(key_in), far_off(value_in), rims, taps, rates, weights)
 
     near = pl.pallas_call(
         functools.partial(near_kernel, span=span, modes=modes, most=4),
-        grid=(steps,),
-        in_specs=[smem, smem, rows_spec(tok_rows), rows_spec(modes), rows_spec(modes)],
-        out_specs=rows_spec(tok_rows),
-        out_shape=jax.ShapeDtypeStruct((tok_rows, chans), f32),
+        in_specs=[smem, smem, vmem, vmem, vmem],
+        out_specs=vmem,
+        out_shape=pltpu.VMEM((tok_rows, chans), f32),
         scratch_shapes=[pltpu.VMEM((2, span) + tile_shape, f32)],
         compiler_params=params,
         cost_estimate=cost(600, 7 * tok_rows * chans),
         name="near_part",
-    )(base, doc_lengths, gates, decay_rate, weight)
+    )(base, doc_lengths, near_by(gates), rates, weights)
 
     q_short = pl.pallas_call(
-        functools.partial(query_kernel, span=span, most=4),
-        grid=(steps,),
-        in_specs=[smem, smem, rows_spec(tok_rows), rim_spec, taps_spec],
-        out_specs=rows_spec(tok_rows),
-        out_shape=jax.ShapeDtypeStruct((tok_rows, chans), f32),
-        scratch_shapes=[pltpu.VMEM((2, span) + tile_shape, f32), pltpu.VMEM((4, wide_rows, LANES), f32)],
+        functools.partial(query_kernel, span=span, most=4, chunk=chunk),
+        in_specs=[smem, smem, hbm, vmem, vmem],
+        out_specs=vmem,
+        out_shape=pltpu.VMEM((tok_rows, chans), f32),
+        scratch_shapes=[
+            pltpu.VMEM((tok_rows, chans), bf16),
+            pltpu.SemaphoreType.DMA((pieces,)),
+            pltpu.VMEM((2, span) + tile_shape, f32),
+            pltpu.VMEM((4, wide_rows, LANES), f32),
+        ],
         compiler_params=params,
         cost_estimate=cost(200, 6 * tok_rows * chans),
         name="query_part",
-    )(base, doc_lengths, query_in, rim_rows, short_taps)
+    )(base, doc_lengths, far_off(query_in), rims, taps)
 
     if not width:
         ends = ends.reshape(modes, blocks, few).transpose(1, 0, 2)
@@ -408,46 +483,57 @@
     rate_few = lax.dynamic_slice_in_dim(decay_rate, ctx_index * few, few, 1)
     enter_few = pl.pallas_call(
         functools.partial(prefix_kernel, span=tok_rows),
-        in_specs=[smem, pl.BlockSpec(memory_space=pltpu.VMEM), pl.BlockSpec(memory_space=pltpu.VMEM)],
-        out_specs=pl.BlockSpec(memory_space=pltpu.VMEM),
+        in_specs=[smem, hbm, vmem],
+        out_specs=hbm,
         out_shape=jax.ShapeDtypeStruct((blocks, modes, few), bf16),
-        scratch_shapes=[pltpu.SMEM((blocks,), f32)],
+        scratch_shapes=[
+            pltpu.VMEM((blocks, modes, few), bf16),
+            pltpu.VMEM((blocks, modes, few), bf16),
+            pltpu.SemaphoreType.DMA((2,)),
+            pltpu.SMEM((blocks,), f32),
+        ],
         compiler_params=params,
         name="block_prefix",
-    )(doc_lengths, moved, rate_few)
+    )(doc_lengths, far_off(moved), near_by(rate_few))
     enter = lax.all_to_all(enter_few, "ctx", split_axis=0, concat_axis=0, tiled=True)
     if not width:
         enter = enter.transpose(1, 0, 2).reshape(modes, chans)
 
     alone = grp == 1
-    out_specs = [rows_spec(tok_rows)]
+    out_specs = [hbm]
     out_shape = [jax.ShapeDtypeStruct((tok_rows, chans), bf16)]
+    scratch = [
+        pltpu.VMEM(end_shape, bf16),
+        pltpu.VMEM((tok_rows, chans), bf16),
+        pltpu.VMEM((tok_rows, chans), bf16),
+        copies(4),
+        pltpu.VMEM((2, span) + tile_shape, f32),
+        pltpu.VMEM((2, wide_rows, LANES), f32),
+        pltpu.VMEM((2, 3, modes, LANES), f32),
+        pltpu.VMEM((tok_rows, LANES), f32),
+    ]
     if alone:
-        out_specs.append(pl.BlockSpec((tok_rows, chans), lambda i: (0, 0)))
+        out_specs.append(hbm)
         out_shape.append(jax.ShapeDtypeStruct((tok_rows, chans), bf16))
+        scratch += [pltpu.VMEM((chans // LANES, tok_rows, LANES), f32), pltpu.VMEM((tok_rows, chans), bf16)]
     else:
-        out_specs += [rows_spec(tok_rows), pl.BlockSpec((tok_rows, LANES), lambda i: (0, 0))]
+        out_specs += [vmem, vmem]
         out_shape += [jax.ShapeDtypeStruct((tok_rows, chans), f32), jax.ShapeDtypeStruct((tok_rows, LANES), f32)]
     outs = pl.pallas_call(
-        functools.partial(final_kernel, span=span, modes=modes, width=width, channels=chans if alone else 0, most=2),
-        grid=(steps,),
-        in_specs=[
-            smem, smem, rows_spec(modes * SUBS), end_spec, rows_spec(tok_rows), rows_spec(tok_rows), rows_spec(tok_rows),
-            rows_spec(modes), rows_spec(modes), pl.BlockSpec((1, chans), lambda i: (0, 0)),
-        ],
+        functools.partial(
+            final_kernel, span=span, modes=modes, width=width, channels=chans if alone else 0, most=2, chunk=chunk
+        ),
+        in_specs=[smem, smem, vmem, hbm, vmem, vmem, hbm, vmem, vmem, vmem],
         out_specs=out_specs,
         out_shape=out_shape,
-        scratch_shapes=[
-            pltpu.VMEM((2, span) + tile_shape, f32),
-            pltpu.VMEM((2, wide_rows, LANES), f32),
-            pltpu.VMEM((2, 3, modes, LANES), f32),
-            pltpu.VMEM((tok_rows, LANES), f32),
-            pltpu.VMEM((chans // LANES, tok_rows, LANES), f32),
-        ],
+        scratch_shapes=scratch,
         compiler_params=params,
         cost_estimate=cost(900, 18 * tok_rows * chans),
         name="far_part",
-    )(base, doc_lengths, states, enter, near, q_short, residual, decay_rate, weight, norm_gain.reshape(1, chans))
+    )(
+        base, doc_lengths, near_by(states), far_off(enter), near_by(near), near_by(q_short), far_off(residual),
+        rates, weights, norm_gain.reshape(1, chans),
+    )
     if alone:
         return tuple(outs)
     hidden_out, hidden, sums = outs

time: 74.4 us -> 80.4 us (1.081)
  local copies, waits for them, and re-layouts: 5.37 us -> 21 us
  Pallas kernels: 44.4 us -> 35 us
  waiting for transfers between devices: 3.87 us -> 5.7 us
  other arithmetic: 2.49 us -> 1.68 us
    unnamed x6 -> x38, local copies, waits for them, and re-layouts: 2.06 us -> 18.9 us
    pallas_call x1, Pallas kernels: 6.96 us -> 3.27 us  [shards(): pl.pallas_call(functools.partial(query_kernel, span=span, most=4, chunk=c...]
    pallas_call x1, Pallas kernels: 9.04 us -> 5.96 us  [shards(): pl.pallas_call(functools.partial(near_kernel, span=span, modes=modes, mos...]
    pallas_call x1, Pallas kernels: 13.8 us -> 10.8 us  [shards(): pl.pallas_call(functools.partial(final_kernel, span=span, modes=modes, wi...]
    all_to_all x1, starting transfers between devices: 5.6 us -> 3.85 us  [shards(): lax.all_to_all(enter_few, 'ctx', split_axis=0, concat_axis=0, tiled=True)]
    all_to_all x1, waiting for transfers between devices: 0.23 us -> 1.92 us  [shards(): moved = lax.all_to_all(ends, 'ctx', split_axis=0, concat_axis=0, tiled=True)]
    dynamic_slice x1, local copies, waits for them, and re-layouts: 1.32 us -> 0.01 us  [shards(): rate_few = lax.dynamic_slice_in_dim(decay_rate, ctx_index * few, few, 1)]
    all_to_all x1, starting transfers between devices: 8.53 us -> 9.46 us  [shards(): moved = lax.all_to_all(ends, 'ctx', split_axis=0, concat_axis=0, tiled=True)]
  transfers between devices with their start and end apart: 3 -> 3, of which waited for: 2 -> 2; matrix products, arithmetic and copies ran while one was open for 5% -> 2% of each run, Pallas kernels for 22% -> 12%
where the time goes in v5:
time: 80.4 us; the launch traced here: 79.8 us
  Pallas kernels  35 us (44%)
  local copies, waits for them, and re-layouts  21 us (26%)
  starting transfers between devices  15.7 us (20%)
  waiting for transfers between devices  5.7 us (7%)
  other arithmetic  1.68 us (2%)
    unnamed x38, local copies, waits for them, and re-layouts  18.9 us
    pallas_call x1, Pallas kernels, shards(): pl.pallas_call(functools.partial(state_kernel, span=span, modes=modes, wi...  12.7 us
    pallas_call x1, Pallas kernels, shards(): pl.pallas_call(functools.partial(final_kernel, span=span, modes=modes, wi...  10.8 us
    all_to_all x1, starting transfers between devices, shards(): moved = lax.all_to_all(ends, 'ctx', split_axis=0, concat_axis=0, tiled=True)  9.46 us
    pallas_call x1, Pallas kernels, shards(): pl.pallas_call(functools.partial(near_kernel, span=span, modes=modes, mos...  5.96 us
    all_to_all x1, starting transfers between devices, shards(): lax.all_to_all(enter_few, 'ctx', split_axis=0, concat_axis=0, tiled=True)  3.85 us
    all_to_all x1, waiting for transfers between devices, shards(): lax.all_to_all(enter_few, 'ctx', split_axis=0, concat_axis=0, tiled=True)  3.78 us
    pallas_call x1, Pallas kernels, shards(): pl.pallas_call(functools.partial(query_kernel, span=span, most=4, chunk=c...  3.27 us
  transfers between devices with their start and end apart: 3, of which 2 were waited for; matrix products, arithmetic and copies ran while one was open for 2% of the time, Pallas kernels for 12%

profile of v5, /device:TPU:0, one launch (start us, length us, event | category | flops | bytes accessed | tf_op | source)
XLA Modules:
  0.0 79.8 jit_solution(12570841649329895931)
XLA Ops:
  0.6 0.0 copy-start.4
  0.6 0.0 copy-start.7
  0.7 1.0 %slice_bitcast_fusion.2 = bf16[1,2,8192]{2,1,0:T(2,128)(2,1)S(1)} fusion(bf16[128,8192]{1,0:T(8,128)(2,1)} %query_ref.1), kind=kLoop, calls=%fused_computation.4 | loop fusion | bytes 65536 | tf_op jit(solution)/shard_map/stack | solution.py:401
  1.7 1.0 %slice_bitcast_fusion = (bf16[1,2,8192]{2,1,0:T(2,128)(2,1)S(1)}, bf16[1,2,8192]{2,1,0:T(2,128)(2,1)S(1)}) fusion(bf16[128,8192]{1,0:T(8,128)(2,1)} %value_ref.1, bf16[128,8192]{1,0:T(8,128)(2,1)} %key_ref.1), kind=kLoop, calls=%fused_computation.2 | loop fusion | bytes 131072 | tf_op jit(solution)/shard_map/stack | solution.py:401
  2.7 0.2 pad_maximum_fusion
  2.9 2.4 %collective-permute-start = (bf16[3,2,8192]{2,1,0:T(2,128)(2,1)S(1)}, bf16[3,2,8192]{2,1,0:T(2,128)(2,1)S(1)}, u32[]{:S(2)}, u32[]{:S(2)}) collective-permute-start(bf16[3,2,8192]{2,1,0:T(2,128)(2,1)S(1)} %pad_maximum_fusion), channel_id=1, source_target_pairs={{0,1},{1,2},{2,3},{3,4},{4,5},{5,6},{6,7},{7,8},{8,9},{9,10},{10,1... | collective-permute-start | bytes 294920 | tf_op jit(solution)/shard_map/ppermute | solution.py:21
  5.3 1.5 %sqrt_multiply_fusion.weight_ref = f32[16,8192]{1,0:T(8,128)S(1)} fusion(f32[16,8192]{1,0:T(8,128)} %param.14, f32[16,8192]{1,0:T(8,128)} %rate_ref.5), kind=kLoop, calls=%fused_computation | loop fusion | flops 393216 | bytes 1572864 | tf_op jit(solution)/shard_map/mul | solution.py:403
  6.8 0.0 collective-permute-done.rim_ref
  6.8 0.0 copy-start.8
  6.8 0.6 copy-done.8
  7.4 0.0 copy-done.4
  7.4 0.0 copy-done.7
  7.4 0.0 copy-start.9
  7.4 0.9 %copy-done.9 = bf16[3,2,8192]{2,1,0:T(2,128)(2,1)S(1)} copy-done((bf16[3,2,8192]{2,1,0:T(2,128)(2,1)S(1)}, bf16[3,2,8192]{2,1,0:T(2,128)(2,1)}, u32[]{:S(2)}) %copy-start.9) | copy-done | bytes 98328
  8.3 0.0 copy-start.13
  8.3 0.7 copy-done.13
  9.0 12.7 %block_states.1 = (bf16[128,8192]{1,0:T(8,128)(2,1)S(1)}, f32[128,8192]{1,0:T(8,128)S(1)}, bf16[32,16,256]{2,1,0:T(8,128)(2,1)S(1)}) custom-call(s32[1]{0:T(128)} %bitcast.base_ref, s32[16]{0:T(128)S(1)} %copy-done.13, bf16[128,8192]{1,0:T(8,128)(2,1)} %key_ref.1, bf16[128,8192]{1,0:T(8,128)(2,1)} %value_ref.1, bf16[3,2,8192]{2,1,0:T(2,128)(2,1)S(1)} %copy-done.9, ...), custom_call_target="tpu_custom_call" | custom-call | flops 65536000 | bytes 12582912 | tf_op jit(solution)/shard_map/block_states/pallas_call | solution.py:426
  21.7 0.0 copy-start.5
  21.7 1.9 %copy-done.5 = f32[128,8192]{1,0:T(8,128)} copy-done((f32[128,8192]{1,0:T(8,128)}, f32[128,8192]{1,0:T(8,128)S(1)}, u32[]{:S(2)}) %copy-start.5) | copy-done | bytes 4194328
  23.6 0.0 copy-start.11
  23.6 0.7 copy-done.11
  24.3 9.5 %all-to-all-start = ((bf16[32,16,256]{2,1,0:T(8,128)(2,1)}), bf16[32,16,256]{2,1,0:T(8,128)(2,1)}, u32[]{:S(2)}, u32[]{:S(2)}) async-start(bf16[32,16,256]{2,1,0:T(8,128)(2,1)} %copy-done.11), calls=%async_computation | async-start | bytes 524288 | tf_op jit(solution)/shard_map/all_to_all | solution.py:481
  33.8 0.0 copy-start.14
  33.8 0.6 copy-done.14
  34.5 6.0 %near_part.1.near_ref = f32[128,8192]{1,0:T(8,128)S(1)} custom-call(s32[1]{0:T(128)} %bitcast.base_ref, s32[16]{0:T(128)S(1)} %copy-done.14, bf16[128,8192]{1,0:T(8,128)(2,1)S(1)} %get-tuple-element.9.gate_ref, f32[16,8192]{1,0:T(8,128)S(1)} %copy-done.4, f32[16,8192]{1,0:T(8,128)S(1)} %sqrt_multiply_fusion.weight_ref), custom_call_target="tpu_custom_call" | custom-call | flops 39321600 | bytes 7340032 | tf_op jit(solution)/shard_map/near_part/pallas_call | solution.py:452
  40.4 0.0 copy-start
  40.4 2.0 %copy-done = f32[128,8192]{1,0:T(8,128)} copy-done((f32[128,8192]{1,0:T(8,128)}, f32[128,8192]{1,0:T(8,128)S(1)}, u32[]{:S(2)}) %copy-start) | copy-done | bytes 4194328
  42.4 1.9 %all-to-all-done.end_in = bf16[32,16,256]{2,1,0:T(8,128)(2,1)} async-done(((bf16[32,16,256]{2,1,0:T(8,128)(2,1)}), bf16[32,16,256]{2,1,0:T(8,128)(2,1)}, u32[]{:S(2)}, u32[]{:S(2)}) %all-to-all-start) | async-done | bytes 262176 | tf_op jit(solution)/shard_map/all_to_all | solution.py:481
  44.4 0.0 copy-start.15
  44.4 0.7 copy-done.15
  45.0 2.3 %block_prefix.1 = bf16[32,16,256]{2,1,0:T(8,128)(2,1)} custom-call(s32[16]{0:T(128)S(1)} %copy-done.15, bf16[32,16,256]{2,1,0:T(8,128)(2,1)} %all-to-all-done.end_in, f32[16,256]{1,0:T(8,128)S(1)} %constant_dynamic-slice_fusion.rate_ref), custom_call_target="tpu_custom_call" | custom-call | tf_op jit(solution)/shard_map/block_prefix/pallas_call | solution.py:484
  47.3 3.8 %all-to-all-start.1 = ((bf16[32,16,256]{2,1,0:T(8,128)(2,1)}), bf16[32,16,256]{2,1,0:T(8,128)(2,1)S(1)}, u32[]{:S(2)}, u32[]{:S(2)}) async-start(bf16[32,16,256]{2,1,0:T(8,128)(2,1)} %block_prefix.1), calls=%async_computation.1 | async-start | bytes 524288 | tf_op jit(solution)/shard_map/all_to_all | solution.py:498
  51.2 0.0 copy-start.10
  51.2 0.9 %copy-done.10 = bf16[3,2,8192]{2,1,0:T(2,128)(2,1)S(1)} copy-done((bf16[3,2,8192]{2,1,0:T(2,128)(2,1)S(1)}, bf16[3,2,8192]{2,1,0:T(2,128)(2,1)}, u32[]{:S(2)}) %copy-start.10) | copy-done | bytes 98328
  52.1 0.0 copy-start.16
  52.1 0.7 copy-done.16
  52.7 0.0 copy-start.12
  52.7 0.0 copy-start.17
  52.7 3.3 %query_part.1.short_ref = f32[128,8192]{1,0:T(8,128)S(1)} custom-call(s32[1]{0:T(128)} %bitcast.base_ref, s32[16]{0:T(128)S(1)} %copy-done.16, bf16[128,8192]{1,0:T(8,128)(2,1)} %query_ref.1, bf16[3,2,8192]{2,1,0:T(2,128)(2,1)S(1)} %copy-done.10, f32[3,3,8192]{2,1,0:T(4,128)S(1)} %copy-done.7), custom_call_target="tpu_custom_call" | custom-call | flops 13107200 | bytes 6291456 | tf_op jit(solution)/shard_map/query_part/pallas_call | solution.py:463
  56.0 0.0 copy-start.2
  56.0 2.0 %copy-done.2 = f32[128,8192]{1,0:T(8,128)} copy-done((f32[128,8192]{1,0:T(8,128)}, f32[128,8192]{1,0:T(8,128)S(1)}, u32[]{:S(2)}) %copy-start.2) | copy-done | bytes 4194328
  58.0 3.8 %all-to-all-done.1.enter_in = bf16[32,16,256]{2,1,0:T(8,128)(2,1)S(1)} async-done(((bf16[32,16,256]{2,1,0:T(8,128)(2,1)}), bf16[32,16,256]{2,1,0:T(8,128)(2,1)S(1)}, u32[]{:S(2)}, u32[]{:S(2)}) %all-to-all-start.1) | async-done | bytes 262176 | tf_op jit(solution)/shard_map/all_to_all | solution.py:498
  61.8 0.0 copy-start.18
  61.8 0.7 copy-done.18
  62.5 0.0 copy-done.12
  62.5 0.0 copy-done.17
  62.5 0.0 copy-start.1
  62.5 2.2 %copy-done.1 = f32[128,8192]{1,0:T(8,128)S(1)} copy-done((f32[128,8192]{1,0:T(8,128)S(1)}, f32[128,8192]{1,0:T(8,128)}, u32[]{:S(2)}) %copy-start.1) | copy-done | bytes 4194328
  64.7 0.0 copy-start.3
  64.7 2.2 %copy-done.3 = f32[128,8192]{1,0:T(8,128)S(1)} copy-done((f32[128,8192]{1,0:T(8,128)S(1)}, f32[128,8192]{1,0:T(8,128)}, u32[]{:S(2)}) %copy-start.3) | copy-done | bytes 4194328
  66.9 0.0 copy-start.6
  66.9 2.2 %copy-done.6 = f32[128,8192]{1,0:T(8,128)S(1)} copy-done((f32[128,8192]{1,0:T(8,128)S(1)}, f32[128,8192]{1,0:T(8,128)}, u32[]{:S(2)}) %copy-start.6) | copy-done | bytes 4194328
  69.1 10.8 %far_part.1 = (bf16[128,8192]{1,0:T(8,128)(2,1)}, bf16[128,8192]{1,0:T(8,128)(2,1)}) custom-call(s32[1]{0:T(128)} %bitcast.base_ref, s32[16]{0:T(128)S(1)} %copy-done.17, f32[128,8192]{1,0:T(8,128)S(1)} %copy-done.6, bf16[32,16,256]{2,1,0:T(8,128)(2,1)} %copy-done.18, f32[128,8192]{1,0:T(8,128)S(1)} %copy-done.1, f32[128,8192]{1,0:T(8,128)S(1)} %copy-done.3, ...), custom_call_target="tpu_custom_call" | custom-call | flops 58982400 | bytes 18874368 | tf_op jit(solution)/shard_map/far_part/pallas_call | solution.py:522
  (1 shorter events, 0.0 us)
Async XLA Ops:
  0.6 6.8 %copy-start.4 = (f32[16,8192]{1,0:T(8,128)S(1)}, f32[16,8192]{1,0:T(8,128)}, u32[]{:S(2)}) copy-start(f32[16,8192]{1,0:T(8,128)} %rate_ref.5) | copy-start | bytes 1572868
  0.6 6.8 %copy-start.7 = (f32[3,3,8192]{2,1,0:T(4,128)S(1)}, f32[3,3,8192]{2,1,0:T(4,128)}, u32[]{:S(2)}) copy-start(f32[3,3,8192]{2,1,0:T(4,128)} %taps_ref.3) | copy-start | bytes 884740
  2.9 3.9 %collective-permute-start = (bf16[3,2,8192]{2,1,0:T(2,128)(2,1)S(1)}, bf16[3,2,8192]{2,1,0:T(2,128)(2,1)S(1)}, u32[]{:S(2)}, u32[]{:S(2)}) collective-permute-start(bf16[3,2,8192]{2,1,0:T(2,128)(2,1)S(1)} %pad_maximum_fusion), channel_id=1, source_target_pairs={{0,1},{1,2},{2,3},{3,4},{4,5},{5,6},{6,7},{7,8},{8,9},{9,10},{10,1... | collective-permute-start | bytes 294920 | tf_op jit(solution)/shard_map/ppermute | solution.py:21
  6.8 0.6 copy-start.8
  7.4 0.9 %copy-start.9 = (bf16[3,2,8192]{2,1,0:T(2,128)(2,1)S(1)}, bf16[3,2,8192]{2,1,0:T(2,128)(2,1)}, u32[]{:S(2)}) copy-start(bf16[3,2,8192]{2,1,0:T(2,128)(2,1)} %copy-done.8) | copy-start | bytes 294916
  8.3 0.7 copy-start.13
  21.7 1.9 %copy-start.5 = (f32[128,8192]{1,0:T(8,128)}, f32[128,8192]{1,0:T(8,128)S(1)}, u32[]{:S(2)}) copy-start(f32[128,8192]{1,0:T(8,128)S(1)} %get-tuple-element.7.state_ref) | copy-start | bytes 12582916
  23.6 0.7 copy-start.11
  24.3 20.0 %all-to-all-start = ((bf16[32,16,256]{2,1,0:T(8,128)(2,1)}), bf16[32,16,256]{2,1,0:T(8,128)(2,1)}, u32[]{:S(2)}, u32[]{:S(2)}) async-start(bf16[32,16,256]{2,1,0:T(8,128)(2,1)} %copy-done.11), calls=%async_computation | async-start | bytes 524288 | tf_op jit(solution)/shard_map/all_to_all | solution.py:481
  33.8 0.7 copy-start.14
  40.4 2.0 %copy-start = (f32[128,8192]{1,0:T(8,128)}, f32[128,8192]{1,0:T(8,128)S(1)}, u32[]{:S(2)}) copy-start(f32[128,8192]{1,0:T(8,128)S(1)} %near_part.1.near_ref) | copy-start | bytes 12582916
  44.4 0.7 copy-start.15
  47.3 14.5 %all-to-all-start.1 = ((bf16[32,16,256]{2,1,0:T(8,128)(2,1)}), bf16[32,16,256]{2,1,0:T(8,128)(2,1)S(1)}, u32[]{:S(2)}, u32[]{:S(2)}) async-start(bf16[32,16,256]{2,1,0:T(8,128)(2,1)} %block_prefix.1), calls=%async_computation.1 | async-start | bytes 524288 | tf_op jit(solution)/shard_map/all_to_all | solution.py:498
  51.2 0.9 %copy-start.10 = (bf16[3,2,8192]{2,1,0:T(2,128)(2,1)S(1)}, bf16[3,2,8192]{2,1,0:T(2,128)(2,1)}, u32[]{:S(2)}) copy-start(bf16[3,2,8192]{2,1,0:T(2,128)(2,1)} %copy-done.8) | copy-start | bytes 294916
  52.1 0.7 copy-start.16
  52.7 9.8 %copy-start.12 = (f32[8192]{0:T(1024)S(1)}, f32[8192]{0:T(1024)}, u32[]{:S(2)}) copy-start(f32[8192]{0:T(1024)} %param.17) | copy-start | bytes 98308
  52.7 9.8 %copy-start.17 = (s32[16]{0:T(128)S(1)}, s32[16]{0:T(128)}, u32[]{:S(2)}) copy-start(s32[16]{0:T(128)} %len_ref.9) | copy-start | bytes 196
  56.0 2.0 %copy-start.2 = (f32[128,8192]{1,0:T(8,128)}, f32[128,8192]{1,0:T(8,128)S(1)}, u32[]{:S(2)}) copy-start(f32[128,8192]{1,0:T(8,128)S(1)} %query_part.1.short_ref) | copy-start | bytes 12582916
  61.8 0.7 copy-start.18
  62.5 2.2 %copy-start.1 = (f32[128,8192]{1,0:T(8,128)S(1)}, f32[128,8192]{1,0:T(8,128)}, u32[]{:S(2)}) copy-start(f32[128,8192]{1,0:T(8,128)} %copy-done) | copy-start | bytes 12582916
  64.7 2.2 %copy-start.3 = (f32[128,8192]{1,0:T(8,128)S(1)}, f32[128,8192]{1,0:T(8,128)}, u32[]{:S(2)}) copy-start(f32[128,8192]{1,0:T(8,128)} %copy-done.2) | copy-start | bytes 12582916
  66.9 2.2 %copy-start.6 = (f32[128,8192]{1,0:T(8,128)S(1)}, f32[128,8192]{1,0:T(8,128)}, u32[]{:S(2)}) copy-start(f32[128,8192]{1,0:T(8,128)} %copy-done.5) | copy-start | bytes 12582916

commit v6 on v5

--- a/solution.py
+++ b/solution.py
@@ -19,6 +19,10 @@
     count = lax.axis_size(axis)
     pairs = [(i, i + by) for i in range(count) if 0 <= i + by < count]
     return lax.ppermute(shard, axis, pairs)
+
+
+def swap(shard, axis):
+    return lax.ppermute(shard, axis, [(i, i ^ 1) for i in range(lax.axis_size(axis))])
 
 
 def doc_start_rows(len_ref, base, span):
@@ -69,13 +73,6 @@
     return pltpu.make_async_copy(src.at[:, cols], dst.at[:, cols], sem.at[c])
 
 
-def end_copy(src, dst, sem, c, chunk, width):
-    if not width:
-        return cols_copy(src, dst, sem, c, chunk)
-    rows = pl.ds(c * (chunk // width), chunk // width)
-    return pltpu.make_async_copy(src.at[rows], dst.at[rows], sem.at[c])
-
-
 def cols_of(lane):
     return pl.ds(lane, LANES)
 
@@ -109,19 +106,23 @@
     ]
 
 
+def half_of(base_ref, rows, chans, lane):
+    half = chans // 2
+    which = lax.div(lane, half)
+    mine = which == lax.rem(lax.div(base_ref[0], rows), 2)
+    return mine, pl.multiple_of(lane - which * half, LANES)
+
+
 def state_kernel(
     base_ref, len_ref, key_ref, value_ref, rim_ref, taps_ref, rate_ref, weight_ref,
-    gate_ref, state_ref, end_out,
-    key_buf, value_buf, end_ref, sems, masks, wide_k, wide_v, tables, ends, held,
-    *, span, modes, width, most, chunk,
+    gate_ref, state_ref, own_ref, give_ref,
+    key_buf, value_buf, sems, masks, wide_k, wide_v, tables, ends, held,
+    *, span, modes, most, chunk,
 ):
     chans = key_buf.shape[1]
 
     def fetches(c):
         return [cols_copy(key_ref, key_buf, sems.at[0], c, chunk), cols_copy(value_ref, value_buf, sems.at[1], c, chunk)]
-
-    def store(c):
-        return end_copy(end_ref, end_out, sems.at[2], c, chunk, width)
 
     for c in range(chans // chunk):
         for copy in fetches(c):
@@ -186,19 +187,21 @@
                     row_of(tables.at[slot, 4], n) * masks[3, 3]
                 ) * pltpu.roll(x, 1, 0)
         for slot, lane in enumerate(lanes):
-            end = ends[slot].astype(bf16)
-            if width:
-                end_ref[lax.div(lane, width), :, cols_of(pl.multiple_of(lax.rem(lane, width), LANES))] = end
-            else:
-                end_ref[:, cols_of(lane)] = end
+            mine, here = half_of(base_ref, key_ref.shape[0], chans, lane)
+
+            @pl.when(mine)
+            def _():
+                own_ref[:, cols_of(here)] = ends[slot]
+
+            @pl.when(jnp.logical_not(mine))
+            def _():
+                give_ref[:, cols_of(here)] = ends[slot]
 
     def before(c):
         for copy in fetches(c):
             copy.wait()
 
-    each_chunk(chans, chunk, before, group, lambda c: store(c).start(), most)
-    for c in range(chans // chunk):
-        store(c).wait()
+    each_chunk(chans, chunk, before, group, lambda c: None, most)
 
 
 def keep_masks(base_ref, len_ref, masks, span):
@@ -266,51 +269,74 @@
     each_chunk(chans, chunk, lambda c: fetch(c).wait(), group, lambda c: None, most)
 
 
-def prefix_kernel(len_ref, end_in, rate_ref, enter_out, end_ref, enter_ref, sems, through, *, span):
-    blocks = end_ref.shape[0]
-    fetch = pltpu.make_async_copy(end_in, end_ref, sems.at[0])
-    fetch.start()
-    for i in range(blocks):
-        through[i] = jnp.float32(1.0)
+def unbroken(len_ref, first, count):
     start = jnp.int32(0)
-    through[0] = jnp.float32(0.0)
+    whole = jnp.where((first <= 0) & (first + count > 0), 0.0, 1.0)
     for d in range(len_ref.shape[0] - 1):
         start = start + len_ref[d]
-        through[lax.div(start, jnp.int32(span))] = jnp.float32(0.0)
-    decay = jnp.exp(-float(span) * rate_ref[...])
-    state = jnp.zeros(decay.shape, f32)
-    fetch.wait()
-    for i in range(blocks):
-        enter_ref[i] = state.astype(bf16)
-        state = end_ref[i].astype(f32) + (decay * through[i]) * state
-    store = pltpu.make_async_copy(enter_ref, enter_out, sems.at[1])
-    store.start()
-    store.wait()
+        whole = jnp.where((start >= first) & (start < first + count), 0.0, whole)
+    return whole.astype(f32)
+
+
+def pair_rates(base_ref, rate_ref, rows, shape):
+    parity = lax.rem(lax.div(base_ref[0], rows), 2)
+    return parity, rate_ref[:, pl.ds(pl.multiple_of(parity * shape[1], LANES), shape[1])]
+
+
+def early_late(parity, own, got):
+    odd = jnp.full(own.shape, parity, jnp.int32) == 1
+    return jnp.where(odd, got, own), jnp.where(odd, own, got)
+
+
+def pair_kernel(base_ref, len_ref, own_ref, got_ref, rate_ref, end_ref, *, rows):
+    parity, rate = pair_rates(base_ref, rate_ref, rows, own_ref.shape)
+    early, late = early_late(parity, own_ref[...], got_ref[...])
+    through = unbroken(len_ref, base_ref[0] + (1 - parity) * rows, rows)
+    end_ref[...] = (late + (jnp.exp(-float(rows) * rate) * through) * early).astype(bf16)
+
+
+def reach_kernel(base_ref, len_ref, near_ref, far_ref, rate_ref, enter_ref, *, rows, reach):
+    parity, rate = pair_rates(base_ref, rate_ref, rows, near_ref.shape)
+    span = 2 * rows * reach
+    through = unbroken(len_ref, base_ref[0] - parity * rows - span, span)
+    enter_ref[...] = (
+        near_ref[...].astype(f32) + (jnp.exp(-float(span) * rate) * through) * far_ref[...].astype(f32)
+    ).astype(enter_ref.dtype)
+
+
+def enter_kernel(base_ref, len_ref, enter_ref, own_ref, got_ref, rate_ref, mine_ref, give_ref, *, rows):
+    parity, rate = pair_rates(base_ref, rate_ref, rows, own_ref.shape)
+    early, _ = early_late(parity, own_ref[...], got_ref[...])
+    through = unbroken(len_ref, base_ref[0] - parity * rows, rows)
+    first = enter_ref[...].astype(f32)
+    second = early + (jnp.exp(-float(rows) * rate) * through) * first
+    give, mine = early_late(parity, second, first)
+    mine_ref[...] = mine
+    give_ref[...] = give
 
 
 def final_kernel(
-    base_ref, len_ref, state_ref, enter_in, near_ref, short_ref, resid_in, rate_ref, weight_ref, gain_ref,
+    base_ref, len_ref, state_ref, mine_ref, got_ref, near_ref, short_ref, resid_in, rate_ref, weight_ref, gain_ref,
     *refs,
-    span, modes, width, channels, most, chunk,
+    span, modes, channels, most, chunk,
 ):
     if channels:
-        hidden_out, normed_out, enter_ref, resid_ref, hidden_ref, sems, masks, wide, tables, sums, whole, normed_ref = refs
+        hidden_out, normed_out, resid_ref, hidden_ref, sems, masks, wide, tables, sums, whole, normed_ref = refs
     else:
-        hidden_out, wide_ref, sum_ref, enter_ref, resid_ref, hidden_ref, sems, masks, wide, tables, sums = refs
+        hidden_out, wide_ref, sum_ref, resid_ref, hidden_ref, sems, masks, wide, tables, sums = refs
     chans = resid_ref.shape[1]
 
-    def fetches(c):
-        return [end_copy(enter_in, enter_ref, sems.at[0], c, chunk, width), cols_copy(resid_in, resid_ref, sems.at[1], c, chunk)]
+    def fetch(c):
+        return cols_copy(resid_in, resid_ref, sems.at[0], c, chunk)
 
     def store(c):
-        return cols_copy(hidden_ref, hidden_out, sems.at[2], c, chunk)
+        return cols_copy(hidden_ref, hidden_out, sems.at[1], c, chunk)
 
     def store_normed(c):
-        return cols_copy(normed_ref, normed_out, sems.at[3], c, chunk)
+        return cols_copy(normed_ref, normed_out, sems.at[2], c, chunk)
 
     for c in range(chans // chunk):
-        for copy in fetches(c):
-            copy.start()
+        fetch(c).start()
     rows, starts = doc_start_rows(len_ref, base_ref[0], span)
     for j in range(span):
         masks[0, j] = flag(starts[j] < rows)
@@ -321,13 +347,12 @@
         sub = lax.broadcasted_iota(jnp.int32, (SUBS, LANES), 0).astype(f32) * (-float(span))
         through = masks[1, 0]
         for slot, lane in enumerate(lanes):
-            if width:
-                enter = enter_ref[lax.div(lane, width), :, cols_of(pl.multiple_of(lax.rem(lane, width), LANES))]
-            else:
-                enter = enter_ref[:, cols_of(lane)]
+            mine, here = half_of(base_ref, resid_ref.shape[0], chans, lane)
+            mine = jnp.full((modes, LANES), mine.astype(jnp.int32), jnp.int32) == 1
+            enter = jnp.where(mine, mine_ref[:, cols_of(here)], got_ref[:, cols_of(here)])
             rate = rate_ref[:, cols_of(lane)]
             tables[slot, 0] = jnp.exp(-rate)
-            tables[slot, 1] = weight_ref[:, cols_of(lane)] * enter.astype(f32)
+            tables[slot, 1] = weight_ref[:, cols_of(lane)] * enter
             tables[slot, 2] = rate
         parts = [
             [
@@ -361,11 +386,7 @@
                 squares = squares + hidden * hidden
             sums[rows, :] = squares
 
-    def before(c):
-        for copy in fetches(c):
-            copy.wait()
-
-    each_chunk(chans, chunk, before, group, lambda c: store(c).start(), most)
+    each_chunk(chans, chunk, lambda c: fetch(c).wait(), group, lambda c: store(c).start(), most)
     if channels:
         inverse = lax.rsqrt(jnp.sum(sums[...], axis=1, keepdims=True) / channels + 1e-06)
         sums[...] = jnp.broadcast_to(inverse, sums.shape)
@@ -392,9 +413,7 @@
     span = tok_rows // SUBS
     blocks = lax.axis_size("ctx")
     grp = lax.axis_size("grp")
-    few = chans // blocks
-    width = few if few % LANES == 0 else 0
-    chunk = min(chans, max(1024, width))
+    chunk = min(chans, 1024)
     pieces = chans // chunk
     ctx_index = lax.axis_index("ctx")
     base = (ctx_index * tok_rows).astype(jnp.int32).reshape(1)
@@ -405,7 +424,7 @@
     smem = pl.BlockSpec(memory_space=pltpu.SMEM)
     vmem = pl.BlockSpec(memory_space=pltpu.VMEM)
     hbm = pl.BlockSpec(memory_space=pltpu.HBM)
-    end_shape = (blocks, modes, few) if width else (modes, chans)
+    half = jax.ShapeDtypeStruct((modes, chans // 2), f32)
     tile_shape = (SUBS, LANES)
     wide_rows = SUBS * (span + 1)
     params = pltpu.CompilerParams(vmem_limit_bytes=16 * MIB)
@@ -423,20 +442,20 @@
         return pl.CostEstimate(flops=per_tile * (chans // LANES) * SUBS * LANES, bytes_accessed=moved, transcendentals=0)
 
     rates, weights, taps, rims = near_by(decay_rate), near_by(weight), near_by(short_taps), near_by(rim_rows)
-    gates, states, ends = pl.pallas_call(
-        functools.partial(state_kernel, span=span, modes=modes, width=width, most=2, chunk=chunk),
+    gates, states, own, give = pl.pallas_call(
+        functools.partial(state_kernel, span=span, modes=modes, most=2, chunk=chunk),
         in_specs=[smem, smem, hbm, hbm, vmem, vmem, vmem, vmem],
-        out_specs=[vmem, vmem, hbm],
+        out_specs=[vmem, vmem, vmem, vmem],
         out_shape=[
             pltpu.VMEM((tok_rows, chans), bf16),
             pltpu.VMEM((modes * SUBS, chans), f32),
-            jax.ShapeDtypeStruct(end_shape, bf16),
+            pltpu.VMEM(half.shape, f32),
+            pltpu.VMEM(half.shape, f32),
         ],
         scratch_shapes=[
             pltpu.VMEM((tok_rows, chans), bf16),
             pltpu.VMEM((tok_rows, chans), bf16),
-            pltpu.VMEM(end_shape, bf16),
-            copies(3),
+            copies(2),
             pltpu.VMEM((4, span) + tile_shape, f32),
             pltpu.VMEM((2, wide_rows, LANES), f32),
             pltpu.VMEM((2, wide_rows, LANES), f32),
@@ -476,37 +495,42 @@
         name="query_part",
     )(base, doc_lengths, far_off(query_in), rims, taps)
 
-    if not width:
-        ends = ends.reshape(modes, blocks, few).transpose(1, 0, 2)
-    moved = lax.all_to_all(ends, "ctx", split_axis=0, concat_axis=0, tiled=True)
-    moved, near = lax.optimization_barrier((moved, near))
-    rate_few = lax.dynamic_slice_in_dim(decay_rate, ctx_index * few, few, 1)
-    enter_few = pl.pallas_call(
-        functools.partial(prefix_kernel, span=tok_rows),
-        in_specs=[smem, hbm, vmem],
-        out_specs=hbm,
-        out_shape=jax.ShapeDtypeStruct((blocks, modes, few), bf16),
-        scratch_shapes=[
-            pltpu.VMEM((blocks, modes, few), bf16),
-            pltpu.VMEM((blocks, modes, few), bf16),
-            pltpu.SemaphoreType.DMA((2,)),
-            pltpu.SMEM((blocks,), f32),
-        ],
-        compiler_params=params,
-        name="block_prefix",
-    )(doc_lengths, far_off(moved), near_by(rate_few))
-    enter = lax.all_to_all(enter_few, "ctx", split_axis=0, concat_axis=0, tiled=True)
-    if not width:
-        enter = enter.transpose(1, 0, 2).reshape(modes, chans)
+    got = swap(give, "ctx")
+
+    def pair_call(kernel, operands, out_shape, name, **static):
+        count = len(operands) + 1
+        return pl.pallas_call(
+            functools.partial(kernel, rows=tok_rows, **static),
+            in_specs=[smem, smem] + [vmem] * count,
+            out_specs=[vmem] * len(out_shape),
+            out_shape=out_shape,
+            compiler_params=params,
+            name=name,
+        )(base, doc_lengths, *[near_by(x) for x in operands], rates)
+
+    sent = pltpu.VMEM(half.shape, bf16)
+    ends = pair_call(pair_kernel, [own, got], [sent], "pair_ends")[0]
+    one_on, two_on = from_behind(ends, "ctx", 2), from_behind(ends, "ctx", 4)
+    one_on, two_on, near = lax.optimization_barrier((one_on, two_on, near))
+    enter = pair_call(reach_kernel, [one_on, two_on], [sent], "reach_2", reach=1)[0]
+    reach = 2
+    while reach < blocks // 8:
+        on = from_behind(enter, "ctx", 2 * reach)
+        on, q_short = lax.optimization_barrier((on, q_short))
+        enter = pair_call(reach_kernel, [enter, on], [sent], "reach_%d" % (2 * reach), reach=reach)[0]
+        reach *= 2
+    mine, give_back = pair_call(
+        enter_kernel, [enter, own, got], [pltpu.VMEM(half.shape, f32), pltpu.VMEM(half.shape, f32)], "pair_enter"
+    )
+    got_back = swap(give_back, "ctx")
 
     alone = grp == 1
     out_specs = [hbm]
     out_shape = [jax.ShapeDtypeStruct((tok_rows, chans), bf16)]
     scratch = [
-        pltpu.VMEM(end_shape, bf16),
         pltpu.VMEM((tok_rows, chans), bf16),
         pltpu.VMEM((tok_rows, chans), bf16),
-        copies(4),
+        copies(3),
         pltpu.VMEM((2, span) + tile_shape, f32),
         pltpu.VMEM((2, wide_rows, LANES), f32),
         pltpu.VMEM((2, 3, modes, LANES), f32),
@@ -521,9 +545,9 @@
         out_shape += [jax.ShapeDtypeStruct((tok_rows, chans), f32), jax.ShapeDtypeStruct((tok_rows, LANES), f32)]
     outs = pl.pallas_call(
         functools.partial(
-            final_kernel, span=span, modes=modes, width=width, channels=chans if alone else 0, most=2, chunk=chunk
+            final_kernel, span=span, modes=modes, channels=chans if alone else 0, most=2, chunk=chunk
         ),
-        in_specs=[smem, smem, vmem, hbm, vmem, vmem, hbm, vmem, vmem, vmem],
+        in_specs=[smem, smem, vmem, vmem, vmem, vmem, vmem, hbm, vmem, vmem, vmem],
         out_specs=out_specs,
         out_shape=out_shape,
         scratch_shapes=scratch,
@@ -531,7 +555,7 @@
         cost_estimate=cost(900, 18 * tok_rows * chans),
         name="far_part",
     )(
-        base, doc_lengths, near_by(states), far_off(enter), near_by(near), near_by(q_short), far_off(residual),
+        base, doc_lengths, near_by(states), near_by(mine), near_by(got_back), near_by(near), near_by(q_short), far_off(residual),
         rates, weights, norm_gain.reshape(1, chans),
     )
     if alone:

time: 80.4 us -> 62.1 us (0.77)
  the two profiles are of different devices: /device:TPU:0 before, /device:TPU:11 now
where the time goes in v6:
time: 62.1 us; the launch traced here: 61.8 us
  Pallas kernels  35.6 us (57%)
  starting transfers between devices  17.5 us (28%)
  waiting for transfers between devices  3.48 us (6%)
  local copies, waits for them, and re-layouts  2.74 us (4%)
  other arithmetic  1.68 us (3%)
  between operations  0.77 us (1%)
    ppermute x4, starting transfers between devices, from_behind(): return lax.ppermute(shard, axis, pairs)  14 us
    pallas_call x1, Pallas kernels, shards(): pl.pallas_call(functools.partial(state_kernel, span=span, modes=modes, mo...  12.9 us
    pallas_call x1, Pallas kernels, shards(): pl.pallas_call(functools.partial(final_kernel, span=span, modes=modes, ch...  10.9 us
    pallas_call x1, Pallas kernels, shards(): pl.pallas_call(functools.partial(near_kernel, span=span, modes=modes, mos...  5.95 us
    ppermute x2, starting transfers between devices, swap(): lax.ppermute(shard, axis, [(i, i ^ 1) for i in range(lax.axis_size(axis))])  3.53 us
    pallas_call x1, Pallas kernels, shards(): pl.pallas_call(functools.partial(query_kernel, span=span, most=4, chunk=c...  3.27 us
    pallas_call x4, Pallas kernels, pair_call(): pl.pallas_call(functools.partial(kernel, rows=tok_rows, **static), in_spe...  2.59 us
    ppermute x2, waiting for transfers between devices, swap(): lax.ppermute(shard, axis, [(i, i ^ 1) for i in range(lax.axis_size(axis))])  2.32 us
  transfers between devices with their start and end apart: 6, of which 4 were waited for; matrix products, arithmetic and copies ran while one was open for 2% of the time, Pallas kernels for 15%

profile of v6, /device:TPU:11, one launch (start us, length us, event | category | flops | bytes accessed | tf_op | source)
XLA Modules:
  0.0 61.8 jit_solution(3030565674798028935)
XLA Ops:
  0.6 0.0 copy-start
  0.6 0.0 copy-start.1
  0.7 1.0 %slice_bitcast_fusion.2 = bf16[1,2,8192]{2,1,0:T(2,128)(2,1)S(1)} fusion(bf16[128,8192]{1,0:T(8,128)(2,1)} %query_ref.1), kind=kLoop, calls=%fused_computation.4 | loop fusion | bytes 65536 | tf_op jit(solution)/shard_map/stack | solution.py:420
  1.7 1.0 %slice_bitcast_fusion = (bf16[1,2,8192]{2,1,0:T(2,128)(2,1)S(1)}, bf16[1,2,8192]{2,1,0:T(2,128)(2,1)S(1)}) fusion(bf16[128,8192]{1,0:T(8,128)(2,1)} %value_ref.1, bf16[128,8192]{1,0:T(8,128)(2,1)} %key_ref.1), kind=kLoop, calls=%fused_computation.2 | loop fusion | bytes 131072 | tf_op jit(solution)/shard_map/stack | solution.py:420
  2.7 0.2 pad_maximum_fusion
  2.9 3.7 %collective-permute-start = (bf16[3,2,8192]{2,1,0:T(2,128)(2,1)S(1)}, bf16[3,2,8192]{2,1,0:T(2,128)(2,1)S(1)}, u32[]{:S(2)}, u32[]{:S(2)}) collective-permute-start(bf16[3,2,8192]{2,1,0:T(2,128)(2,1)S(1)} %pad_maximum_fusion), channel_id=1, source_target_pairs={{0,1},{1,2},{2,3},{3,4},{4,5},{5,6},{6,7},{7,8},{8,9},{9,10},{10,1... | collective-permute-start | bytes 294920 | tf_op jit(solution)/shard_map/ppermute | solution.py:21
  6.6 1.5 %sqrt_multiply_fusion.weight_ref = f32[16,8192]{1,0:T(8,128)S(1)} fusion(f32[16,8192]{1,0:T(8,128)} %param.14, f32[16,8192]{1,0:T(8,128)} %rate_ref.13), kind=kLoop, calls=%fused_computation | loop fusion | flops 393216 | bytes 1572864 | tf_op jit(solution)/shard_map/mul | solution.py:422
  8.1 0.1 collective-permute-done.rim_ref
  8.2 0.0 copy-done
  8.2 0.0 copy-done.1
  8.2 0.0 copy-start.3
  8.2 0.7 %copy-done.3 = s32[16]{0:T(128)S(1)} copy-done((s32[16]{0:T(128)S(1)}, s32[16]{0:T(128)}, u32[]{:S(2)}) %copy-start.3) | copy-done | bytes 88
  8.9 12.9 %block_states.1 = (bf16[128,8192]{1,0:T(8,128)(2,1)S(1)}, f32[128,8192]{1,0:T(8,128)S(1)}, f32[16,4096]{1,0:T(8,128)S(1)}, f32[16,4096]{1,0:T(8,128)S(1)}) custom-call(s32[1]{0:T(128)} %bitcast.base_ref, s32[16]{0:T(128)S(1)} %copy-done.3, bf16[128,8192]{1,0:T(8,128)(2,1)} %key_ref.1, bf16[128,8192]{1,0:T(8,128)(2,1)} %value_ref.1, ...), custom_call_target="tpu_custom_call" | custom-call | flops 65536000 | bytes 12582912 | tf_op jit(solution)/shard_map/block_states/pallas_call | solution.py:445
  21.8 1.4 %collective-permute-start.1 = (f32[16,4096]{1,0:T(8,128)S(1)}, f32[16,4096]{1,0:T(8,128)S(1)}, u32[]{:S(2)}, u32[]{:S(2)}) collective-permute-start(f32[16,4096]{1,0:T(8,128)S(1)} %get-tuple-element.15), channel_id=1, source_target_pairs={{0,1},{1,0},{2,3},{3,2},{4,5},{5,4},{6,7},{7,6},{8,9},{9,8},{10,11... | collective-permute-start | bytes 786440 | tf_op jit(solution)/shard_map/ppermute | solution.py:25
  23.2 1.2 %collective-permute-done.1.got_ref = f32[16,4096]{1,0:T(8,128)S(1)} collective-permute-done((f32[16,4096]{1,0:T(8,128)S(1)}, f32[16,4096]{1,0:T(8,128)S(1)}, u32[]{:S(2)}, u32[]{:S(2)}) %collective-permute-start.1) | collective-permute-done | bytes 262176 | tf_op jit(solution)/shard_map/ppermute | solution.py:25
  24.3 0.6 %pair_ends.1 = bf16[16,4096]{1,0:T(8,128)(2,1)S(1)} custom-call(s32[1]{0:T(128)} %bitcast.base_ref, s32[16]{0:T(128)S(1)} %copy-done.3, f32[16,4096]{1,0:T(8,128)S(1)} %get-tuple-element.14.own_ref, f32[16,4096]{1,0:T(8,128)S(1)} %collective-permute-done.1.got_ref, f32[16,8192]{1,0:T(8,128)S(1)} %copy-done), custom_call_target="tpu_custom_call" | custom-call | tf_op jit(solution)/shard_map/pair_ends/pallas_call | solution.py:502
  25.0 3.1 %collective-permute-start.3 = (bf16[16,4096]{1,0:T(8,128)(2,1)S(1)}, bf16[16,4096]{1,0:T(8,128)(2,1)S(1)}, u32[]{:S(2)}, u32[]{:S(2)}) collective-permute-start(bf16[16,4096]{1,0:T(8,128)(2,1)S(1)} %pair_ends.1), channel_id=1, source_target_pairs={{0,4},{1,5},{2,6},{3,7},{4,8},{5,9},{6,10},{7,11},{8,12},{9,13},{1... | collective-permute-start | bytes 393224 | tf_op jit(solution)/shard_map/ppermute | solution.py:21
  28.1 4.9 %collective-permute-start.2 = (bf16[16,4096]{1,0:T(8,128)(2,1)S(1)}, bf16[16,4096]{1,0:T(8,128)(2,1)S(1)}, u32[]{:S(2)}, u32[]{:S(2)}) collective-permute-start(bf16[16,4096]{1,0:T(8,128)(2,1)S(1)} %pair_ends.1), channel_id=1, source_target_pairs={{0,2},{1,3},{2,4},{3,5},{4,6},{5,7},{6,8},{7,9},{8,10},{9,11},{10,... | collective-permute-start | bytes 393224 | tf_op jit(solution)/shard_map/ppermute | solution.py:21
  33.1 6.0 %near_part.1.near_ref = f32[128,8192]{1,0:T(8,128)S(1)} custom-call(s32[1]{0:T(128)} %bitcast.base_ref, s32[16]{0:T(128)S(1)} %copy-done.3, bf16[128,8192]{1,0:T(8,128)(2,1)S(1)} %get-tuple-element.16.gate_ref, f32[16,8192]{1,0:T(8,128)S(1)} %copy-done, f32[16,8192]{1,0:T(8,128)S(1)} %sqrt_multiply_fusion.weight_ref), custom_call_target="tpu_custom_call" | custom-call | flops 39321600 | bytes 7340032 | tf_op jit(solution)/shard_map/near_part/pallas_call | solution.py:471
  39.0 0.0 collective-permute-done.3.far_ref
  39.0 0.0 collective-permute-done.2.near_ref
  39.0 0.6 %reach_2.1.near_ref = bf16[16,4096]{1,0:T(8,128)(2,1)S(1)} custom-call(s32[1]{0:T(128)} %bitcast.base_ref, s32[16]{0:T(128)S(1)} %copy-done.3, bf16[16,4096]{1,0:T(8,128)(2,1)S(1)} %collective-permute-done.2.near_ref, bf16[16,4096]{1,0:T(8,128)(2,1)S(1)} %collective-permute-done.3.far_ref, f32[16,8192]{1,0:T(8,128)S(1)} %copy-done), custom_call_target="tpu_custom_call" | custom-call | tf_op jit(solution)/shard_map/reach_2/pallas_call | solution.py:502
  39.7 0.0 copy-start.4
  39.7 2.2 %collective-permute-start.4 = (bf16[16,4096]{1,0:T(8,128)(2,1)S(1)}, bf16[16,4096]{1,0:T(8,128)(2,1)S(1)}, u32[]{:S(2)}, u32[]{:S(2)}) collective-permute-start(bf16[16,4096]{1,0:T(8,128)(2,1)S(1)} %reach_2.1.near_ref), channel_id=1, source_target_pairs={{0,4},{1,5},{2,6},{3,7},{4,8},{5,9},{6,10},{7,11},{8,12},{9,13},{1... | collective-permute-start | bytes 393224 | tf_op jit(solution)/shard_map/ppermute | solution.py:21
  41.9 3.3 %query_part.1.short_ref = f32[128,8192]{1,0:T(8,128)S(1)} custom-call(s32[1]{0:T(128)} %bitcast.base_ref, s32[16]{0:T(128)S(1)} %copy-done.3, bf16[128,8192]{1,0:T(8,128)(2,1)} %query_ref.1, bf16[3,2,8192]{2,1,0:T(2,128)(2,1)S(1)} %collective-permute-done.rim_ref, f32[3,3,8192]{2,1,0:T(4,128)S(1)} %copy-done.1), custom_call_target="tpu_custom_call" | custom-call | flops 13107200 | bytes 6291456 | tf_op jit(solution)/shard_map/query_part/pallas_call | solution.py:482
  45.2 0.0 copy-start.2
  45.2 1.1 %collective-permute-done.4.far_ref = bf16[16,4096]{1,0:T(8,128)(2,1)S(1)} collective-permute-done((bf16[16,4096]{1,0:T(8,128)(2,1)S(1)}, bf16[16,4096]{1,0:T(8,128)(2,1)S(1)}, u32[]{:S(2)}, u32[]{:S(2)}) %collective-permute-start.4) | collective-permute-done | bytes 131104 | tf_op jit(solution)/shard_map/ppermute | solution.py:21
  46.3 0.0 copy-done.4
  46.3 0.6 %reach_4.1.enter_ref = bf16[16,4096]{1,0:T(8,128)(2,1)S(1)} custom-call(s32[1]{0:T(128)} %bitcast.base_ref, s32[16]{0:T(128)S(1)} %copy-done.4, bf16[16,4096]{1,0:T(8,128)(2,1)S(1)} %reach_2.1.near_ref, bf16[16,4096]{1,0:T(8,128)(2,1)S(1)} %collective-permute-done.4.far_ref, f32[16,8192]{1,0:T(8,128)S(1)} %copy-done), custom_call_target="tpu_custom_call" | custom-call | tf_op jit(solution)/shard_map/reach_4/pallas_call | solution.py:502
  46.9 0.7 %pair_enter.1 = (f32[16,4096]{1,0:T(8,128)S(1)}, f32[16,4096]{1,0:T(8,128)S(1)}) custom-call(s32[1]{0:T(128)} %bitcast.base_ref, s32[16]{0:T(128)S(1)} %copy-done.4, bf16[16,4096]{1,0:T(8,128)(2,1)S(1)} %reach_4.1.enter_ref, f32[16,4096]{1,0:T(8,128)S(1)} %get-tuple-element.14.own_ref, f32[16,4096]{1,0:T(8,128)S(1)} %collective-permute-done.1.got_ref, ...), custom_call_target="tpu_custom_call" | custom-call | tf_op jit(solution)/shard_map/pair_enter/pallas_call | solution.py:502
  47.6 2.2 %collective-permute-start.5 = (f32[16,4096]{1,0:T(8,128)S(1)}, f32[16,4096]{1,0:T(8,128)S(1)}, u32[]{:S(2)}, u32[]{:S(2)}) collective-permute-start(f32[16,4096]{1,0:T(8,128)S(1)} %get-tuple-element.21), channel_id=1, source_target_pairs={{0,1},{1,0},{2,3},{3,2},{4,5},{5,4},{6,7},{7,6},{8,9},{9,8},{10,11... | collective-permute-start | bytes 786440 | tf_op jit(solution)/shard_map/ppermute | solution.py:25
  49.8 1.2 %collective-permute-done.5.got_ref = f32[16,4096]{1,0:T(8,128)S(1)} collective-permute-done((f32[16,4096]{1,0:T(8,128)S(1)}, f32[16,4096]{1,0:T(8,128)S(1)}, u32[]{:S(2)}, u32[]{:S(2)}) %collective-permute-start.5) | collective-permute-done | bytes 262176 | tf_op jit(solution)/shard_map/ppermute | solution.py:25
  50.9 0.0 copy-done.2
  50.9 10.9 %far_part.1 = (bf16[128,8192]{1,0:T(8,128)(2,1)}, bf16[128,8192]{1,0:T(8,128)(2,1)}) custom-call(s32[1]{0:T(128)} %bitcast.base_ref, s32[16]{0:T(128)S(1)} %copy-done.4, f32[128,8192]{1,0:T(8,128)S(1)} %get-tuple-element.13.state_ref, f32[16,4096]{1,0:T(8,128)S(1)} %get-tuple-element.20.mine_ref, f32[16,4096]{1,0:T(8,128)S(1)} %collective-permute-done.5.got_ref, ...), custom_call_target="tpu_custom_call" | custom-call | flops 58982400 | bytes 18874368 | tf_op jit(solution)/shard_map/far_part/pallas_call | solution.py:546
Async XLA Ops:
  0.6 7.6 %copy-start = (f32[16,8192]{1,0:T(8,128)S(1)}, f32[16,8192]{1,0:T(8,128)}, u32[]{:S(2)}) copy-start(f32[16,8192]{1,0:T(8,128)} %rate_ref.13) | copy-start | bytes 1572868
  0.6 7.6 %copy-start.1 = (f32[3,3,8192]{2,1,0:T(4,128)S(1)}, f32[3,3,8192]{2,1,0:T(4,128)}, u32[]{:S(2)}) copy-start(f32[3,3,8192]{2,1,0:T(4,128)} %taps_ref.3) | copy-start | bytes 884740
  2.9 5.3 %collective-permute-start = (bf16[3,2,8192]{2,1,0:T(2,128)(2,1)S(1)}, bf16[3,2,8192]{2,1,0:T(2,128)(2,1)S(1)}, u32[]{:S(2)}, u32[]{:S(2)}) collective-permute-start(bf16[3,2,8192]{2,1,0:T(2,128)(2,1)S(1)} %pad_maximum_fusion), channel_id=1, source_target_pairs={{0,1},{1,2},{2,3},{3,4},{4,5},{5,6},{6,7},{7,8},{8,9},{9,10},{10,1... | collective-permute-start | bytes 294920 | tf_op jit(solution)/shard_map/ppermute | solution.py:21
  8.2 0.7 %copy-start.3 = (s32[16]{0:T(128)S(1)}, s32[16]{0:T(128)}, u32[]{:S(2)}) copy-start(s32[16]{0:T(128)} %len_ref.15) | copy-start | bytes 196
  21.8 2.5 %collective-permute-start.1 = (f32[16,4096]{1,0:T(8,128)S(1)}, f32[16,4096]{1,0:T(8,128)S(1)}, u32[]{:S(2)}, u32[]{:S(2)}) collective-permute-start(f32[16,4096]{1,0:T(8,128)S(1)} %get-tuple-element.15), channel_id=1, source_target_pairs={{0,1},{1,0},{2,3},{3,2},{4,5},{5,4},{6,7},{7,6},{8,9},{9,8},{10,11... | collective-permute-start | bytes 786440 | tf_op jit(solution)/shard_map/ppermute | solution.py:25
  25.0 14.0 %collective-permute-start.3 = (bf16[16,4096]{1,0:T(8,128)(2,1)S(1)}, bf16[16,4096]{1,0:T(8,128)(2,1)S(1)}, u32[]{:S(2)}, u32[]{:S(2)}) collective-permute-start(bf16[16,4096]{1,0:T(8,128)(2,1)S(1)} %pair_ends.1), channel_id=1, source_target_pairs={{0,4},{1,5},{2,6},{3,7},{4,8},{5,9},{6,10},{7,11},{8,12},{9,13},{1... | collective-permute-start | bytes 393224 | tf_op jit(solution)/shard_map/ppermute | solution.py:21
  28.1 10.9 %collective-permute-start.2 = (bf16[16,4096]{1,0:T(8,128)(2,1)S(1)}, bf16[16,4096]{1,0:T(8,128)(2,1)S(1)}, u32[]{:S(2)}, u32[]{:S(2)}) collective-permute-start(bf16[16,4096]{1,0:T(8,128)(2,1)S(1)} %pair_ends.1), channel_id=1, source_target_pairs={{0,2},{1,3},{2,4},{3,5},{4,6},{5,7},{6,8},{7,9},{8,10},{9,11},{10,... | collective-permute-start | bytes 393224 | tf_op jit(solution)/shard_map/ppermute | solution.py:21
  39.7 6.6 %copy-start.4 = (s32[16]{0:T(128)S(1)}, s32[16]{0:T(128)}, u32[]{:S(2)}) copy-start(s32[16]{0:T(128)} %len_ref.15) | copy-start | bytes 196
  39.7 6.6 %collective-permute-start.4 = (bf16[16,4096]{1,0:T(8,128)(2,1)S(1)}, bf16[16,4096]{1,0:T(8,128)(2,1)S(1)}, u32[]{:S(2)}, u32[]{:S(2)}) collective-permute-start(bf16[16,4096]{1,0:T(8,128)(2,1)S(1)} %reach_2.1.near_ref), channel_id=1, source_target_pairs={{0,4},{1,5},{2,6},{3,7},{4,8},{5,9},{6,10},{7,11},{8,12},{9,13},{1... | collective-permute-start | bytes 393224 | tf_op jit(solution)/shard_map/ppermute | solution.py:21
  45.2 5.7 %copy-start.2 = (f32[8192]{0:T(1024)S(1)}, f32[8192]{0:T(1024)}, u32[]{:S(2)}) copy-start(f32[8192]{0:T(1024)} %param.17) | copy-start | bytes 98308
  47.6 3.3 %collective-permute-start.5 = (f32[16,4096]{1,0:T(8,128)S(1)}, f32[16,4096]{1,0:T(8,128)S(1)}, u32[]{:S(2)}, u32[]{:S(2)}) collective-permute-start(f32[16,4096]{1,0:T(8,128)S(1)} %get-tuple-element.21), channel_id=1, source_target_pairs={{0,1},{1,0},{2,3},{3,2},{4,5},{5,4},{6,7},{7,6},{8,9},{9,8},{10,11... | collective-permute-start | bytes 786440 | tf_op jit(solution)/shard_map/ppermute | solution.py:25

commit v7 on v6

--- a/solution.py
+++ b/solution.py
@@ -11,6 +11,7 @@
 SUBS = 8
 LANES = 128
 MIB = 1024 * 1024
+A_TILES, N_TILES, Q_TILES, F_TILES = 4, 2, 8, 4
 f32 = jnp.float32
 bf16 = jnp.bfloat16
 
@@ -202,6 +203,19 @@
             copy.wait()
 
     each_chunk(chans, chunk, before, group, lambda c: None, most)
+
+
+def tail_kernel(query_ref, key_ref, value_ref, tail_ref, bufs, sems):
+    rows, count = query_ref.shape[0], bufs.shape[1]
+    copies = [
+        pltpu.make_async_copy(ref.at[pl.ds(rows - count, count)], bufs.at[i], sems.at[i])
+        for i, ref in enumerate((query_ref, key_ref, value_ref))
+    ]
+    for copy in copies:
+        copy.start()
+    for i, copy in enumerate(copies):
+        copy.wait()
+        tail_ref[i] = bufs[i].astype(f32)[count - 2 :].astype(bf16)
 
 
 def keep_masks(base_ref, len_ref, masks, span):
@@ -295,20 +309,22 @@
     end_ref[...] = (late + (jnp.exp(-float(rows) * rate) * through) * early).astype(bf16)
 
 
-def reach_kernel(base_ref, len_ref, near_ref, far_ref, rate_ref, enter_ref, *, rows, reach):
+def reached(base_ref, len_ref, near_ref, far_ref, rate_ref, rows, reach):
     parity, rate = pair_rates(base_ref, rate_ref, rows, near_ref.shape)
     span = 2 * rows * reach
     through = unbroken(len_ref, base_ref[0] - parity * rows - span, span)
-    enter_ref[...] = (
-        near_ref[...].astype(f32) + (jnp.exp(-float(span) * rate) * through) * far_ref[...].astype(f32)
-    ).astype(enter_ref.dtype)
-
-
-def enter_kernel(base_ref, len_ref, enter_ref, own_ref, got_ref, rate_ref, mine_ref, give_ref, *, rows):
+    return near_ref[...].astype(f32) + (jnp.exp(-float(span) * rate) * through) * far_ref[...].astype(f32)
+
+
+def reach_kernel(base_ref, len_ref, near_ref, far_ref, rate_ref, enter_ref, *, rows, reach):
+    enter_ref[...] = reached(base_ref, len_ref, near_ref, far_ref, rate_ref, rows, reach).astype(bf16)
+
+
+def enter_kernel(base_ref, len_ref, near_ref, far_ref, own_ref, got_ref, rate_ref, mine_ref, give_ref, *, rows, reach):
+    first = reached(base_ref, len_ref, near_ref, far_ref, rate_ref, rows, reach)
     parity, rate = pair_rates(base_ref, rate_ref, rows, own_ref.shape)
     early, _ = early_late(parity, own_ref[...], got_ref[...])
     through = unbroken(len_ref, base_ref[0] - parity * rows, rows)
-    first = enter_ref[...].astype(f32)
     second = early + (jnp.exp(-float(rows) * rate) * through) * first
     give, mine = early_late(parity, second, first)
     mine_ref[...] = mine
@@ -417,8 +433,6 @@
     pieces = chans // chunk
     ctx_index = lax.axis_index("ctx")
     base = (ctx_index * tok_rows).astype(jnp.int32).reshape(1)
-    tails = jnp.stack([query_in[tok_rows - 2 :], key_in[tok_rows - 2 :], value_in[tok_rows - 2 :]])
-    rim_rows = from_behind(tails, "ctx", 1)
     weight = residues * jnp.sqrt(-jnp.expm1(-2.0 * decay_rate))
 
     smem = pl.BlockSpec(memory_space=pltpu.SMEM)
@@ -429,6 +443,8 @@
     wide_rows = SUBS * (span + 1)
     params = pltpu.CompilerParams(vmem_limit_bytes=16 * MIB)
 
+    lengths = pltpu.with_memory_space_constraint(doc_lengths, pltpu.HBM)
+
     def near_by(x):
         return pltpu.with_memory_space_constraint(x, pltpu.VMEM)
 
@@ -441,9 +457,19 @@
     def cost(per_tile, moved):
         return pl.CostEstimate(flops=per_tile * (chans // LANES) * SUBS * LANES, bytes_accessed=moved, transcendentals=0)
 
+    tails = pl.pallas_call(
+        tail_kernel,
+        in_specs=[hbm, hbm, hbm],
+        out_specs=vmem,
+        out_shape=pltpu.VMEM((3, 2, chans), bf16),
+        scratch_shapes=[pltpu.VMEM((3, 16, chans), bf16), pltpu.SemaphoreType.DMA((3,))],
+        compiler_params=params,
+        name="tails",
+    )(far_off(query_in), far_off(key_in), far_off(value_in))
+    rim_rows = from_behind(tails, "ctx", 1)
     rates, weights, taps, rims = near_by(decay_rate), near_by(weight), near_by(short_taps), near_by(rim_rows)
     gates, states, own, give = pl.pallas_call(
-        functools.partial(state_kernel, span=span, modes=modes, most=2, chunk=chunk),
+        functools.partial(state_kernel, span=span, modes=modes, most=A_TILES, chunk=chunk),
         in_specs=[smem, smem, hbm, hbm, vmem, vmem, vmem, vmem],
         out_specs=[vmem, vmem, vmem, vmem],
         out_shape=[
@@ -457,19 +483,19 @@
             pltpu.VMEM((tok_rows, chans), bf16),
             copies(2),
             pltpu.VMEM((4, span) + tile_shape, f32),
-            pltpu.VMEM((2, wide_rows, LANES), f32),
-            pltpu.VMEM((2, wide_rows, LANES), f32),
-            pltpu.VMEM((2, 5, modes, LANES), f32),
-            pltpu.VMEM((2, modes, LANES), f32),
-            pltpu.VMEM((2, span) + tile_shape, f32),
+            pltpu.VMEM((A_TILES, wide_rows, LANES), f32),
+            pltpu.VMEM((A_TILES, wide_rows, LANES), f32),
+            pltpu.VMEM((A_TILES, 5, modes, LANES), f32),
+            pltpu.VMEM((A_TILES, modes, LANES), f32),
+            pltpu.VMEM((A_TILES, span) + tile_shape, f32),
         ],
         compiler_params=params,
         cost_estimate=cost(1000, 12 * tok_rows * chans),
         name="block_states",
-    )(base, doc_lengths, far_off(key_in), far_off(value_in), rims, taps, rates, weights)
+    )(base, lengths, far_off(key_in), far_off(value_in), rims, taps, rates, weights)
 
     near = pl.pallas_call(
-        functools.partial(near_kernel, span=span, modes=modes, most=4),
+        functools.partial(near_kernel, span=span, modes=modes, most=N_TILES),
         in_specs=[smem, smem, vmem, vmem, vmem],
         out_specs=vmem,
         out_shape=pltpu.VMEM((tok_rows, chans), f32),
@@ -477,10 +503,10 @@
         compiler_params=params,
         cost_estimate=cost(600, 7 * tok_rows * chans),
         name="near_part",
-    )(base, doc_lengths, near_by(gates), rates, weights)
+    )(base, lengths, near_by(gates), rates, weights)
 
     q_short = pl.pallas_call(
-        functools.partial(query_kernel, span=span, most=4, chunk=chunk),
+        functools.partial(query_kernel, span=span, most=Q_TILES, chunk=chunk),
         in_specs=[smem, smem, hbm, vmem, vmem],
         out_specs=vmem,
         out_shape=pltpu.VMEM((tok_rows, chans), f32),
@@ -488,12 +514,12 @@
             pltpu.VMEM((tok_rows, chans), bf16),
             pltpu.SemaphoreType.DMA((pieces,)),
             pltpu.VMEM((2, span) + tile_shape, f32),
-            pltpu.VMEM((4, wide_rows, LANES), f32),
+            pltpu.VMEM((Q_TILES, wide_rows, LANES), f32),
         ],
         compiler_params=params,
         cost_estimate=cost(200, 6 * tok_rows * chans),
         name="query_part",
-    )(base, doc_lengths, far_off(query_in), rims, taps)
+    )(base, lengths, far_off(query_in), rims, taps)
 
     got = swap(give, "ctx")
 
@@ -506,21 +532,24 @@
             out_shape=out_shape,
             compiler_params=params,
             name=name,
-        )(base, doc_lengths, *[near_by(x) for x in operands], rates)
+        )(base, lengths, *[near_by(x) for x in operands], rates)
 
     sent = pltpu.VMEM(half.shape, bf16)
     ends = pair_call(pair_kernel, [own, got], [sent], "pair_ends")[0]
     one_on, two_on = from_behind(ends, "ctx", 2), from_behind(ends, "ctx", 4)
     one_on, two_on, near = lax.optimization_barrier((one_on, two_on, near))
-    enter = pair_call(reach_kernel, [one_on, two_on], [sent], "reach_2", reach=1)[0]
-    reach = 2
-    while reach < blocks // 8:
-        on = from_behind(enter, "ctx", 2 * reach)
-        on, q_short = lax.optimization_barrier((on, q_short))
+    enter, on, reach = one_on, two_on, 1
+    while 2 * reach < blocks // 8:
         enter = pair_call(reach_kernel, [enter, on], [sent], "reach_%d" % (2 * reach), reach=reach)[0]
         reach *= 2
+        on = from_behind(enter, "ctx", 2 * reach)
+    on, q_short = lax.optimization_barrier((on, q_short))
     mine, give_back = pair_call(
-        enter_kernel, [enter, own, got], [pltpu.VMEM(half.shape, f32), pltpu.VMEM(half.shape, f32)], "pair_enter"
+        enter_kernel,
+        [enter, on, own, got],
+        [pltpu.VMEM(half.shape, f32), pltpu.VMEM(half.shape, f32)],
+        "pair_enter",
+        reach=reach,
     )
     got_back = swap(give_back, "ctx")
 
@@ -532,8 +561,8 @@
         pltpu.VMEM((tok_rows, chans), bf16),
         copies(3),
         pltpu.VMEM((2, span) + tile_shape, f32),
-        pltpu.VMEM((2, wide_rows, LANES), f32),
-        pltpu.VMEM((2, 3, modes, LANES), f32),
+        pltpu.VMEM((F_TILES, wide_rows, LANES), f32),
+        pltpu.VMEM((F_TILES, 3, modes, LANES), f32),
         pltpu.VMEM((tok_rows, LANES), f32),
     ]
     if alone:
@@ -545,7 +574,7 @@
         out_shape += [jax.ShapeDtypeStruct((tok_rows, chans), f32), jax.ShapeDtypeStruct((tok_rows, LANES), f32)]
     outs = pl.pallas_call(
         functools.partial(
-            final_kernel, span=span, modes=modes, channels=chans if alone else 0, most=2, chunk=chunk
+            final_kernel, span=span, modes=modes, channels=chans if alone else 0, most=F_TILES, chunk=chunk
         ),
         in_specs=[smem, smem, vmem, vmem, vmem, vmem, vmem, hbm, vmem, vmem, vmem],
         out_specs=out_specs,
@@ -555,7 +584,7 @@
         cost_estimate=cost(900, 18 * tok_rows * chans),
         name="far_part",
     )(
-        base, doc_lengths, near_by(states), near_by(mine), near_by(got_back), near_by(near), near_by(q_short), far_off(residual),
+        base, lengths, near_by(states), near_by(mine), near_by(got_back), near_by(near), near_by(q_short), far_off(residual),
         rates, weights, norm_gain.reshape(1, chans),
     )
     if alone:

time: 62.1 us -> 60.6 us (0.976)
  local copies, waits for them, and re-layouts: 2.74 us -> 0.02 us
  other arithmetic: 1.68 us -> 0.32 us
  Pallas kernels: 35.6 us -> 36.9 us
  waiting for transfers between devices: 3.48 us -> 4.64 us
    another operation x2 -> x0, local copies, waits for them, and re-layouts: 2.06 us -> none  [shards(): jnp.stack([query_in[tok_rows - 2:], key_in[tok_rows - 2:], value_in[tok_r...]
    pallas_call x1 -> x2, Pallas kernels: 3.27 us -> 4.57 us  [the longest x1 3.31 us: shards(): pl.pallas_call(functools.partial(query_kernel, span=span, most=Q_TILES, c...]
    mul x1, other arithmetic: 1.52 us -> 0.32 us  [shards(): weight = residues * jnp.sqrt(-jnp.expm1(-2.0 * decay_rate))]
    ppermute x4, waiting for transfers between devices: 1.16 us -> 2.31 us  [from_behind(): return lax.ppermute(shard, axis, pairs)]
    unnamed x10 -> x8, local copies, waits for them, and re-layouts: 0.68 us -> 0.02 us
    pallas_call x4 -> x3, Pallas kernels: 2.59 us -> 2.38 us  [pair_call(): pl.pallas_call(functools.partial(kernel, rows=tok_rows, **static), in_spe...]
  transfers between devices with their start and end apart: 6 -> 6, of which waited for: 4 -> 4; matrix products, arithmetic and copies ran while one was open for 2% -> 1% of each run, Pallas kernels for 15% -> 15%
where the time goes in v7:
time: 60.6 us; the launch traced here: 60.2 us
  Pallas kernels  36.9 us (61%)
  starting transfers between devices  17.5 us (29%)
  waiting for transfers between devices  4.64 us (8%)
  between operations  0.78 us (1%)
    ppermute x4, starting transfers between devices, from_behind(): return lax.ppermute(shard, axis, pairs)  14 us
    pallas_call x1, Pallas kernels, shards(): pl.pallas_call(functools.partial(state_kernel, span=span, modes=modes, mo...  13.3 us
    pallas_call x1, Pallas kernels, shards(): pl.pallas_call(functools.partial(final_kernel, span=span, modes=modes, ch...  10.8 us
    pallas_call x1, Pallas kernels, shards(): pl.pallas_call(functools.partial(near_kernel, span=span, modes=modes, mos...  5.9 us
    ppermute x2, starting transfers between devices, swap(): lax.ppermute(shard, axis, [(i, i ^ 1) for i in range(lax.axis_size(axis))])  3.53 us
    pallas_call x1, Pallas kernels, shards(): pl.pallas_call(functools.partial(query_kernel, span=span, most=Q_TILES, c...  3.31 us
    pallas_call x3, Pallas kernels, pair_call(): pl.pallas_call(functools.partial(kernel, rows=tok_rows, **static), in_spe...  2.38 us
    ppermute x2, waiting for transfers between devices, swap(): lax.ppermute(shard, axis, [(i, i ^ 1) for i in range(lax.axis_size(axis))])  2.32 us
  transfers between devices with their start and end apart: 6, of which 4 were waited for; matrix products, arithmetic and copies ran while one was open for 1% of the time, Pallas kernels for 15%

profile of v7, /device:TPU:11, one launch (start us, length us, event | category | flops | bytes accessed | tf_op | source)
XLA Modules:
  0.0 60.2 jit_solution(1799748795478344103)
XLA Ops:
  0.6 0.0 copy-start
  0.6 0.0 copy-start.3
  0.7 0.0 copy-start.1
  0.7 1.3 %tails.1 = bf16[3,2,8192]{2,1,0:T(2,128)(2,1)S(1)} custom-call(bf16[128,8192]{1,0:T(8,128)(2,1)} %query_ref.3, bf16[128,8192]{1,0:T(8,128)(2,1)} %key_ref.3, bf16[128,8192]{1,0:T(8,128)(2,1)} %value_ref.3), custom_call_target="tpu_custom_call" | custom-call | tf_op jit(solution)/shard_map/tails/pallas_call | solution.py:460
  1.9 3.7 %collective-permute-start = (bf16[3,2,8192]{2,1,0:T(2,128)(2,1)S(1)}, bf16[3,2,8192]{2,1,0:T(2,128)(2,1)S(1)}, u32[]{:S(2)}, u32[]{:S(2)}) collective-permute-start(bf16[3,2,8192]{2,1,0:T(2,128)(2,1)S(1)} %tails.1), channel_id=1, source_target_pairs={{0,1},{1,2},{2,3},{3,4},{4,5},{5,6},{6,7},{7,8},{8,9},{9,10},{10,1... | collective-permute-start | bytes 294920 | tf_op jit(solution)/shard_map/ppermute | solution.py:22
  5.6 0.0 copy-done
  5.6 0.0 copy-done.3
  5.6 0.3 sqrt_multiply_fusion.weight_ref
  6.0 1.3 %collective-permute-done.rim_ref = bf16[3,2,8192]{2,1,0:T(2,128)(2,1)S(1)} collective-permute-done((bf16[3,2,8192]{2,1,0:T(2,128)(2,1)S(1)}, bf16[3,2,8192]{2,1,0:T(2,128)(2,1)S(1)}, u32[]{:S(2)}, u32[]{:S(2)}) %collective-permute-start) | collective-permute-done | bytes 98336 | tf_op jit(solution)/shard_map/ppermute | solution.py:22
  7.2 0.0 copy-done.1
  7.2 13.3 %block_states.1 = (bf16[128,8192]{1,0:T(8,128)(2,1)S(1)}, f32[128,8192]{1,0:T(8,128)S(1)}, f32[16,4096]{1,0:T(8,128)S(1)}, f32[16,4096]{1,0:T(8,128)S(1)}) custom-call(s32[1]{0:T(128)} %bitcast.base_ref, s32[16]{0:T(128)} %len_ref.13, bf16[128,8192]{1,0:T(8,128)(2,1)} %key_ref.3, bf16[128,8192]{1,0:T(8,128)(2,1)} %value_ref.3, ...), custom_call_target="tpu_custom_call" | custom-call | flops 65536000 | bytes 12582912 | tf_op jit(solution)/shard_map/block_states/pallas_call | solution.py:471
  20.6 1.4 %collective-permute-start.1 = (f32[16,4096]{1,0:T(8,128)S(1)}, f32[16,4096]{1,0:T(8,128)S(1)}, u32[]{:S(2)}, u32[]{:S(2)}) collective-permute-start(f32[16,4096]{1,0:T(8,128)S(1)} %get-tuple-element.15), channel_id=1, source_target_pairs={{0,1},{1,0},{2,3},{3,2},{4,5},{5,4},{6,7},{7,6},{8,9},{9,8},{10,11... | collective-permute-start | bytes 786440 | tf_op jit(solution)/shard_map/ppermute | solution.py:26
  21.9 1.2 %collective-permute-done.1.got_ref = f32[16,4096]{1,0:T(8,128)S(1)} collective-permute-done((f32[16,4096]{1,0:T(8,128)S(1)}, f32[16,4096]{1,0:T(8,128)S(1)}, u32[]{:S(2)}, u32[]{:S(2)}) %collective-permute-start.1) | collective-permute-done | bytes 262176 | tf_op jit(solution)/shard_map/ppermute | solution.py:26
  23.1 0.8 %pair_ends.1 = bf16[16,4096]{1,0:T(8,128)(2,1)S(1)} custom-call(s32[1]{0:T(128)} %bitcast.base_ref, s32[16]{0:T(128)} %len_ref.13, f32[16,4096]{1,0:T(8,128)S(1)} %get-tuple-element.14.own_ref, f32[16,4096]{1,0:T(8,128)S(1)} %collective-permute-done.1.got_ref, f32[16,8192]{1,0:T(8,128)S(1)} %copy-done), custom_call_target="tpu_custom_call" | custom-call | tf_op jit(solution)/shard_map/pair_ends/pallas_call | solution.py:528
  23.9 3.1 %collective-permute-start.3 = (bf16[16,4096]{1,0:T(8,128)(2,1)S(1)}, bf16[16,4096]{1,0:T(8,128)(2,1)S(1)}, u32[]{:S(2)}, u32[]{:S(2)}) collective-permute-start(bf16[16,4096]{1,0:T(8,128)(2,1)S(1)} %pair_ends.1), channel_id=1, source_target_pairs={{0,4},{1,5},{2,6},{3,7},{4,8},{5,9},{6,10},{7,11},{8,12},{9,13},{1... | collective-permute-start | bytes 393224 | tf_op jit(solution)/shard_map/ppermute | solution.py:22
  27.0 4.9 %collective-permute-start.2 = (bf16[16,4096]{1,0:T(8,128)(2,1)S(1)}, bf16[16,4096]{1,0:T(8,128)(2,1)S(1)}, u32[]{:S(2)}, u32[]{:S(2)}) collective-permute-start(bf16[16,4096]{1,0:T(8,128)(2,1)S(1)} %pair_ends.1), channel_id=1, source_target_pairs={{0,2},{1,3},{2,4},{3,5},{4,6},{5,7},{6,8},{7,9},{8,10},{9,11},{10,... | collective-permute-start | bytes 393224 | tf_op jit(solution)/shard_map/ppermute | solution.py:22
  31.9 5.9 %near_part.1.near_ref = f32[128,8192]{1,0:T(8,128)S(1)} custom-call(s32[1]{0:T(128)} %bitcast.base_ref, s32[16]{0:T(128)} %len_ref.13, bf16[128,8192]{1,0:T(8,128)(2,1)S(1)} %get-tuple-element.16.gate_ref, f32[16,8192]{1,0:T(8,128)S(1)} %copy-done, f32[16,8192]{1,0:T(8,128)S(1)} %sqrt_multiply_fusion.weight_ref), custom_call_target="tpu_custom_call" | custom-call | flops 39321600 | bytes 7340032 | tf_op jit(solution)/shard_map/near_part/pallas_call | solution.py:497
  37.9 0.0 collective-permute-done.3.far_ref
  37.9 0.0 collective-permute-done.2.near_ref
  37.9 0.8 %reach_2.1.near_ref = bf16[16,4096]{1,0:T(8,128)(2,1)S(1)} custom-call(s32[1]{0:T(128)} %bitcast.base_ref, s32[16]{0:T(128)} %len_ref.13, bf16[16,4096]{1,0:T(8,128)(2,1)S(1)} %collective-permute-done.2.near_ref, bf16[16,4096]{1,0:T(8,128)(2,1)S(1)} %collective-permute-done.3.far_ref, f32[16,8192]{1,0:T(8,128)S(1)} %copy-done), custom_call_target="tpu_custom_call" | custom-call | tf_op jit(solution)/shard_map/reach_2/pallas_call | solution.py:528
  38.6 0.0 copy-start.2
  38.6 2.2 %collective-permute-start.4 = (bf16[16,4096]{1,0:T(8,128)(2,1)S(1)}, bf16[16,4096]{1,0:T(8,128)(2,1)S(1)}, u32[]{:S(2)}, u32[]{:S(2)}) collective-permute-start(bf16[16,4096]{1,0:T(8,128)(2,1)S(1)} %reach_2.1.near_ref), channel_id=1, source_target_pairs={{0,4},{1,5},{2,6},{3,7},{4,8},{5,9},{6,10},{7,11},{8,12},{9,13},{1... | collective-permute-start | bytes 393224 | tf_op jit(solution)/shard_map/ppermute | solution.py:22
  40.9 3.3 %query_part.1.short_ref = f32[128,8192]{1,0:T(8,128)S(1)} custom-call(s32[1]{0:T(128)} %bitcast.base_ref, s32[16]{0:T(128)} %len_ref.13, bf16[128,8192]{1,0:T(8,128)(2,1)} %query_ref.3, bf16[3,2,8192]{2,1,0:T(2,128)(2,1)S(1)} %collective-permute-done.rim_ref, f32[3,3,8192]{2,1,0:T(4,128)S(1)} %copy-done.1), custom_call_target="tpu_custom_call" | custom-call | flops 13107200 | bytes 6291456 | tf_op jit(solution)/shard_map/query_part/pallas_call | solution.py:508
  44.2 1.0 %collective-permute-done.4.far_ref = bf16[16,4096]{1,0:T(8,128)(2,1)S(1)} collective-permute-done((bf16[16,4096]{1,0:T(8,128)(2,1)S(1)}, bf16[16,4096]{1,0:T(8,128)(2,1)S(1)}, u32[]{:S(2)}, u32[]{:S(2)}) %collective-permute-start.4) | collective-permute-done | bytes 131104 | tf_op jit(solution)/shard_map/ppermute | solution.py:22
  45.3 0.9 %pair_enter.1 = (f32[16,4096]{1,0:T(8,128)S(1)}, f32[16,4096]{1,0:T(8,128)S(1)}) custom-call(s32[1]{0:T(128)} %bitcast.base_ref, s32[16]{0:T(128)} %len_ref.13, bf16[16,4096]{1,0:T(8,128)(2,1)S(1)} %reach_2.1.near_ref, bf16[16,4096]{1,0:T(8,128)(2,1)S(1)} %collective-permute-done.4.far_ref, f32[16,4096]{1,0:T(8,128)S(1)} %get-tuple-element.14.own_ref, ...), custom_call_target="tpu_custom_call" | custom-call | tf_op jit(solution)/shard_map/pair_enter/pallas_call | solution.py:528
  46.1 2.2 %collective-permute-start.5 = (f32[16,4096]{1,0:T(8,128)S(1)}, f32[16,4096]{1,0:T(8,128)S(1)}, u32[]{:S(2)}, u32[]{:S(2)}) collective-permute-start(f32[16,4096]{1,0:T(8,128)S(1)} %get-tuple-element.21), channel_id=1, source_target_pairs={{0,1},{1,0},{2,3},{3,2},{4,5},{5,4},{6,7},{7,6},{8,9},{9,8},{10,11... | collective-permute-start | bytes 786440 | tf_op jit(solution)/shard_map/ppermute | solution.py:26
  48.3 1.2 %collective-permute-done.5.got_ref = f32[16,4096]{1,0:T(8,128)S(1)} collective-permute-done((f32[16,4096]{1,0:T(8,128)S(1)}, f32[16,4096]{1,0:T(8,128)S(1)}, u32[]{:S(2)}, u32[]{:S(2)}) %collective-permute-start.5) | collective-permute-done | bytes 262176 | tf_op jit(solution)/shard_map/ppermute | solution.py:26
  49.4 0.0 copy-done.2
  49.4 10.8 %far_part.1 = (bf16[128,8192]{1,0:T(8,128)(2,1)}, bf16[128,8192]{1,0:T(8,128)(2,1)}) custom-call(s32[1]{0:T(128)} %bitcast.base_ref, s32[16]{0:T(128)} %len_ref.13, f32[128,8192]{1,0:T(8,128)S(1)} %get-tuple-element.13.state_ref, f32[16,4096]{1,0:T(8,128)S(1)} %get-tuple-element.20.mine_ref, f32[16,4096]{1,0:T(8,128)S(1)} %collective-permute-done.5.got_ref, ...), custom_call_target="tpu_custom_call" | custom-call | flops 58982400 | bytes 18874368 | tf_op jit(solution)/shard_map/far_part/pallas_call | solution.py:575
Async XLA Ops:
  0.6 5.0 %copy-start = (f32[16,8192]{1,0:T(8,128)S(1)}, f32[16,8192]{1,0:T(8,128)}, u32[]{:S(2)}) copy-start(f32[16,8192]{1,0:T(8,128)} %rate_ref.11) | copy-start | bytes 1572868
  0.6 5.0 %copy-start.3 = (f32[16,8192]{1,0:T(8,128)S(1)}, f32[16,8192]{1,0:T(8,128)}, u32[]{:S(2)}) copy-start(f32[16,8192]{1,0:T(8,128)} %param.14) | copy-start | bytes 1572868
  0.7 6.6 %copy-start.1 = (f32[3,3,8192]{2,1,0:T(4,128)S(1)}, f32[3,3,8192]{2,1,0:T(4,128)}, u32[]{:S(2)}) copy-start(f32[3,3,8192]{2,1,0:T(4,128)} %taps_ref.3) | copy-start | bytes 884740
  1.9 5.3 %collective-permute-start = (bf16[3,2,8192]{2,1,0:T(2,128)(2,1)S(1)}, bf16[3,2,8192]{2,1,0:T(2,128)(2,1)S(1)}, u32[]{:S(2)}, u32[]{:S(2)}) collective-permute-start(bf16[3,2,8192]{2,1,0:T(2,128)(2,1)S(1)} %tails.1), channel_id=1, source_target_pairs={{0,1},{1,2},{2,3},{3,4},{4,5},{5,6},{6,7},{7,8},{8,9},{9,10},{10,1... | collective-permute-start | bytes 294920 | tf_op jit(solution)/shard_map/ppermute | solution.py:22
  20.6 2.5 %collective-permute-start.1 = (f32[16,4096]{1,0:T(8,128)S(1)}, f32[16,4096]{1,0:T(8,128)S(1)}, u32[]{:S(2)}, u32[]{:S(2)}) collective-permute-start(f32[16,4096]{1,0:T(8,128)S(1)} %get-tuple-element.15), channel_id=1, source_target_pairs={{0,1},{1,0},{2,3},{3,2},{4,5},{5,4},{6,7},{7,6},{8,9},{9,8},{10,11... | collective-permute-start | bytes 786440 | tf_op jit(solution)/shard_map/ppermute | solution.py:26
  23.9 14.0 %collective-permute-start.3 = (bf16[16,4096]{1,0:T(8,128)(2,1)S(1)}, bf16[16,4096]{1,0:T(8,128)(2,1)S(1)}, u32[]{:S(2)}, u32[]{:S(2)}) collective-permute-start(bf16[16,4096]{1,0:T(8,128)(2,1)S(1)} %pair_ends.1), channel_id=1, source_target_pairs={{0,4},{1,5},{2,6},{3,7},{4,8},{5,9},{6,10},{7,11},{8,12},{9,13},{1... | collective-permute-start | bytes 393224 | tf_op jit(solution)/shard_map/ppermute | solution.py:22
  27.0 10.8 %collective-permute-start.2 = (bf16[16,4096]{1,0:T(8,128)(2,1)S(1)}, bf16[16,4096]{1,0:T(8,128)(2,1)S(1)}, u32[]{:S(2)}, u32[]{:S(2)}) collective-permute-start(bf16[16,4096]{1,0:T(8,128)(2,1)S(1)} %pair_ends.1), channel_id=1, source_target_pairs={{0,2},{1,3},{2,4},{3,5},{4,6},{5,7},{6,8},{7,9},{8,10},{9,11},{10,... | collective-permute-start | bytes 393224 | tf_op jit(solution)/shard_map/ppermute | solution.py:22
  38.6 10.8 %copy-start.2 = (f32[8192]{0:T(1024)S(1)}, f32[8192]{0:T(1024)}, u32[]{:S(2)}) copy-start(f32[8192]{0:T(1024)} %param.17) | copy-start | bytes 98308
  38.6 6.6 %collective-permute-start.4 = (bf16[16,4096]{1,0:T(8,128)(2,1)S(1)}, bf16[16,4096]{1,0:T(8,128)(2,1)S(1)}, u32[]{:S(2)}, u32[]{:S(2)}) collective-permute-start(bf16[16,4096]{1,0:T(8,128)(2,1)S(1)} %reach_2.1.near_ref), channel_id=1, source_target_pairs={{0,4},{1,5},{2,6},{3,7},{4,8},{5,9},{6,10},{7,11},{8,12},{9,13},{1... | collective-permute-start | bytes 393224 | tf_op jit(solution)/shard_map/ppermute | solution.py:22
  46.1 3.3 %collective-permute-start.5 = (f32[16,4096]{1,0:T(8,128)S(1)}, f32[16,4096]{1,0:T(8,128)S(1)}, u32[]{:S(2)}, u32[]{:S(2)}) collective-permute-start(f32[16,4096]{1,0:T(8,128)S(1)} %get-tuple-element.21), channel_id=1, source_target_pairs={{0,1},{1,0},{2,3},{3,2},{4,5},{5,4},{6,7},{7,6},{8,9},{9,8},{10,11... | collective-permute-start | bytes 786440 | tf_op jit(solution)/shard_map/ppermute | solution.py:26

commit v8 on v7

--- a/solution.py
+++ b/solution.py
@@ -11,7 +11,8 @@
 SUBS = 8
 LANES = 128
 MIB = 1024 * 1024
-A_TILES, N_TILES, Q_TILES, F_TILES = 4, 2, 8, 4
+A_TILES, N_TILES, Q_TILES, F_TILES = 2, 2, 4, 4
+NEAR_PARTS = 4
 f32 = jnp.float32
 bf16 = jnp.bfloat16
 
@@ -82,21 +83,21 @@
     return jnp.broadcast_to(ref[pl.ds(index, 1), :], (SUBS, LANES))
 
 
-def spread(x, wide, span):
+def spread(x, wide, span, pad=1):
     x = x.astype(f32)
     for b in range(SUBS):
-        wide[pl.ds(b * (span + 1), span), :] = x[b * span : (b + 1) * span]
-
-
-def steps_of(wide, span):
-    return [wide[pl.ds(j, SUBS, stride=span + 1), :] for j in range(span)]
+        wide[pl.ds(b * (span + pad), span), :] = x[b * span : (b + 1) * span]
+
+
+def steps_of(wide, span, pad=1):
+    return [wide[pl.ds(j, SUBS, stride=span + pad), :] for j in range(span)]
 
 
 def short_conv(steps, rim, taps, keep_one, keep_two):
     top = lax.broadcasted_iota(jnp.int32, (SUBS, LANES), 0) == 0
-    rim = rim.astype(f32)
-    behind_one = jnp.where(top, jnp.broadcast_to(rim[1:2], (SUBS, LANES)), pltpu.roll(steps[-1], 1, 0))
-    behind_two = jnp.where(top, jnp.broadcast_to(rim[0:1], (SUBS, LANES)), pltpu.roll(steps[-2], 1, 0))
+    ahead = [0.0, 0.0] if rim is None else [jnp.broadcast_to(rim[m : m + 1].astype(f32), (SUBS, LANES)) for m in range(2)]
+    behind_one = jnp.where(top, ahead[1], pltpu.roll(steps[-1], 1, 0))
+    behind_two = jnp.where(top, ahead[0], pltpu.roll(steps[-2], 1, 0))
     padded = [behind_two, behind_one] + steps
     taps = [jnp.broadcast_to(taps[m : m + 1], (SUBS, LANES)) for m in range(3)]
     return [
@@ -225,7 +226,8 @@
         masks[1, j] = flag(starts[j] < rows + (j - 1))
 
 
-def near_kernel(base_ref, len_ref, gate_ref, rate_ref, weight_ref, near_ref, masks, *, span, modes, most):
+def near_kernel(base_ref, len_ref, gate_ref, rate_ref, weight_ref, *refs, span, modes, most, first, count):
+    near_ref, masks = refs[-2:]
     keep_masks(base_ref, len_ref, masks, span)
 
     def group(lanes):
@@ -256,10 +258,10 @@
                     total = total + parts[lag] * live[j - lag]
                 near_ref[pl.ds(j * SUBS, SUBS), cols_of(lane)] = total
 
-    each_group(gate_ref.shape[1] // LANES, most, group)
-
-
-def query_kernel(base_ref, len_ref, query_ref, rim_ref, taps_ref, short_ref, query_buf, sems, masks, wide_q, *, span, most, chunk):
+    each_group(count // LANES, most, lambda lanes: group([pl.multiple_of(first + lane, LANES) for lane in lanes]))
+
+
+def query_kernel(base_ref, len_ref, query_ref, taps_ref, short_ref, query_buf, sems, masks, wide_q, *, span, most, chunk):
     chans = query_buf.shape[1]
 
     def fetch(c):
@@ -271,12 +273,12 @@
 
     def group(lanes):
         for slot, lane in enumerate(lanes):
-            spread(query_buf[:, cols_of(lane)], wide_q.at[slot], span)
+            spread(query_buf[:, cols_of(lane)], wide_q.at[slot], span, 0)
         for slot, lane in enumerate(lanes):
             cols = cols_of(lane)
             keep_one = [masks[0, j] for j in range(span)]
             keep_two = [masks[1, j] for j in range(span)]
-            q_short = short_conv(steps_of(wide_q.at[slot], span), rim_ref[0, :, cols], taps_ref[0, :, cols], keep_one, keep_two)
+            q_short = short_conv(steps_of(wide_q.at[slot], span, 0), None, taps_ref[0, :, cols], keep_one, keep_two)
             for j in range(span):
                 short_ref[pl.ds(j * SUBS, SUBS), cols] = q_short[j]
 
@@ -332,7 +334,7 @@
 
 
 def final_kernel(
-    base_ref, len_ref, state_ref, mine_ref, got_ref, near_ref, short_ref, resid_in, rate_ref, weight_ref, gain_ref,
+    base_ref, len_ref, state_ref, mine_ref, got_ref, near_ref, short_ref, resid_in, rim_ref, taps_ref, rate_ref, weight_ref, gain_ref,
     *refs,
     span, modes, channels, most, chunk,
 ):
@@ -357,6 +359,10 @@
     for j in range(span):
         masks[0, j] = flag(starts[j] < rows)
     masks[1, 0] = flag(starts[0] < base_ref[0])
+    top = flag(lax.broadcasted_iota(jnp.int32, (SUBS, LANES), 0) == 0)
+    masks[1, 1] = top * flag(starts[0] < rows)
+    masks[1, 2] = top * flag(starts[0] < rows - 1)
+    masks[1, 3] = top * flag(starts[1] < rows)
     sums[...] = jnp.zeros(sums.shape, f32)
 
     def group(lanes):
@@ -381,6 +387,12 @@
         for slot, lane in enumerate(lanes):
             part = parts[slot]
             decay = [row_of(tables.at[slot, 0], n) for n in range(modes)]
+            rim = rim_ref[0, :, cols_of(lane)].astype(f32)
+            tap = taps_ref[0, :, cols_of(lane)]
+            edge = [
+                (tap[1:2] * rim[1:2]) * masks[1, 1] + (tap[2:3] * rim[0:1]) * masks[1, 2],
+                (tap[2:3] * rim[1:2]) * masks[1, 3],
+            ]
             for j in range(span):
                 part = [part[n] * decay[n] for n in range(modes)]
                 total = part
@@ -388,7 +400,10 @@
                     total = [total[m] + total[m + 1] for m in range(0, len(total), 2)]
                 conv = near_ref[pl.ds(j * SUBS, SUBS), cols_of(lane)] + total[0] * masks[0, j]
                 conv = conv.astype(bf16).astype(f32)
-                wide[slot, pl.ds(j, SUBS, stride=span + 1), :] = short_ref[pl.ds(j * SUBS, SUBS), cols_of(lane)] * conv
+                short = short_ref[pl.ds(j * SUBS, SUBS), cols_of(lane)]
+                if j < 2:
+                    short = short + edge[j]
+                wide[slot, pl.ds(j, SUBS, stride=span + 1), :] = short * conv
         for b in range(SUBS):
             rows = pl.ds(b * span, span)
             squares = sums[rows, :]
@@ -467,6 +482,22 @@
         name="tails",
     )(far_off(query_in), far_off(key_in), far_off(value_in))
     rim_rows = from_behind(tails, "ctx", 1)
+    q_short = pl.pallas_call(
+        functools.partial(query_kernel, span=span, most=Q_TILES, chunk=chunk),
+        in_specs=[smem, smem, hbm, vmem],
+        out_specs=vmem,
+        out_shape=pltpu.VMEM((tok_rows, chans), f32),
+        scratch_shapes=[
+            pltpu.VMEM((tok_rows, chans), bf16),
+            pltpu.SemaphoreType.DMA((pieces,)),
+            pltpu.VMEM((2, span) + tile_shape, f32),
+            pltpu.VMEM((Q_TILES, wide_rows, LANES), f32),
+        ],
+        compiler_params=params,
+        cost_estimate=cost(200, 6 * tok_rows * chans),
+        name="query_part",
+    )(base, lengths, far_off(query_in), near_by(short_taps))
+    rim_rows, q_short = lax.optimization_barrier((rim_rows, q_short))
     rates, weights, taps, rims = near_by(decay_rate), near_by(weight), near_by(short_taps), near_by(rim_rows)
     gates, states, own, give = pl.pallas_call(
         functools.partial(state_kernel, span=span, modes=modes, most=A_TILES, chunk=chunk),
@@ -494,34 +525,26 @@
         name="block_states",
     )(base, lengths, far_off(key_in), far_off(value_in), rims, taps, rates, weights)
 
-    near = pl.pallas_call(
-        functools.partial(near_kernel, span=span, modes=modes, most=N_TILES),
-        in_specs=[smem, smem, vmem, vmem, vmem],
-        out_specs=vmem,
-        out_shape=pltpu.VMEM((tok_rows, chans), f32),
-        scratch_shapes=[pltpu.VMEM((2, span) + tile_shape, f32)],
-        compiler_params=params,
-        cost_estimate=cost(600, 7 * tok_rows * chans),
-        name="near_part",
-    )(base, lengths, near_by(gates), rates, weights)
-
-    q_short = pl.pallas_call(
-        functools.partial(query_kernel, span=span, most=Q_TILES, chunk=chunk),
-        in_specs=[smem, smem, hbm, vmem, vmem],
-        out_specs=vmem,
-        out_shape=pltpu.VMEM((tok_rows, chans), f32),
-        scratch_shapes=[
-            pltpu.VMEM((tok_rows, chans), bf16),
-            pltpu.SemaphoreType.DMA((pieces,)),
-            pltpu.VMEM((2, span) + tile_shape, f32),
-            pltpu.VMEM((Q_TILES, wide_rows, LANES), f32),
-        ],
-        compiler_params=params,
-        cost_estimate=cost(200, 6 * tok_rows * chans),
-        name="query_part",
-    )(base, lengths, far_off(query_in), rims, taps)
+    def near_piece(part, near):
+        count = chans // NEAR_PARTS
+        before = [] if near is None else [near_by(near)]
+        return pl.pallas_call(
+            functools.partial(
+                near_kernel, span=span, modes=modes, most=N_TILES, first=part * count, count=count
+            ),
+            in_specs=[smem, smem, vmem, vmem, vmem] + [vmem] * len(before),
+            out_specs=vmem,
+            out_shape=pltpu.VMEM((tok_rows, chans), f32),
+            scratch_shapes=[pltpu.VMEM((2, span) + tile_shape, f32)],
+            compiler_params=params,
+            input_output_aliases={5: 0} if before else {},
+            cost_estimate=cost(600 // NEAR_PARTS, 7 * tok_rows * count),
+            name="near_part_%d" % part,
+        )(base, lengths, near_by(gates), rates, weights, *before)
 
     got = swap(give, "ctx")
+    near = near_piece(0, None)
+    got, near = lax.optimization_barrier((got, near))
 
     def pair_call(kernel, operands, out_shape, name, **static):
         count = len(operands) + 1
@@ -537,13 +560,15 @@
     sent = pltpu.VMEM(half.shape, bf16)
     ends = pair_call(pair_kernel, [own, got], [sent], "pair_ends")[0]
     one_on, two_on = from_behind(ends, "ctx", 2), from_behind(ends, "ctx", 4)
+    near = near_piece(1, near)
     one_on, two_on, near = lax.optimization_barrier((one_on, two_on, near))
     enter, on, reach = one_on, two_on, 1
     while 2 * reach < blocks // 8:
         enter = pair_call(reach_kernel, [enter, on], [sent], "reach_%d" % (2 * reach), reach=reach)[0]
         reach *= 2
         on = from_behind(enter, "ctx", 2 * reach)
-    on, q_short = lax.optimization_barrier((on, q_short))
+    near = near_piece(2, near)
+    on, near = lax.optimization_barrier((on, near))
     mine, give_back = pair_call(
         enter_kernel,
         [enter, on, own, got],
@@ -552,6 +577,7 @@
         reach=reach,
     )
     got_back = swap(give_back, "ctx")
+    near = near_piece(3, near)
 
     alone = grp == 1
     out_specs = [hbm]
@@ -576,7 +602,7 @@
         functools.partial(
             final_kernel, span=span, modes=modes, channels=chans if alone else 0, most=F_TILES, chunk=chunk
         ),
-        in_specs=[smem, smem, vmem, vmem, vmem, vmem, vmem, hbm, vmem, vmem, vmem],
+        in_specs=[smem, smem, vmem, vmem, vmem, vmem, vmem, hbm, vmem, vmem, vmem, vmem, vmem],
         out_specs=out_specs,
         out_shape=out_shape,
         scratch_shapes=scratch,
@@ -585,7 +611,7 @@
         name="far_part",
     )(
         base, lengths, near_by(states), near_by(mine), near_by(got_back), near_by(near), near_by(q_short), far_off(residual),
-        rates, weights, norm_gain.reshape(1, chans),
+        rims, taps, rates, weights, norm_gain.reshape(1, chans),
     )
     if alone:
         return tuple(outs)

time: 60.6 us -> 61.7 us (1.018)
  the two profiles are of different devices: /device:TPU:11 before, /device:TPU:9 now
where the time goes in v8:
time: 61.7 us; the launch traced here: 61.3 us
  Pallas kernels  39.9 us (65%)
  starting transfers between devices  15.5 us (25%)
  waiting for transfers between devices  4.72 us (8%)
  between operations  0.83 us (1%)
    pallas_call x1, Pallas kernels, shards(): pl.pallas_call(functools.partial(state_kernel, span=span, modes=modes, mo...  13.1 us
    ppermute x4, starting transfers between devices, from_behind(): return lax.ppermute(shard, axis, pairs)  12.4 us
    pallas_call x1, Pallas kernels, shards(): pl.pallas_call(functools.partial(final_kernel, span=span, modes=modes, ch...  10.9 us
    pallas_call x4, Pallas kernels, near_piece(): pl.pallas_call(functools.partial(near_kernel, span=span, modes=modes, mos...  8.1 us
    ppermute x4, waiting for transfers between devices, from_behind(): return lax.ppermute(shard, axis, pairs)  4.72 us
    pallas_call x1, Pallas kernels, shards(): pl.pallas_call(functools.partial(query_kernel, span=span, most=Q_TILES, c...  4.15 us
    ppermute x2, starting transfers between devices, swap(): lax.ppermute(shard, axis, [(i, i ^ 1) for i in range(lax.axis_size(axis))])  3.13 us
    pallas_call x3, Pallas kernels, pair_call(): pl.pallas_call(functools.partial(kernel, rows=tok_rows, **static), in_spe...  2.38 us
  transfers between devices with their start and end apart: 6, of which 2 were waited for; matrix products, arithmetic and copies ran while one was open for 1% of the time, Pallas kernels for 20%

profile of v8, /device:TPU:9, one launch (start us, length us, event | category | flops | bytes accessed | tf_op | source)
XLA Modules:
  0.0 61.3 jit_solution(6579500163816547630)
XLA Ops:
  0.6 0.0 copy-start
  0.6 0.0 copy-start.3
  0.7 0.0 copy-start.1
  0.7 1.3 %tails.1 = bf16[3,2,8192]{2,1,0:T(2,128)(2,1)S(1)} custom-call(bf16[128,8192]{1,0:T(8,128)(2,1)} %query_ref.3, bf16[128,8192]{1,0:T(8,128)(2,1)} %key_ref.3, bf16[128,8192]{1,0:T(8,128)(2,1)} %value_ref.3), custom_call_target="tpu_custom_call" | custom-call | tf_op jit(solution)/shard_map/tails/pallas_call | solution.py:475
  1.9 3.7 %collective-permute-start = (bf16[3,2,8192]{2,1,0:T(2,128)(2,1)S(1)}, bf16[3,2,8192]{2,1,0:T(2,128)(2,1)S(1)}, u32[]{:S(2)}, u32[]{:S(2)}) collective-permute-start(bf16[3,2,8192]{2,1,0:T(2,128)(2,1)S(1)} %tails.1), channel_id=1, source_target_pairs={{0,1},{1,2},{2,3},{3,4},{4,5},{5,6},{6,7},{7,8},{8,9},{9,10},{10,1... | collective-permute-start | bytes 294920 | tf_op jit(solution)/shard_map/ppermute | solution.py:23
  5.6 0.0 copy-done
  5.6 0.0 copy-done.3
  5.6 0.3 sqrt_multiply_fusion.weight_ref
  6.0 0.0 copy-done.1
  6.0 4.1 %query_part.1.short_ref = f32[128,8192]{1,0:T(8,128)S(1)} custom-call(s32[1]{0:T(128)} %bitcast.base_ref, s32[16]{0:T(128)} %len_ref.19, bf16[128,8192]{1,0:T(8,128)(2,1)} %query_ref.3, f32[3,3,8192]{2,1,0:T(4,128)S(1)} %copy-done.1), custom_call_target="tpu_custom_call" | custom-call | flops 13107200 | bytes 6291456 | tf_op jit(solution)/shard_map/query_part/pallas_call | solution.py:485
  10.1 0.0 collective-permute-done.rim_ref
  10.1 13.1 %block_states.1 = (bf16[128,8192]{1,0:T(8,128)(2,1)S(1)}, f32[128,8192]{1,0:T(8,128)S(1)}, f32[16,4096]{1,0:T(8,128)S(1)}, f32[16,4096]{1,0:T(8,128)S(1)}) custom-call(s32[1]{0:T(128)} %bitcast.base_ref, s32[16]{0:T(128)} %len_ref.19, bf16[128,8192]{1,0:T(8,128)(2,1)} %key_ref.3, bf16[128,8192]{1,0:T(8,128)(2,1)} %value_ref.3, ...), custom_call_target="tpu_custom_call" | custom-call | flops 65536000 | bytes 12582912 | tf_op jit(solution)/shard_map/block_states/pallas_call | solution.py:502
  23.2 0.3 collective-permute-start.1
  23.5 2.0 %near_part_0.1.refs_0_ = f32[128,8192]{1,0:T(8,128)S(1)} custom-call(s32[1]{0:T(128)} %bitcast.base_ref, s32[16]{0:T(128)} %len_ref.19, bf16[128,8192]{1,0:T(8,128)(2,1)S(1)} %get-tuple-element.21.gate_ref, f32[16,8192]{1,0:T(8,128)S(1)} %copy-done, f32[16,8192]{1,0:T(8,128)S(1)} %sqrt_multiply_fusion.weight_ref), custom_call_target="tpu_custom_call" | custom-call | flops 9830400 | bytes 1835008 | tf_op jit(solution)/shard_map/near_part_0/pallas_call | solution.py:531
  25.5 0.0 collective-permute-done.1.got_ref
  25.5 0.8 %pair_ends.1 = bf16[16,4096]{1,0:T(8,128)(2,1)S(1)} custom-call(s32[1]{0:T(128)} %bitcast.base_ref, s32[16]{0:T(128)} %len_ref.19, f32[16,4096]{1,0:T(8,128)S(1)} %get-tuple-element.19.own_ref, f32[16,4096]{1,0:T(8,128)S(1)} %collective-permute-done.1.got_ref, f32[16,8192]{1,0:T(8,128)S(1)} %copy-done), custom_call_target="tpu_custom_call" | custom-call | tf_op jit(solution)/shard_map/pair_ends/pallas_call | solution.py:551
  26.3 3.0 %collective-permute-start.3 = (bf16[16,4096]{1,0:T(8,128)(2,1)S(1)}, bf16[16,4096]{1,0:T(8,128)(2,1)S(1)}, u32[]{:S(2)}, u32[]{:S(2)}) collective-permute-start(bf16[16,4096]{1,0:T(8,128)(2,1)S(1)} %pair_ends.1), channel_id=1, source_target_pairs={{0,4},{1,5},{2,6},{3,7},{4,8},{5,9},{6,10},{7,11},{8,12},{9,13},{1... | collective-permute-start | bytes 393224 | tf_op jit(solution)/shard_map/ppermute | solution.py:23
  29.3 3.1 %collective-permute-start.2 = (bf16[16,4096]{1,0:T(8,128)(2,1)S(1)}, bf16[16,4096]{1,0:T(8,128)(2,1)S(1)}, u32[]{:S(2)}, u32[]{:S(2)}) collective-permute-start(bf16[16,4096]{1,0:T(8,128)(2,1)S(1)} %pair_ends.1), channel_id=1, source_target_pairs={{0,2},{1,3},{2,4},{3,5},{4,6},{5,7},{6,8},{7,9},{8,10},{9,11},{10,... | collective-permute-start | bytes 393224 | tf_op jit(solution)/shard_map/ppermute | solution.py:23
  32.4 2.0 %near_part_1.1.refs_0_ = f32[128,8192]{1,0:T(8,128)S(1)} custom-call(s32[1]{0:T(128)} %bitcast.base_ref, s32[16]{0:T(128)} %len_ref.19, bf16[128,8192]{1,0:T(8,128)(2,1)S(1)} %get-tuple-element.21.gate_ref, f32[16,8192]{1,0:T(8,128)S(1)} %copy-done, f32[16,8192]{1,0:T(8,128)S(1)} %sqrt_multiply_fusion.weight_ref, ...), custom_call_target="tpu_custom_call", output_to_operand_aliasing={{}: (5, {})} | custom-call | flops 9830400 | bytes 1835008 | tf_op jit(solution)/shard_map/near_part_1/pallas_call | solution.py:531
  34.4 0.0 collective-permute-done.3.far_ref
  34.4 2.8 %collective-permute-done.2.near_ref = bf16[16,4096]{1,0:T(8,128)(2,1)S(1)} collective-permute-done((bf16[16,4096]{1,0:T(8,128)(2,1)S(1)}, bf16[16,4096]{1,0:T(8,128)(2,1)S(1)}, u32[]{:S(2)}, u32[]{:S(2)}) %collective-permute-start.2) | collective-permute-done | bytes 131104 | tf_op jit(solution)/shard_map/ppermute | solution.py:23
  37.2 0.8 %reach_2.1.near_ref = bf16[16,4096]{1,0:T(8,128)(2,1)S(1)} custom-call(s32[1]{0:T(128)} %bitcast.base_ref, s32[16]{0:T(128)} %len_ref.19, bf16[16,4096]{1,0:T(8,128)(2,1)S(1)} %collective-permute-done.2.near_ref, bf16[16,4096]{1,0:T(8,128)(2,1)S(1)} %collective-permute-done.3.far_ref, f32[16,8192]{1,0:T(8,128)S(1)} %copy-done), custom_call_target="tpu_custom_call" | custom-call | tf_op jit(solution)/shard_map/reach_2/pallas_call | solution.py:551
  38.0 2.6 %collective-permute-start.4 = (bf16[16,4096]{1,0:T(8,128)(2,1)S(1)}, bf16[16,4096]{1,0:T(8,128)(2,1)S(1)}, u32[]{:S(2)}, u32[]{:S(2)}) collective-permute-start(bf16[16,4096]{1,0:T(8,128)(2,1)S(1)} %reach_2.1.near_ref), channel_id=1, source_target_pairs={{0,4},{1,5},{2,6},{3,7},{4,8},{5,9},{6,10},{7,11},{8,12},{9,13},{1... | collective-permute-start | bytes 393224 | tf_op jit(solution)/shard_map/ppermute | solution.py:23
  40.6 2.0 %near_part_2.1.refs_0_ = f32[128,8192]{1,0:T(8,128)S(1)} custom-call(s32[1]{0:T(128)} %bitcast.base_ref, s32[16]{0:T(128)} %len_ref.19, bf16[128,8192]{1,0:T(8,128)(2,1)S(1)} %get-tuple-element.21.gate_ref, f32[16,8192]{1,0:T(8,128)S(1)} %copy-done, f32[16,8192]{1,0:T(8,128)S(1)} %sqrt_multiply_fusion.weight_ref, ...), custom_call_target="tpu_custom_call", output_to_operand_aliasing={{}: (5, {})} | custom-call | flops 9830400 | bytes 1835008 | tf_op jit(solution)/shard_map/near_part_2/pallas_call | solution.py:531
  42.6 1.9 %collective-permute-done.4.far_ref = bf16[16,4096]{1,0:T(8,128)(2,1)S(1)} collective-permute-done((bf16[16,4096]{1,0:T(8,128)(2,1)S(1)}, bf16[16,4096]{1,0:T(8,128)(2,1)S(1)}, u32[]{:S(2)}, u32[]{:S(2)}) %collective-permute-start.4) | collective-permute-done | bytes 131104 | tf_op jit(solution)/shard_map/ppermute | solution.py:23
  44.6 0.9 %pair_enter.1 = (f32[16,4096]{1,0:T(8,128)S(1)}, f32[16,4096]{1,0:T(8,128)S(1)}) custom-call(s32[1]{0:T(128)} %bitcast.base_ref, s32[16]{0:T(128)} %len_ref.19, bf16[16,4096]{1,0:T(8,128)(2,1)S(1)} %reach_2.1.near_ref, bf16[16,4096]{1,0:T(8,128)(2,1)S(1)} %collective-permute-done.4.far_ref, f32[16,4096]{1,0:T(8,128)S(1)} %get-tuple-element.19.own_ref, ...), custom_call_target="tpu_custom_call" | custom-call | tf_op jit(solution)/shard_map/pair_enter/pallas_call | solution.py:551
  45.4 0.0 copy-start.2
  45.4 2.9 %collective-permute-start.5 = (f32[16,4096]{1,0:T(8,128)S(1)}, f32[16,4096]{1,0:T(8,128)S(1)}, u32[]{:S(2)}, u32[]{:S(2)}) collective-permute-start(f32[16,4096]{1,0:T(8,128)S(1)} %get-tuple-element.29), channel_id=1, source_target_pairs={{0,1},{1,0},{2,3},{3,2},{4,5},{5,4},{6,7},{7,6},{8,9},{9,8},{10,11... | collective-permute-start | bytes 786440 | tf_op jit(solution)/shard_map/ppermute | solution.py:27
  48.3 2.0 %near_part_3.1.near_ref = f32[128,8192]{1,0:T(8,128)S(1)} custom-call(s32[1]{0:T(128)} %bitcast.base_ref, s32[16]{0:T(128)} %len_ref.19, bf16[128,8192]{1,0:T(8,128)(2,1)S(1)} %get-tuple-element.21.gate_ref, f32[16,8192]{1,0:T(8,128)S(1)} %copy-done, f32[16,8192]{1,0:T(8,128)S(1)} %sqrt_multiply_fusion.weight_ref, ...), custom_call_target="tpu_custom_call", output_to_operand_aliasing={{}: (5, {})} | custom-call | flops 9830400 | bytes 1835008 | tf_op jit(solution)/shard_map/near_part_3/pallas_call | solution.py:531
  50.3 0.0 collective-permute-done.5.got_ref
  50.3 0.0 copy-done.2
  50.4 10.9 %far_part.1 = (bf16[128,8192]{1,0:T(8,128)(2,1)}, bf16[128,8192]{1,0:T(8,128)(2,1)}) custom-call(s32[1]{0:T(128)} %bitcast.base_ref, s32[16]{0:T(128)} %len_ref.19, f32[128,8192]{1,0:T(8,128)S(1)} %get-tuple-element.18.state_ref, f32[16,4096]{1,0:T(8,128)S(1)} %get-tuple-element.28.mine_ref, f32[16,4096]{1,0:T(8,128)S(1)} %collective-permute-done.5.got_ref, ...), custom_call_target="tpu_custom_call" | custom-call | flops 58982400 | bytes 18874368 | tf_op jit(solution)/shard_map/far_part/pallas_call | solution.py:601
Async XLA Ops:
  0.6 5.0 %copy-start = (f32[16,8192]{1,0:T(8,128)S(1)}, f32[16,8192]{1,0:T(8,128)}, u32[]{:S(2)}) copy-start(f32[16,8192]{1,0:T(8,128)} %rate_ref.17) | copy-start | bytes 1572868
  0.6 5.0 %copy-start.3 = (f32[16,8192]{1,0:T(8,128)S(1)}, f32[16,8192]{1,0:T(8,128)}, u32[]{:S(2)}) copy-start(f32[16,8192]{1,0:T(8,128)} %param.14) | copy-start | bytes 1572868
  0.7 5.3 %copy-start.1 = (f32[3,3,8192]{2,1,0:T(4,128)S(1)}, f32[3,3,8192]{2,1,0:T(4,128)}, u32[]{:S(2)}) copy-start(f32[3,3,8192]{2,1,0:T(4,128)} %taps_ref.5) | copy-start | bytes 884740
  1.9 8.2 %collective-permute-start = (bf16[3,2,8192]{2,1,0:T(2,128)(2,1)S(1)}, bf16[3,2,8192]{2,1,0:T(2,128)(2,1)S(1)}, u32[]{:S(2)}, u32[]{:S(2)}) collective-permute-start(bf16[3,2,8192]{2,1,0:T(2,128)(2,1)S(1)} %tails.1), channel_id=1, source_target_pairs={{0,1},{1,2},{2,3},{3,4},{4,5},{5,6},{6,7},{7,8},{8,9},{9,10},{10,1... | collective-permute-start | bytes 294920 | tf_op jit(solution)/shard_map/ppermute | solution.py:23
  23.2 2.3 %collective-permute-start.1 = (f32[16,4096]{1,0:T(8,128)S(1)}, f32[16,4096]{1,0:T(8,128)S(1)}, u32[]{:S(2)}, u32[]{:S(2)}) collective-permute-start(f32[16,4096]{1,0:T(8,128)S(1)} %get-tuple-element.20), channel_id=1, source_target_pairs={{0,1},{1,0},{2,3},{3,2},{4,5},{5,4},{6,7},{7,6},{8,9},{9,8},{10,11... | collective-permute-start | bytes 786440 | tf_op jit(solution)/shard_map/ppermute | solution.py:27
  26.3 8.1 %collective-permute-start.3 = (bf16[16,4096]{1,0:T(8,128)(2,1)S(1)}, bf16[16,4096]{1,0:T(8,128)(2,1)S(1)}, u32[]{:S(2)}, u32[]{:S(2)}) collective-permute-start(bf16[16,4096]{1,0:T(8,128)(2,1)S(1)} %pair_ends.1), channel_id=1, source_target_pairs={{0,4},{1,5},{2,6},{3,7},{4,8},{5,9},{6,10},{7,11},{8,12},{9,13},{1... | collective-permute-start | bytes 393224 | tf_op jit(solution)/shard_map/ppermute | solution.py:23
  29.3 7.9 %collective-permute-start.2 = (bf16[16,4096]{1,0:T(8,128)(2,1)S(1)}, bf16[16,4096]{1,0:T(8,128)(2,1)S(1)}, u32[]{:S(2)}, u32[]{:S(2)}) collective-permute-start(bf16[16,4096]{1,0:T(8,128)(2,1)S(1)} %pair_ends.1), channel_id=1, source_target_pairs={{0,2},{1,3},{2,4},{3,5},{4,6},{5,7},{6,8},{7,9},{8,10},{9,11},{10,... | collective-permute-start | bytes 393224 | tf_op jit(solution)/shard_map/ppermute | solution.py:23
  38.0 6.6 %collective-permute-start.4 = (bf16[16,4096]{1,0:T(8,128)(2,1)S(1)}, bf16[16,4096]{1,0:T(8,128)(2,1)S(1)}, u32[]{:S(2)}, u32[]{:S(2)}) collective-permute-start(bf16[16,4096]{1,0:T(8,128)(2,1)S(1)} %reach_2.1.near_ref), channel_id=1, source_target_pairs={{0,4},{1,5},{2,6},{3,7},{4,8},{5,9},{6,10},{7,11},{8,12},{9,13},{1... | collective-permute-start | bytes 393224 | tf_op jit(solution)/shard_map/ppermute | solution.py:23
  45.4 4.9 %copy-start.2 = (f32[8192]{0:T(1024)S(1)}, f32[8192]{0:T(1024)}, u32[]{:S(2)}) copy-start(f32[8192]{0:T(1024)} %param.17) | copy-start | bytes 98308
  45.4 4.9 %collective-permute-start.5 = (f32[16,4096]{1,0:T(8,128)S(1)}, f32[16,4096]{1,0:T(8,128)S(1)}, u32[]{:S(2)}, u32[]{:S(2)}) collective-permute-start(f32[16,4096]{1,0:T(8,128)S(1)} %get-tuple-element.29), channel_id=1, source_target_pairs={{0,1},{1,0},{2,3},{3,2},{4,5},{5,4},{6,7},{7,6},{8,9},{9,8},{10,11... | collective-permute-start | bytes 786440 | tf_op jit(solution)/shard_map/ppermute | solution.py:27

commit v9 on v8

--- a/solution.py
+++ b/solution.py
@@ -12,7 +12,7 @@
 LANES = 128
 MIB = 1024 * 1024
 A_TILES, N_TILES, Q_TILES, F_TILES = 2, 2, 4, 4
-NEAR_PARTS = 4
+NEAR_PARTS = 2
 f32 = jnp.float32
 bf16 = jnp.bfloat16
 
@@ -83,29 +83,28 @@
     return jnp.broadcast_to(ref[pl.ds(index, 1), :], (SUBS, LANES))
 
 
-def spread(x, wide, span, pad=1):
+def spread(x, wide, span):
     x = x.astype(f32)
     for b in range(SUBS):
-        wide[pl.ds(b * (span + pad), span), :] = x[b * span : (b + 1) * span]
-
-
-def steps_of(wide, span, pad=1):
-    return [wide[pl.ds(j, SUBS, stride=span + pad), :] for j in range(span)]
-
-
-def short_conv(steps, rim, taps, keep_one, keep_two):
-    top = lax.broadcasted_iota(jnp.int32, (SUBS, LANES), 0) == 0
-    ahead = [0.0, 0.0] if rim is None else [jnp.broadcast_to(rim[m : m + 1].astype(f32), (SUBS, LANES)) for m in range(2)]
-    behind_one = jnp.where(top, ahead[1], pltpu.roll(steps[-1], 1, 0))
-    behind_two = jnp.where(top, ahead[0], pltpu.roll(steps[-2], 1, 0))
-    padded = [behind_two, behind_one] + steps
-    taps = [jnp.broadcast_to(taps[m : m + 1], (SUBS, LANES)) for m in range(3)]
-    return [
-        taps[0] * padded[j + 2]
-        + (taps[1] * padded[j + 1]) * keep_one[j]
-        + (taps[2] * padded[j]) * keep_two[j]
-        for j in range(len(steps))
-    ]
+        wide[pl.ds(b * (span + 1), span), :] = x[b * span : (b + 1) * span]
+
+
+class Conv:
+    def __init__(self, wide, rim, taps, span):
+        self.wide, self.span = wide, span
+        self.taps = [jnp.broadcast_to(taps[m : m + 1], (SUBS, LANES)) for m in range(3)]
+        top = lax.broadcasted_iota(jnp.int32, (SUBS, LANES), 0) == 0
+        ahead = [0.0, 0.0] if rim is None else [jnp.broadcast_to(rim[m : m + 1].astype(f32), (SUBS, LANES)) for m in range(2)]
+        self.behind = [jnp.where(top, ahead[m], pltpu.roll(self.row(span - 2 + m), 1, 0)) for m in range(2)]
+
+    def row(self, j):
+        return self.wide[pl.ds(j, SUBS, stride=self.span + 1), :]
+
+    def step(self, j, keep_one, keep_two):
+        here = self.row(j)
+        two, one = self.behind
+        self.behind = [one, here]
+        return self.taps[0] * here + (self.taps[1] * one) * keep_one + (self.taps[2] * two) * keep_two
 
 
 def half_of(base_ref, rows, chans, lane):
@@ -156,18 +155,26 @@
             for m, by in enumerate((1, span, 2 * span, 4 * span)):
                 tables[slot, m] = jnp.exp(-float(by) * rate)
             tables[slot, 4] = weight_ref[:, cols_of(lane)]
-        for slot, lane in enumerate(lanes):
-            cols = cols_of(lane)
-            keep_one = [masks[0, j] for j in range(span)]
-            keep_two = [masks[1, j] for j in range(span)]
-            k_short = short_conv(steps_of(wide_k.at[slot], span), rim_ref[1, :, cols], taps_ref[1, :, cols], keep_one, keep_two)
-            v_short = short_conv(steps_of(wide_v.at[slot], span), rim_ref[2, :, cols], taps_ref[2, :, cols], keep_one, keep_two)
-            for j in range(0, span, 2):
-                pair = jnp.concatenate([k_short[j] * v_short[j], k_short[j + 1] * v_short[j + 1]], axis=0).astype(bf16)
-                gate_ref[pl.ds(j * SUBS, 2 * SUBS), cols] = pair
+        convs = [
+            [
+                Conv(wide.at[slot], rim_ref[i, :, cols_of(lane)], taps_ref[i, :, cols_of(lane)], span)
+                for i, wide in ((1, wide_k), (2, wide_v))
+            ]
+            for slot, lane in enumerate(lanes)
+        ]
+        last = [None] * len(lanes)
+        for j in range(span):
+            keep_one, keep_two = masks[0, j], masks[1, j]
+            for slot, lane in enumerate(lanes):
+                k_short, v_short = [conv.step(j, keep_one, keep_two) for conv in convs[slot]]
+                if j % 2 == 0:
+                    last[slot] = k_short * v_short
+                    continue
+                pair = jnp.concatenate([last[slot], k_short * v_short], axis=0).astype(bf16)
+                gate_ref[pl.ds((j - 1) * SUBS, 2 * SUBS), cols_of(lane)] = pair
                 pair = pair.astype(f32)
-                held[slot, j] = pair[:SUBS] * masks[2, j]
-                held[slot, j + 1] = pair[SUBS:] * masks[2, j + 1]
+                held[slot, j - 1] = pair[:SUBS] * masks[2, j - 1]
+                held[slot, j] = pair[SUBS:] * masks[2, j]
         states = []
         for slot, lane in enumerate(lanes):
             decay = [row_of(tables.at[slot, 0], n) for n in range(modes)]
@@ -177,17 +184,19 @@
                 state = [decay[n] * state[n] + gate for n in range(modes)]
             states.append(state)
         for m, shift in enumerate((1, 2, 4)):
+            joined = masks[3, m] > 0.0
             for slot in range(len(lanes)):
                 states[slot] = [
-                    x + (row_of(tables.at[slot, m + 1], n) * masks[3, m]) * pltpu.roll(x, shift, 0)
+                    x + jnp.where(joined, row_of(tables.at[slot, m + 1], n) * pltpu.roll(x, shift, 0), 0.0)
                     for n, x in enumerate(states[slot])
                 ]
+        inner = masks[3, 3] > 0.0
         for slot, lane in enumerate(lanes):
             for n, x in enumerate(states[slot]):
                 ends[slot, pl.ds(n, 1), :] = x[SUBS - 1 :]
-                state_ref[pl.ds(n * SUBS, SUBS), cols_of(lane)] = (
-                    row_of(tables.at[slot, 4], n) * masks[3, 3]
-                ) * pltpu.roll(x, 1, 0)
+                state_ref[pl.ds(n * SUBS, SUBS), cols_of(lane)] = jnp.where(
+                    inner, row_of(tables.at[slot, 4], n) * pltpu.roll(x, 1, 0), 0.0
+                )
         for slot, lane in enumerate(lanes):
             mine, here = half_of(base_ref, key_ref.shape[0], chans, lane)
 
@@ -273,14 +282,12 @@
 
     def group(lanes):
         for slot, lane in enumerate(lanes):
-            spread(query_buf[:, cols_of(lane)], wide_q.at[slot], span, 0)
-        for slot, lane in enumerate(lanes):
-            cols = cols_of(lane)
-            keep_one = [masks[0, j] for j in range(span)]
-            keep_two = [masks[1, j] for j in range(span)]
-            q_short = short_conv(steps_of(wide_q.at[slot], span, 0), None, taps_ref[0, :, cols], keep_one, keep_two)
-            for j in range(span):
-                short_ref[pl.ds(j * SUBS, SUBS), cols] = q_short[j]
+            spread(query_buf[:, cols_of(lane)], wide_q.at[slot], span)
+        convs = [Conv(wide_q.at[slot], None, taps_ref[0, :, cols_of(lane)], span) for slot, lane in enumerate(lanes)]
+        for j in range(span):
+            keep_one, keep_two = masks[0, j], masks[1, j]
+            for slot, lane in enumerate(lanes):
+                short_ref[pl.ds(j * SUBS, SUBS), cols_of(lane)] = convs[slot].step(j, keep_one, keep_two)
 
     each_chunk(chans, chunk, lambda c: fetch(c).wait(), group, lambda c: None, most)
 
@@ -543,8 +550,6 @@
         )(base, lengths, near_by(gates), rates, weights, *before)
 
     got = swap(give, "ctx")
-    near = near_piece(0, None)
-    got, near = lax.optimization_barrier((got, near))
 
     def pair_call(kernel, operands, out_shape, name, **static):
         count = len(operands) + 1
@@ -560,14 +565,14 @@
     sent = pltpu.VMEM(half.shape, bf16)
     ends = pair_call(pair_kernel, [own, got], [sent], "pair_ends")[0]
     one_on, two_on = from_behind(ends, "ctx", 2), from_behind(ends, "ctx", 4)
-    near = near_piece(1, near)
+    near = near_piece(0, None)
     one_on, two_on, near = lax.optimization_barrier((one_on, two_on, near))
     enter, on, reach = one_on, two_on, 1
     while 2 * reach < blocks // 8:
         enter = pair_call(reach_kernel, [enter, on], [sent], "reach_%d" % (2 * reach), reach=reach)[0]
         reach *= 2
         on = from_behind(enter, "ctx", 2 * reach)
-    near = near_piece(2, near)
+    near = near_piece(1, near)
     on, near = lax.optimization_barrier((on, near))
     mine, give_back = pair_call(
         enter_kernel,
@@ -577,7 +582,6 @@
         reach=reach,
     )
     got_back = swap(give_back, "ctx")
-    near = near_piece(3, near)
 
     alone = grp == 1
     out_specs = [hbm]

time: 61.7 us -> 59.6 us (0.966)
  Pallas kernels: 39.9 us -> 37.7 us
    ppermute x2, waiting for transfers between devices: 0.01 us -> 2.32 us  [swap(): lax.ppermute(shard, axis, [(i, i ^ 1) for i in range(lax.axis_size(axis))])]
    ppermute x4, waiting for transfers between devices: 4.72 us -> 2.62 us  [from_behind(): return lax.ppermute(shard, axis, pairs)]
    pallas_call x4 -> x2, Pallas kernels: 8.1 us -> 6.64 us  [near_piece(): pl.pallas_call(functools.partial(near_kernel, span=span, modes=modes, mos...]
    pallas_call x1, Pallas kernels: 4.15 us -> 3.43 us  [shards(): pl.pallas_call(functools.partial(query_kernel, span=span, most=Q_TILES, c...]
  transfers between devices with their start and end apart: 6 -> 6, of which waited for: 2 -> 4; matrix products, arithmetic and copies ran while one was open for 1% -> 1% of each run, Pallas kernels for 20% -> 17%
where the time goes in v9:
time: 59.6 us; the launch traced here: 59.2 us
  Pallas kernels  37.7 us (63%)
  starting transfers between devices  15.4 us (26%)
  waiting for transfers between devices  4.95 us (8%)
  between operations  0.8 us (1%)
    pallas_call x1, Pallas kernels, shards(): pl.pallas_call(functools.partial(state_kernel, span=span, modes=modes, mo...  13.1 us
    ppermute x4, starting transfers between devices, from_behind(): return lax.ppermute(shard, axis, pairs)  11.9 us
    pallas_call x1, Pallas kernels, shards(): pl.pallas_call(functools.partial(final_kernel, span=span, modes=modes, ch...  10.9 us
    pallas_call x2, Pallas kernels, near_piece(): pl.pallas_call(functools.partial(near_kernel, span=span, modes=modes, mos...  6.64 us
    ppermute x2, starting transfers between devices, swap(): lax.ppermute(shard, axis, [(i, i ^ 1) for i in range(lax.axis_size(axis))])  3.46 us
    pallas_call x1, Pallas kernels, shards(): pl.pallas_call(functools.partial(query_kernel, span=span, most=Q_TILES, c...  3.43 us
    ppermute x4, waiting for transfers between devices, from_behind(): return lax.ppermute(shard, axis, pairs)  2.62 us
    pallas_call x3, Pallas kernels, pair_call(): pl.pallas_call(functools.partial(kernel, rows=tok_rows, **static), in_spe...  2.37 us
  transfers between devices with their start and end apart: 6, of which 4 were waited for; matrix products, arithmetic and copies ran while one was open for 1% of the time, Pallas kernels for 17%

profile of v9, /device:TPU:9, one launch (start us, length us, event | category | flops | bytes accessed | tf_op | source)
XLA Modules:
  0.0 59.2 jit_solution(7330888155408551673)
XLA Ops:
  0.6 0.0 copy-start
  0.6 0.0 copy-start.3
  0.7 0.0 copy-start.1
  0.7 1.3 %tails.1 = bf16[3,2,8192]{2,1,0:T(2,128)(2,1)S(1)} custom-call(bf16[128,8192]{1,0:T(8,128)(2,1)} %query_ref.3, bf16[128,8192]{1,0:T(8,128)(2,1)} %key_ref.3, bf16[128,8192]{1,0:T(8,128)(2,1)} %value_ref.3), custom_call_target="tpu_custom_call" | custom-call | tf_op jit(solution)/shard_map/tails/pallas_call | solution.py:482
  1.9 3.7 %collective-permute-start = (bf16[3,2,8192]{2,1,0:T(2,128)(2,1)S(1)}, bf16[3,2,8192]{2,1,0:T(2,128)(2,1)S(1)}, u32[]{:S(2)}, u32[]{:S(2)}) collective-permute-start(bf16[3,2,8192]{2,1,0:T(2,128)(2,1)S(1)} %tails.1), channel_id=1, source_target_pairs={{0,1},{1,2},{2,3},{3,4},{4,5},{5,6},{6,7},{7,8},{8,9},{9,10},{10,1... | collective-permute-start | bytes 294920 | tf_op jit(solution)/shard_map/ppermute | solution.py:23
  5.6 0.0 copy-done
  5.6 0.0 copy-done.3
  5.6 0.3 sqrt_multiply_fusion.weight_ref
  6.0 0.0 copy-done.1
  6.0 3.4 %query_part.1.short_ref = f32[128,8192]{1,0:T(8,128)S(1)} custom-call(s32[1]{0:T(128)} %bitcast.base_ref, s32[16]{0:T(128)} %len_ref.15, bf16[128,8192]{1,0:T(8,128)(2,1)} %query_ref.3, f32[3,3,8192]{2,1,0:T(4,128)S(1)} %copy-done.1), custom_call_target="tpu_custom_call" | custom-call | flops 13107200 | bytes 6291456 | tf_op jit(solution)/shard_map/query_part/pallas_call | solution.py:492
  9.4 0.0 collective-permute-done.rim_ref
  9.4 13.1 %block_states.1 = (bf16[128,8192]{1,0:T(8,128)(2,1)S(1)}, f32[128,8192]{1,0:T(8,128)S(1)}, f32[16,4096]{1,0:T(8,128)S(1)}, f32[16,4096]{1,0:T(8,128)S(1)}) custom-call(s32[1]{0:T(128)} %bitcast.base_ref, s32[16]{0:T(128)} %len_ref.15, bf16[128,8192]{1,0:T(8,128)(2,1)} %key_ref.3, bf16[128,8192]{1,0:T(8,128)(2,1)} %value_ref.3, ...), custom_call_target="tpu_custom_call" | custom-call | flops 65536000 | bytes 12582912 | tf_op jit(solution)/shard_map/block_states/pallas_call | solution.py:509
  22.5 1.0 %collective-permute-start.1 = (f32[16,4096]{1,0:T(8,128)S(1)}, f32[16,4096]{1,0:T(8,128)S(1)}, u32[]{:S(2)}, u32[]{:S(2)}) collective-permute-start(f32[16,4096]{1,0:T(8,128)S(1)} %get-tuple-element.18), channel_id=1, source_target_pairs={{0,1},{1,0},{2,3},{3,2},{4,5},{5,4},{6,7},{7,6},{8,9},{9,8},{10,11... | collective-permute-start | bytes 786440 | tf_op jit(solution)/shard_map/ppermute | solution.py:27
  23.5 1.2 %collective-permute-done.1.got_ref = f32[16,4096]{1,0:T(8,128)S(1)} collective-permute-done((f32[16,4096]{1,0:T(8,128)S(1)}, f32[16,4096]{1,0:T(8,128)S(1)}, u32[]{:S(2)}, u32[]{:S(2)}) %collective-permute-start.1) | collective-permute-done | bytes 262176 | tf_op jit(solution)/shard_map/ppermute | solution.py:27
  24.6 0.8 %pair_ends.1 = bf16[16,4096]{1,0:T(8,128)(2,1)S(1)} custom-call(s32[1]{0:T(128)} %bitcast.base_ref, s32[16]{0:T(128)} %len_ref.15, f32[16,4096]{1,0:T(8,128)S(1)} %get-tuple-element.17.own_ref, f32[16,4096]{1,0:T(8,128)S(1)} %collective-permute-done.1.got_ref, f32[16,8192]{1,0:T(8,128)S(1)} %copy-done), custom_call_target="tpu_custom_call" | custom-call | tf_op jit(solution)/shard_map/pair_ends/pallas_call | solution.py:556
  25.4 2.6 %collective-permute-start.3 = (bf16[16,4096]{1,0:T(8,128)(2,1)S(1)}, bf16[16,4096]{1,0:T(8,128)(2,1)S(1)}, u32[]{:S(2)}, u32[]{:S(2)}) collective-permute-start(bf16[16,4096]{1,0:T(8,128)(2,1)S(1)} %pair_ends.1), channel_id=1, source_target_pairs={{0,4},{1,5},{2,6},{3,7},{4,8},{5,9},{6,10},{7,11},{8,12},{9,13},{1... | collective-permute-start | bytes 393224 | tf_op jit(solution)/shard_map/ppermute | solution.py:23
  28.0 3.1 %collective-permute-start.2 = (bf16[16,4096]{1,0:T(8,128)(2,1)S(1)}, bf16[16,4096]{1,0:T(8,128)(2,1)S(1)}, u32[]{:S(2)}, u32[]{:S(2)}) collective-permute-start(bf16[16,4096]{1,0:T(8,128)(2,1)S(1)} %pair_ends.1), channel_id=1, source_target_pairs={{0,2},{1,3},{2,4},{3,5},{4,6},{5,7},{6,8},{7,9},{8,10},{9,11},{10,... | collective-permute-start | bytes 393224 | tf_op jit(solution)/shard_map/ppermute | solution.py:23
  31.2 3.3 %near_part_0.1.refs_0_ = f32[128,8192]{1,0:T(8,128)S(1)} custom-call(s32[1]{0:T(128)} %bitcast.base_ref, s32[16]{0:T(128)} %len_ref.15, bf16[128,8192]{1,0:T(8,128)(2,1)S(1)} %get-tuple-element.19.gate_ref, f32[16,8192]{1,0:T(8,128)S(1)} %copy-done, f32[16,8192]{1,0:T(8,128)S(1)} %sqrt_multiply_fusion.weight_ref), custom_call_target="tpu_custom_call" | custom-call | flops 19660800 | bytes 3670016 | tf_op jit(solution)/shard_map/near_part_0/pallas_call | solution.py:538
  34.5 0.0 collective-permute-done.3.far_ref
  34.5 1.9 %collective-permute-done.2.near_ref = bf16[16,4096]{1,0:T(8,128)(2,1)S(1)} collective-permute-done((bf16[16,4096]{1,0:T(8,128)(2,1)S(1)}, bf16[16,4096]{1,0:T(8,128)(2,1)S(1)}, u32[]{:S(2)}, u32[]{:S(2)}) %collective-permute-start.2) | collective-permute-done | bytes 131104 | tf_op jit(solution)/shard_map/ppermute | solution.py:23
  36.4 0.8 %reach_2.1.near_ref = bf16[16,4096]{1,0:T(8,128)(2,1)S(1)} custom-call(s32[1]{0:T(128)} %bitcast.base_ref, s32[16]{0:T(128)} %len_ref.15, bf16[16,4096]{1,0:T(8,128)(2,1)S(1)} %collective-permute-done.2.near_ref, bf16[16,4096]{1,0:T(8,128)(2,1)S(1)} %collective-permute-done.3.far_ref, f32[16,8192]{1,0:T(8,128)S(1)} %copy-done), custom_call_target="tpu_custom_call" | custom-call | tf_op jit(solution)/shard_map/reach_2/pallas_call | solution.py:556
  37.1 0.0 copy-start.2
  37.1 2.5 %collective-permute-start.4 = (bf16[16,4096]{1,0:T(8,128)(2,1)S(1)}, bf16[16,4096]{1,0:T(8,128)(2,1)S(1)}, u32[]{:S(2)}, u32[]{:S(2)}) collective-permute-start(bf16[16,4096]{1,0:T(8,128)(2,1)S(1)} %reach_2.1.near_ref), channel_id=1, source_target_pairs={{0,4},{1,5},{2,6},{3,7},{4,8},{5,9},{6,10},{7,11},{8,12},{9,13},{1... | collective-permute-start | bytes 393224 | tf_op jit(solution)/shard_map/ppermute | solution.py:23
  39.7 3.3 %near_part_1.1.near_ref = f32[128,8192]{1,0:T(8,128)S(1)} custom-call(s32[1]{0:T(128)} %bitcast.base_ref, s32[16]{0:T(128)} %len_ref.15, bf16[128,8192]{1,0:T(8,128)(2,1)S(1)} %get-tuple-element.19.gate_ref, f32[16,8192]{1,0:T(8,128)S(1)} %copy-done, f32[16,8192]{1,0:T(8,128)S(1)} %sqrt_multiply_fusion.weight_ref, ...), custom_call_target="tpu_custom_call", output_to_operand_aliasing={{}: (5, {})} | custom-call | flops 19660800 | bytes 3670016 | tf_op jit(solution)/shard_map/near_part_1/pallas_call | solution.py:538
  43.0 0.7 %collective-permute-done.4.far_ref = bf16[16,4096]{1,0:T(8,128)(2,1)S(1)} collective-permute-done((bf16[16,4096]{1,0:T(8,128)(2,1)S(1)}, bf16[16,4096]{1,0:T(8,128)(2,1)S(1)}, u32[]{:S(2)}, u32[]{:S(2)}) %collective-permute-start.4) | collective-permute-done | bytes 131104 | tf_op jit(solution)/shard_map/ppermute | solution.py:23
  43.7 0.9 %pair_enter.1 = (f32[16,4096]{1,0:T(8,128)S(1)}, f32[16,4096]{1,0:T(8,128)S(1)}) custom-call(s32[1]{0:T(128)} %bitcast.base_ref, s32[16]{0:T(128)} %len_ref.15, bf16[16,4096]{1,0:T(8,128)(2,1)S(1)} %reach_2.1.near_ref, bf16[16,4096]{1,0:T(8,128)(2,1)S(1)} %collective-permute-done.4.far_ref, f32[16,4096]{1,0:T(8,128)S(1)} %get-tuple-element.17.own_ref, ...), custom_call_target="tpu_custom_call" | custom-call | tf_op jit(solution)/shard_map/pair_enter/pallas_call | solution.py:556
  44.6 2.5 %collective-permute-start.5 = (f32[16,4096]{1,0:T(8,128)S(1)}, f32[16,4096]{1,0:T(8,128)S(1)}, u32[]{:S(2)}, u32[]{:S(2)}) collective-permute-start(f32[16,4096]{1,0:T(8,128)S(1)} %get-tuple-element.25), channel_id=1, source_target_pairs={{0,1},{1,0},{2,3},{3,2},{4,5},{5,4},{6,7},{7,6},{8,9},{9,8},{10,11... | collective-permute-start | bytes 786440 | tf_op jit(solution)/shard_map/ppermute | solution.py:27
  47.1 1.2 %collective-permute-done.5.got_ref = f32[16,4096]{1,0:T(8,128)S(1)} collective-permute-done((f32[16,4096]{1,0:T(8,128)S(1)}, f32[16,4096]{1,0:T(8,128)S(1)}, u32[]{:S(2)}, u32[]{:S(2)}) %collective-permute-start.5) | collective-permute-done | bytes 262176 | tf_op jit(solution)/shard_map/ppermute | solution.py:27
  48.3 0.0 copy-done.2
  48.3 10.9 %far_part.1 = (bf16[128,8192]{1,0:T(8,128)(2,1)}, bf16[128,8192]{1,0:T(8,128)(2,1)}) custom-call(s32[1]{0:T(128)} %bitcast.base_ref, s32[16]{0:T(128)} %len_ref.15, f32[128,8192]{1,0:T(8,128)S(1)} %get-tuple-element.16.state_ref, f32[16,4096]{1,0:T(8,128)S(1)} %get-tuple-element.24.mine_ref, f32[16,4096]{1,0:T(8,128)S(1)} %collective-permute-done.5.got_ref, ...), custom_call_target="tpu_custom_call" | custom-call | flops 58982400 | bytes 18874368 | tf_op jit(solution)/shard_map/far_part/pallas_call | solution.py:605
Async XLA Ops:
  0.6 5.0 %copy-start = (f32[16,8192]{1,0:T(8,128)S(1)}, f32[16,8192]{1,0:T(8,128)}, u32[]{:S(2)}) copy-start(f32[16,8192]{1,0:T(8,128)} %rate_ref.13) | copy-start | bytes 1572868
  0.6 5.0 %copy-start.3 = (f32[16,8192]{1,0:T(8,128)S(1)}, f32[16,8192]{1,0:T(8,128)}, u32[]{:S(2)}) copy-start(f32[16,8192]{1,0:T(8,128)} %param.14) | copy-start | bytes 1572868
  0.7 5.3 %copy-start.1 = (f32[3,3,8192]{2,1,0:T(4,128)S(1)}, f32[3,3,8192]{2,1,0:T(4,128)}, u32[]{:S(2)}) copy-start(f32[3,3,8192]{2,1,0:T(4,128)} %taps_ref.5) | copy-start | bytes 884740
  1.9 7.5 %collective-permute-start = (bf16[3,2,8192]{2,1,0:T(2,128)(2,1)S(1)}, bf16[3,2,8192]{2,1,0:T(2,128)(2,1)S(1)}, u32[]{:S(2)}, u32[]{:S(2)}) collective-permute-start(bf16[3,2,8192]{2,1,0:T(2,128)(2,1)S(1)} %tails.1), channel_id=1, source_target_pairs={{0,1},{1,2},{2,3},{3,4},{4,5},{5,6},{6,7},{7,8},{8,9},{9,10},{10,1... | collective-permute-start | bytes 294920 | tf_op jit(solution)/shard_map/ppermute | solution.py:23
  22.5 2.1 %collective-permute-start.1 = (f32[16,4096]{1,0:T(8,128)S(1)}, f32[16,4096]{1,0:T(8,128)S(1)}, u32[]{:S(2)}, u32[]{:S(2)}) collective-permute-start(f32[16,4096]{1,0:T(8,128)S(1)} %get-tuple-element.18), channel_id=1, source_target_pairs={{0,1},{1,0},{2,3},{3,2},{4,5},{5,4},{6,7},{7,6},{8,9},{9,8},{10,11... | collective-permute-start | bytes 786440 | tf_op jit(solution)/shard_map/ppermute | solution.py:27
  25.4 9.1 %collective-permute-start.3 = (bf16[16,4096]{1,0:T(8,128)(2,1)S(1)}, bf16[16,4096]{1,0:T(8,128)(2,1)S(1)}, u32[]{:S(2)}, u32[]{:S(2)}) collective-permute-start(bf16[16,4096]{1,0:T(8,128)(2,1)S(1)} %pair_ends.1), channel_id=1, source_target_pairs={{0,4},{1,5},{2,6},{3,7},{4,8},{5,9},{6,10},{7,11},{8,12},{9,13},{1... | collective-permute-start | bytes 393224 | tf_op jit(solution)/shard_map/ppermute | solution.py:23
  28.0 8.3 %collective-permute-start.2 = (bf16[16,4096]{1,0:T(8,128)(2,1)S(1)}, bf16[16,4096]{1,0:T(8,128)(2,1)S(1)}, u32[]{:S(2)}, u32[]{:S(2)}) collective-permute-start(bf16[16,4096]{1,0:T(8,128)(2,1)S(1)} %pair_ends.1), channel_id=1, source_target_pairs={{0,2},{1,3},{2,4},{3,5},{4,6},{5,7},{6,8},{7,9},{8,10},{9,11},{10,... | collective-permute-start | bytes 393224 | tf_op jit(solution)/shard_map/ppermute | solution.py:23
  37.1 11.1 %copy-start.2 = (f32[8192]{0:T(1024)S(1)}, f32[8192]{0:T(1024)}, u32[]{:S(2)}) copy-start(f32[8192]{0:T(1024)} %param.17) | copy-start | bytes 98308
  37.1 6.6 %collective-permute-start.4 = (bf16[16,4096]{1,0:T(8,128)(2,1)S(1)}, bf16[16,4096]{1,0:T(8,128)(2,1)S(1)}, u32[]{:S(2)}, u32[]{:S(2)}) collective-permute-start(bf16[16,4096]{1,0:T(8,128)(2,1)S(1)} %reach_2.1.near_ref), channel_id=1, source_target_pairs={{0,4},{1,5},{2,6},{3,7},{4,8},{5,9},{6,10},{7,11},{8,12},{9,13},{1... | collective-permute-start | bytes 393224 | tf_op jit(solution)/shard_map/ppermute | solution.py:23
  44.6 3.6 %collective-permute-start.5 = (f32[16,4096]{1,0:T(8,128)S(1)}, f32[16,4096]{1,0:T(8,128)S(1)}, u32[]{:S(2)}, u32[]{:S(2)}) collective-permute-start(f32[16,4096]{1,0:T(8,128)S(1)} %get-tuple-element.25), channel_id=1, source_target_pairs={{0,1},{1,0},{2,3},{3,2},{4,5},{5,4},{6,7},{7,6},{8,9},{9,8},{10,11... | collective-permute-start | bytes 786440 | tf_op jit(solution)/shard_map/ppermute | solution.py:27

commit v10 on v9

--- a/solution.py
+++ b/solution.py
@@ -80,7 +80,7 @@
 
 
 def row_of(ref, index):
-    return jnp.broadcast_to(ref[pl.ds(index, 1), :], (SUBS, LANES))
+    return ref[pl.ds(index, SUBS, stride=0), :]
 
 
 def spread(x, wide, span):
@@ -107,6 +107,20 @@
         return self.taps[0] * here + (self.taps[1] * one) * keep_one + (self.taps[2] * two) * keep_two
 
 
+def sub_passes(base_ref, len_ref, passes, span):
+    for b in range(SUBS):
+        passes[b] = jnp.float32(1.0)
+    start = jnp.int32(0)
+    for d in range(len_ref.shape[0]):
+        at = start - base_ref[0]
+
+        @pl.when((at >= 0) & (at < SUBS * span))
+        def _():
+            passes[lax.div(at, jnp.int32(span))] = jnp.float32(0.0)
+
+        start = start + len_ref[d]
+
+
 def half_of(base_ref, rows, chans, lane):
     half = chans // 2
     which = lax.div(lane, half)
@@ -114,10 +128,14 @@
     return mine, pl.multiple_of(lane - which * half, LANES)
 
 
+def sub_state(state_ref, lane, b, modes):
+    return state_ref[lax.div(lane, LANES), pl.ds(b * (modes + 1), modes), :]
+
+
 def state_kernel(
-    base_ref, len_ref, key_ref, value_ref, rim_ref, taps_ref, rate_ref, weight_ref,
+    base_ref, len_ref, key_ref, value_ref, rim_ref, taps_ref, rate_ref,
     gate_ref, state_ref, own_ref, give_ref,
-    key_buf, value_buf, sems, masks, wide_k, wide_v, tables, ends, held,
+    key_buf, value_buf, sems, masks, passes, wide_k, wide_v, tables, held,
     *, span, modes, most, chunk,
 ):
     chans = key_buf.shape[1]
@@ -135,15 +153,7 @@
             masks[0, j] = flag(starts[j] < rows + j)
             masks[1, j] = flag(starts[j] < rows + (j - 1))
             masks[2, j] = flag(starts[span - 1] <= rows + j)
-        sub = lax.broadcasted_iota(jnp.int32, (SUBS, LANES), 0)
-        through = flag(starts[span - 1] < rows)
-        one = through * flag(sub >= 1)
-        two = one * pltpu.roll(one, 1, 0) * flag(sub >= 2)
-        four = two * pltpu.roll(two, 2, 0) * flag(sub >= 4)
-        masks[3, 0] = one
-        masks[3, 1] = two
-        masks[3, 2] = four
-        masks[3, 3] = flag(sub >= 1)
+        sub_passes(base_ref, len_ref, passes, span)
 
     prepare()
 
@@ -152,9 +162,7 @@
             spread(key_buf[:, cols_of(lane)], wide_k.at[slot], span)
             spread(value_buf[:, cols_of(lane)], wide_v.at[slot], span)
             rate = rate_ref[:, cols_of(lane)]
-            for m, by in enumerate((1, span, 2 * span, 4 * span)):
-                tables[slot, m] = jnp.exp(-float(by) * rate)
-            tables[slot, 4] = weight_ref[:, cols_of(lane)]
+            tables[slot] = jnp.exp(-rate)
         convs = [
             [
                 Conv(wide.at[slot], rim_ref[i, :, cols_of(lane)], taps_ref[i, :, cols_of(lane)], span)
@@ -175,38 +183,28 @@
                 pair = pair.astype(f32)
                 held[slot, j - 1] = pair[:SUBS] * masks[2, j - 1]
                 held[slot, j] = pair[SUBS:] * masks[2, j]
-        states = []
         for slot, lane in enumerate(lanes):
-            decay = [row_of(tables.at[slot, 0], n) for n in range(modes)]
+            decay = [row_of(tables.at[slot], n) for n in range(modes)]
             state = [held[slot, 0]] * modes
             for j in range(1, span):
                 gate = held[slot, j]
                 state = [decay[n] * state[n] + gate for n in range(modes)]
-            states.append(state)
-        for m, shift in enumerate((1, 2, 4)):
-            joined = masks[3, m] > 0.0
-            for slot in range(len(lanes)):
-                states[slot] = [
-                    x + jnp.where(joined, row_of(tables.at[slot, m + 1], n) * pltpu.roll(x, shift, 0), 0.0)
-                    for n, x in enumerate(states[slot])
-                ]
-        inner = masks[3, 3] > 0.0
+            for n in range(modes):
+                state_ref[lax.div(lane, LANES), pl.ds(n, SUBS, stride=modes + 1), :] = state[n]
         for slot, lane in enumerate(lanes):
-            for n, x in enumerate(states[slot]):
-                ends[slot, pl.ds(n, 1), :] = x[SUBS - 1 :]
-                state_ref[pl.ds(n * SUBS, SUBS), cols_of(lane)] = jnp.where(
-                    inner, row_of(tables.at[slot, 4], n) * pltpu.roll(x, 1, 0), 0.0
-                )
-        for slot, lane in enumerate(lanes):
+            leap = jnp.exp(-float(span) * rate_ref[:, cols_of(lane)])
+            end = sub_state(state_ref, lane, 0, modes)
+            for b in range(1, SUBS):
+                end = (leap * passes[b]) * end + sub_state(state_ref, lane, b, modes)
             mine, here = half_of(base_ref, key_ref.shape[0], chans, lane)
 
             @pl.when(mine)
             def _():
-                own_ref[:, cols_of(here)] = ends[slot]
+                own_ref[:, cols_of(here)] = end
 
             @pl.when(jnp.logical_not(mine))
             def _():
-                give_ref[:, cols_of(here)] = ends[slot]
+                give_ref[:, cols_of(here)] = end
 
     def before(c):
         for copy in fetches(c):
@@ -236,24 +234,28 @@
 
 
 def near_kernel(base_ref, len_ref, gate_ref, rate_ref, weight_ref, *refs, span, modes, most, first, count):
-    near_ref, masks = refs[-2:]
+    near_ref, masks, sums, tap_rows = refs[-4:]
     keep_masks(base_ref, len_ref, masks, span)
 
     def group(lanes):
-        taps = []
-        for lane in lanes:
+        for slot, lane in enumerate(lanes):
             decay = jnp.exp(-rate_ref[:, cols_of(lane)])
             term = weight_ref[:, cols_of(lane)]
-            parts = []
             for lag in range(span):
                 part = term[:SUBS]
                 for n in range(SUBS, modes, SUBS):
                     part = part + term[n : n + SUBS]
-                parts.append(part)
+                sums[slot, pl.ds(lag * (SUBS + 1), SUBS), :] = part
                 term = term * decay
-            taps.append(parts)
-        for shift in (1, 2, 4):
-            taps = [[part + pltpu.roll(part, shift, 0) for part in parts] for parts in taps]
+        for slot in range(len(lanes)):
+            for first_lag in range(0, span, SUBS):
+                total = [
+                    sums[slot, pl.ds(first_lag * (SUBS + 1) + m, SUBS, stride=SUBS + 1), :] for m in range(SUBS)
+                ]
+                while len(total) > 1:
+                    total = [total[m] + total[m + 1] for m in range(0, len(total), 2)]
+                tap_rows[slot, pl.ds(first_lag, SUBS), :] = total[0]
+        taps = [[row_of(tap_rows.at[slot], lag) for lag in range(span)] for slot in range(len(lanes))]
         for parts, lane in zip(taps, lanes):
             live = []
             for j in range(span):
@@ -346,9 +348,9 @@
     span, modes, channels, most, chunk,
 ):
     if channels:
-        hidden_out, normed_out, resid_ref, hidden_ref, sems, masks, wide, tables, sums, whole, normed_ref = refs
+        hidden_out, normed_out, resid_ref, hidden_ref, sems, masks, passes, wide, tables, starts_at, sums, whole, normed_ref = refs
     else:
-        hidden_out, wide_ref, sum_ref, resid_ref, hidden_ref, sems, masks, wide, tables, sums = refs
+        hidden_out, wide_ref, sum_ref, resid_ref, hidden_ref, sems, masks, passes, wide, tables, starts_at, sums = refs
     chans = resid_ref.shape[1]
 
     def fetch(c):
@@ -365,7 +367,7 @@
     rows, starts = doc_start_rows(len_ref, base_ref[0], span)
     for j in range(span):
         masks[0, j] = flag(starts[j] < rows)
-    masks[1, 0] = flag(starts[0] < base_ref[0])
+    sub_passes(base_ref, len_ref, passes, span)
     top = flag(lax.broadcasted_iota(jnp.int32, (SUBS, LANES), 0) == 0)
     masks[1, 1] = top * flag(starts[0] < rows)
     masks[1, 2] = top * flag(starts[0] < rows - 1)
@@ -373,27 +375,21 @@
     sums[...] = jnp.zeros(sums.shape, f32)
 
     def group(lanes):
-        sub = lax.broadcasted_iota(jnp.int32, (SUBS, LANES), 0).astype(f32) * (-float(span))
-        through = masks[1, 0]
         for slot, lane in enumerate(lanes):
             mine, here = half_of(base_ref, resid_ref.shape[0], chans, lane)
             mine = jnp.full((modes, LANES), mine.astype(jnp.int32), jnp.int32) == 1
-            enter = jnp.where(mine, mine_ref[:, cols_of(here)], got_ref[:, cols_of(here)])
+            state = jnp.where(mine, mine_ref[:, cols_of(here)], got_ref[:, cols_of(here)])
             rate = rate_ref[:, cols_of(lane)]
-            tables[slot, 0] = jnp.exp(-rate)
-            tables[slot, 1] = weight_ref[:, cols_of(lane)] * enter
-            tables[slot, 2] = rate
-        parts = [
-            [
-                state_ref[pl.ds(n * SUBS, SUBS), cols_of(lane)]
-                + (row_of(tables.at[slot, 1], n) * through) * jnp.exp(row_of(tables.at[slot, 2], n) * sub)
-                for n in range(modes)
-            ]
-            for slot, lane in enumerate(lanes)
-        ]
+            weight = weight_ref[:, cols_of(lane)]
+            tables[slot] = jnp.exp(-rate)
+            leap = jnp.exp(-float(span) * rate)
+            for b in range(SUBS):
+                starts_at[slot, pl.ds(b * (modes + 1), modes), :] = weight * state
+                if b < SUBS - 1:
+                    state = (leap * passes[b]) * state + sub_state(state_ref, lane, b, modes)
         for slot, lane in enumerate(lanes):
-            part = parts[slot]
-            decay = [row_of(tables.at[slot, 0], n) for n in range(modes)]
+            part = [starts_at[slot, pl.ds(n, SUBS, stride=modes + 1), :] for n in range(modes)]
+            decay = [row_of(tables.at[slot], n) for n in range(modes)]
             rim = rim_ref[0, :, cols_of(lane)].astype(f32)
             tap = taps_ref[0, :, cols_of(lane)]
             edge = [
@@ -508,11 +504,11 @@
     rates, weights, taps, rims = near_by(decay_rate), near_by(weight), near_by(short_taps), near_by(rim_rows)
     gates, states, own, give = pl.pallas_call(
         functools.partial(state_kernel, span=span, modes=modes, most=A_TILES, chunk=chunk),
-        in_specs=[smem, smem, hbm, hbm, vmem, vmem, vmem, vmem],
+        in_specs=[smem, smem, hbm, hbm, vmem, vmem, vmem],
         out_specs=[vmem, vmem, vmem, vmem],
         out_shape=[
             pltpu.VMEM((tok_rows, chans), bf16),
-            pltpu.VMEM((modes * SUBS, chans), f32),
+            pltpu.VMEM((chans // LANES, SUBS * (modes + 1), LANES), f32),
             pltpu.VMEM(half.shape, f32),
             pltpu.VMEM(half.shape, f32),
         ],
@@ -520,17 +516,17 @@
             pltpu.VMEM((tok_rows, chans), bf16),
             pltpu.VMEM((tok_rows, chans), bf16),
             copies(2),
-            pltpu.VMEM((4, span) + tile_shape, f32),
+            pltpu.VMEM((3, span) + tile_shape, f32),
+            pltpu.SMEM((SUBS,), f32),
             pltpu.VMEM((A_TILES, wide_rows, LANES), f32),
             pltpu.VMEM((A_TILES, wide_rows, LANES), f32),
-            pltpu.VMEM((A_TILES, 5, modes, LANES), f32),
             pltpu.VMEM((A_TILES, modes, LANES), f32),
             pltpu.VMEM((A_TILES, span) + tile_shape, f32),
         ],
         compiler_params=params,
         cost_estimate=cost(1000, 12 * tok_rows * chans),
         name="block_states",
-    )(base, lengths, far_off(key_in), far_off(value_in), rims, taps, rates, weights)
+    )(base, lengths, far_off(key_in), far_off(value_in), rims, taps, rates)
 
     def near_piece(part, near):
         count = chans // NEAR_PARTS
@@ -542,7 +538,11 @@
             in_specs=[smem, smem, vmem, vmem, vmem] + [vmem] * len(before),
             out_specs=vmem,
             out_shape=pltpu.VMEM((tok_rows, chans), f32),
-            scratch_shapes=[pltpu.VMEM((2, span) + tile_shape, f32)],
+            scratch_shapes=[
+                pltpu.VMEM((2, span) + tile_shape, f32),
+                pltpu.VMEM((N_TILES, span * (SUBS + 1), LANES), f32),
+                pltpu.VMEM((N_TILES, span, LANES), f32),
+            ],
             compiler_params=params,
             input_output_aliases={5: 0} if before else {},
             cost_estimate=cost(600 // NEAR_PARTS, 7 * tok_rows * count),
@@ -591,8 +591,10 @@
         pltpu.VMEM((tok_rows, chans), bf16),
         copies(3),
         pltpu.VMEM((2, span) + tile_shape, f32),
+        pltpu.SMEM((SUBS,), f32),
         pltpu.VMEM((F_TILES, wide_rows, LANES), f32),
-        pltpu.VMEM((F_TILES, 3, modes, LANES), f32),
+        pltpu.VMEM((F_TILES, modes, LANES), f32),
+        pltpu.VMEM((F_TILES, SUBS * (modes + 1), LANES), f32),
         pltpu.VMEM((tok_rows, LANES), f32),
     ]
     if alone:

time: 59.6 us -> 57.7 us (0.968)
  Pallas kernels: 37.7 us -> 35.7 us
    pallas_call x1, Pallas kernels: 13.1 us -> 12.1 us  [shards(): pl.pallas_call(functools.partial(state_kernel, span=span, modes=modes, mo...]
where the time goes in v10:
time: 57.7 us; the launch traced here: 57.3 us
  Pallas kernels  35.7 us (62%)
  starting transfers between devices  15.5 us (27%)
  waiting for transfers between devices  5.02 us (9%)
  between operations  0.8 us (1%)
    pallas_call x1, Pallas kernels, shards(): pl.pallas_call(functools.partial(state_kernel, span=span, modes=modes, mo...  12.1 us
    ppermute x4, starting transfers between devices, from_behind(): return lax.ppermute(shard, axis, pairs)  11.9 us
    pallas_call x1, Pallas kernels, shards(): pl.pallas_call(functools.partial(final_kernel, span=span, modes=modes, ch...  10.3 us
    pallas_call x2, Pallas kernels, near_piece(): pl.pallas_call(functools.partial(near_kernel, span=span, modes=modes, mos...  6.18 us
    pallas_call x1, Pallas kernels, shards(): pl.pallas_call(functools.partial(query_kernel, span=span, most=Q_TILES, c...  3.56 us
    ppermute x2, starting transfers between devices, swap(): lax.ppermute(shard, axis, [(i, i ^ 1) for i in range(lax.axis_size(axis))])  3.51 us
    ppermute x4, waiting for transfers between devices, from_behind(): return lax.ppermute(shard, axis, pairs)  2.7 us
    pallas_call x3, Pallas kernels, pair_call(): pl.pallas_call(functools.partial(kernel, rows=tok_rows, **static), in_spe...  2.36 us
  transfers between devices with their start and end apart: 6, of which 4 were waited for; matrix products, arithmetic and copies ran while one was open for 1% of the time, Pallas kernels for 17%

profile of v10, /device:TPU:9, one launch (start us, length us, event | category | flops | bytes accessed | tf_op | source)
XLA Modules:
  0.0 57.3 jit_solution(18428656530126555197)
XLA Ops:
  0.6 0.0 copy-start.1
  0.6 1.2 %tails.1 = bf16[3,2,8192]{2,1,0:T(2,128)(2,1)S(1)} custom-call(bf16[128,8192]{1,0:T(8,128)(2,1)} %query_ref.3, bf16[128,8192]{1,0:T(8,128)(2,1)} %key_ref.3, bf16[128,8192]{1,0:T(8,128)(2,1)} %value_ref.3), custom_call_target="tpu_custom_call" | custom-call | tf_op jit(solution)/shard_map/tails/pallas_call | solution.py:478
  1.8 3.7 %collective-permute-start = (bf16[3,2,8192]{2,1,0:T(2,128)(2,1)S(1)}, bf16[3,2,8192]{2,1,0:T(2,128)(2,1)S(1)}, u32[]{:S(2)}, u32[]{:S(2)}) collective-permute-start(bf16[3,2,8192]{2,1,0:T(2,128)(2,1)S(1)} %tails.1), channel_id=1, source_target_pairs={{0,1},{1,2},{2,3},{3,4},{4,5},{5,6},{6,7},{7,8},{8,9},{9,10},{10,1... | collective-permute-start | bytes 294920 | tf_op jit(solution)/shard_map/ppermute | solution.py:23
  5.5 0.0 copy-done.1
  5.5 0.0 copy-start
  5.6 3.6 %query_part.1.short_ref = f32[128,8192]{1,0:T(8,128)S(1)} custom-call(s32[1]{0:T(128)} %bitcast.base_ref, s32[16]{0:T(128)} %len_ref.15, bf16[128,8192]{1,0:T(8,128)(2,1)} %query_ref.3, f32[3,3,8192]{2,1,0:T(4,128)S(1)} %copy-done.1), custom_call_target="tpu_custom_call" | custom-call | flops 13107200 | bytes 6291456 | tf_op jit(solution)/shard_map/query_part/pallas_call | solution.py:488
  9.1 0.0 copy-start.3
  9.1 0.0 collective-permute-done.rim_ref
  9.2 0.0 copy-done
  9.2 12.1 %block_states.1 = (bf16[128,8192]{1,0:T(8,128)(2,1)S(1)}, f32[64,136,128]{2,1,0:T(8,128)S(1)}, f32[16,4096]{1,0:T(8,128)S(1)}, f32[16,4096]{1,0:T(8,128)S(1)}) custom-call(s32[1]{0:T(128)} %bitcast.base_ref, s32[16]{0:T(128)} %len_ref.15, bf16[128,8192]{1,0:T(8,128)(2,1)} %key_ref.3, bf16[128,8192]{1,0:T(8,128)(2,1)} %value_ref.3, ...), custom_call_target="tpu_custom_call" | custom-call | flops 65536000 | bytes 12582912 | tf_op jit(solution)/shard_map/block_states/pallas_call | solution.py:505
  21.2 1.0 %collective-permute-start.1 = (f32[16,4096]{1,0:T(8,128)S(1)}, f32[16,4096]{1,0:T(8,128)S(1)}, u32[]{:S(2)}, u32[]{:S(2)}) collective-permute-start(f32[16,4096]{1,0:T(8,128)S(1)} %get-tuple-element.18), channel_id=1, source_target_pairs={{0,1},{1,0},{2,3},{3,2},{4,5},{5,4},{6,7},{7,6},{8,9},{9,8},{10,11... | collective-permute-start | bytes 786440 | tf_op jit(solution)/shard_map/ppermute | solution.py:27
  22.2 1.2 %collective-permute-done.1.got_ref = f32[16,4096]{1,0:T(8,128)S(1)} collective-permute-done((f32[16,4096]{1,0:T(8,128)S(1)}, f32[16,4096]{1,0:T(8,128)S(1)}, u32[]{:S(2)}, u32[]{:S(2)}) %collective-permute-start.1) | collective-permute-done | bytes 262176 | tf_op jit(solution)/shard_map/ppermute | solution.py:27
  23.4 0.8 %pair_ends.1 = bf16[16,4096]{1,0:T(8,128)(2,1)S(1)} custom-call(s32[1]{0:T(128)} %bitcast.base_ref, s32[16]{0:T(128)} %len_ref.15, f32[16,4096]{1,0:T(8,128)S(1)} %get-tuple-element.17.own_ref, f32[16,4096]{1,0:T(8,128)S(1)} %collective-permute-done.1.got_ref, f32[16,8192]{1,0:T(8,128)S(1)} %copy-done), custom_call_target="tpu_custom_call" | custom-call | tf_op jit(solution)/shard_map/pair_ends/pallas_call | solution.py:556
  24.2 2.6 %collective-permute-start.3 = (bf16[16,4096]{1,0:T(8,128)(2,1)S(1)}, bf16[16,4096]{1,0:T(8,128)(2,1)S(1)}, u32[]{:S(2)}, u32[]{:S(2)}) collective-permute-start(bf16[16,4096]{1,0:T(8,128)(2,1)S(1)} %pair_ends.1), channel_id=1, source_target_pairs={{0,4},{1,5},{2,6},{3,7},{4,8},{5,9},{6,10},{7,11},{8,12},{9,13},{1... | collective-permute-start | bytes 393224 | tf_op jit(solution)/shard_map/ppermute | solution.py:23
  26.7 3.1 %collective-permute-start.2 = (bf16[16,4096]{1,0:T(8,128)(2,1)S(1)}, bf16[16,4096]{1,0:T(8,128)(2,1)S(1)}, u32[]{:S(2)}, u32[]{:S(2)}) collective-permute-start(bf16[16,4096]{1,0:T(8,128)(2,1)S(1)} %pair_ends.1), channel_id=1, source_target_pairs={{0,2},{1,3},{2,4},{3,5},{4,6},{5,7},{6,8},{7,9},{8,10},{9,11},{10,... | collective-permute-start | bytes 393224 | tf_op jit(solution)/shard_map/ppermute | solution.py:23
  29.9 0.0 copy-done.3
  29.9 0.3 sqrt_multiply_fusion.weight_ref
  30.2 3.1 %near_part_0.1.refs_0_ = f32[128,8192]{1,0:T(8,128)S(1)} custom-call(s32[1]{0:T(128)} %bitcast.base_ref, s32[16]{0:T(128)} %len_ref.15, bf16[128,8192]{1,0:T(8,128)(2,1)S(1)} %get-tuple-element.19.gate_ref, f32[16,8192]{1,0:T(8,128)S(1)} %copy-done, f32[16,8192]{1,0:T(8,128)S(1)} %sqrt_multiply_fusion.weight_ref), custom_call_target="tpu_custom_call" | custom-call | flops 19660800 | bytes 3670016 | tf_op jit(solution)/shard_map/near_part_0/pallas_call | solution.py:534
  33.3 0.0 collective-permute-done.3.far_ref
  33.3 1.8 %collective-permute-done.2.near_ref = bf16[16,4096]{1,0:T(8,128)(2,1)S(1)} collective-permute-done((bf16[16,4096]{1,0:T(8,128)(2,1)S(1)}, bf16[16,4096]{1,0:T(8,128)(2,1)S(1)}, u32[]{:S(2)}, u32[]{:S(2)}) %collective-permute-start.2) | collective-permute-done | bytes 131104 | tf_op jit(solution)/shard_map/ppermute | solution.py:23
  35.1 0.8 %reach_2.1.near_ref = bf16[16,4096]{1,0:T(8,128)(2,1)S(1)} custom-call(s32[1]{0:T(128)} %bitcast.base_ref, s32[16]{0:T(128)} %len_ref.15, bf16[16,4096]{1,0:T(8,128)(2,1)S(1)} %collective-permute-done.2.near_ref, bf16[16,4096]{1,0:T(8,128)(2,1)S(1)} %collective-permute-done.3.far_ref, f32[16,8192]{1,0:T(8,128)S(1)} %copy-done), custom_call_target="tpu_custom_call" | custom-call | tf_op jit(solution)/shard_map/reach_2/pallas_call | solution.py:556
  35.8 0.0 copy-start.2
  35.9 2.6 %collective-permute-start.4 = (bf16[16,4096]{1,0:T(8,128)(2,1)S(1)}, bf16[16,4096]{1,0:T(8,128)(2,1)S(1)}, u32[]{:S(2)}, u32[]{:S(2)}) collective-permute-start(bf16[16,4096]{1,0:T(8,128)(2,1)S(1)} %reach_2.1.near_ref), channel_id=1, source_target_pairs={{0,4},{1,5},{2,6},{3,7},{4,8},{5,9},{6,10},{7,11},{8,12},{9,13},{1... | collective-permute-start | bytes 393224 | tf_op jit(solution)/shard_map/ppermute | solution.py:23
  38.4 3.1 %near_part_1.1.near_ref = f32[128,8192]{1,0:T(8,128)S(1)} custom-call(s32[1]{0:T(128)} %bitcast.base_ref, s32[16]{0:T(128)} %len_ref.15, bf16[128,8192]{1,0:T(8,128)(2,1)S(1)} %get-tuple-element.19.gate_ref, f32[16,8192]{1,0:T(8,128)S(1)} %copy-done, f32[16,8192]{1,0:T(8,128)S(1)} %sqrt_multiply_fusion.weight_ref, ...), custom_call_target="tpu_custom_call", output_to_operand_aliasing={{}: (5, {})} | custom-call | flops 19660800 | bytes 3670016 | tf_op jit(solution)/shard_map/near_part_1/pallas_call | solution.py:534
  41.5 0.9 %collective-permute-done.4.far_ref = bf16[16,4096]{1,0:T(8,128)(2,1)S(1)} collective-permute-done((bf16[16,4096]{1,0:T(8,128)(2,1)S(1)}, bf16[16,4096]{1,0:T(8,128)(2,1)S(1)}, u32[]{:S(2)}, u32[]{:S(2)}) %collective-permute-start.4) | collective-permute-done | bytes 131104 | tf_op jit(solution)/shard_map/ppermute | solution.py:23
  42.5 0.8 %pair_enter.1 = (f32[16,4096]{1,0:T(8,128)S(1)}, f32[16,4096]{1,0:T(8,128)S(1)}) custom-call(s32[1]{0:T(128)} %bitcast.base_ref, s32[16]{0:T(128)} %len_ref.15, bf16[16,4096]{1,0:T(8,128)(2,1)S(1)} %reach_2.1.near_ref, bf16[16,4096]{1,0:T(8,128)(2,1)S(1)} %collective-permute-done.4.far_ref, f32[16,4096]{1,0:T(8,128)S(1)} %get-tuple-element.17.own_ref, ...), custom_call_target="tpu_custom_call" | custom-call | tf_op jit(solution)/shard_map/pair_enter/pallas_call | solution.py:556
  43.3 2.5 %collective-permute-start.5 = (f32[16,4096]{1,0:T(8,128)S(1)}, f32[16,4096]{1,0:T(8,128)S(1)}, u32[]{:S(2)}, u32[]{:S(2)}) collective-permute-start(f32[16,4096]{1,0:T(8,128)S(1)} %get-tuple-element.25), channel_id=1, source_target_pairs={{0,1},{1,0},{2,3},{3,2},{4,5},{5,4},{6,7},{7,6},{8,9},{9,8},{10,11... | collective-permute-start | bytes 786440 | tf_op jit(solution)/shard_map/ppermute | solution.py:27
  45.8 1.2 %collective-permute-done.5.got_ref = f32[16,4096]{1,0:T(8,128)S(1)} collective-permute-done((f32[16,4096]{1,0:T(8,128)S(1)}, f32[16,4096]{1,0:T(8,128)S(1)}, u32[]{:S(2)}, u32[]{:S(2)}) %collective-permute-start.5) | collective-permute-done | bytes 262176 | tf_op jit(solution)/shard_map/ppermute | solution.py:27
  47.0 0.0 copy-done.2
  47.0 10.3 %far_part.1 = (bf16[128,8192]{1,0:T(8,128)(2,1)}, bf16[128,8192]{1,0:T(8,128)(2,1)}) custom-call(s32[1]{0:T(128)} %bitcast.base_ref, s32[16]{0:T(128)} %len_ref.15, f32[64,136,128]{2,1,0:T(8,128)S(1)} %get-tuple-element.16.state_ref, f32[16,4096]{1,0:T(8,128)S(1)} %get-tuple-element.24.mine_ref, f32[16,4096]{1,0:T(8,128)S(1)} %collective-permute-done.5.got_ref, ...), custom_call_target="tpu_custom_call" | custom-call | flops 58982400 | bytes 18874368 | tf_op jit(solution)/shard_map/far_part/pallas_call | solution.py:607
Async XLA Ops:
  0.6 4.9 %copy-start.1 = (f32[3,3,8192]{2,1,0:T(4,128)S(1)}, f32[3,3,8192]{2,1,0:T(4,128)}, u32[]{:S(2)}) copy-start(f32[3,3,8192]{2,1,0:T(4,128)} %taps_ref.5) | copy-start | bytes 884740
  1.8 7.3 %collective-permute-start = (bf16[3,2,8192]{2,1,0:T(2,128)(2,1)S(1)}, bf16[3,2,8192]{2,1,0:T(2,128)(2,1)S(1)}, u32[]{:S(2)}, u32[]{:S(2)}) collective-permute-start(bf16[3,2,8192]{2,1,0:T(2,128)(2,1)S(1)} %tails.1), channel_id=1, source_target_pairs={{0,1},{1,2},{2,3},{3,4},{4,5},{5,6},{6,7},{7,8},{8,9},{9,10},{10,1... | collective-permute-start | bytes 294920 | tf_op jit(solution)/shard_map/ppermute | solution.py:23
  5.5 3.6 %copy-start = (f32[16,8192]{1,0:T(8,128)S(1)}, f32[16,8192]{1,0:T(8,128)}, u32[]{:S(2)}) copy-start(f32[16,8192]{1,0:T(8,128)} %rate_ref.13) | copy-start | bytes 1572868
  9.1 20.7 %copy-start.3 = (f32[16,8192]{1,0:T(8,128)S(1)}, f32[16,8192]{1,0:T(8,128)}, u32[]{:S(2)}) copy-start(f32[16,8192]{1,0:T(8,128)} %param.14) | copy-start | bytes 1572868
  21.2 2.2 %collective-permute-start.1 = (f32[16,4096]{1,0:T(8,128)S(1)}, f32[16,4096]{1,0:T(8,128)S(1)}, u32[]{:S(2)}, u32[]{:S(2)}) collective-permute-start(f32[16,4096]{1,0:T(8,128)S(1)} %get-tuple-element.18), channel_id=1, source_target_pairs={{0,1},{1,0},{2,3},{3,2},{4,5},{5,4},{6,7},{7,6},{8,9},{9,8},{10,11... | collective-permute-start | bytes 786440 | tf_op jit(solution)/shard_map/ppermute | solution.py:27
  24.2 9.1 %collective-permute-start.3 = (bf16[16,4096]{1,0:T(8,128)(2,1)S(1)}, bf16[16,4096]{1,0:T(8,128)(2,1)S(1)}, u32[]{:S(2)}, u32[]{:S(2)}) collective-permute-start(bf16[16,4096]{1,0:T(8,128)(2,1)S(1)} %pair_ends.1), channel_id=1, source_target_pairs={{0,4},{1,5},{2,6},{3,7},{4,8},{5,9},{6,10},{7,11},{8,12},{9,13},{1... | collective-permute-start | bytes 393224 | tf_op jit(solution)/shard_map/ppermute | solution.py:23
  26.7 8.3 %collective-permute-start.2 = (bf16[16,4096]{1,0:T(8,128)(2,1)S(1)}, bf16[16,4096]{1,0:T(8,128)(2,1)S(1)}, u32[]{:S(2)}, u32[]{:S(2)}) collective-permute-start(bf16[16,4096]{1,0:T(8,128)(2,1)S(1)} %pair_ends.1), channel_id=1, source_target_pairs={{0,2},{1,3},{2,4},{3,5},{4,6},{5,7},{6,8},{7,9},{8,10},{9,11},{10,... | collective-permute-start | bytes 393224 | tf_op jit(solution)/shard_map/ppermute | solution.py:23
  35.8 11.1 %copy-start.2 = (f32[8192]{0:T(1024)S(1)}, f32[8192]{0:T(1024)}, u32[]{:S(2)}) copy-start(f32[8192]{0:T(1024)} %param.17) | copy-start | bytes 98308
  35.9 6.6 %collective-permute-start.4 = (bf16[16,4096]{1,0:T(8,128)(2,1)S(1)}, bf16[16,4096]{1,0:T(8,128)(2,1)S(1)}, u32[]{:S(2)}, u32[]{:S(2)}) collective-permute-start(bf16[16,4096]{1,0:T(8,128)(2,1)S(1)} %reach_2.1.near_ref), channel_id=1, source_target_pairs={{0,4},{1,5},{2,6},{3,7},{4,8},{5,9},{6,10},{7,11},{8,12},{9,13},{1... | collective-permute-start | bytes 393224 | tf_op jit(solution)/shard_map/ppermute | solution.py:23
  43.3 3.6 %collective-permute-start.5 = (f32[16,4096]{1,0:T(8,128)S(1)}, f32[16,4096]{1,0:T(8,128)S(1)}, u32[]{:S(2)}, u32[]{:S(2)}) collective-permute-start(f32[16,4096]{1,0:T(8,128)S(1)} %get-tuple-element.25), channel_id=1, source_target_pairs={{0,1},{1,0},{2,3},{3,2},{4,5},{5,4},{6,7},{7,6},{8,9},{9,8},{10,11... | collective-permute-start | bytes 786440 | tf_op jit(solution)/shard_map/ppermute | solution.py:27

commit v11 on v10

--- a/solution.py
+++ b/solution.py
@@ -107,25 +107,15 @@
         return self.taps[0] * here + (self.taps[1] * one) * keep_one + (self.taps[2] * two) * keep_two
 
 
-def sub_passes(base_ref, len_ref, passes, span):
-    for b in range(SUBS):
-        passes[b] = jnp.float32(1.0)
-    start = jnp.int32(0)
-    for d in range(len_ref.shape[0]):
-        at = start - base_ref[0]
-
-        @pl.when((at >= 0) & (at < SUBS * span))
-        def _():
-            passes[lax.div(at, jnp.int32(span))] = jnp.float32(0.0)
-
-        start = start + len_ref[d]
-
-
-def half_of(base_ref, rows, chans, lane):
+def half_of(chans, lane):
     half = chans // 2
     which = lax.div(lane, half)
-    mine = which == lax.rem(lax.div(base_ref[0], rows), 2)
+    mine = which == lax.rem(lax.axis_index("ctx"), 2)
     return mine, pl.multiple_of(lane - which * half, LANES)
+
+
+def twice(mask, modes):
+    return jnp.concatenate([mask] * (modes // SUBS), axis=0)
 
 
 def sub_state(state_ref, lane, b, modes):
@@ -133,9 +123,9 @@
 
 
 def state_kernel(
-    base_ref, len_ref, key_ref, value_ref, rim_ref, taps_ref, rate_ref,
+    masks, key_ref, value_ref, rim_ref, taps_ref, rate_ref,
     gate_ref, state_ref, own_ref, give_ref,
-    key_buf, value_buf, sems, masks, passes, wide_k, wide_v, tables, held,
+    key_buf, value_buf, sems, wide_k, wide_v, tables, held,
     *, span, modes, most, chunk,
 ):
     chans = key_buf.shape[1]
@@ -147,15 +137,7 @@
         for copy in fetches(c):
             copy.start()
 
-    def prepare():
-        rows, starts = doc_start_rows(len_ref, base_ref[0], span)
-        for j in range(span):
-            masks[0, j] = flag(starts[j] < rows + j)
-            masks[1, j] = flag(starts[j] < rows + (j - 1))
-            masks[2, j] = flag(starts[span - 1] <= rows + j)
-        sub_passes(base_ref, len_ref, passes, span)
-
-    prepare()
+    at = Masks(span)
 
     def group(lanes):
         for slot, lane in enumerate(lanes):
@@ -172,7 +154,7 @@
         ]
         last = [None] * len(lanes)
         for j in range(span):
-            keep_one, keep_two = masks[0, j], masks[1, j]
+            keep_one, keep_two = masks[at.one + j], masks[at.two + j]
             for slot, lane in enumerate(lanes):
                 k_short, v_short = [conv.step(j, keep_one, keep_two) for conv in convs[slot]]
                 if j % 2 == 0:
@@ -181,8 +163,8 @@
                 pair = jnp.concatenate([last[slot], k_short * v_short], axis=0).astype(bf16)
                 gate_ref[pl.ds((j - 1) * SUBS, 2 * SUBS), cols_of(lane)] = pair
                 pair = pair.astype(f32)
-                held[slot, j - 1] = pair[:SUBS] * masks[2, j - 1]
-                held[slot, j] = pair[SUBS:] * masks[2, j]
+                held[slot, j - 1] = pair[:SUBS] * masks[at.last + j - 1]
+                held[slot, j] = pair[SUBS:] * masks[at.last + j]
         for slot, lane in enumerate(lanes):
             decay = [row_of(tables.at[slot], n) for n in range(modes)]
             state = [held[slot, 0]] * modes
@@ -195,8 +177,8 @@
             leap = jnp.exp(-float(span) * rate_ref[:, cols_of(lane)])
             end = sub_state(state_ref, lane, 0, modes)
             for b in range(1, SUBS):
-                end = (leap * passes[b]) * end + sub_state(state_ref, lane, b, modes)
-            mine, here = half_of(base_ref, key_ref.shape[0], chans, lane)
+                end = (leap * twice(masks[at.passes + b], modes)) * end + sub_state(state_ref, lane, b, modes)
+            mine, here = half_of(chans, lane)
 
             @pl.when(mine)
             def _():
@@ -226,16 +208,57 @@
         tail_ref[i] = bufs[i].astype(f32)[count - 2 :].astype(bf16)
 
 
-def keep_masks(base_ref, len_ref, masks, span):
+def unbroken(len_ref, first, count):
+    start = jnp.int32(0)
+    whole = jnp.where((first <= 0) & (first + count > 0), 0.0, 1.0)
+    for d in range(len_ref.shape[0] - 1):
+        start = start + len_ref[d]
+        whole = jnp.where((start >= first) & (start < first + count), 0.0, whole)
+    return whole.astype(f32)
+
+
+class Masks:
+    def __init__(self, span):
+        self.one, self.two, self.last, self.enter = 0, span, 2 * span, 3 * span
+        self.passes = 4 * span
+        self.edges = self.passes + SUBS
+        self.late = self.edges + 3
+        self.early = self.late + 1
+        self.reach = self.late + 2
+
+    def count(self, reaches):
+        return self.reach + reaches
+
+
+def write_masks(base_ref, len_ref, masks, span, reaches):
+    at = Masks(span)
     rows, starts = doc_start_rows(len_ref, base_ref[0], span)
     for j in range(span):
-        masks[0, j] = flag(starts[j] < rows + j)
-        masks[1, j] = flag(starts[j] < rows + (j - 1))
-
-
-def near_kernel(base_ref, len_ref, gate_ref, rate_ref, weight_ref, *refs, span, modes, most, first, count):
-    near_ref, masks, sums, tap_rows = refs[-4:]
-    keep_masks(base_ref, len_ref, masks, span)
+        masks[at.one + j] = flag(starts[j] < rows + j)
+        masks[at.two + j] = flag(starts[j] < rows + (j - 1))
+        masks[at.last + j] = flag(starts[span - 1] <= rows + j)
+        masks[at.enter + j] = flag(starts[j] < rows)
+    top = flag(lax.broadcasted_iota(jnp.int32, (SUBS, LANES), 0) == 0)
+    masks[at.edges] = top * masks[at.one]
+    masks[at.edges + 1] = top * masks[at.two]
+    masks[at.edges + 2] = top * masks[at.two + 1]
+    size = SUBS * span
+    parity = lax.rem(lax.div(base_ref[0], size), 2)
+    pair_at = base_ref[0] - parity * size
+    ranges = [(base_ref[0] + b * span, span) for b in range(SUBS)]
+    flags = [at.passes + b for b in range(SUBS)]
+    ranges += [(pair_at + size, size), (pair_at, size)]
+    flags += [at.late, at.early]
+    for m in range(reaches):
+        ranges.append((pair_at - (2 * size << m), 2 * size << m))
+        flags.append(at.reach + m)
+    for index, (first, count) in zip(flags, ranges):
+        masks[index] = jnp.full((SUBS, LANES), unbroken(len_ref, first, count), f32)
+
+
+def near_kernel(masks, gate_ref, rate_ref, weight_ref, *refs, span, modes, most, first, count):
+    near_ref, sums, tap_rows = refs[-3:]
+    at = Masks(span)
 
     def group(lanes):
         for slot, lane in enumerate(lanes):
@@ -261,7 +284,7 @@
             for j in range(span):
                 if j % 2 == 0:
                     pair = gate_ref[pl.ds(j * SUBS, 2 * SUBS), cols_of(lane)].astype(f32)
-                keep = masks[0, j]
+                keep = masks[at.one + j]
                 live = [g * keep for g in live]
                 live.append(pair[(j % 2) * SUBS : (j % 2 + 1) * SUBS])
                 total = parts[0] * live[j]
@@ -272,7 +295,7 @@
     each_group(count // LANES, most, lambda lanes: group([pl.multiple_of(first + lane, LANES) for lane in lanes]))
 
 
-def query_kernel(base_ref, len_ref, query_ref, taps_ref, short_ref, query_buf, sems, masks, wide_q, *, span, most, chunk):
+def query_kernel(base_ref, len_ref, query_ref, taps_ref, short_ref, masks, query_buf, sems, wide_q, *, span, most, chunk, reaches):
     chans = query_buf.shape[1]
 
     def fetch(c):
@@ -280,77 +303,30 @@
 
     for c in range(chans // chunk):
         fetch(c).start()
-    keep_masks(base_ref, len_ref, masks, span)
+    write_masks(base_ref, len_ref, masks, span, reaches)
+    at = Masks(span)
 
     def group(lanes):
         for slot, lane in enumerate(lanes):
             spread(query_buf[:, cols_of(lane)], wide_q.at[slot], span)
         convs = [Conv(wide_q.at[slot], None, taps_ref[0, :, cols_of(lane)], span) for slot, lane in enumerate(lanes)]
         for j in range(span):
-            keep_one, keep_two = masks[0, j], masks[1, j]
+            keep_one, keep_two = masks[at.one + j], masks[at.two + j]
             for slot, lane in enumerate(lanes):
                 short_ref[pl.ds(j * SUBS, SUBS), cols_of(lane)] = convs[slot].step(j, keep_one, keep_two)
 
     each_chunk(chans, chunk, lambda c: fetch(c).wait(), group, lambda c: None, most)
 
 
-def unbroken(len_ref, first, count):
-    start = jnp.int32(0)
-    whole = jnp.where((first <= 0) & (first + count > 0), 0.0, 1.0)
-    for d in range(len_ref.shape[0] - 1):
-        start = start + len_ref[d]
-        whole = jnp.where((start >= first) & (start < first + count), 0.0, whole)
-    return whole.astype(f32)
-
-
-def pair_rates(base_ref, rate_ref, rows, shape):
-    parity = lax.rem(lax.div(base_ref[0], rows), 2)
-    return parity, rate_ref[:, pl.ds(pl.multiple_of(parity * shape[1], LANES), shape[1])]
-
-
-def early_late(parity, own, got):
-    odd = jnp.full(own.shape, parity, jnp.int32) == 1
-    return jnp.where(odd, got, own), jnp.where(odd, own, got)
-
-
-def pair_kernel(base_ref, len_ref, own_ref, got_ref, rate_ref, end_ref, *, rows):
-    parity, rate = pair_rates(base_ref, rate_ref, rows, own_ref.shape)
-    early, late = early_late(parity, own_ref[...], got_ref[...])
-    through = unbroken(len_ref, base_ref[0] + (1 - parity) * rows, rows)
-    end_ref[...] = (late + (jnp.exp(-float(rows) * rate) * through) * early).astype(bf16)
-
-
-def reached(base_ref, len_ref, near_ref, far_ref, rate_ref, rows, reach):
-    parity, rate = pair_rates(base_ref, rate_ref, rows, near_ref.shape)
-    span = 2 * rows * reach
-    through = unbroken(len_ref, base_ref[0] - parity * rows - span, span)
-    return near_ref[...].astype(f32) + (jnp.exp(-float(span) * rate) * through) * far_ref[...].astype(f32)
-
-
-def reach_kernel(base_ref, len_ref, near_ref, far_ref, rate_ref, enter_ref, *, rows, reach):
-    enter_ref[...] = reached(base_ref, len_ref, near_ref, far_ref, rate_ref, rows, reach).astype(bf16)
-
-
-def enter_kernel(base_ref, len_ref, near_ref, far_ref, own_ref, got_ref, rate_ref, mine_ref, give_ref, *, rows, reach):
-    first = reached(base_ref, len_ref, near_ref, far_ref, rate_ref, rows, reach)
-    parity, rate = pair_rates(base_ref, rate_ref, rows, own_ref.shape)
-    early, _ = early_late(parity, own_ref[...], got_ref[...])
-    through = unbroken(len_ref, base_ref[0] - parity * rows, rows)
-    second = early + (jnp.exp(-float(rows) * rate) * through) * first
-    give, mine = early_late(parity, second, first)
-    mine_ref[...] = mine
-    give_ref[...] = give
-
-
 def final_kernel(
-    base_ref, len_ref, state_ref, mine_ref, got_ref, near_ref, short_ref, resid_in, rim_ref, taps_ref, rate_ref, weight_ref, gain_ref,
+    masks, state_ref, mine_ref, got_ref, near_ref, short_ref, resid_in, rim_ref, taps_ref, rate_ref, weight_ref, gain_ref,
     *refs,
     span, modes, channels, most, chunk,
 ):
     if channels:
-        hidden_out, normed_out, resid_ref, hidden_ref, sems, masks, passes, wide, tables, starts_at, sums, whole, normed_ref = refs
+        hidden_out, normed_out, resid_ref, hidden_ref, sems, wide, tables, starts_at, sums, whole, normed_ref = refs
     else:
-        hidden_out, wide_ref, sum_ref, resid_ref, hidden_ref, sems, masks, passes, wide, tables, starts_at, sums = refs
+        hidden_out, wide_ref, sum_ref, resid_ref, hidden_ref, sems, wide, tables, starts_at, sums = refs
     chans = resid_ref.shape[1]
 
     def fetch(c):
@@ -364,19 +340,12 @@
 
     for c in range(chans // chunk):
         fetch(c).start()
-    rows, starts = doc_start_rows(len_ref, base_ref[0], span)
-    for j in range(span):
-        masks[0, j] = flag(starts[j] < rows)
-    sub_passes(base_ref, len_ref, passes, span)
-    top = flag(lax.broadcasted_iota(jnp.int32, (SUBS, LANES), 0) == 0)
-    masks[1, 1] = top * flag(starts[0] < rows)
-    masks[1, 2] = top * flag(starts[0] < rows - 1)
-    masks[1, 3] = top * flag(starts[1] < rows)
+    at = Masks(span)
     sums[...] = jnp.zeros(sums.shape, f32)
 
     def group(lanes):
         for slot, lane in enumerate(lanes):
-            mine, here = half_of(base_ref, resid_ref.shape[0], chans, lane)
+            mine, here = half_of(chans, lane)
             mine = jnp.full((modes, LANES), mine.astype(jnp.int32), jnp.int32) == 1
             state = jnp.where(mine, mine_ref[:, cols_of(here)], got_ref[:, cols_of(here)])
             rate = rate_ref[:, cols_of(lane)]
@@ -386,22 +355,22 @@
             for b in range(SUBS):
                 starts_at[slot, pl.ds(b * (modes + 1), modes), :] = weight * state
                 if b < SUBS - 1:
-                    state = (leap * passes[b]) * state + sub_state(state_ref, lane, b, modes)
+                    state = (leap * twice(masks[at.passes + b], modes)) * state + sub_state(state_ref, lane, b, modes)
         for slot, lane in enumerate(lanes):
             part = [starts_at[slot, pl.ds(n, SUBS, stride=modes + 1), :] for n in range(modes)]
             decay = [row_of(tables.at[slot], n) for n in range(modes)]
             rim = rim_ref[0, :, cols_of(lane)].astype(f32)
             tap = taps_ref[0, :, cols_of(lane)]
             edge = [
-                (tap[1:2] * rim[1:2]) * masks[1, 1] + (tap[2:3] * rim[0:1]) * masks[1, 2],
-                (tap[2:3] * rim[1:2]) * masks[1, 3],
+                (tap[1:2] * rim[1:2]) * masks[at.edges] + (tap[2:3] * rim[0:1]) * masks[at.edges + 1],
+                (tap[2:3] * rim[1:2]) * masks[at.edges + 2],
             ]
             for j in range(span):
                 part = [part[n] * decay[n] for n in range(modes)]
                 total = part
                 while len(total) > 1:
                     total = [total[m] + total[m + 1] for m in range(0, len(total), 2)]
-                conv = near_ref[pl.ds(j * SUBS, SUBS), cols_of(lane)] + total[0] * masks[0, j]
+                conv = near_ref[pl.ds(j * SUBS, SUBS), cols_of(lane)] + total[0] * masks[at.enter + j]
                 conv = conv.astype(bf16).astype(f32)
                 short = short_ref[pl.ds(j * SUBS, SUBS), cols_of(lane)]
                 if j < 2:
@@ -485,15 +454,16 @@
         name="tails",
     )(far_off(query_in), far_off(key_in), far_off(value_in))
     rim_rows = from_behind(tails, "ctx", 1)
-    q_short = pl.pallas_call(
-        functools.partial(query_kernel, span=span, most=Q_TILES, chunk=chunk),
+    reaches = max(1, (blocks // 8).bit_length() - 1)
+    mask_shape = (Masks(span).count(reaches),) + tile_shape
+    q_short, masks = pl.pallas_call(
+        functools.partial(query_kernel, span=span, most=Q_TILES, chunk=chunk, reaches=reaches),
         in_specs=[smem, smem, hbm, vmem],
-        out_specs=vmem,
-        out_shape=pltpu.VMEM((tok_rows, chans), f32),
+        out_specs=[vmem, vmem],
+        out_shape=[pltpu.VMEM((tok_rows, chans), f32), pltpu.VMEM(mask_shape, f32)],
         scratch_shapes=[
             pltpu.VMEM((tok_rows, chans), bf16),
             pltpu.SemaphoreType.DMA((pieces,)),
-            pltpu.VMEM((2, span) + tile_shape, f32),
             pltpu.VMEM((Q_TILES, wide_rows, LANES), f32),
         ],
         compiler_params=params,
@@ -504,7 +474,7 @@
     rates, weights, taps, rims = near_by(decay_rate), near_by(weight), near_by(short_taps), near_by(rim_rows)
     gates, states, own, give = pl.pallas_call(
         functools.partial(state_kernel, span=span, modes=modes, most=A_TILES, chunk=chunk),
-        in_specs=[smem, smem, hbm, hbm, vmem, vmem, vmem],
+        in_specs=[vmem, hbm, hbm, vmem, vmem, vmem],
         out_specs=[vmem, vmem, vmem, vmem],
         out_shape=[
             pltpu.VMEM((tok_rows, chans), bf16),
@@ -516,8 +486,6 @@
             pltpu.VMEM((tok_rows, chans), bf16),
             pltpu.VMEM((tok_rows, chans), bf16),
             copies(2),
-            pltpu.VMEM((3, span) + tile_shape, f32),
-            pltpu.SMEM((SUBS,), f32),
             pltpu.VMEM((A_TILES, wide_rows, LANES), f32),
             pltpu.VMEM((A_TILES, wide_rows, LANES), f32),
             pltpu.VMEM((A_TILES, modes, LANES), f32),
@@ -526,7 +494,7 @@
         compiler_params=params,
         cost_estimate=cost(1000, 12 * tok_rows * chans),
         name="block_states",
-    )(base, lengths, far_off(key_in), far_off(value_in), rims, taps, rates)
+    )(near_by(masks), far_off(key_in), far_off(value_in), rims, taps, rates)
 
     def near_piece(part, near):
         count = chans // NEAR_PARTS
@@ -535,52 +503,42 @@
             functools.partial(
                 near_kernel, span=span, modes=modes, most=N_TILES, first=part * count, count=count
             ),
-            in_specs=[smem, smem, vmem, vmem, vmem] + [vmem] * len(before),
+            in_specs=[vmem] * (4 + len(before)),
             out_specs=vmem,
             out_shape=pltpu.VMEM((tok_rows, chans), f32),
             scratch_shapes=[
-                pltpu.VMEM((2, span) + tile_shape, f32),
                 pltpu.VMEM((N_TILES, span * (SUBS + 1), LANES), f32),
                 pltpu.VMEM((N_TILES, span, LANES), f32),
             ],
             compiler_params=params,
-            input_output_aliases={5: 0} if before else {},
+            input_output_aliases={4: 0} if before else {},
             cost_estimate=cost(600 // NEAR_PARTS, 7 * tok_rows * count),
             name="near_part_%d" % part,
-        )(base, lengths, near_by(gates), rates, weights, *before)
+        )(near_by(masks), near_by(gates), rates, weights, *before)
 
     got = swap(give, "ctx")
 
-    def pair_call(kernel, operands, out_shape, name, **static):
-        count = len(operands) + 1
-        return pl.pallas_call(
-            functools.partial(kernel, rows=tok_rows, **static),
-            in_specs=[smem, smem] + [vmem] * count,
-            out_specs=[vmem] * len(out_shape),
-            out_shape=out_shape,
-            compiler_params=params,
-            name=name,
-        )(base, lengths, *[near_by(x) for x in operands], rates)
-
-    sent = pltpu.VMEM(half.shape, bf16)
-    ends = pair_call(pair_kernel, [own, got], [sent], "pair_ends")[0]
+    odd = lax.rem(ctx_index, 2) == 1
+    few_rates = lax.dynamic_slice_in_dim(decay_rate, lax.rem(ctx_index, 2) * half.shape[1], half.shape[1], 1)
+    at = Masks(span)
+
+    def leap(rows, index):
+        return jnp.exp(-float(rows) * few_rates) * masks[index, 0, 0]
+
+    early, late = jnp.where(odd, got, own), jnp.where(odd, own, got)
+    ends = (late + leap(tok_rows, at.late) * early).astype(bf16)
     one_on, two_on = from_behind(ends, "ctx", 2), from_behind(ends, "ctx", 4)
     near = near_piece(0, None)
     one_on, two_on, near = lax.optimization_barrier((one_on, two_on, near))
-    enter, on, reach = one_on, two_on, 1
-    while 2 * reach < blocks // 8:
-        enter = pair_call(reach_kernel, [enter, on], [sent], "reach_%d" % (2 * reach), reach=reach)[0]
-        reach *= 2
-        on = from_behind(enter, "ctx", 2 * reach)
+    enter, on = one_on, two_on
+    for m in range(reaches - 1):
+        enter = (enter.astype(f32) + leap(2 * tok_rows << m, at.reach + m) * on.astype(f32)).astype(bf16)
+        on = from_behind(enter, "ctx", 4 << m)
     near = near_piece(1, near)
     on, near = lax.optimization_barrier((on, near))
-    mine, give_back = pair_call(
-        enter_kernel,
-        [enter, on, own, got],
-        [pltpu.VMEM(half.shape, f32), pltpu.VMEM(half.shape, f32)],
-        "pair_enter",
-        reach=reach,
-    )
+    first = enter.astype(f32) + leap(2 * tok_rows << (reaches - 1), at.reach + reaches - 1) * on.astype(f32)
+    second = early + leap(tok_rows, at.early) * first
+    mine, give_back = jnp.where(odd, second, first), jnp.where(odd, first, second)
     got_back = swap(give_back, "ctx")
 
     alone = grp == 1
@@ -590,8 +548,6 @@
         pltpu.VMEM((tok_rows, chans), bf16),
         pltpu.VMEM((tok_rows, chans), bf16),
         copies(3),
-        pltpu.VMEM((2, span) + tile_shape, f32),
-        pltpu.SMEM((SUBS,), f32),
         pltpu.VMEM((F_TILES, wide_rows, LANES), f32),
         pltpu.VMEM((F_TILES, modes, LANES), f32),
         pltpu.VMEM((F_TILES, SUBS * (modes + 1), LANES), f32),
@@ -608,7 +564,7 @@
         functools.partial(
             final_kernel, span=span, modes=modes, channels=chans if alone else 0, most=F_TILES, chunk=chunk
         ),
-        in_specs=[smem, smem, vmem, vmem, vmem, vmem, vmem, hbm, vmem, vmem, vmem, vmem, vmem],
+        in_specs=[vmem, vmem, vmem, vmem, vmem, vmem, hbm, vmem, vmem, vmem, vmem, vmem],
         out_specs=out_specs,
         out_shape=out_shape,
         scratch_shapes=scratch,
@@ -616,7 +572,7 @@
         cost_estimate=cost(900, 18 * tok_rows * chans),
         name="far_part",
     )(
-        base, lengths, near_by(states), near_by(mine), near_by(got_back), near_by(near), near_by(q_short), far_off(residual),
+        near_by(masks), near_by(states), near_by(mine), near_by(got_back), near_by(near), near_by(q_short), far_off(residual),
         rims, taps, rates, weights, norm_gain.reshape(1, chans),
     )
     if alone:

time: 57.7 us -> 63.8 us (1.11)
  other arithmetic: 0.32 us -> 6.41 us
  local copies, waits for them, and re-layouts: 0.02 us -> 5.4 us
  Pallas kernels: 35.7 us -> 30.9 us
  starting transfers between devices: 15.5 us -> 14 us
  waiting for transfers between devices: 5.02 us -> 5.94 us
    unnamed x8 -> x20, local copies, waits for them, and re-layouts: 0.02 us -> 4.8 us
    convert_element_type x0 -> x2, other arithmetic: none -> 2.64 us  [the longest x1 1.73 us: shards(): ends = (late + leap(tok_rows, at.late) * early).astype(bf16)]
    select_n x0 -> x1, other arithmetic: none -> 2.42 us  [shards(): jnp.where(odd, first, second)]
    pallas_call x3 -> x0, Pallas kernels: 2.36 us -> none  [pair_call(): pl.pallas_call(functools.partial(kernel, rows=tok_rows, **static), in_spe...]
    ppermute x2, starting transfers between devices: 3.51 us -> 1.54 us  [swap(): lax.ppermute(shard, axis, [(i, i ^ 1) for i in range(lax.axis_size(axis))])]
    pallas_call x2, Pallas kernels: 6.18 us -> 4.67 us  [near_piece(): pl.pallas_call(functools.partial(near_kernel, span=span, modes=modes, mos...]
    mul x1, other arithmetic: 0.32 us -> 1.36 us  [shards(): weight = residues * jnp.sqrt(-jnp.expm1(-2.0 * decay_rate))]
    ppermute x4, waiting for transfers between devices: 2.7 us -> 3.5 us  [from_behind(): return lax.ppermute(shard, axis, pairs)]
  transfers between devices with their start and end apart: 6 -> 6, of which waited for: 4 -> 4; matrix products, arithmetic and copies ran while one was open for 1% -> 3% of each run, Pallas kernels for 17% -> 13%
where the time goes in v11:
time: 63.8 us; the launch traced here: 63.5 us
  Pallas kernels  30.9 us (48%)
  starting transfers between devices  14 us (22%)
  other arithmetic  6.41 us (10%)
  waiting for transfers between devices  5.94 us (9%)
  local copies, waits for them, and re-layouts  5.4 us (8%)
  between operations  0.81 us (1%)
    ppermute x4, starting transfers between devices, from_behind(): return lax.ppermute(shard, axis, pairs)  12.5 us
    pallas_call x1, Pallas kernels, shards(): pl.pallas_call(functools.partial(state_kernel, span=span, modes=modes, mo...  11.8 us
    pallas_call x1, Pallas kernels, shards(): pl.pallas_call(functools.partial(final_kernel, span=span, modes=modes, ch...  9.83 us
    unnamed x20, local copies, waits for them, and re-layouts  4.8 us
    pallas_call x2, Pallas kernels, near_piece(): pl.pallas_call(functools.partial(near_kernel, span=span, modes=modes, mos...  4.67 us
    ppermute x4, waiting for transfers between devices, from_behind(): return lax.ppermute(shard, axis, pairs)  3.5 us
    pallas_call x1, Pallas kernels, shards(): pl.pallas_call(functools.partial(query_kernel, span=span, most=Q_TILES, c...  3.41 us
    ppermute x2, waiting for transfers between devices, swap(): lax.ppermute(shard, axis, [(i, i ^ 1) for i in range(lax.axis_size(axis))])  2.44 us
  transfers between devices with their start and end apart: 6, of which 4 were waited for; matrix products, arithmetic and copies ran while one was open for 3% of the time, Pallas kernels for 13%

profile of v11, /device:TPU:9, one launch (start us, length us, event | category | flops | bytes accessed | tf_op | source)
XLA Modules:
  0.0 63.5 jit_solution(11281823355071089155)
XLA Ops:
  0.6 0.0 copy-start.4
  0.6 1.2 %tails.1 = bf16[3,2,8192]{2,1,0:T(2,128)(2,1)S(1)} custom-call(bf16[128,8192]{1,0:T(8,128)(2,1)} %query_ref.3, bf16[128,8192]{1,0:T(8,128)(2,1)} %key_ref.3, bf16[128,8192]{1,0:T(8,128)(2,1)} %value_ref.3), custom_call_target="tpu_custom_call" | custom-call | tf_op jit(solution)/shard_map/tails/pallas_call | solution.py:447
  1.8 0.0 copy-start
  1.9 3.8 %collective-permute-start = (bf16[3,2,8192]{2,1,0:T(2,128)(2,1)S(1)}, bf16[3,2,8192]{2,1,0:T(2,128)(2,1)S(1)}, u32[]{:S(2)}, u32[]{:S(2)}) collective-permute-start(bf16[3,2,8192]{2,1,0:T(2,128)(2,1)S(1)} %tails.1), channel_id=1, source_target_pairs={{0,1},{1,2},{2,3},{3,4},{4,5},{5,6},{6,7},{7,8},{8,9},{9,10},{10,1... | collective-permute-start | bytes 294920 | tf_op jit(solution)/shard_map/ppermute | solution.py:23
  5.7 0.0 copy-done.4
  5.7 3.4 %query_part.1 = (f32[128,8192]{1,0:T(8,128)S(1)}, f32[79,8,128]{2,1,0:T(8,128)S(1)}) custom-call(s32[1]{0:T(128)} %bitcast.base_ref, s32[16]{0:T(128)} %len_ref.1, bf16[128,8192]{1,0:T(8,128)(2,1)} %query_ref.3, f32[3,3,8192]{2,1,0:T(4,128)S(1)} %copy-done.4), custom_call_target="tpu_custom_call" | custom-call | flops 13107200 | bytes 6291456 | tf_op jit(solution)/shard_map/query_part/pallas_call | solution.py:459
  9.1 0.0 copy-start.2
  9.1 2.0 %copy-done.2 = f32[128,8192]{1,0:T(8,128)} copy-done((f32[128,8192]{1,0:T(8,128)}, f32[128,8192]{1,0:T(8,128)S(1)}, u32[]{:S(2)}) %copy-start.2) | copy-done | bytes 4194328
  11.1 0.0 collective-permute-done.rim_ref
  11.1 0.0 copy-done
  11.1 11.8 %block_states.1 = (bf16[128,8192]{1,0:T(8,128)(2,1)S(1)}, f32[64,136,128]{2,1,0:T(8,128)S(1)}, f32[16,4096]{1,0:T(8,128)S(1)}, f32[16,4096]{1,0:T(8,128)}) custom-call(f32[79,8,128]{2,1,0:T(8,128)S(1)} %get-tuple-element.15.masks, bf16[128,8192]{1,0:T(8,128)(2,1)} %key_ref.3, bf16[128,8192]{1,0:T(8,128)(2,1)} %value_ref.3, ...), custom_call_target="tpu_custom_call" | custom-call | flops 65536000 | bytes 12582912 | tf_op jit(solution)/shard_map/block_states/pallas_call | solution.py:475
  22.9 0.0 copy-start.1
  22.9 2.0 %copy-done.1 = f32[64,136,128]{2,1,0:T(8,128)} copy-done((f32[64,136,128]{2,1,0:T(8,128)}, f32[64,136,128]{2,1,0:T(8,128)S(1)}, u32[]{:S(2)}) %copy-start.1) | copy-done | bytes 4456472
  25.0 0.0 copy-start.5
  25.0 0.7 %copy-done.5 = f32[16,4096]{1,0:T(8,128)} copy-done((f32[16,4096]{1,0:T(8,128)}, f32[16,4096]{1,0:T(8,128)S(1)}, u32[]{:S(2)}) %copy-start.5) | copy-done | bytes 262168
  25.7 0.0 collective-permute-start.1
  25.7 0.6 fusion.2
  26.3 1.3 %collective-permute-done.1 = f32[16,4096]{1,0:T(8,128)} collective-permute-done((f32[16,4096]{1,0:T(8,128)}, f32[16,4096]{1,0:T(8,128)}, u32[]{:S(2)}, u32[]{:S(2)}) %collective-permute-start.1) | collective-permute-done | bytes 262176 | tf_op jit(solution)/shard_map/ppermute | solution.py:27
  27.6 1.7 %add_convert_fusion.1 = bf16[16,4096]{1,0:T(8,128)(2,1)S(1)} fusion(f32[16,4096]{1,0:T(8,128)} %copy-done.5, f32[16,4096]{1,0:T(8,128)} %collective-permute-done.1, f32[16,8192]{1,0:T(8,128)S(1)} %copy-done, s32[]{:T(128)S(6)} %select_n.27, f32[]{:T(128)} %bitcast.2, pred[]{:T(512)S(6)} %eq.3), kind=kLoop, calls=%fused_computation.4 | loop fusion | flops 458752 | bytes 917513 | tf_op jit(solution)/shard_map/convert_element_type | solution.py:529
  29.3 3.1 %collective-permute-start.3 = (bf16[16,4096]{1,0:T(8,128)(2,1)S(1)}, bf16[16,4096]{1,0:T(8,128)(2,1)S(1)}, u32[]{:S(2)}, u32[]{:S(2)}) collective-permute-start(bf16[16,4096]{1,0:T(8,128)(2,1)S(1)} %add_convert_fusion.1), channel_id=1, source_target_pairs={{0,4},{1,5},{2,6},{3,7},{4,8},{5,9},{6,10},{7,11},{8,12},{9,13},{1... | collective-permute-start | bytes 393224 | tf_op jit(solution)/shard_map/ppermute | solution.py:23
  32.5 3.1 %collective-permute-start.2 = (bf16[16,4096]{1,0:T(8,128)(2,1)S(1)}, bf16[16,4096]{1,0:T(8,128)(2,1)S(1)}, u32[]{:S(2)}, u32[]{:S(2)}) collective-permute-start(bf16[16,4096]{1,0:T(8,128)(2,1)S(1)} %add_convert_fusion.1), channel_id=1, source_target_pairs={{0,2},{1,3},{2,4},{3,5},{4,6},{5,7},{6,8},{7,9},{8,10},{9,11},{10,... | collective-permute-start | bytes 393224 | tf_op jit(solution)/shard_map/ppermute | solution.py:23
  35.6 1.4 %sqrt_multiply_fusion.weight_ref = f32[16,8192]{1,0:T(8,128)S(1)} fusion(f32[16,8192]{1,0:T(8,128)} %param.14, f32[16,8192]{1,0:T(8,128)S(1)} %copy-done), kind=kLoop, calls=%fused_computation | loop fusion | flops 393216 | bytes 1572864 | tf_op jit(solution)/shard_map/mul | solution.py:423
  36.9 2.3 %near_part_0.1.refs_0_ = f32[128,8192]{1,0:T(8,128)S(1)} custom-call(f32[79,8,128]{2,1,0:T(8,128)S(1)} %get-tuple-element.15.masks, bf16[128,8192]{1,0:T(8,128)(2,1)S(1)} %get-tuple-element.21.gate_ref, f32[16,8192]{1,0:T(8,128)S(1)} %copy-done, f32[16,8192]{1,0:T(8,128)S(1)} %sqrt_multiply_fusion.weight_ref), custom_call_target="tpu_custom_call" | custom-call | flops 19660800 | bytes 3670016 | tf_op jit(solution)/shard_map/near_part_0/pallas_call | solution.py:502
  39.3 0.0 collective-permute-done.3
  39.3 1.5 %collective-permute-done.2 = bf16[16,4096]{1,0:T(8,128)(2,1)S(1)} collective-permute-done((bf16[16,4096]{1,0:T(8,128)(2,1)S(1)}, bf16[16,4096]{1,0:T(8,128)(2,1)S(1)}, u32[]{:S(2)}, u32[]{:S(2)}) %collective-permute-start.2) | collective-permute-done | bytes 131104 | tf_op jit(solution)/shard_map/ppermute | solution.py:23
  40.8 0.0 slice-start
  40.8 0.9 %add_convert_fusion = bf16[16,4096]{1,0:T(8,128)(2,1)S(1)} fusion(bf16[16,4096]{1,0:T(8,128)(2,1)S(1)} %collective-permute-done.3, bf16[16,4096]{1,0:T(8,128)(2,1)S(1)} %collective-permute-done.2, f32[16,8192]{1,0:T(8,128)S(1)} %copy-done, s32[]{:T(128)S(6)} %select_n.27, f32[]{:T(128)} %bitcast.3), kind=kLoop, calls=%fused_computation.3 | loop fusion | flops 458752 | bytes 655368 | tf_op jit(solution)/shard_map/convert_element_type | solution.py:535
  41.7 0.0 copy-start.6
  41.7 0.0 slice-start.1
  41.7 0.0 copy-start.7
  41.7 2.4 %collective-permute-start.4 = (bf16[16,4096]{1,0:T(8,128)(2,1)S(1)}, bf16[16,4096]{1,0:T(8,128)(2,1)S(1)}, u32[]{:S(2)}, u32[]{:S(2)}) collective-permute-start(bf16[16,4096]{1,0:T(8,128)(2,1)S(1)} %add_convert_fusion), channel_id=1, source_target_pairs={{0,4},{1,5},{2,6},{3,7},{4,8},{5,9},{6,10},{7,11},{8,12},{9,13},{1... | collective-permute-start | bytes 393224 | tf_op jit(solution)/shard_map/ppermute | solution.py:23
  44.1 0.0 copy-start.3
  44.1 2.3 %near_part_1.1.near_ref = f32[128,8192]{1,0:T(8,128)S(1)} custom-call(f32[79,8,128]{2,1,0:T(8,128)S(1)} %get-tuple-element.15.masks, bf16[128,8192]{1,0:T(8,128)(2,1)S(1)} %get-tuple-element.21.gate_ref, f32[16,8192]{1,0:T(8,128)S(1)} %copy-done, f32[16,8192]{1,0:T(8,128)S(1)} %sqrt_multiply_fusion.weight_ref, ...), custom_call_target="tpu_custom_call", output_to_operand_aliasing={{}: (4, {})} | custom-call | flops 19660800 | bytes 3670016 | tf_op jit(solution)/shard_map/near_part_1/pallas_call | solution.py:502
  46.5 2.0 %collective-permute-done.4 = bf16[16,4096]{1,0:T(8,128)(2,1)S(1)} collective-permute-done((bf16[16,4096]{1,0:T(8,128)(2,1)S(1)}, bf16[16,4096]{1,0:T(8,128)(2,1)S(1)}, u32[]{:S(2)}, u32[]{:S(2)}) %collective-permute-start.4) | collective-permute-done | bytes 131104 | tf_op jit(solution)/shard_map/ppermute | solution.py:23
  48.5 0.0 copy-done.6
  48.5 2.4 %fusion = (f32[16,4096]{1,0:T(8,128)S(1)}, f32[16,4096]{1,0:T(8,128)S(1)}) fusion(f32[16,8192]{1,0:T(8,128)S(1)} %copy-done, s32[]{:T(128)S(6)} %select_n.27, f32[]{:T(128)} %bitcast.1, pred[]{:T(512)S(6)} %eq.3, f32[16,4096]{1,0:T(8,128)} %collective-permute-done.1, f32[16,4096]{1,0:T(8,128)S(1)} %copy-done.6, ...), kind=kLoop, calls=%fused_computation.6 | loop fusion | flops 851968 | bytes 1572877 | tf_op jit(solution)/shard_map/jit(_where)/select_n | solution.py:541
  50.9 1.5 %collective-permute-start.5 = (f32[16,4096]{1,0:T(8,128)S(1)}, f32[16,4096]{1,0:T(8,128)S(1)}, u32[]{:S(2)}, u32[]{:S(2)}) collective-permute-start(f32[16,4096]{1,0:T(8,128)S(1)} %get-tuple-element.28), channel_id=1, source_target_pairs={{0,1},{1,0},{2,3},{3,2},{4,5},{5,4},{6,7},{7,6},{8,9},{9,8},{10,11... | collective-permute-start | bytes 786440 | tf_op jit(solution)/shard_map/ppermute | solution.py:27
  52.4 1.2 %collective-permute-done.5.got_ref = f32[16,4096]{1,0:T(8,128)S(1)} collective-permute-done((f32[16,4096]{1,0:T(8,128)S(1)}, f32[16,4096]{1,0:T(8,128)S(1)}, u32[]{:S(2)}, u32[]{:S(2)}) %collective-permute-start.5) | collective-permute-done | bytes 262176 | tf_op jit(solution)/shard_map/ppermute | solution.py:27
  53.6 0.0 slice-done
  53.6 0.0 slice-done.1
  53.6 0.0 copy-done.7
  53.6 0.0 copy-done.3
  53.6 9.8 %far_part.1 = (bf16[128,8192]{1,0:T(8,128)(2,1)}, bf16[128,8192]{1,0:T(8,128)(2,1)}) custom-call(f32[79,8,128]{2,1,0:T(8,128)S(1)} %get-tuple-element.15.masks, f32[64,136,128]{2,1,0:T(8,128)S(1)} %bitcast.7, f32[16,4096]{1,0:T(8,128)S(1)} %get-tuple-element.29.mine_ref, f32[16,4096]{1,0:T(8,128)S(1)} %collective-permute-done.5.got_ref, ...), custom_call_target="tpu_custom_call" | custom-call | flops 58982400 | bytes 18874368 | tf_op jit(solution)/shard_map/far_part/pallas_call | solution.py:563
  (1 shorter events, 0.0 us)
Async XLA Ops:
  0.6 5.1 %copy-start.4 = (f32[3,3,8192]{2,1,0:T(4,128)S(1)}, f32[3,3,8192]{2,1,0:T(4,128)}, u32[]{:S(2)}) copy-start(f32[3,3,8192]{2,1,0:T(4,128)} %taps_ref.5) | copy-start | bytes 884740
  1.8 9.3 %copy-start = (f32[16,8192]{1,0:T(8,128)S(1)}, f32[16,8192]{1,0:T(8,128)}, u32[]{:S(2)}) copy-start(f32[16,8192]{1,0:T(8,128)} %rate_ref.7) | copy-start | bytes 1572868
  1.9 9.3 %collective-permute-start = (bf16[3,2,8192]{2,1,0:T(2,128)(2,1)S(1)}, bf16[3,2,8192]{2,1,0:T(2,128)(2,1)S(1)}, u32[]{:S(2)}, u32[]{:S(2)}) collective-permute-start(bf16[3,2,8192]{2,1,0:T(2,128)(2,1)S(1)} %tails.1), channel_id=1, source_target_pairs={{0,1},{1,2},{2,3},{3,4},{4,5},{5,6},{6,7},{7,8},{8,9},{9,10},{10,1... | collective-permute-start | bytes 294920 | tf_op jit(solution)/shard_map/ppermute | solution.py:23
  9.1 2.0 %copy-start.2 = (f32[128,8192]{1,0:T(8,128)}, f32[128,8192]{1,0:T(8,128)S(1)}, u32[]{:S(2)}) copy-start(f32[128,8192]{1,0:T(8,128)S(1)} %get-tuple-element.27.short_ref) | copy-start | bytes 12582916
  22.9 2.1 %copy-start.1 = (f32[64,136,128]{2,1,0:T(8,128)}, f32[64,136,128]{2,1,0:T(8,128)S(1)}, u32[]{:S(2)}) copy-start(f32[64,136,128]{2,1,0:T(8,128)S(1)} %get-tuple-element.18.state_ref) | copy-start | bytes 13369348
  25.0 0.7 %copy-start.5 = (f32[16,4096]{1,0:T(8,128)}, f32[16,4096]{1,0:T(8,128)S(1)}, u32[]{:S(2)}) copy-start(f32[16,4096]{1,0:T(8,128)S(1)} %get-tuple-element.20) | copy-start | bytes 786436
  25.7 1.9 %collective-permute-start.1 = (f32[16,4096]{1,0:T(8,128)}, f32[16,4096]{1,0:T(8,128)}, u32[]{:S(2)}, u32[]{:S(2)}) collective-permute-start(f32[16,4096]{1,0:T(8,128)} %get-tuple-element.19), channel_id=1, source_target_pairs={{0,1},{1,0},{2,3},{3,2},{4,5},{5,4},{6,7},{7,6},{8,9},{9,8},{10,11... | collective-permute-start | bytes 786440 | tf_op jit(solution)/shard_map/ppermute | solution.py:27
  29.3 10.0 %collective-permute-start.3 = (bf16[16,4096]{1,0:T(8,128)(2,1)S(1)}, bf16[16,4096]{1,0:T(8,128)(2,1)S(1)}, u32[]{:S(2)}, u32[]{:S(2)}) collective-permute-start(bf16[16,4096]{1,0:T(8,128)(2,1)S(1)} %add_convert_fusion.1), channel_id=1, source_target_pairs={{0,4},{1,5},{2,6},{3,7},{4,8},{5,9},{6,10},{7,11},{8,12},{9,13},{1... | collective-permute-start | bytes 393224 | tf_op jit(solution)/shard_map/ppermute | solution.py:23
  32.5 8.3 %collective-permute-start.2 = (bf16[16,4096]{1,0:T(8,128)(2,1)S(1)}, bf16[16,4096]{1,0:T(8,128)(2,1)S(1)}, u32[]{:S(2)}, u32[]{:S(2)}) collective-permute-start(bf16[16,4096]{1,0:T(8,128)(2,1)S(1)} %add_convert_fusion.1), channel_id=1, source_target_pairs={{0,2},{1,3},{2,4},{3,5},{4,6},{5,7},{6,8},{7,9},{8,10},{9,11},{10,... | collective-permute-start | bytes 393224 | tf_op jit(solution)/shard_map/ppermute | solution.py:23
  40.8 12.8 %slice-start = ((s8[4456448]{0:T(1024)(128)(4,1)}), s8[4194304]{0:T(1024)(128)(4,1)S(1)}, s32[]{:S(2)}) async-start(s8[4456448]{0:T(1024)(128)(4,1)} %bitcast.6), calls=%async_computation | async-start | bytes 8388608
  41.7 6.8 %copy-start.6 = (f32[16,4096]{1,0:T(8,128)S(1)}, f32[16,4096]{1,0:T(8,128)}, u32[]{:S(2)}) copy-start(f32[16,4096]{1,0:T(8,128)} %copy-done.5) | copy-start | bytes 786436
  41.7 11.9 %slice-start.1 = ((s8[4456448]{0:T(1024)(128)(4,1)}), s8[262144]{0:T(1024)(128)(4,1)S(1)}, s32[]{:S(2)}) async-start(s8[4456448]{0:T(1024)(128)(4,1)} %bitcast.6), calls=%async_computation.1 | async-start | bytes 524288
  41.7 11.9 %copy-start.7 = (f32[8192]{0:T(1024)S(1)}, f32[8192]{0:T(1024)}, u32[]{:S(2)}) copy-start(f32[8192]{0:T(1024)} %param.17) | copy-start | bytes 98308
  41.7 6.7 %collective-permute-start.4 = (bf16[16,4096]{1,0:T(8,128)(2,1)S(1)}, bf16[16,4096]{1,0:T(8,128)(2,1)S(1)}, u32[]{:S(2)}, u32[]{:S(2)}) collective-permute-start(bf16[16,4096]{1,0:T(8,128)(2,1)S(1)} %add_convert_fusion), channel_id=1, source_target_pairs={{0,4},{1,5},{2,6},{3,7},{4,8},{5,9},{6,10},{7,11},{8,12},{9,13},{1... | collective-permute-start | bytes 393224 | tf_op jit(solution)/shard_map/ppermute | solution.py:23
  44.1 9.5 %copy-start.3 = (f32[128,8192]{1,0:T(8,128)S(1)}, f32[128,8192]{1,0:T(8,128)}, u32[]{:S(2)}) copy-start(f32[128,8192]{1,0:T(8,128)} %copy-done.2) | copy-start | bytes 12582916
  50.9 2.7 %collective-permute-start.5 = (f32[16,4096]{1,0:T(8,128)S(1)}, f32[16,4096]{1,0:T(8,128)S(1)}, u32[]{:S(2)}, u32[]{:S(2)}) collective-permute-start(f32[16,4096]{1,0:T(8,128)S(1)} %get-tuple-element.28), channel_id=1, source_target_pairs={{0,1},{1,0},{2,3},{3,2},{4,5},{5,4},{6,7},{7,6},{8,9},{9,8},{10,11... | collective-permute-start | bytes 786440 | tf_op jit(solution)/shard_map/ppermute | solution.py:27

commit v12 on v11

--- a/solution.py
+++ b/solution.py
@@ -316,6 +316,43 @@
                 short_ref[pl.ds(j * SUBS, SUBS), cols_of(lane)] = convs[slot].step(j, keep_one, keep_two)
 
     each_chunk(chans, chunk, lambda c: fetch(c).wait(), group, lambda c: None, most)
+
+
+def pair_rates(rate_ref, count):
+    parity = lax.rem(lax.axis_index("ctx"), 2)
+    return parity, rate_ref[:, pl.ds(pl.multiple_of(parity * count, LANES), count)]
+
+
+def early_late(parity, own, got):
+    odd = jnp.full(own.shape, parity, jnp.int32) == 1
+    return jnp.where(odd, got, own), jnp.where(odd, own, got)
+
+
+def leap(masks, index, rate, rows):
+    return jnp.exp(-float(rows) * rate) * masks[index][0:1, 0:1]
+
+
+def pair_kernel(masks, own_ref, got_ref, rate_ref, end_ref, *, rows, index):
+    parity, rate = pair_rates(rate_ref, own_ref.shape[1])
+    early, late = early_late(parity, own_ref[...], got_ref[...])
+    end_ref[...] = (late + leap(masks, index, rate, rows) * early).astype(bf16)
+
+
+def reach_kernel(masks, near_ref, far_ref, rate_ref, enter_ref, *, rows, index):
+    _, rate = pair_rates(rate_ref, near_ref.shape[1])
+    enter_ref[...] = (near_ref[...].astype(f32) + leap(masks, index, rate, rows) * far_ref[...].astype(f32)).astype(bf16)
+
+
+def enter_kernel(
+    masks, near_ref, far_ref, own_ref, got_ref, rate_ref, mine_ref, give_ref, *, rows, index, block, block_index
+):
+    parity, rate = pair_rates(rate_ref, own_ref.shape[1])
+    first = near_ref[...].astype(f32) + leap(masks, index, rate, rows) * far_ref[...].astype(f32)
+    early, _ = early_late(parity, own_ref[...], got_ref[...])
+    second = early + leap(masks, block_index, rate, block) * first
+    give, mine = early_late(parity, second, first)
+    mine_ref[...] = mine
+    give_ref[...] = give
 
 
 def final_kernel(
@@ -518,27 +555,41 @@
 
     got = swap(give, "ctx")
 
-    odd = lax.rem(ctx_index, 2) == 1
-    few_rates = lax.dynamic_slice_in_dim(decay_rate, lax.rem(ctx_index, 2) * half.shape[1], half.shape[1], 1)
     at = Masks(span)
 
-    def leap(rows, index):
-        return jnp.exp(-float(rows) * few_rates) * masks[index, 0, 0]
-
-    early, late = jnp.where(odd, got, own), jnp.where(odd, own, got)
-    ends = (late + leap(tok_rows, at.late) * early).astype(bf16)
+    def pair_call(kernel, operands, out_shape, name, **static):
+        return pl.pallas_call(
+            functools.partial(kernel, **static),
+            in_specs=[vmem] * (len(operands) + 2),
+            out_specs=[vmem] * len(out_shape),
+            out_shape=out_shape,
+            compiler_params=params,
+            name=name,
+        )(near_by(masks), *[near_by(x) for x in operands], rates)
+
+    sent, kept = pltpu.VMEM(half.shape, bf16), pltpu.VMEM(half.shape, f32)
+    ends = pair_call(pair_kernel, [own, got], [sent], "pair_ends", rows=tok_rows, index=at.late)[0]
     one_on, two_on = from_behind(ends, "ctx", 2), from_behind(ends, "ctx", 4)
     near = near_piece(0, None)
     one_on, two_on, near = lax.optimization_barrier((one_on, two_on, near))
     enter, on = one_on, two_on
     for m in range(reaches - 1):
-        enter = (enter.astype(f32) + leap(2 * tok_rows << m, at.reach + m) * on.astype(f32)).astype(bf16)
+        enter = pair_call(
+            reach_kernel, [enter, on], [sent], "reach_%d" % m, rows=2 * tok_rows << m, index=at.reach + m
+        )[0]
         on = from_behind(enter, "ctx", 4 << m)
     near = near_piece(1, near)
     on, near = lax.optimization_barrier((on, near))
-    first = enter.astype(f32) + leap(2 * tok_rows << (reaches - 1), at.reach + reaches - 1) * on.astype(f32)
-    second = early + leap(tok_rows, at.early) * first
-    mine, give_back = jnp.where(odd, second, first), jnp.where(odd, first, second)
+    mine, give_back = pair_call(
+        enter_kernel,
+        [enter, on, own, got],
+        [kept, kept],
+        "pair_enter",
+        rows=2 * tok_rows << (reaches - 1),
+        index=at.reach + reaches - 1,
+        block=tok_rows,
+        block_index=at.early,
+    )
     got_back = swap(give_back, "ctx")
 
     alone = grp == 1

time: 63.8 us -> 54.6 us (0.86)
  other arithmetic: 6.41 us -> 0.32 us
  local copies, waits for them, and re-layouts: 5.4 us -> 0.02 us
  starting transfers between devices: 14 us -> 16.3 us
    unnamed x20 -> x8, local copies, waits for them, and re-layouts: 4.8 us -> 0.02 us
    convert_element_type x2 -> x0, other arithmetic: 2.64 us -> none  [the longest x1 1.73 us: shards(): ends = (late + leap(tok_rows, at.late) * early).astype(bf16)]
    ppermute x2, starting transfers between devices: 1.54 us -> 4.02 us  [swap(): lax.ppermute(shard, axis, [(i, i ^ 1) for i in range(lax.axis_size(axis))])]
    select_n x1 -> x0, other arithmetic: 2.42 us -> none  [shards(): jnp.where(odd, first, second)]
    mul x1, other arithmetic: 1.36 us -> 0.32 us  [shards(): weight = residues * jnp.sqrt(-jnp.expm1(-2.0 * decay_rate))]
  transfers between devices with their start and end apart: 6 -> 6, of which waited for: 4 -> 4; matrix products, arithmetic and copies ran while one was open for 3% -> 1% of each run, Pallas kernels for 13% -> 15%
where the time goes in v12:
time: 54.6 us; the launch traced here: 54.3 us
  Pallas kernels  31 us (57%)
  starting transfers between devices  16.3 us (30%)
  waiting for transfers between devices  5.79 us (11%)
  between operations  0.8 us (1%)
    ppermute x4, starting transfers between devices, from_behind(): return lax.ppermute(shard, axis, pairs)  12.3 us
    pallas_call x1, Pallas kernels, shards(): pl.pallas_call(functools.partial(state_kernel, span=span, modes=modes, mo...  11.3 us
    pallas_call x1, Pallas kernels, shards(): pl.pallas_call(functools.partial(final_kernel, span=span, modes=modes, ch...  9.83 us
    pallas_call x2, Pallas kernels, near_piece(): pl.pallas_call(functools.partial(near_kernel, span=span, modes=modes, mos...  4.67 us
    ppermute x2, starting transfers between devices, swap(): lax.ppermute(shard, axis, [(i, i ^ 1) for i in range(lax.axis_size(axis))])  4.02 us
    ppermute x4, waiting for transfers between devices, from_behind(): return lax.ppermute(shard, axis, pairs)  3.47 us
    pallas_call x1, Pallas kernels, shards(): pl.pallas_call(functools.partial(query_kernel, span=span, most=Q_TILES, c...  3.42 us
    ppermute x2, waiting for transfers between devices, swap(): lax.ppermute(shard, axis, [(i, i ^ 1) for i in range(lax.axis_size(axis))])  2.32 us
  transfers between devices with their start and end apart: 6, of which 4 were waited for; matrix products, arithmetic and copies ran while one was open for 1% of the time, Pallas kernels for 15%

profile of v12, /device:TPU:9, one launch (start us, length us, event | category | flops | bytes accessed | tf_op | source)
XLA Modules:
  0.0 54.3 jit_solution(17672369879445959676)
XLA Ops:
  0.6 0.0 copy-start.1
  0.6 1.2 %tails.1 = bf16[3,2,8192]{2,1,0:T(2,128)(2,1)S(1)} custom-call(bf16[128,8192]{1,0:T(8,128)(2,1)} %query_ref.3, bf16[128,8192]{1,0:T(8,128)(2,1)} %key_ref.3, bf16[128,8192]{1,0:T(8,128)(2,1)} %value_ref.3), custom_call_target="tpu_custom_call" | custom-call | tf_op jit(solution)/shard_map/tails/pallas_call | solution.py:484
  1.8 0.0 copy-start
  1.9 3.8 %collective-permute-start = (bf16[3,2,8192]{2,1,0:T(2,128)(2,1)S(1)}, bf16[3,2,8192]{2,1,0:T(2,128)(2,1)S(1)}, u32[]{:S(2)}, u32[]{:S(2)}) collective-permute-start(bf16[3,2,8192]{2,1,0:T(2,128)(2,1)S(1)} %tails.1), channel_id=1, source_target_pairs={{0,1},{1,2},{2,3},{3,4},{4,5},{5,6},{6,7},{7,8},{8,9},{9,10},{10,1... | collective-permute-start | bytes 294920 | tf_op jit(solution)/shard_map/ppermute | solution.py:23
  5.7 0.0 copy-done.1
  5.7 3.4 %query_part.1 = (f32[128,8192]{1,0:T(8,128)S(1)}, f32[79,8,128]{2,1,0:T(8,128)S(1)}) custom-call(s32[1]{0:T(128)} %bitcast.base_ref, s32[16]{0:T(128)} %len_ref.1, bf16[128,8192]{1,0:T(8,128)(2,1)} %query_ref.3, f32[3,3,8192]{2,1,0:T(4,128)S(1)} %copy-done.1), custom_call_target="tpu_custom_call" | custom-call | flops 13107200 | bytes 6291456 | tf_op jit(solution)/shard_map/query_part/pallas_call | solution.py:496
  9.1 0.0 collective-permute-done.rim_ref
  9.1 0.0 copy-done
  9.1 0.0 copy-start.3
  9.2 11.3 %block_states.1 = (bf16[128,8192]{1,0:T(8,128)(2,1)S(1)}, f32[64,136,128]{2,1,0:T(8,128)S(1)}, f32[16,4096]{1,0:T(8,128)S(1)}, f32[16,4096]{1,0:T(8,128)S(1)}) custom-call(f32[79,8,128]{2,1,0:T(8,128)S(1)} %get-tuple-element.17.masks, bf16[128,8192]{1,0:T(8,128)(2,1)} %key_ref.3, bf16[128,8192]{1,0:T(8,128)(2,1)} %value_ref.3, ...), custom_call_target="tpu_custom_call" | custom-call | flops 65536000 | bytes 12582912 | tf_op jit(solution)/shard_map/block_states/pallas_call | solution.py:512
  20.5 1.3 %collective-permute-start.1 = (f32[16,4096]{1,0:T(8,128)S(1)}, f32[16,4096]{1,0:T(8,128)S(1)}, u32[]{:S(2)}, u32[]{:S(2)}) collective-permute-start(f32[16,4096]{1,0:T(8,128)S(1)} %get-tuple-element.22), channel_id=1, source_target_pairs={{0,1},{1,0},{2,3},{3,2},{4,5},{5,4},{6,7},{7,6},{8,9},{9,8},{10,11... | collective-permute-start | bytes 786440 | tf_op jit(solution)/shard_map/ppermute | solution.py:27
  21.8 1.2 %collective-permute-done.1.got_ref = f32[16,4096]{1,0:T(8,128)S(1)} collective-permute-done((f32[16,4096]{1,0:T(8,128)S(1)}, f32[16,4096]{1,0:T(8,128)S(1)}, u32[]{:S(2)}, u32[]{:S(2)}) %collective-permute-start.1) | collective-permute-done | bytes 262176 | tf_op jit(solution)/shard_map/ppermute | solution.py:27
  22.9 0.2 pair_ends.1
  23.1 2.3 %collective-permute-start.3 = (bf16[16,4096]{1,0:T(8,128)(2,1)S(1)}, bf16[16,4096]{1,0:T(8,128)(2,1)S(1)}, u32[]{:S(2)}, u32[]{:S(2)}) collective-permute-start(bf16[16,4096]{1,0:T(8,128)(2,1)S(1)} %pair_ends.1), channel_id=1, source_target_pairs={{0,4},{1,5},{2,6},{3,7},{4,8},{5,9},{6,10},{7,11},{8,12},{9,13},{1... | collective-permute-start | bytes 393224 | tf_op jit(solution)/shard_map/ppermute | solution.py:23
  25.4 3.1 %collective-permute-start.2 = (bf16[16,4096]{1,0:T(8,128)(2,1)S(1)}, bf16[16,4096]{1,0:T(8,128)(2,1)S(1)}, u32[]{:S(2)}, u32[]{:S(2)}) collective-permute-start(bf16[16,4096]{1,0:T(8,128)(2,1)S(1)} %pair_ends.1), channel_id=1, source_target_pairs={{0,2},{1,3},{2,4},{3,5},{4,6},{5,7},{6,8},{7,9},{8,10},{9,11},{10,... | collective-permute-start | bytes 393224 | tf_op jit(solution)/shard_map/ppermute | solution.py:23
  28.5 0.0 copy-done.3
  28.5 0.3 sqrt_multiply_fusion.weight_ref
  28.9 2.3 %near_part_0.1.refs_0_ = f32[128,8192]{1,0:T(8,128)S(1)} custom-call(f32[79,8,128]{2,1,0:T(8,128)S(1)} %get-tuple-element.17.masks, bf16[128,8192]{1,0:T(8,128)(2,1)S(1)} %get-tuple-element.23.gate_ref, f32[16,8192]{1,0:T(8,128)S(1)} %copy-done, f32[16,8192]{1,0:T(8,128)S(1)} %sqrt_multiply_fusion.weight_ref), custom_call_target="tpu_custom_call" | custom-call | flops 19660800 | bytes 3670016 | tf_op jit(solution)/shard_map/near_part_0/pallas_call | solution.py:539
  31.2 0.0 collective-permute-done.3.far_ref
  31.2 2.3 %collective-permute-done.2.near_ref = bf16[16,4096]{1,0:T(8,128)(2,1)S(1)} collective-permute-done((bf16[16,4096]{1,0:T(8,128)(2,1)S(1)}, bf16[16,4096]{1,0:T(8,128)(2,1)S(1)}, u32[]{:S(2)}, u32[]{:S(2)}) %collective-permute-start.2) | collective-permute-done | bytes 131104 | tf_op jit(solution)/shard_map/ppermute | solution.py:23
  33.5 0.1 reach_0.1.near_ref
  33.6 0.0 copy-start.2
  33.6 3.1 %collective-permute-start.4 = (bf16[16,4096]{1,0:T(8,128)(2,1)S(1)}, bf16[16,4096]{1,0:T(8,128)(2,1)S(1)}, u32[]{:S(2)}, u32[]{:S(2)}) collective-permute-start(bf16[16,4096]{1,0:T(8,128)(2,1)S(1)} %reach_0.1.near_ref), channel_id=1, source_target_pairs={{0,4},{1,5},{2,6},{3,7},{4,8},{5,9},{6,10},{7,11},{8,12},{9,13},{1... | collective-permute-start | bytes 393224 | tf_op jit(solution)/shard_map/ppermute | solution.py:23
  36.7 2.3 %near_part_1.1.near_ref = f32[128,8192]{1,0:T(8,128)S(1)} custom-call(f32[79,8,128]{2,1,0:T(8,128)S(1)} %get-tuple-element.17.masks, bf16[128,8192]{1,0:T(8,128)(2,1)S(1)} %get-tuple-element.23.gate_ref, f32[16,8192]{1,0:T(8,128)S(1)} %copy-done, f32[16,8192]{1,0:T(8,128)S(1)} %sqrt_multiply_fusion.weight_ref, ...), custom_call_target="tpu_custom_call", output_to_operand_aliasing={{}: (4, {})} | custom-call | flops 19660800 | bytes 3670016 | tf_op jit(solution)/shard_map/near_part_1/pallas_call | solution.py:539
  39.1 1.2 %collective-permute-done.4.far_ref = bf16[16,4096]{1,0:T(8,128)(2,1)S(1)} collective-permute-done((bf16[16,4096]{1,0:T(8,128)(2,1)S(1)}, bf16[16,4096]{1,0:T(8,128)(2,1)S(1)}, u32[]{:S(2)}, u32[]{:S(2)}) %collective-permute-start.4) | collective-permute-done | bytes 131104 | tf_op jit(solution)/shard_map/ppermute | solution.py:23
  40.3 0.3 pair_enter.1
  40.5 2.7 %collective-permute-start.5 = (f32[16,4096]{1,0:T(8,128)S(1)}, f32[16,4096]{1,0:T(8,128)S(1)}, u32[]{:S(2)}, u32[]{:S(2)}) collective-permute-start(f32[16,4096]{1,0:T(8,128)S(1)} %get-tuple-element.29), channel_id=1, source_target_pairs={{0,1},{1,0},{2,3},{3,2},{4,5},{5,4},{6,7},{7,6},{8,9},{9,8},{10,11... | collective-permute-start | bytes 786440 | tf_op jit(solution)/shard_map/ppermute | solution.py:27
  43.3 1.2 %collective-permute-done.5.got_ref = f32[16,4096]{1,0:T(8,128)S(1)} collective-permute-done((f32[16,4096]{1,0:T(8,128)S(1)}, f32[16,4096]{1,0:T(8,128)S(1)}, u32[]{:S(2)}, u32[]{:S(2)}) %collective-permute-start.5) | collective-permute-done | bytes 262176 | tf_op jit(solution)/shard_map/ppermute | solution.py:27
  44.4 0.0 copy-done.2
  44.4 9.8 %far_part.1 = (bf16[128,8192]{1,0:T(8,128)(2,1)}, bf16[128,8192]{1,0:T(8,128)(2,1)}) custom-call(f32[79,8,128]{2,1,0:T(8,128)S(1)} %get-tuple-element.17.masks, f32[64,136,128]{2,1,0:T(8,128)S(1)} %get-tuple-element.20.state_ref, f32[16,4096]{1,0:T(8,128)S(1)} %get-tuple-element.28.mine_ref, f32[16,4096]{1,0:T(8,128)S(1)} %collective-permute-done.5.got_ref, ...), custom_call_target="tpu_custom_call" | custom-call | flops 58982400 | bytes 18874368 | tf_op jit(solution)/shard_map/far_part/pallas_call | solution.py:614
Async XLA Ops:
  0.6 5.1 %copy-start.1 = (f32[3,3,8192]{2,1,0:T(4,128)S(1)}, f32[3,3,8192]{2,1,0:T(4,128)}, u32[]{:S(2)}) copy-start(f32[3,3,8192]{2,1,0:T(4,128)} %taps_ref.5) | copy-start | bytes 884740
  1.8 7.3 %copy-start = (f32[16,8192]{1,0:T(8,128)S(1)}, f32[16,8192]{1,0:T(8,128)}, u32[]{:S(2)}) copy-start(f32[16,8192]{1,0:T(8,128)} %rate_ref.13) | copy-start | bytes 1572868
  1.9 7.3 %collective-permute-start = (bf16[3,2,8192]{2,1,0:T(2,128)(2,1)S(1)}, bf16[3,2,8192]{2,1,0:T(2,128)(2,1)S(1)}, u32[]{:S(2)}, u32[]{:S(2)}) collective-permute-start(bf16[3,2,8192]{2,1,0:T(2,128)(2,1)S(1)} %tails.1), channel_id=1, source_target_pairs={{0,1},{1,2},{2,3},{3,4},{4,5},{5,6},{6,7},{7,8},{8,9},{9,10},{10,1... | collective-permute-start | bytes 294920 | tf_op jit(solution)/shard_map/ppermute | solution.py:23
  9.1 19.4 %copy-start.3 = (f32[16,8192]{1,0:T(8,128)S(1)}, f32[16,8192]{1,0:T(8,128)}, u32[]{:S(2)}) copy-start(f32[16,8192]{1,0:T(8,128)} %param.14) | copy-start | bytes 1572868
  20.5 2.5 %collective-permute-start.1 = (f32[16,4096]{1,0:T(8,128)S(1)}, f32[16,4096]{1,0:T(8,128)S(1)}, u32[]{:S(2)}, u32[]{:S(2)}) collective-permute-start(f32[16,4096]{1,0:T(8,128)S(1)} %get-tuple-element.22), channel_id=1, source_target_pairs={{0,1},{1,0},{2,3},{3,2},{4,5},{5,4},{6,7},{7,6},{8,9},{9,8},{10,11... | collective-permute-start | bytes 786440 | tf_op jit(solution)/shard_map/ppermute | solution.py:27
  23.1 8.1 %collective-permute-start.3 = (bf16[16,4096]{1,0:T(8,128)(2,1)S(1)}, bf16[16,4096]{1,0:T(8,128)(2,1)S(1)}, u32[]{:S(2)}, u32[]{:S(2)}) collective-permute-start(bf16[16,4096]{1,0:T(8,128)(2,1)S(1)} %pair_ends.1), channel_id=1, source_target_pairs={{0,4},{1,5},{2,6},{3,7},{4,8},{5,9},{6,10},{7,11},{8,12},{9,13},{1... | collective-permute-start | bytes 393224 | tf_op jit(solution)/shard_map/ppermute | solution.py:23
  25.4 8.1 %collective-permute-start.2 = (bf16[16,4096]{1,0:T(8,128)(2,1)S(1)}, bf16[16,4096]{1,0:T(8,128)(2,1)S(1)}, u32[]{:S(2)}, u32[]{:S(2)}) collective-permute-start(bf16[16,4096]{1,0:T(8,128)(2,1)S(1)} %pair_ends.1), channel_id=1, source_target_pairs={{0,2},{1,3},{2,4},{3,5},{4,6},{5,7},{6,8},{7,9},{8,10},{9,11},{10,... | collective-permute-start | bytes 393224 | tf_op jit(solution)/shard_map/ppermute | solution.py:23
  33.6 10.8 %copy-start.2 = (f32[8192]{0:T(1024)S(1)}, f32[8192]{0:T(1024)}, u32[]{:S(2)}) copy-start(f32[8192]{0:T(1024)} %param.17) | copy-start | bytes 98308
  33.6 6.6 %collective-permute-start.4 = (bf16[16,4096]{1,0:T(8,128)(2,1)S(1)}, bf16[16,4096]{1,0:T(8,128)(2,1)S(1)}, u32[]{:S(2)}, u32[]{:S(2)}) collective-permute-start(bf16[16,4096]{1,0:T(8,128)(2,1)S(1)} %reach_0.1.near_ref), channel_id=1, source_target_pairs={{0,4},{1,5},{2,6},{3,7},{4,8},{5,9},{6,10},{7,11},{8,12},{9,13},{1... | collective-permute-start | bytes 393224 | tf_op jit(solution)/shard_map/ppermute | solution.py:23
  40.5 3.9 %collective-permute-start.5 = (f32[16,4096]{1,0:T(8,128)S(1)}, f32[16,4096]{1,0:T(8,128)S(1)}, u32[]{:S(2)}, u32[]{:S(2)}) collective-permute-start(f32[16,4096]{1,0:T(8,128)S(1)} %get-tuple-element.29), channel_id=1, source_target_pairs={{0,1},{1,0},{2,3},{3,2},{4,5},{5,4},{6,7},{7,6},{8,9},{9,8},{10,11... | collective-permute-start | bytes 786440 | tf_op jit(solution)/shard_map/ppermute | solution.py:27

commit v13 on v12

--- a/solution.py
+++ b/solution.py
@@ -107,11 +107,9 @@
         return self.taps[0] * here + (self.taps[1] * one) * keep_one + (self.taps[2] * two) * keep_two
 
 
-def half_of(chans, lane):
-    half = chans // 2
-    which = lax.div(lane, half)
-    mine = which == lax.rem(lax.axis_index("ctx"), 2)
-    return mine, pl.multiple_of(lane - which * half, LANES)
+def half_start(chans, own):
+    parity = lax.rem(lax.axis_index("ctx"), 2)
+    return pl.multiple_of((parity if own else 1 - parity) * (chans // 2), LANES)
 
 
 def twice(mask, modes):
@@ -123,26 +121,17 @@
 
 
 def state_kernel(
-    masks, key_ref, value_ref, rim_ref, taps_ref, rate_ref,
-    gate_ref, state_ref, own_ref, give_ref,
-    key_buf, value_buf, sems, wide_k, wide_v, tables, held,
-    *, span, modes, most, chunk,
+    masks, key_ref, value_ref, rim_ref, taps_ref, rate_ref, *refs, span, modes, most, own
 ):
-    chans = key_buf.shape[1]
-
-    def fetches(c):
-        return [cols_copy(key_ref, key_buf, sems.at[0], c, chunk), cols_copy(value_ref, value_buf, sems.at[1], c, chunk)]
-
-    for c in range(chans // chunk):
-        for copy in fetches(c):
-            copy.start()
-
+    gate_ref, state_ref, end_ref, wide_k, wide_v, tables, held = refs[-7:]
+    half = key_ref.shape[1] // 2
+    first = half_start(2 * half, own)
     at = Masks(span)
 
     def group(lanes):
         for slot, lane in enumerate(lanes):
-            spread(key_buf[:, cols_of(lane)], wide_k.at[slot], span)
-            spread(value_buf[:, cols_of(lane)], wide_v.at[slot], span)
+            spread(key_ref[:, cols_of(lane)], wide_k.at[slot], span)
+            spread(value_ref[:, cols_of(lane)], wide_v.at[slot], span)
             rate = rate_ref[:, cols_of(lane)]
             tables[slot] = jnp.exp(-rate)
         convs = [
@@ -178,21 +167,9 @@
             end = sub_state(state_ref, lane, 0, modes)
             for b in range(1, SUBS):
                 end = (leap * twice(masks[at.passes + b], modes)) * end + sub_state(state_ref, lane, b, modes)
-            mine, here = half_of(chans, lane)
-
-            @pl.when(mine)
-            def _():
-                own_ref[:, cols_of(here)] = end
-
-            @pl.when(jnp.logical_not(mine))
-            def _():
-                give_ref[:, cols_of(here)] = end
-
-    def before(c):
-        for copy in fetches(c):
-            copy.wait()
-
-    each_chunk(chans, chunk, before, group, lambda c: None, most)
+            end_ref[:, cols_of(pl.multiple_of(lane - first, LANES))] = end
+
+    each_group(half // LANES, most, lambda lanes: group([pl.multiple_of(first + lane, LANES) for lane in lanes]))
 
 
 def tail_kernel(query_ref, key_ref, value_ref, tail_ref, bufs, sems):
@@ -356,35 +333,34 @@
 
 
 def final_kernel(
-    masks, state_ref, mine_ref, got_ref, near_ref, short_ref, resid_in, rim_ref, taps_ref, rate_ref, weight_ref, gain_ref,
-    *refs,
-    span, modes, channels, most, chunk,
+    masks, state_ref, enter_ref, near_ref, short_ref, resid_ref, rim_ref, taps_ref, rate_ref, weight_ref, *refs,
+    span, modes, channels, most, chunk, own,
 ):
-    if channels:
-        hidden_out, normed_out, resid_ref, hidden_ref, sems, wide, tables, starts_at, sums, whole, normed_ref = refs
+    if own:
+        hidden_out, whole, sums, hidden_ref, sems, wide, tables, starts_at = refs
+    elif channels:
+        gain_ref, _, _, _, hidden_out, whole, sums, normed_out, hidden_ref, sems, wide, tables, starts_at, normed_ref = refs
     else:
-        hidden_out, wide_ref, sum_ref, resid_ref, hidden_ref, sems, wide, tables, starts_at, sums = refs
+        _, _, _, hidden_out, whole, sums, hidden_ref, sems, wide, tables, starts_at = refs
     chans = resid_ref.shape[1]
-
-    def fetch(c):
-        return cols_copy(resid_in, resid_ref, sems.at[0], c, chunk)
+    half = chans // 2
+    first = half_start(chans, own)
+    at = Masks(span)
 
     def store(c):
-        return cols_copy(hidden_ref, hidden_out, sems.at[1], c, chunk)
+        here = pl.ds(pl.multiple_of(c * chunk, chunk), chunk)
+        there = pl.ds(pl.multiple_of(first + c * chunk, chunk), chunk)
+        return pltpu.make_async_copy(hidden_ref.at[:, here], hidden_out.at[:, there], sems.at[0, c])
 
     def store_normed(c):
-        return cols_copy(normed_ref, normed_out, sems.at[2], c, chunk)
-
-    for c in range(chans // chunk):
-        fetch(c).start()
-    at = Masks(span)
-    sums[...] = jnp.zeros(sums.shape, f32)
+        return cols_copy(normed_ref, normed_out, sems.at[1], c, chunk)
+
+    if own:
+        sums[...] = jnp.zeros(sums.shape, f32)
 
     def group(lanes):
         for slot, lane in enumerate(lanes):
-            mine, here = half_of(chans, lane)
-            mine = jnp.full((modes, LANES), mine.astype(jnp.int32), jnp.int32) == 1
-            state = jnp.where(mine, mine_ref[:, cols_of(here)], got_ref[:, cols_of(here)])
+            state = enter_ref[:, cols_of(pl.multiple_of(lane - first, LANES))]
             rate = rate_ref[:, cols_of(lane)]
             weight = weight_ref[:, cols_of(lane)]
             tables[slot] = jnp.exp(-rate)
@@ -418,16 +394,20 @@
             squares = sums[rows, :]
             for slot, lane in enumerate(lanes):
                 hidden = wide[slot, pl.ds(b * (span + 1), span), :] + resid_ref[rows, cols_of(lane)].astype(f32)
-                if channels:
-                    whole[lax.div(lane, LANES), rows, :] = hidden
-                else:
-                    wide_ref[rows, cols_of(lane)] = hidden
-                hidden_ref[rows, cols_of(lane)] = hidden.astype(bf16)
+                whole[lax.div(lane, LANES), rows, :] = hidden
+                hidden_ref[rows, cols_of(pl.multiple_of(lane - first, LANES))] = hidden.astype(bf16)
                 squares = squares + hidden * hidden
             sums[rows, :] = squares
 
-    each_chunk(chans, chunk, lambda c: fetch(c).wait(), group, lambda c: store(c).start(), most)
-    if channels:
+    each_chunk(
+        half,
+        chunk,
+        lambda c: None,
+        lambda lanes: group([pl.multiple_of(first + lane, LANES) for lane in lanes]),
+        lambda c: store(c).start(),
+        most,
+    )
+    if channels and not own:
         inverse = lax.rsqrt(jnp.sum(sums[...], axis=1, keepdims=True) / channels + 1e-06)
         sums[...] = jnp.broadcast_to(inverse, sums.shape)
 
@@ -439,9 +419,7 @@
         each_chunk(chans, chunk, lambda c: None, scale, lambda c: store_normed(c).start(), 4)
         for c in range(chans // chunk):
             store_normed(c).wait()
-    else:
-        sum_ref[...] = sums[...]
-    for c in range(chans // chunk):
+    for c in range(half // chunk):
         store(c).wait()
 
 
@@ -453,7 +431,7 @@
     span = tok_rows // SUBS
     blocks = lax.axis_size("ctx")
     grp = lax.axis_size("grp")
-    chunk = min(chans, 1024)
+    chunk = min(chans // 2, 1024)
     pieces = chans // chunk
     ctx_index = lax.axis_index("ctx")
     base = (ctx_index * tok_rows).astype(jnp.int32).reshape(1)
@@ -462,7 +440,6 @@
     smem = pl.BlockSpec(memory_space=pltpu.SMEM)
     vmem = pl.BlockSpec(memory_space=pltpu.VMEM)
     hbm = pl.BlockSpec(memory_space=pltpu.HBM)
-    half = jax.ShapeDtypeStruct((modes, chans // 2), f32)
     tile_shape = (SUBS, LANES)
     wide_rows = SUBS * (span + 1)
     params = pltpu.CompilerParams(vmem_limit_bytes=16 * MIB)
@@ -509,29 +486,36 @@
     )(base, lengths, far_off(query_in), near_by(short_taps))
     rim_rows, q_short = lax.optimization_barrier((rim_rows, q_short))
     rates, weights, taps, rims = near_by(decay_rate), near_by(weight), near_by(short_taps), near_by(rim_rows)
-    gates, states, own, give = pl.pallas_call(
-        functools.partial(state_kernel, span=span, modes=modes, most=A_TILES, chunk=chunk),
-        in_specs=[vmem, hbm, hbm, vmem, vmem, vmem],
-        out_specs=[vmem, vmem, vmem, vmem],
-        out_shape=[
-            pltpu.VMEM((tok_rows, chans), bf16),
-            pltpu.VMEM((chans // LANES, SUBS * (modes + 1), LANES), f32),
-            pltpu.VMEM(half.shape, f32),
-            pltpu.VMEM(half.shape, f32),
-        ],
-        scratch_shapes=[
-            pltpu.VMEM((tok_rows, chans), bf16),
-            pltpu.VMEM((tok_rows, chans), bf16),
-            copies(2),
-            pltpu.VMEM((A_TILES, wide_rows, LANES), f32),
-            pltpu.VMEM((A_TILES, wide_rows, LANES), f32),
-            pltpu.VMEM((A_TILES, modes, LANES), f32),
-            pltpu.VMEM((A_TILES, span) + tile_shape, f32),
-        ],
-        compiler_params=params,
-        cost_estimate=cost(1000, 12 * tok_rows * chans),
-        name="block_states",
-    )(near_by(masks), far_off(key_in), far_off(value_in), rims, taps, rates)
+    kept = pltpu.VMEM((modes, chans // 2), f32)
+    sent = pltpu.VMEM((modes, chans // 2), bf16)
+    keys, values = near_by(key_in), near_by(value_in)
+
+    def states_of(own, before):
+        return pl.pallas_call(
+            functools.partial(state_kernel, span=span, modes=modes, most=A_TILES, own=own),
+            in_specs=[vmem] * (6 + len(before)),
+            out_specs=[vmem] * 3,
+            out_shape=[
+                pltpu.VMEM((tok_rows, chans), bf16),
+                pltpu.VMEM((chans // LANES, SUBS * (modes + 1), LANES), f32),
+                kept,
+            ],
+            scratch_shapes=[
+                pltpu.VMEM((A_TILES, wide_rows, LANES), f32),
+                pltpu.VMEM((A_TILES, wide_rows, LANES), f32),
+                pltpu.VMEM((A_TILES, modes, LANES), f32),
+                pltpu.VMEM((A_TILES, span) + tile_shape, f32),
+            ],
+            input_output_aliases={6 + i: i for i in range(len(before))},
+            compiler_params=params,
+            cost_estimate=cost(500, 6 * tok_rows * chans),
+            name="block_states_own" if own else "block_states_give",
+        )(near_by(masks), keys, values, rims, taps, rates, *[near_by(x) for x in before])
+
+    gates, states, give = states_of(False, [])
+    got = swap(give, "ctx")
+    gates, states, own = states_of(True, [gates, states])
+    got, gates, states, own = lax.optimization_barrier((got, gates, states, own))
 
     def near_piece(part, near):
         count = chans // NEAR_PARTS
@@ -567,7 +551,6 @@
             name=name,
         )(near_by(masks), *[near_by(x) for x in operands], rates)
 
-    sent, kept = pltpu.VMEM(half.shape, bf16), pltpu.VMEM(half.shape, f32)
     ends = pair_call(pair_kernel, [own, got], [sent], "pair_ends", rows=tok_rows, index=at.late)[0]
     one_on, two_on = from_behind(ends, "ctx", 2), from_behind(ends, "ctx", 4)
     near = near_piece(0, None)
@@ -593,42 +576,55 @@
     got_back = swap(give_back, "ctx")
 
     alone = grp == 1
-    out_specs = [hbm]
-    out_shape = [jax.ShapeDtypeStruct((tok_rows, chans), bf16)]
-    scratch = [
-        pltpu.VMEM((tok_rows, chans), bf16),
-        pltpu.VMEM((tok_rows, chans), bf16),
-        copies(3),
-        pltpu.VMEM((F_TILES, wide_rows, LANES), f32),
-        pltpu.VMEM((F_TILES, modes, LANES), f32),
-        pltpu.VMEM((F_TILES, SUBS * (modes + 1), LANES), f32),
-        pltpu.VMEM((tok_rows, LANES), f32),
-    ]
+    resid = near_by(residual)
+
+    def finish(own, enter, before):
+        last = alone and not own
+        out_specs = [hbm, vmem, vmem]
+        out_shape = [
+            jax.ShapeDtypeStruct((tok_rows, chans), bf16),
+            pltpu.VMEM((chans // LANES, tok_rows, LANES), f32),
+            pltpu.VMEM((tok_rows, LANES), f32),
+        ]
+        scratch = [
+            pltpu.VMEM((tok_rows, chans // 2), bf16),
+            copies(2),
+            pltpu.VMEM((F_TILES, wide_rows, LANES), f32),
+            pltpu.VMEM((F_TILES, modes, LANES), f32),
+            pltpu.VMEM((F_TILES, SUBS * (modes + 1), LANES), f32),
+        ]
+        operands = [near_by(x) for x in (masks, states, enter, near, q_short)] + [resid, rims, taps, rates, weights]
+        if last:
+            operands.append(near_by(norm_gain.reshape(1, chans)))
+            out_specs.append(hbm)
+            out_shape.append(jax.ShapeDtypeStruct((tok_rows, chans), bf16))
+            scratch.append(pltpu.VMEM((tok_rows, chans), bf16))
+        count = len(operands)
+        in_specs = [vmem] * count
+        if before:
+            operands += [far_off(before[0]), near_by(before[1]), near_by(before[2])]
+            in_specs += [hbm, vmem, vmem]
+        return pl.pallas_call(
+            functools.partial(
+                final_kernel, span=span, modes=modes, channels=chans if alone else 0, most=F_TILES, chunk=chunk, own=own
+            ),
+            in_specs=in_specs,
+            out_specs=out_specs,
+            out_shape=out_shape,
+            scratch_shapes=scratch,
+            input_output_aliases={count + i: i for i in range(len(before))},
+            compiler_params=params,
+            cost_estimate=cost(450, 9 * tok_rows * chans),
+            name="far_part_own" if own else "far_part_other",
+        )(*operands)
+
+    before = finish(True, mine, [])
+    got_back, *before = lax.optimization_barrier((got_back, *before))
+    outs = finish(False, got_back, before)
     if alone:
-        out_specs.append(hbm)
-        out_shape.append(jax.ShapeDtypeStruct((tok_rows, chans), bf16))
-        scratch += [pltpu.VMEM((chans // LANES, tok_rows, LANES), f32), pltpu.VMEM((tok_rows, chans), bf16)]
-    else:
-        out_specs += [vmem, vmem]
-        out_shape += [jax.ShapeDtypeStruct((tok_rows, chans), f32), jax.ShapeDtypeStruct((tok_rows, LANES), f32)]
-    outs = pl.pallas_call(
-        functools.partial(
-            final_kernel, span=span, modes=modes, channels=chans if alone else 0, most=F_TILES, chunk=chunk
-        ),
-        in_specs=[vmem, vmem, vmem, vmem, vmem, vmem, hbm, vmem, vmem, vmem, vmem, vmem],
-        out_specs=out_specs,
-        out_shape=out_shape,
-        scratch_shapes=scratch,
-        compiler_params=params,
-        cost_estimate=cost(900, 18 * tok_rows * chans),
-        name="far_part",
-    )(
-        near_by(masks), near_by(states), near_by(mine), near_by(got_back), near_by(near), near_by(q_short), far_off(residual),
-        rims, taps, rates, weights, norm_gain.reshape(1, chans),
-    )
-    if alone:
-        return tuple(outs)
-    hidden_out, hidden, sums = outs
+        return (outs[0], outs[3])
+    hidden_out, whole, sums = outs
+    hidden = whole.transpose(1, 0, 2).reshape(tok_rows, chans)
     square_sum = lax.psum(jnp.sum(sums, axis=1), "grp")
     inverse_rms = lax.rsqrt(square_sum / (chans * grp) + 1e-06)
     normed = (hidden * inverse_rms[:, None] * norm_gain[None, :]).astype(bf16)

time: 54.6 us -> 51.5 us (0.943)
  Pallas kernels: 31 us -> 28.7 us
  waiting for transfers between devices: 5.79 us -> 3.81 us
  local copies, waits for them, and re-layouts: 0.02 us -> 1.61 us
    pallas_call x2 -> x4, Pallas kernels: 21.1 us -> 18.7 us  [the longest x2 9.71 us: finish(): pl.pallas_call(functools.partial(final_kernel, span=span, modes=modes, ch...]
    ppermute x2, waiting for transfers between devices: 2.32 us -> 0.01 us  [swap(): lax.ppermute(shard, axis, [(i, i ^ 1) for i in range(lax.axis_size(axis))])]
    unnamed x8 -> x14, local copies, waits for them, and re-layouts: 0.02 us -> 1.61 us
  transfers between devices with their start and end apart: 6 -> 6, of which waited for: 4 -> 3; matrix products, arithmetic and copies ran while one was open for 1% -> 1% of each run, Pallas kernels for 15% -> 33%
where the time goes in v13:
time: 51.5 us; the launch traced here: 51.2 us
  Pallas kernels  28.7 us (56%)
  starting transfers between devices  16 us (31%)
  waiting for transfers between devices  3.81 us (7%)
  local copies, waits for them, and re-layouts  1.61 us (3%)
  between operations  0.85 us (2%)
    ppermute x4, starting transfers between devices, from_behind(): return lax.ppermute(shard, axis, pairs)  12.2 us
    pallas_call x2, Pallas kernels, finish(): pl.pallas_call(functools.partial(final_kernel, span=span, modes=modes, ch...  9.71 us
    pallas_call x2, Pallas kernels, states_of(): pl.pallas_call(functools.partial(state_kernel, span=span, modes=modes, mo...  9.03 us
    pallas_call x2, Pallas kernels, near_piece(): pl.pallas_call(functools.partial(near_kernel, span=span, modes=modes, mos...  4.67 us
    ppermute x2, starting transfers between devices, swap(): lax.ppermute(shard, axis, [(i, i ^ 1) for i in range(lax.axis_size(axis))])  3.81 us
    ppermute x4, waiting for transfers between devices, from_behind(): return lax.ppermute(shard, axis, pairs)  3.8 us
    pallas_call x1, Pallas kernels, shards(): pl.pallas_call(functools.partial(query_kernel, span=span, most=Q_TILES, c...  3.42 us
    unnamed x14, local copies, waits for them, and re-layouts  1.61 us
  transfers between devices with their start and end apart: 6, of which 3 were waited for; matrix products, arithmetic and copies ran while one was open for 1% of the time, Pallas kernels for 33%

profile of v13, /device:TPU:9, one launch (start us, length us, event | category | flops | bytes accessed | tf_op | source)
XLA Modules:
  0.0 51.2 jit_solution(11470202992213507728)
XLA Ops:
  0.6 0.0 copy-start.3
  0.6 0.0 copy-start.1
  0.6 1.3 %tails.1 = bf16[3,2,8192]{2,1,0:T(2,128)(2,1)S(1)} custom-call(bf16[128,8192]{1,0:T(8,128)(2,1)} %query_ref.3, bf16[128,8192]{1,0:T(8,128)(2,1)} %key_ref.5, bf16[128,8192]{1,0:T(8,128)(2,1)} %value_ref.5), custom_call_target="tpu_custom_call" | custom-call | tf_op jit(solution)/shard_map/tails/pallas_call | solution.py:461
  2.0 0.0 copy-start
  2.0 3.8 %collective-permute-start = (bf16[3,2,8192]{2,1,0:T(2,128)(2,1)S(1)}, bf16[3,2,8192]{2,1,0:T(2,128)(2,1)S(1)}, u32[]{:S(2)}, u32[]{:S(2)}) collective-permute-start(bf16[3,2,8192]{2,1,0:T(2,128)(2,1)S(1)} %tails.1), channel_id=1, source_target_pairs={{0,1},{1,2},{2,3},{3,4},{4,5},{5,6},{6,7},{7,8},{8,9},{9,10},{10,1... | collective-permute-start | bytes 294920 | tf_op jit(solution)/shard_map/ppermute | solution.py:23
  5.8 0.0 copy-done.3
  5.8 3.4 %query_part.1 = (f32[128,8192]{1,0:T(8,128)S(1)}, f32[79,8,128]{2,1,0:T(8,128)S(1)}) custom-call(s32[1]{0:T(128)} %bitcast.base_ref, s32[16]{0:T(128)} %len_ref.1, bf16[128,8192]{1,0:T(8,128)(2,1)} %query_ref.3, f32[3,3,8192]{2,1,0:T(4,128)S(1)} %copy-done.3), custom_call_target="tpu_custom_call" | custom-call | flops 13107200 | bytes 6291456 | tf_op jit(solution)/shard_map/query_part/pallas_call | solution.py:473
  9.2 0.0 collective-permute-done.rim_ref
  9.2 0.0 copy-done.1
  9.3 0.0 copy-done
  9.3 0.0 copy-start.2
  9.3 1.6 %copy-done.2 = bf16[128,8192]{1,0:T(8,128)(2,1)S(1)} copy-done((bf16[128,8192]{1,0:T(8,128)(2,1)S(1)}, bf16[128,8192]{1,0:T(8,128)(2,1)}, u32[]{:S(2)}) %copy-start.2) | copy-done | bytes 2097176
  10.9 4.5 %block_states_give.1 = (bf16[128,8192]{1,0:T(8,128)(2,1)S(1)}, f32[64,136,128]{2,1,0:T(8,128)S(1)}, f32[16,4096]{1,0:T(8,128)S(1)}) custom-call(f32[79,8,128]{2,1,0:T(8,128)S(1)} %get-tuple-element.31.masks, bf16[128,8192]{1,0:T(8,128)(2,1)S(1)} %copy-done.1, bf16[128,8192]{1,0:T(8,128)(2,1)S(1)} %copy-done.2, ...), custom_call_target="tpu_custom_call" | custom-call | flops 32768000 | bytes 6291456 | tf_op jit(solution)/shard_map/block_states_give/pallas_call | solution.py:494
  15.4 1.3 %collective-permute-start.1 = (f32[16,4096]{1,0:T(8,128)S(1)}, f32[16,4096]{1,0:T(8,128)S(1)}, u32[]{:S(2)}, u32[]{:S(2)}) collective-permute-start(f32[16,4096]{1,0:T(8,128)S(1)} %get-tuple-element.34), channel_id=1, source_target_pairs={{0,1},{1,0},{2,3},{3,2},{4,5},{5,4},{6,7},{7,6},{8,9},{9,8},{10,11... | collective-permute-start | bytes 786440 | tf_op jit(solution)/shard_map/ppermute | solution.py:27
  16.7 0.0 copy-start.6
  16.7 4.5 %block_states_own.1 = (bf16[128,8192]{1,0:T(8,128)(2,1)S(1)}, f32[64,136,128]{2,1,0:T(8,128)S(1)}, f32[16,4096]{1,0:T(8,128)S(1)}) custom-call(f32[79,8,128]{2,1,0:T(8,128)S(1)} %get-tuple-element.31.masks, bf16[128,8192]{1,0:T(8,128)(2,1)S(1)} %copy-done.1, bf16[128,8192]{1,0:T(8,128)(2,1)S(1)} %copy-done.2, ...), custom_call_target="tpu_custom_call", output_to_operand_aliasing={{0}: (6, {}), {1}: (7, {})} | custom-call | flops 32768000 | bytes 6291456 | tf_op jit(solution)/shard_map/block_states_own/pallas_call | solution.py:494
  21.2 0.0 collective-permute-done.1.got_ref
  21.2 0.2 pair_ends.1
  21.4 2.2 %collective-permute-start.3 = (bf16[16,4096]{1,0:T(8,128)(2,1)S(1)}, bf16[16,4096]{1,0:T(8,128)(2,1)S(1)}, u32[]{:S(2)}, u32[]{:S(2)}) collective-permute-start(bf16[16,4096]{1,0:T(8,128)(2,1)S(1)} %pair_ends.1), channel_id=1, source_target_pairs={{0,4},{1,5},{2,6},{3,7},{4,8},{5,9},{6,10},{7,11},{8,12},{9,13},{1... | collective-permute-start | bytes 393224 | tf_op jit(solution)/shard_map/ppermute | solution.py:23
  23.7 2.8 %collective-permute-start.2 = (bf16[16,4096]{1,0:T(8,128)(2,1)S(1)}, bf16[16,4096]{1,0:T(8,128)(2,1)S(1)}, u32[]{:S(2)}, u32[]{:S(2)}) collective-permute-start(bf16[16,4096]{1,0:T(8,128)(2,1)S(1)} %pair_ends.1), channel_id=1, source_target_pairs={{0,2},{1,3},{2,4},{3,5},{4,6},{5,7},{6,8},{7,9},{8,10},{9,11},{10,... | collective-permute-start | bytes 393224 | tf_op jit(solution)/shard_map/ppermute | solution.py:23
  26.5 0.0 copy-done.6
  26.5 0.3 sqrt_multiply_fusion.weight_ref
  26.8 2.3 %near_part_0.1.refs_0_ = f32[128,8192]{1,0:T(8,128)S(1)} custom-call(f32[79,8,128]{2,1,0:T(8,128)S(1)} %get-tuple-element.31.masks, bf16[128,8192]{1,0:T(8,128)(2,1)S(1)} %get-tuple-element.42.gate_ref, f32[16,8192]{1,0:T(8,128)S(1)} %copy-done, f32[16,8192]{1,0:T(8,128)S(1)} %sqrt_multiply_fusion.weight_ref), custom_call_target="tpu_custom_call" | custom-call | flops 19660800 | bytes 3670016 | tf_op jit(solution)/shard_map/near_part_0/pallas_call | solution.py:523
  29.1 0.1 collective-permute-done.3.far_ref
  29.3 2.7 %collective-permute-done.2.near_ref = bf16[16,4096]{1,0:T(8,128)(2,1)S(1)} collective-permute-done((bf16[16,4096]{1,0:T(8,128)(2,1)S(1)}, bf16[16,4096]{1,0:T(8,128)(2,1)S(1)}, u32[]{:S(2)}, u32[]{:S(2)}) %collective-permute-start.2) | collective-permute-done | bytes 131104 | tf_op jit(solution)/shard_map/ppermute | solution.py:23
  32.0 0.1 reach_0.1.near_ref
  32.1 3.3 %collective-permute-start.4 = (bf16[16,4096]{1,0:T(8,128)(2,1)S(1)}, bf16[16,4096]{1,0:T(8,128)(2,1)S(1)}, u32[]{:S(2)}, u32[]{:S(2)}) collective-permute-start(bf16[16,4096]{1,0:T(8,128)(2,1)S(1)} %reach_0.1.near_ref), channel_id=1, source_target_pairs={{0,4},{1,5},{2,6},{3,7},{4,8},{5,9},{6,10},{7,11},{8,12},{9,13},{1... | collective-permute-start | bytes 393224 | tf_op jit(solution)/shard_map/ppermute | solution.py:23
  35.4 0.0 copy-start.4
  35.4 2.3 %near_part_1.1.near_ref = f32[128,8192]{1,0:T(8,128)S(1)} custom-call(f32[79,8,128]{2,1,0:T(8,128)S(1)} %get-tuple-element.31.masks, bf16[128,8192]{1,0:T(8,128)(2,1)S(1)} %get-tuple-element.42.gate_ref, f32[16,8192]{1,0:T(8,128)S(1)} %copy-done, f32[16,8192]{1,0:T(8,128)S(1)} %sqrt_multiply_fusion.weight_ref, ...), custom_call_target="tpu_custom_call", output_to_operand_aliasing={{}: (4, {})} | custom-call | flops 19660800 | bytes 3670016 | tf_op jit(solution)/shard_map/near_part_1/pallas_call | solution.py:523
  37.7 1.0 %collective-permute-done.4.far_ref = bf16[16,4096]{1,0:T(8,128)(2,1)S(1)} collective-permute-done((bf16[16,4096]{1,0:T(8,128)(2,1)S(1)}, bf16[16,4096]{1,0:T(8,128)(2,1)S(1)}, u32[]{:S(2)}, u32[]{:S(2)}) %collective-permute-start.4) | collective-permute-done | bytes 131104 | tf_op jit(solution)/shard_map/ppermute | solution.py:23
  38.7 0.3 pair_enter.1
  39.0 2.5 %collective-permute-start.5 = (f32[16,4096]{1,0:T(8,128)S(1)}, f32[16,4096]{1,0:T(8,128)S(1)}, u32[]{:S(2)}, u32[]{:S(2)}) collective-permute-start(f32[16,4096]{1,0:T(8,128)S(1)} %get-tuple-element.47), channel_id=1, source_target_pairs={{0,1},{1,0},{2,3},{3,2},{4,5},{5,4},{6,7},{7,6},{8,9},{9,8},{10,11... | collective-permute-start | bytes 786440 | tf_op jit(solution)/shard_map/ppermute | solution.py:27
  41.5 0.0 copy-done.4
  41.5 0.0 copy-start.5
  41.5 4.4 %far_part_own.1 = (bf16[128,8192]{1,0:T(8,128)(2,1)}, f32[64,128,128]{2,1,0:T(8,128)S(1)}, f32[128,128]{1,0:T(8,128)S(1)}) custom-call(f32[79,8,128]{2,1,0:T(8,128)S(1)} %get-tuple-element.31.masks, f32[64,136,128]{2,1,0:T(8,128)S(1)} %get-tuple-element.40.state_ref, f32[16,4096]{1,0:T(8,128)S(1)} %get-tuple-element.48.enter_ref, ...), custom_call_target="tpu_custom_call" | custom-call | flops 29491200 | bytes 9437184 | tf_op jit(solution)/shard_map/far_part_own/pallas_call | solution.py:607
  45.9 0.0 collective-permute-done.5.enter_ref
  45.9 0.0 copy-done.5
  45.9 5.3 %far_part_other.1 = (bf16[128,8192]{1,0:T(8,128)(2,1)}, f32[64,128,128]{2,1,0:T(8,128)S(1)}, f32[128,128]{1,0:T(8,128)S(1)}, bf16[128,8192]{1,0:T(8,128)(2,1)}) custom-call(f32[79,8,128]{2,1,0:T(8,128)S(1)} %get-tuple-element.31.masks, ...), custom_call_target="tpu_custom_call", output_to_operand_aliasing={{0}: (11, {}), {1}: (12, {}), {2}: (13, {})} | custom-call | flops 29491200 | bytes 9437184 | tf_op jit(solution)/shard_map/far_part_other/pallas_call | solution.py:607
Async XLA Ops:
  0.6 5.2 %copy-start.3 = (f32[3,3,8192]{2,1,0:T(4,128)S(1)}, f32[3,3,8192]{2,1,0:T(4,128)}, u32[]{:S(2)}) copy-start(f32[3,3,8192]{2,1,0:T(4,128)} %taps_ref.9) | copy-start | bytes 884740
  0.6 8.6 %copy-start.1 = (bf16[128,8192]{1,0:T(8,128)(2,1)S(1)}, bf16[128,8192]{1,0:T(8,128)(2,1)}, u32[]{:S(2)}) copy-start(bf16[128,8192]{1,0:T(8,128)(2,1)} %key_ref.5) | copy-start | bytes 6291460
  2.0 7.3 %copy-start = (f32[16,8192]{1,0:T(8,128)S(1)}, f32[16,8192]{1,0:T(8,128)}, u32[]{:S(2)}) copy-start(f32[16,8192]{1,0:T(8,128)} %rate_ref.17) | copy-start | bytes 1572868
  2.0 7.3 %collective-permute-start = (bf16[3,2,8192]{2,1,0:T(2,128)(2,1)S(1)}, bf16[3,2,8192]{2,1,0:T(2,128)(2,1)S(1)}, u32[]{:S(2)}, u32[]{:S(2)}) collective-permute-start(bf16[3,2,8192]{2,1,0:T(2,128)(2,1)S(1)} %tails.1), channel_id=1, source_target_pairs={{0,1},{1,2},{2,3},{3,4},{4,5},{5,6},{6,7},{7,8},{8,9},{9,10},{10,1... | collective-permute-start | bytes 294920 | tf_op jit(solution)/shard_map/ppermute | solution.py:23
  9.3 1.6 %copy-start.2 = (bf16[128,8192]{1,0:T(8,128)(2,1)S(1)}, bf16[128,8192]{1,0:T(8,128)(2,1)}, u32[]{:S(2)}) copy-start(bf16[128,8192]{1,0:T(8,128)(2,1)} %value_ref.5) | copy-start | bytes 6291460
  15.4 5.8 %collective-permute-start.1 = (f32[16,4096]{1,0:T(8,128)S(1)}, f32[16,4096]{1,0:T(8,128)S(1)}, u32[]{:S(2)}, u32[]{:S(2)}) collective-permute-start(f32[16,4096]{1,0:T(8,128)S(1)} %get-tuple-element.34), channel_id=1, source_target_pairs={{0,1},{1,0},{2,3},{3,2},{4,5},{5,4},{6,7},{7,6},{8,9},{9,8},{10,11... | collective-permute-start | bytes 786440 | tf_op jit(solution)/shard_map/ppermute | solution.py:27
  16.7 9.8 %copy-start.6 = (f32[16,8192]{1,0:T(8,128)S(1)}, f32[16,8192]{1,0:T(8,128)}, u32[]{:S(2)}) copy-start(f32[16,8192]{1,0:T(8,128)} %param.14) | copy-start | bytes 1572868
  21.4 7.9 %collective-permute-start.3 = (bf16[16,4096]{1,0:T(8,128)(2,1)S(1)}, bf16[16,4096]{1,0:T(8,128)(2,1)S(1)}, u32[]{:S(2)}, u32[]{:S(2)}) collective-permute-start(bf16[16,4096]{1,0:T(8,128)(2,1)S(1)} %pair_ends.1), channel_id=1, source_target_pairs={{0,4},{1,5},{2,6},{3,7},{4,8},{5,9},{6,10},{7,11},{8,12},{9,13},{1... | collective-permute-start | bytes 393224 | tf_op jit(solution)/shard_map/ppermute | solution.py:23
  23.7 8.3 %collective-permute-start.2 = (bf16[16,4096]{1,0:T(8,128)(2,1)S(1)}, bf16[16,4096]{1,0:T(8,128)(2,1)S(1)}, u32[]{:S(2)}, u32[]{:S(2)}) collective-permute-start(bf16[16,4096]{1,0:T(8,128)(2,1)S(1)} %pair_ends.1), channel_id=1, source_target_pairs={{0,2},{1,3},{2,4},{3,5},{4,6},{5,7},{6,8},{7,9},{8,10},{9,11},{10,... | collective-permute-start | bytes 393224 | tf_op jit(solution)/shard_map/ppermute | solution.py:23
  32.1 6.6 %collective-permute-start.4 = (bf16[16,4096]{1,0:T(8,128)(2,1)S(1)}, bf16[16,4096]{1,0:T(8,128)(2,1)S(1)}, u32[]{:S(2)}, u32[]{:S(2)}) collective-permute-start(bf16[16,4096]{1,0:T(8,128)(2,1)S(1)} %reach_0.1.near_ref), channel_id=1, source_target_pairs={{0,4},{1,5},{2,6},{3,7},{4,8},{5,9},{6,10},{7,11},{8,12},{9,13},{1... | collective-permute-start | bytes 393224 | tf_op jit(solution)/shard_map/ppermute | solution.py:23
  35.4 6.1 %copy-start.4 = (bf16[128,8192]{1,0:T(8,128)(2,1)S(1)}, bf16[128,8192]{1,0:T(8,128)(2,1)}, u32[]{:S(2)}) copy-start(bf16[128,8192]{1,0:T(8,128)(2,1)} %resid_ref.3) | copy-start | bytes 6291460
  39.0 6.9 %collective-permute-start.5 = (f32[16,4096]{1,0:T(8,128)S(1)}, f32[16,4096]{1,0:T(8,128)S(1)}, u32[]{:S(2)}, u32[]{:S(2)}) collective-permute-start(f32[16,4096]{1,0:T(8,128)S(1)} %get-tuple-element.47), channel_id=1, source_target_pairs={{0,1},{1,0},{2,3},{3,2},{4,5},{5,4},{6,7},{7,6},{8,9},{9,8},{10,11... | collective-permute-start | bytes 786440 | tf_op jit(solution)/shard_map/ppermute | solution.py:27
  41.5 4.4 %copy-start.5 = (f32[8192]{0:T(1024)S(1)}, f32[8192]{0:T(1024)}, u32[]{:S(2)}) copy-start(f32[8192]{0:T(1024)} %param.17) | copy-start | bytes 98308

commit v14 on v13

--- a/solution.py
+++ b/solution.py
@@ -272,27 +272,40 @@
     each_group(count // LANES, most, lambda lanes: group([pl.multiple_of(first + lane, LANES) for lane in lanes]))
 
 
-def query_kernel(base_ref, len_ref, query_ref, taps_ref, short_ref, masks, query_buf, sems, wide_q, *, span, most, chunk, reaches):
-    chans = query_buf.shape[1]
+def query_kernel(*refs, span, most, chunk, reaches, first, count):
+    if reaches:
+        base_ref, len_ref, query_ref, taps_ref, value_in, short_ref, masks, value_ref, query_buf, sems, wide_q, value_sem = refs
+        value_copy = pltpu.make_async_copy(value_in, value_ref, value_sem)
+    else:
+        masks, query_ref, taps_ref, _, short_ref, query_buf, sems, wide_q = refs
 
     def fetch(c):
-        return cols_copy(query_ref, query_buf, sems, c, chunk)
-
-    for c in range(chans // chunk):
+        there = pl.ds(first + c * chunk if isinstance(c, int) else pl.multiple_of(first + c * chunk, chunk), chunk)
+        here = pl.ds(c * chunk if isinstance(c, int) else pl.multiple_of(c * chunk, chunk), chunk)
+        return pltpu.make_async_copy(query_ref.at[:, there], query_buf.at[:, here], sems.at[c])
+
+    for c in range(count // chunk):
         fetch(c).start()
-    write_masks(base_ref, len_ref, masks, span, reaches)
+    if reaches:
+        value_copy.start()
+        write_masks(base_ref, len_ref, masks, span, reaches)
     at = Masks(span)
 
     def group(lanes):
         for slot, lane in enumerate(lanes):
             spread(query_buf[:, cols_of(lane)], wide_q.at[slot], span)
-        convs = [Conv(wide_q.at[slot], None, taps_ref[0, :, cols_of(lane)], span) for slot, lane in enumerate(lanes)]
+        convs = [
+            Conv(wide_q.at[slot], None, taps_ref[0, :, cols_of(pl.multiple_of(first + lane, LANES))], span)
+            for slot, lane in enumerate(lanes)
+        ]
         for j in range(span):
             keep_one, keep_two = masks[at.one + j], masks[at.two + j]
             for slot, lane in enumerate(lanes):
-                short_ref[pl.ds(j * SUBS, SUBS), cols_of(lane)] = convs[slot].step(j, keep_one, keep_two)
-
-    each_chunk(chans, chunk, lambda c: fetch(c).wait(), group, lambda c: None, most)
+                short_ref[pl.ds(j * SUBS, SUBS), cols_of(pl.multiple_of(first + lane, LANES))] = convs[slot].step(j, keep_one, keep_two)
+
+    each_chunk(count, chunk, lambda c: fetch(c).wait(), group, lambda c: None, most)
+    if reaches:
+        value_copy.wait()
 
 
 def pair_rates(rate_ref, count):
@@ -470,25 +483,44 @@
     rim_rows = from_behind(tails, "ctx", 1)
     reaches = max(1, (blocks // 8).bit_length() - 1)
     mask_shape = (Masks(span).count(reaches),) + tile_shape
-    q_short, masks = pl.pallas_call(
-        functools.partial(query_kernel, span=span, most=Q_TILES, chunk=chunk, reaches=reaches),
-        in_specs=[smem, smem, hbm, vmem],
-        out_specs=[vmem, vmem],
-        out_shape=[pltpu.VMEM((tok_rows, chans), f32), pltpu.VMEM(mask_shape, f32)],
-        scratch_shapes=[
-            pltpu.VMEM((tok_rows, chans), bf16),
-            pltpu.SemaphoreType.DMA((pieces,)),
+
+    def query_piece(part, masks, before):
+        count = chans // 2
+        scratch = [
+            pltpu.VMEM((tok_rows, count), bf16),
+            pltpu.SemaphoreType.DMA((count // chunk,)),
             pltpu.VMEM((Q_TILES, wide_rows, LANES), f32),
-        ],
-        compiler_params=params,
-        cost_estimate=cost(200, 6 * tok_rows * chans),
-        name="query_part",
-    )(base, lengths, far_off(query_in), near_by(short_taps))
-    rim_rows, q_short = lax.optimization_barrier((rim_rows, q_short))
+        ]
+        out_shape = [pltpu.VMEM((tok_rows, chans), f32)]
+        if part == 0:
+            operands = [base, lengths, far_off(query_in), near_by(short_taps), far_off(value_in)]
+            in_specs = [smem, smem, hbm, vmem, hbm]
+            out_shape += [pltpu.VMEM(mask_shape, f32), pltpu.VMEM((tok_rows, chans), bf16)]
+            scratch.append(pltpu.SemaphoreType.DMA(()))
+        else:
+            operands = [near_by(masks), far_off(query_in), near_by(short_taps), near_by(before)]
+            in_specs = [vmem, hbm, vmem, vmem]
+        return pl.pallas_call(
+            functools.partial(
+                query_kernel, span=span, most=Q_TILES, chunk=chunk, reaches=0 if part else reaches,
+                first=part * count, count=count,
+            ),
+            in_specs=in_specs,
+            out_specs=[vmem] * len(out_shape),
+            out_shape=out_shape,
+            scratch_shapes=scratch,
+            input_output_aliases={3: 0} if part else {},
+            compiler_params=params,
+            cost_estimate=cost(100, 3 * tok_rows * chans),
+            name="query_part_%d" % part,
+        )(*operands)
+
+    q_short, masks, values = query_piece(0, None, None)
+    rim_rows, q_short, values = lax.optimization_barrier((rim_rows, q_short, values))
     rates, weights, taps, rims = near_by(decay_rate), near_by(weight), near_by(short_taps), near_by(rim_rows)
     kept = pltpu.VMEM((modes, chans // 2), f32)
     sent = pltpu.VMEM((modes, chans // 2), bf16)
-    keys, values = near_by(key_in), near_by(value_in)
+    keys, values = near_by(key_in), near_by(values)
 
     def states_of(own, before):
         return pl.pallas_call(
@@ -552,8 +584,11 @@
         )(near_by(masks), *[near_by(x) for x in operands], rates)
 
     ends = pair_call(pair_kernel, [own, got], [sent], "pair_ends", rows=tok_rows, index=at.late)[0]
-    one_on, two_on = from_behind(ends, "ctx", 2), from_behind(ends, "ctx", 4)
+    two_on = from_behind(ends, "ctx", 4)
     near = near_piece(0, None)
+    ends, near = lax.optimization_barrier((ends, near))
+    one_on = from_behind(ends, "ctx", 2)
+    near = near_piece(1, near)
     one_on, two_on, near = lax.optimization_barrier((one_on, two_on, near))
     enter, on = one_on, two_on
     for m in range(reaches - 1):
@@ -561,8 +596,8 @@
             reach_kernel, [enter, on], [sent], "reach_%d" % m, rows=2 * tok_rows << m, index=at.reach + m
         )[0]
         on = from_behind(enter, "ctx", 4 << m)
-    near = near_piece(1, near)
-    on, near = lax.optimization_barrier((on, near))
+    q_short = query_piece(1, masks, q_short)[0]
+    on, q_short = lax.optimization_barrier((on, q_short))
     mine, give_back = pair_call(
         enter_kernel,
         [enter, on, own, got],

time: 51.5 us -> 52.3 us (1.016)
  local copies, waits for them, and re-layouts: 1.61 us -> 0.03 us
  waiting for transfers between devices: 3.81 us -> 5.33 us
  Pallas kernels: 28.7 us -> 30 us
    unnamed x14 -> x12, local copies, waits for them, and re-layouts: 1.61 us -> 0.03 us
    ppermute x4, waiting for transfers between devices: 3.8 us -> 5.33 us  [from_behind(): return lax.ppermute(shard, axis, pairs)]
    pallas_call x1 -> x2, Pallas kernels: 3.42 us -> 4.78 us  [query_piece(): pl.pallas_call(functools.partial(query_kernel, span=span, most=Q_TILES, c...]
    ppermute x4, starting transfers between devices: 12.2 us -> 11.3 us  [from_behind(): return lax.ppermute(shard, axis, pairs)]
  transfers between devices with their start and end apart: 6 -> 6, of which waited for: 3 -> 2; matrix products, arithmetic and copies ran while one was open for 1% -> 1% of each run, Pallas kernels for 33% -> 35%
where the time goes in v14:
time: 52.3 us; the launch traced here: 52.1 us
  Pallas kernels  30 us (57%)
  starting transfers between devices  15.6 us (30%)
  waiting for transfers between devices  5.33 us (10%)
  between operations  0.85 us (2%)
    ppermute x4, starting transfers between devices, from_behind(): return lax.ppermute(shard, axis, pairs)  11.3 us
    pallas_call x2, Pallas kernels, finish(): pl.pallas_call(functools.partial(final_kernel, span=span, modes=modes, ch...  9.7 us
    pallas_call x2, Pallas kernels, states_of(): pl.pallas_call(functools.partial(state_kernel, span=span, modes=modes, mo...  9.08 us
    ppermute x4, waiting for transfers between devices, from_behind(): return lax.ppermute(shard, axis, pairs)  5.33 us
    pallas_call x2, Pallas kernels, query_piece(): pl.pallas_call(functools.partial(query_kernel, span=span, most=Q_TILES, c...  4.78 us
    pallas_call x2, Pallas kernels, near_piece(): pl.pallas_call(functools.partial(near_kernel, span=span, modes=modes, mos...  4.67 us
    ppermute x2, starting transfers between devices, swap(): lax.ppermute(shard, axis, [(i, i ^ 1) for i in range(lax.axis_size(axis))])  4.27 us
    pallas_call x1, Pallas kernels, shards(): pl.pallas_call(tail_kernel, in_specs=[hbm, hbm, hbm], out_specs=vmem, out...  1.2 us
  transfers between devices with their start and end apart: 6, of which 2 were waited for; matrix products, arithmetic and copies ran while one was open for 1% of the time, Pallas kernels for 35%

profile of v14, /device:TPU:9, one launch (start us, length us, event | category | flops | bytes accessed | tf_op | source)
XLA Modules:
  0.0 52.1 jit_solution(12678038318685361254)
XLA Ops:
  0.6 0.0 copy-start.2
  0.6 1.2 %tails.1 = bf16[3,2,8192]{2,1,0:T(2,128)(2,1)S(1)} custom-call(bf16[128,8192]{1,0:T(8,128)(2,1)} %refs_1_.3, bf16[128,8192]{1,0:T(8,128)(2,1)} %key_ref.5, bf16[128,8192]{1,0:T(8,128)(2,1)} %value_ref.1), custom_call_target="tpu_custom_call" | custom-call | tf_op jit(solution)/shard_map/tails/pallas_call | solution.py:474
  1.8 3.7 %collective-permute-start = (bf16[3,2,8192]{2,1,0:T(2,128)(2,1)S(1)}, bf16[3,2,8192]{2,1,0:T(2,128)(2,1)S(1)}, u32[]{:S(2)}, u32[]{:S(2)}) collective-permute-start(bf16[3,2,8192]{2,1,0:T(2,128)(2,1)S(1)} %tails.1), channel_id=1, source_target_pairs={{0,1},{1,2},{2,3},{3,4},{4,5},{5,6},{6,7},{7,8},{8,9},{9,10},{10,1... | collective-permute-start | bytes 294920 | tf_op jit(solution)/shard_map/ppermute | solution.py:23
  5.5 0.0 copy-done.2
  5.5 0.0 copy-start
  5.6 0.0 copy-start.1
  5.6 2.8 %query_part_0.1 = (f32[128,8192]{1,0:T(8,128)S(1)}, f32[79,8,128]{2,1,0:T(8,128)S(1)}, bf16[128,8192]{1,0:T(8,128)(2,1)S(1)}) custom-call(s32[1]{0:T(128)} %bitcast.refs_0_, s32[16]{0:T(128)} %refs_1_.2, bf16[128,8192]{1,0:T(8,128)(2,1)} %refs_1_.3, f32[3,3,8192]{2,1,0:T(4,128)S(1)} %copy-done.2, bf16[128,8192]{1,0:T(8,128)(2,1)} %value_ref.1), custom_call_target="tpu_custom_call" | custom-call | flops 6553600 | bytes 3145728 | tf_op jit(solution)/shard_map/query_part_0/pallas_call | solution.py:503
  8.4 0.0 collective-permute-done.rim_ref
  8.4 0.0 copy-done
  8.4 0.0 copy-done.1
  8.4 0.0 copy-start.5
  8.4 4.5 %block_states_give.1 = (bf16[128,8192]{1,0:T(8,128)(2,1)S(1)}, f32[64,136,128]{2,1,0:T(8,128)S(1)}, f32[16,4096]{1,0:T(8,128)S(1)}) custom-call(f32[79,8,128]{2,1,0:T(8,128)S(1)} %get-tuple-element.35.masks.refs_0_, bf16[128,8192]{1,0:T(8,128)(2,1)S(1)} %copy-done.1, bf16[128,8192]{1,0:T(8,128)(2,1)S(1)} %get-tuple-element.38.value_ref, ...), custom_call_target="tpu_custom_call" | custom-call | flops 32768000 | bytes 6291456 | tf_op jit(solution)/shard_map/block_states_give/pallas_call | solution.py:526
  12.9 1.9 %collective-permute-start.1 = (f32[16,4096]{1,0:T(8,128)S(1)}, f32[16,4096]{1,0:T(8,128)S(1)}, u32[]{:S(2)}, u32[]{:S(2)}) collective-permute-start(f32[16,4096]{1,0:T(8,128)S(1)} %get-tuple-element.40), channel_id=1, source_target_pairs={{0,1},{1,0},{2,3},{3,2},{4,5},{5,4},{6,7},{7,6},{8,9},{9,8},{10,11... | collective-permute-start | bytes 786440 | tf_op jit(solution)/shard_map/ppermute | solution.py:27
  14.9 0.0 copy-done.5
  14.9 0.3 sqrt_multiply_fusion.weight_ref
  15.2 4.5 %block_states_own.1 = (bf16[128,8192]{1,0:T(8,128)(2,1)S(1)}, f32[64,136,128]{2,1,0:T(8,128)S(1)}, f32[16,4096]{1,0:T(8,128)S(1)}) custom-call(f32[79,8,128]{2,1,0:T(8,128)S(1)} %get-tuple-element.35.masks.refs_0_, bf16[128,8192]{1,0:T(8,128)(2,1)S(1)} %copy-done.1, ...), custom_call_target="tpu_custom_call", output_to_operand_aliasing={{0}: (6, {}), {1}: (7, {})} | custom-call | flops 32768000 | bytes 6291456 | tf_op jit(solution)/shard_map/block_states_own/pallas_call | solution.py:526
  19.7 0.0 collective-permute-done.1.got_ref
  19.7 0.2 pair_ends.1
  19.9 2.2 %collective-permute-start.3 = (bf16[16,4096]{1,0:T(8,128)(2,1)S(1)}, bf16[16,4096]{1,0:T(8,128)(2,1)S(1)}, u32[]{:S(2)}, u32[]{:S(2)}) collective-permute-start(bf16[16,4096]{1,0:T(8,128)(2,1)S(1)} %pair_ends.1), channel_id=1, source_target_pairs={{0,4},{1,5},{2,6},{3,7},{4,8},{5,9},{6,10},{7,11},{8,12},{9,13},{1... | collective-permute-start | bytes 393224 | tf_op jit(solution)/shard_map/ppermute | solution.py:23
  22.2 2.3 %near_part_0.1.refs_0_ = f32[128,8192]{1,0:T(8,128)S(1)} custom-call(f32[79,8,128]{2,1,0:T(8,128)S(1)} %get-tuple-element.35.masks.refs_0_, bf16[128,8192]{1,0:T(8,128)(2,1)S(1)} %get-tuple-element.48.gate_ref, f32[16,8192]{1,0:T(8,128)S(1)} %copy-done, f32[16,8192]{1,0:T(8,128)S(1)} %sqrt_multiply_fusion.weight_ref), custom_call_target="tpu_custom_call" | custom-call | flops 19660800 | bytes 3670016 | tf_op jit(solution)/shard_map/near_part_0/pallas_call | solution.py:555
  24.5 2.2 %collective-permute-start.2 = (bf16[16,4096]{1,0:T(8,128)(2,1)S(1)}, bf16[16,4096]{1,0:T(8,128)(2,1)S(1)}, u32[]{:S(2)}, u32[]{:S(2)}) collective-permute-start(bf16[16,4096]{1,0:T(8,128)(2,1)S(1)} %pair_ends.1), channel_id=1, source_target_pairs={{0,2},{1,3},{2,4},{3,5},{4,6},{5,7},{6,8},{7,9},{8,10},{9,11},{10,... | collective-permute-start | bytes 393224 | tf_op jit(solution)/shard_map/ppermute | solution.py:23
  26.7 2.3 %near_part_1.1.near_ref = f32[128,8192]{1,0:T(8,128)S(1)} custom-call(f32[79,8,128]{2,1,0:T(8,128)S(1)} %get-tuple-element.35.masks.refs_0_, bf16[128,8192]{1,0:T(8,128)(2,1)S(1)} %get-tuple-element.48.gate_ref, f32[16,8192]{1,0:T(8,128)S(1)} %copy-done, f32[16,8192]{1,0:T(8,128)S(1)} %sqrt_multiply_fusion.weight_ref, ...), custom_call_target="tpu_custom_call", output_to_operand_aliasing={{}: (4, {})} | custom-call | flops 19660800 | bytes 3670016 | tf_op jit(solution)/shard_map/near_part_1/pallas_call | solution.py:555
  29.1 0.0 collective-permute-done.3.far_ref
  29.1 3.9 %collective-permute-done.2.near_ref = bf16[16,4096]{1,0:T(8,128)(2,1)S(1)} collective-permute-done((bf16[16,4096]{1,0:T(8,128)(2,1)S(1)}, bf16[16,4096]{1,0:T(8,128)(2,1)S(1)}, u32[]{:S(2)}, u32[]{:S(2)}) %collective-permute-start.2) | collective-permute-done | bytes 131104 | tf_op jit(solution)/shard_map/ppermute | solution.py:23
  33.0 0.1 reach_0.1.near_ref
  33.1 3.1 %collective-permute-start.4 = (bf16[16,4096]{1,0:T(8,128)(2,1)S(1)}, bf16[16,4096]{1,0:T(8,128)(2,1)S(1)}, u32[]{:S(2)}, u32[]{:S(2)}) collective-permute-start(bf16[16,4096]{1,0:T(8,128)(2,1)S(1)} %reach_0.1.near_ref), channel_id=1, source_target_pairs={{0,4},{1,5},{2,6},{3,7},{4,8},{5,9},{6,10},{7,11},{8,12},{9,13},{1... | collective-permute-start | bytes 393224 | tf_op jit(solution)/shard_map/ppermute | solution.py:23
  36.3 0.0 copy-start.3
  36.3 2.0 %query_part_1.1.short_ref = f32[128,8192]{1,0:T(8,128)S(1)} custom-call(f32[79,8,128]{2,1,0:T(8,128)S(1)} %get-tuple-element.35.masks.refs_0_, bf16[128,8192]{1,0:T(8,128)(2,1)} %refs_1_.3, f32[3,3,8192]{2,1,0:T(4,128)S(1)} %copy-done.2, f32[128,8192]{1,0:T(8,128)S(1)} %get-tuple-element.53.refs_3_), custom_call_target="tpu_custom_call", output_to_operand_aliasing={{}: (3, {})} | custom-call | flops 6553600 | bytes 3145728 | tf_op jit(solution)/shard_map/query_part_1/pallas_call | solution.py:503
  38.3 1.4 %collective-permute-done.4.far_ref = bf16[16,4096]{1,0:T(8,128)(2,1)S(1)} collective-permute-done((bf16[16,4096]{1,0:T(8,128)(2,1)S(1)}, bf16[16,4096]{1,0:T(8,128)(2,1)S(1)}, u32[]{:S(2)}, u32[]{:S(2)}) %collective-permute-start.4) | collective-permute-done | bytes 131104 | tf_op jit(solution)/shard_map/ppermute | solution.py:23
  39.7 0.3 pair_enter.1
  40.0 2.3 %collective-permute-start.5 = (f32[16,4096]{1,0:T(8,128)S(1)}, f32[16,4096]{1,0:T(8,128)S(1)}, u32[]{:S(2)}, u32[]{:S(2)}) collective-permute-start(f32[16,4096]{1,0:T(8,128)S(1)} %get-tuple-element.55), channel_id=1, source_target_pairs={{0,1},{1,0},{2,3},{3,2},{4,5},{5,4},{6,7},{7,6},{8,9},{9,8},{10,11... | collective-permute-start | bytes 786440 | tf_op jit(solution)/shard_map/ppermute | solution.py:27
  42.4 0.0 copy-done.3
  42.4 0.0 copy-start.4
  42.4 4.4 %far_part_own.1 = (bf16[128,8192]{1,0:T(8,128)(2,1)}, f32[64,128,128]{2,1,0:T(8,128)S(1)}, f32[128,128]{1,0:T(8,128)S(1)}) custom-call(f32[79,8,128]{2,1,0:T(8,128)S(1)} %get-tuple-element.35.masks.refs_0_, f32[64,136,128]{2,1,0:T(8,128)S(1)} %get-tuple-element.46.state_ref, f32[16,4096]{1,0:T(8,128)S(1)} %get-tuple-element.56.enter_ref, ...), custom_call_target="tpu_custom_call" | custom-call | flops 29491200 | bytes 9437184 | tf_op jit(solution)/shard_map/far_part_own/pallas_call | solution.py:642
  46.8 0.0 collective-permute-done.5.enter_ref
  46.8 0.0 copy-done.4
  46.8 5.3 %far_part_other.1 = (bf16[128,8192]{1,0:T(8,128)(2,1)}, f32[64,128,128]{2,1,0:T(8,128)S(1)}, f32[128,128]{1,0:T(8,128)S(1)}, bf16[128,8192]{1,0:T(8,128)(2,1)}) custom-call(f32[79,8,128]{2,1,0:T(8,128)S(1)} %get-tuple-element.35.masks.refs_0_, ...), custom_call_target="tpu_custom_call", output_to_operand_aliasing={{0}: (11, {}), {1}: (12, {}), {2}: (13, {})} | custom-call | flops 29491200 | bytes 9437184 | tf_op jit(solution)/shard_map/far_part_other/pallas_call | solution.py:642
Async XLA Ops:
  0.6 4.9 %copy-start.2 = (f32[3,3,8192]{2,1,0:T(4,128)S(1)}, f32[3,3,8192]{2,1,0:T(4,128)}, u32[]{:S(2)}) copy-start(f32[3,3,8192]{2,1,0:T(4,128)} %taps_ref.7) | copy-start | bytes 884740
  1.8 6.5 %collective-permute-start = (bf16[3,2,8192]{2,1,0:T(2,128)(2,1)S(1)}, bf16[3,2,8192]{2,1,0:T(2,128)(2,1)S(1)}, u32[]{:S(2)}, u32[]{:S(2)}) collective-permute-start(bf16[3,2,8192]{2,1,0:T(2,128)(2,1)S(1)} %tails.1), channel_id=1, source_target_pairs={{0,1},{1,2},{2,3},{3,4},{4,5},{5,6},{6,7},{7,8},{8,9},{9,10},{10,1... | collective-permute-start | bytes 294920 | tf_op jit(solution)/shard_map/ppermute | solution.py:23
  5.5 2.8 %copy-start = (f32[16,8192]{1,0:T(8,128)S(1)}, f32[16,8192]{1,0:T(8,128)}, u32[]{:S(2)}) copy-start(f32[16,8192]{1,0:T(8,128)} %rate_ref.17) | copy-start | bytes 1572868
  5.6 2.8 %copy-start.1 = (bf16[128,8192]{1,0:T(8,128)(2,1)S(1)}, bf16[128,8192]{1,0:T(8,128)(2,1)}, u32[]{:S(2)}) copy-start(bf16[128,8192]{1,0:T(8,128)(2,1)} %key_ref.5) | copy-start | bytes 6291460
  8.4 6.5 %copy-start.5 = (f32[16,8192]{1,0:T(8,128)S(1)}, f32[16,8192]{1,0:T(8,128)}, u32[]{:S(2)}) copy-start(f32[16,8192]{1,0:T(8,128)} %param.14) | copy-start | bytes 1572868
  12.9 6.8 %collective-permute-start.1 = (f32[16,4096]{1,0:T(8,128)S(1)}, f32[16,4096]{1,0:T(8,128)S(1)}, u32[]{:S(2)}, u32[]{:S(2)}) collective-permute-start(f32[16,4096]{1,0:T(8,128)S(1)} %get-tuple-element.40), channel_id=1, source_target_pairs={{0,1},{1,0},{2,3},{3,2},{4,5},{5,4},{6,7},{7,6},{8,9},{9,8},{10,11... | collective-permute-start | bytes 786440 | tf_op jit(solution)/shard_map/ppermute | solution.py:27
  19.9 9.2 %collective-permute-start.3 = (bf16[16,4096]{1,0:T(8,128)(2,1)S(1)}, bf16[16,4096]{1,0:T(8,128)(2,1)S(1)}, u32[]{:S(2)}, u32[]{:S(2)}) collective-permute-start(bf16[16,4096]{1,0:T(8,128)(2,1)S(1)} %pair_ends.1), channel_id=1, source_target_pairs={{0,4},{1,5},{2,6},{3,7},{4,8},{5,9},{6,10},{7,11},{8,12},{9,13},{1... | collective-permute-start | bytes 393224 | tf_op jit(solution)/shard_map/ppermute | solution.py:23
  24.5 8.5 %collective-permute-start.2 = (bf16[16,4096]{1,0:T(8,128)(2,1)S(1)}, bf16[16,4096]{1,0:T(8,128)(2,1)S(1)}, u32[]{:S(2)}, u32[]{:S(2)}) collective-permute-start(bf16[16,4096]{1,0:T(8,128)(2,1)S(1)} %pair_ends.1), channel_id=1, source_target_pairs={{0,2},{1,3},{2,4},{3,5},{4,6},{5,7},{6,8},{7,9},{8,10},{9,11},{10,... | collective-permute-start | bytes 393224 | tf_op jit(solution)/shard_map/ppermute | solution.py:23
  33.1 6.6 %collective-permute-start.4 = (bf16[16,4096]{1,0:T(8,128)(2,1)S(1)}, bf16[16,4096]{1,0:T(8,128)(2,1)S(1)}, u32[]{:S(2)}, u32[]{:S(2)}) collective-permute-start(bf16[16,4096]{1,0:T(8,128)(2,1)S(1)} %reach_0.1.near_ref), channel_id=1, source_target_pairs={{0,4},{1,5},{2,6},{3,7},{4,8},{5,9},{6,10},{7,11},{8,12},{9,13},{1... | collective-permute-start | bytes 393224 | tf_op jit(solution)/shard_map/ppermute | solution.py:23
  36.3 6.1 %copy-start.3 = (bf16[128,8192]{1,0:T(8,128)(2,1)S(1)}, bf16[128,8192]{1,0:T(8,128)(2,1)}, u32[]{:S(2)}) copy-start(bf16[128,8192]{1,0:T(8,128)(2,1)} %resid_ref.3) | copy-start | bytes 6291460
  40.0 6.8 %collective-permute-start.5 = (f32[16,4096]{1,0:T(8,128)S(1)}, f32[16,4096]{1,0:T(8,128)S(1)}, u32[]{:S(2)}, u32[]{:S(2)}) collective-permute-start(f32[16,4096]{1,0:T(8,128)S(1)} %get-tuple-element.55), channel_id=1, source_target_pairs={{0,1},{1,0},{2,3},{3,2},{4,5},{5,4},{6,7},{7,6},{8,9},{9,8},{10,11... | collective-permute-start | bytes 786440 | tf_op jit(solution)/shard_map/ppermute | solution.py:27
  42.4 4.4 %copy-start.4 = (f32[8192]{0:T(1024)S(1)}, f32[8192]{0:T(1024)}, u32[]{:S(2)}) copy-start(f32[8192]{0:T(1024)} %param.17) | copy-start | bytes 98308

commit v15 on v14

--- a/solution.py
+++ b/solution.py
@@ -274,8 +274,10 @@
 
 def query_kernel(*refs, span, most, chunk, reaches, first, count):
     if reaches:
-        base_ref, len_ref, query_ref, taps_ref, value_in, short_ref, masks, value_ref, query_buf, sems, wide_q, value_sem = refs
-        value_copy = pltpu.make_async_copy(value_in, value_ref, value_sem)
+        base_ref, len_ref, query_ref, taps_in, rate_in, short_ref, masks, taps_ref, rate_ref, query_buf, sems, wide_q, param_sems = refs
+        taps_copy = pltpu.make_async_copy(taps_in, taps_ref, param_sems.at[0])
+        rate_copy = pltpu.make_async_copy(rate_in, rate_ref, param_sems.at[1])
+        taps_copy.start()
     else:
         masks, query_ref, taps_ref, _, short_ref, query_buf, sems, wide_q = refs
 
@@ -287,8 +289,9 @@
     for c in range(count // chunk):
         fetch(c).start()
     if reaches:
-        value_copy.start()
+        rate_copy.start()
         write_masks(base_ref, len_ref, masks, span, reaches)
+        taps_copy.wait()
     at = Masks(span)
 
     def group(lanes):
@@ -305,7 +308,7 @@
 
     each_chunk(count, chunk, lambda c: fetch(c).wait(), group, lambda c: None, most)
     if reaches:
-        value_copy.wait()
+        rate_copy.wait()
 
 
 def pair_rates(rate_ref, count):
@@ -493,12 +496,14 @@
         ]
         out_shape = [pltpu.VMEM((tok_rows, chans), f32)]
         if part == 0:
-            operands = [base, lengths, far_off(query_in), near_by(short_taps), far_off(value_in)]
-            in_specs = [smem, smem, hbm, vmem, hbm]
-            out_shape += [pltpu.VMEM(mask_shape, f32), pltpu.VMEM((tok_rows, chans), bf16)]
-            scratch.append(pltpu.SemaphoreType.DMA(()))
+            operands = [base, lengths, far_off(query_in), far_off(short_taps), far_off(decay_rate)]
+            in_specs = [smem, smem, hbm, hbm, hbm]
+            out_shape += [
+                pltpu.VMEM(mask_shape, f32), pltpu.VMEM(short_taps.shape, f32), pltpu.VMEM(decay_rate.shape, f32)
+            ]
+            scratch.append(pltpu.SemaphoreType.DMA((2,)))
         else:
-            operands = [near_by(masks), far_off(query_in), near_by(short_taps), near_by(before)]
+            operands = [near_by(masks), far_off(query_in), taps, near_by(before)]
             in_specs = [vmem, hbm, vmem, vmem]
         return pl.pallas_call(
             functools.partial(
@@ -515,12 +520,12 @@
             name="query_part_%d" % part,
         )(*operands)
 
-    q_short, masks, values = query_piece(0, None, None)
-    rim_rows, q_short, values = lax.optimization_barrier((rim_rows, q_short, values))
-    rates, weights, taps, rims = near_by(decay_rate), near_by(weight), near_by(short_taps), near_by(rim_rows)
+    q_short, masks, taps, rates = query_piece(0, None, None)
+    rim_rows, q_short = lax.optimization_barrier((rim_rows, q_short))
+    rates, weights, taps, rims = near_by(rates), near_by(weight), near_by(taps), near_by(rim_rows)
     kept = pltpu.VMEM((modes, chans // 2), f32)
     sent = pltpu.VMEM((modes, chans // 2), bf16)
-    keys, values = near_by(key_in), near_by(values)
+    keys, values = near_by(key_in), near_by(value_in)
 
     def states_of(own, before):
         return pl.pallas_call(
@@ -584,11 +589,8 @@
         )(near_by(masks), *[near_by(x) for x in operands], rates)
 
     ends = pair_call(pair_kernel, [own, got], [sent], "pair_ends", rows=tok_rows, index=at.late)[0]
-    two_on = from_behind(ends, "ctx", 4)
+    one_on, two_on = from_behind(ends, "ctx", 2), from_behind(ends, "ctx", 4)
     near = near_piece(0, None)
-    ends, near = lax.optimization_barrier((ends, near))
-    one_on = from_behind(ends, "ctx", 2)
-    near = near_piece(1, near)
     one_on, two_on, near = lax.optimization_barrier((one_on, two_on, near))
     enter, on = one_on, two_on
     for m in range(reaches - 1):
@@ -596,8 +598,8 @@
             reach_kernel, [enter, on], [sent], "reach_%d" % m, rows=2 * tok_rows << m, index=at.reach + m
         )[0]
         on = from_behind(enter, "ctx", 4 << m)
-    q_short = query_piece(1, masks, q_short)[0]
-    on, q_short = lax.optimization_barrier((on, q_short))
+    q_short, near = query_piece(1, masks, q_short)[0], near_piece(1, near)
+    on, q_short, near = lax.optimization_barrier((on, q_short, near))
     mine, give_back = pair_call(
         enter_kernel,
         [enter, on, own, got],

time: 52.3 us -> 52.1 us (level); the launches traced: 52.1 us -> 51.1 us
  waiting for transfers between devices: 5.33 us -> 3.55 us
  local copies, waits for them, and re-layouts: 0.03 us -> 1.61 us
  starting transfers between devices: 15.6 us -> 15 us
    ppermute x4, waiting for transfers between devices: 5.33 us -> 3.55 us  [from_behind(): return lax.ppermute(shard, axis, pairs)]
    unnamed x12, local copies, waits for them, and re-layouts: 0.03 us -> 1.61 us
    ppermute x2, starting transfers between devices: 4.27 us -> 3.61 us  [swap(): lax.ppermute(shard, axis, [(i, i ^ 1) for i in range(lax.axis_size(axis))])]
  transfers between devices with their start and end apart: 6 -> 6, of which waited for: 2 -> 2; matrix products, arithmetic and copies ran while one was open for 1% -> 1% of each run, Pallas kernels for 35% -> 36%
where the time goes in v15:
time: 52.1 us; the launch traced here: 51.1 us
  Pallas kernels  29.7 us (57%)
  starting transfers between devices  15 us (29%)
  waiting for transfers between devices  3.55 us (7%)
  local copies, waits for them, and re-layouts  1.61 us (3%)
  between operations  0.84 us (2%)
    ppermute x4, starting transfers between devices, from_behind(): return lax.ppermute(shard, axis, pairs)  11.4 us
    pallas_call x2, Pallas kernels, finish(): pl.pallas_call(functools.partial(final_kernel, span=span, modes=modes, ch...  9.7 us
    pallas_call x2, Pallas kernels, states_of(): pl.pallas_call(functools.partial(state_kernel, span=span, modes=modes, mo...  9.03 us
    pallas_call x2, Pallas kernels, near_piece(): pl.pallas_call(functools.partial(near_kernel, span=span, modes=modes, mos...  4.67 us
    pallas_call x2, Pallas kernels, query_piece(): pl.pallas_call(functools.partial(query_kernel, span=span, most=Q_TILES, c...  4.6 us
    ppermute x2, starting transfers between devices, swap(): lax.ppermute(shard, axis, [(i, i ^ 1) for i in range(lax.axis_size(axis))])  3.61 us
    ppermute x4, waiting for transfers between devices, from_behind(): return lax.ppermute(shard, axis, pairs)  3.55 us
    unnamed x12, local copies, waits for them, and re-layouts  1.61 us
  transfers between devices with their start and end apart: 6, of which 2 were waited for; matrix products, arithmetic and copies ran while one was open for 1% of the time, Pallas kernels for 36%

profile of v15, /device:TPU:9, one launch (start us, length us, event | category | flops | bytes accessed | tf_op | source)
XLA Modules:
  0.0 51.1 jit_solution(15432423327041426117)
XLA Ops:
  0.6 1.2 %tails.1 = bf16[3,2,8192]{2,1,0:T(2,128)(2,1)S(1)} custom-call(bf16[128,8192]{1,0:T(8,128)(2,1)} %refs_1_.3, bf16[128,8192]{1,0:T(8,128)(2,1)} %key_ref.5, bf16[128,8192]{1,0:T(8,128)(2,1)} %value_ref.5), custom_call_target="tpu_custom_call" | custom-call | tf_op jit(solution)/shard_map/tails/pallas_call | solution.py:477
  1.8 0.0 copy-start
  1.8 3.8 %collective-permute-start = (bf16[3,2,8192]{2,1,0:T(2,128)(2,1)S(1)}, bf16[3,2,8192]{2,1,0:T(2,128)(2,1)S(1)}, u32[]{:S(2)}, u32[]{:S(2)}) collective-permute-start(bf16[3,2,8192]{2,1,0:T(2,128)(2,1)S(1)} %tails.1), channel_id=1, source_target_pairs={{0,1},{1,2},{2,3},{3,4},{4,5},{5,6},{6,7},{7,8},{8,9},{9,10},{10,1... | collective-permute-start | bytes 294920 | tf_op jit(solution)/shard_map/ppermute | solution.py:23
  5.6 2.7 %query_part_0.1 = (f32[128,8192]{1,0:T(8,128)S(1)}, f32[79,8,128]{2,1,0:T(8,128)S(1)}, f32[3,3,8192]{2,1,0:T(4,128)S(1)}, f32[16,8192]{1,0:T(8,128)S(1)}) custom-call(s32[1]{0:T(128)} %bitcast.refs_0_, s32[16]{0:T(128)} %refs_1_.2, bf16[128,8192]{1,0:T(8,128)(2,1)} %refs_1_.3, f32[3,3,8192]{2,1,0:T(4,128)} %refs_3_.1, f32[16,8192]{1,0:T(8,128)} %refs_4_.1), custom_call_target="tpu_custom_call" | custom-call | flops 6553600 | bytes 3145728 | tf_op jit(solution)/shard_map/query_part_0/pallas_call | solution.py:508
  8.4 0.0 collective-permute-done.rim_ref
  8.4 0.0 copy-done
  8.4 0.0 copy-start.1
  8.4 1.6 %copy-done.1 = bf16[128,8192]{1,0:T(8,128)(2,1)S(1)} copy-done((bf16[128,8192]{1,0:T(8,128)(2,1)S(1)}, bf16[128,8192]{1,0:T(8,128)(2,1)}, u32[]{:S(2)}) %copy-start.1) | copy-done | bytes 2097176
  10.0 4.5 %block_states_give.1 = (bf16[128,8192]{1,0:T(8,128)(2,1)S(1)}, f32[64,136,128]{2,1,0:T(8,128)S(1)}, f32[16,4096]{1,0:T(8,128)S(1)}) custom-call(f32[79,8,128]{2,1,0:T(8,128)S(1)} %get-tuple-element.34.masks.refs_0_, bf16[128,8192]{1,0:T(8,128)(2,1)S(1)} %copy-done, bf16[128,8192]{1,0:T(8,128)(2,1)S(1)} %copy-done.1, ...), custom_call_target="tpu_custom_call" | custom-call | flops 32768000 | bytes 6291456 | tf_op jit(solution)/shard_map/block_states_give/pallas_call | solution.py:531
  14.5 2.0 %collective-permute-start.1 = (f32[16,4096]{1,0:T(8,128)S(1)}, f32[16,4096]{1,0:T(8,128)S(1)}, u32[]{:S(2)}, u32[]{:S(2)}) collective-permute-start(f32[16,4096]{1,0:T(8,128)S(1)} %get-tuple-element.39), channel_id=1, source_target_pairs={{0,1},{1,0},{2,3},{3,2},{4,5},{5,4},{6,7},{7,6},{8,9},{9,8},{10,11... | collective-permute-start | bytes 786440 | tf_op jit(solution)/shard_map/ppermute | solution.py:27
  16.5 0.0 copy-start.4
  16.5 0.0 copy-start.5
  16.5 4.5 %block_states_own.1 = (bf16[128,8192]{1,0:T(8,128)(2,1)S(1)}, f32[64,136,128]{2,1,0:T(8,128)S(1)}, f32[16,4096]{1,0:T(8,128)S(1)}) custom-call(f32[79,8,128]{2,1,0:T(8,128)S(1)} %get-tuple-element.34.masks.refs_0_, bf16[128,8192]{1,0:T(8,128)(2,1)S(1)} %copy-done, bf16[128,8192]{1,0:T(8,128)(2,1)S(1)} %copy-done.1, ...), custom_call_target="tpu_custom_call", output_to_operand_aliasing={{0}: (6, {}), {1}: (7, {})} | custom-call | flops 32768000 | bytes 6291456 | tf_op jit(solution)/shard_map/block_states_own/pallas_call | solution.py:531
  21.0 0.0 collective-permute-done.1.got_ref
  21.1 0.2 pair_ends.1
  21.2 2.2 %collective-permute-start.3 = (bf16[16,4096]{1,0:T(8,128)(2,1)S(1)}, bf16[16,4096]{1,0:T(8,128)(2,1)S(1)}, u32[]{:S(2)}, u32[]{:S(2)}) collective-permute-start(bf16[16,4096]{1,0:T(8,128)(2,1)S(1)} %pair_ends.1), channel_id=1, source_target_pairs={{0,4},{1,5},{2,6},{3,7},{4,8},{5,9},{6,10},{7,11},{8,12},{9,13},{1... | collective-permute-start | bytes 393224 | tf_op jit(solution)/shard_map/ppermute | solution.py:23
  23.5 2.2 %collective-permute-start.2 = (bf16[16,4096]{1,0:T(8,128)(2,1)S(1)}, bf16[16,4096]{1,0:T(8,128)(2,1)S(1)}, u32[]{:S(2)}, u32[]{:S(2)}) collective-permute-start(bf16[16,4096]{1,0:T(8,128)(2,1)S(1)} %pair_ends.1), channel_id=1, source_target_pairs={{0,2},{1,3},{2,4},{3,5},{4,6},{5,7},{6,8},{7,9},{8,10},{9,11},{10,... | collective-permute-start | bytes 393224 | tf_op jit(solution)/shard_map/ppermute | solution.py:23
  25.7 0.0 copy-done.4
  25.7 0.0 copy-done.5
  25.7 0.3 sqrt_multiply_fusion.weight_ref
  26.1 2.3 %near_part_0.1.refs_0_ = f32[128,8192]{1,0:T(8,128)S(1)} custom-call(f32[79,8,128]{2,1,0:T(8,128)S(1)} %get-tuple-element.34.masks.refs_0_, bf16[128,8192]{1,0:T(8,128)(2,1)S(1)} %get-tuple-element.47.gate_ref, f32[16,8192]{1,0:T(8,128)S(1)} %get-tuple-element.38.rate_ref, f32[16,8192]{1,0:T(8,128)S(1)} %sqrt_multiply_fusion.weight_ref), custom_call_target="tpu_custom_call" | custom-call | flops 19660800 | bytes 3670016 | tf_op jit(solution)/shard_map/near_part_0/pallas_call | solution.py:560
  28.4 0.7 %collective-permute-done.3.far_ref = bf16[16,4096]{1,0:T(8,128)(2,1)S(1)} collective-permute-done((bf16[16,4096]{1,0:T(8,128)(2,1)S(1)}, bf16[16,4096]{1,0:T(8,128)(2,1)S(1)}, u32[]{:S(2)}, u32[]{:S(2)}) %collective-permute-start.3) | collective-permute-done | bytes 131104 | tf_op jit(solution)/shard_map/ppermute | solution.py:23
  29.1 2.8 %collective-permute-done.2.near_ref = bf16[16,4096]{1,0:T(8,128)(2,1)S(1)} collective-permute-done((bf16[16,4096]{1,0:T(8,128)(2,1)S(1)}, bf16[16,4096]{1,0:T(8,128)(2,1)S(1)}, u32[]{:S(2)}, u32[]{:S(2)}) %collective-permute-start.2) | collective-permute-done | bytes 131104 | tf_op jit(solution)/shard_map/ppermute | solution.py:23
  31.9 0.1 reach_0.1.near_ref
  32.1 3.1 %collective-permute-start.4 = (bf16[16,4096]{1,0:T(8,128)(2,1)S(1)}, bf16[16,4096]{1,0:T(8,128)(2,1)S(1)}, u32[]{:S(2)}, u32[]{:S(2)}) collective-permute-start(bf16[16,4096]{1,0:T(8,128)(2,1)S(1)} %reach_0.1.near_ref), channel_id=1, source_target_pairs={{0,4},{1,5},{2,6},{3,7},{4,8},{5,9},{6,10},{7,11},{8,12},{9,13},{1... | collective-permute-start | bytes 393224 | tf_op jit(solution)/shard_map/ppermute | solution.py:23
  35.2 1.8 %query_part_1.1.short_ref = f32[128,8192]{1,0:T(8,128)S(1)} custom-call(f32[79,8,128]{2,1,0:T(8,128)S(1)} %get-tuple-element.34.masks.refs_0_, bf16[128,8192]{1,0:T(8,128)(2,1)} %refs_1_.3, f32[3,3,8192]{2,1,0:T(4,128)S(1)} %get-tuple-element.37.taps_ref.refs_2_, f32[128,8192]{1,0:T(8,128)S(1)} %get-tuple-element.50.refs_3_), custom_call_target="tpu_custom_call", output_to_operand_aliasing={{}: (3, {})} | custom-call | flops 6553600 | bytes 3145728 | tf_op jit(solution)/shard_map/query_part_1/pallas_call | solution.py:508
  37.1 0.0 copy-start.2
  37.1 2.3 %near_part_1.1.near_ref = f32[128,8192]{1,0:T(8,128)S(1)} custom-call(f32[79,8,128]{2,1,0:T(8,128)S(1)} %get-tuple-element.34.masks.refs_0_, bf16[128,8192]{1,0:T(8,128)(2,1)S(1)} %get-tuple-element.47.gate_ref, f32[16,8192]{1,0:T(8,128)S(1)} %get-tuple-element.38.rate_ref, ...), custom_call_target="tpu_custom_call", output_to_operand_aliasing={{}: (4, {})} | custom-call | flops 19660800 | bytes 3670016 | tf_op jit(solution)/shard_map/near_part_1/pallas_call | solution.py:560
  39.4 0.0 collective-permute-done.4.far_ref
  39.4 0.3 pair_enter.1
  39.7 1.6 %collective-permute-start.5 = (f32[16,4096]{1,0:T(8,128)S(1)}, f32[16,4096]{1,0:T(8,128)S(1)}, u32[]{:S(2)}, u32[]{:S(2)}) collective-permute-start(f32[16,4096]{1,0:T(8,128)S(1)} %get-tuple-element.53), channel_id=1, source_target_pairs={{0,1},{1,0},{2,3},{3,2},{4,5},{5,4},{6,7},{7,6},{8,9},{9,8},{10,11... | collective-permute-start | bytes 786440 | tf_op jit(solution)/shard_map/ppermute | solution.py:27
  41.3 0.0 copy-done.2
  41.3 0.0 copy-start.3
  41.3 4.4 %far_part_own.1 = (bf16[128,8192]{1,0:T(8,128)(2,1)}, f32[64,128,128]{2,1,0:T(8,128)S(1)}, f32[128,128]{1,0:T(8,128)S(1)}) custom-call(f32[79,8,128]{2,1,0:T(8,128)S(1)} %get-tuple-element.34.masks.refs_0_, f32[64,136,128]{2,1,0:T(8,128)S(1)} %get-tuple-element.45.state_ref, f32[16,4096]{1,0:T(8,128)S(1)} %get-tuple-element.54.enter_ref, ...), custom_call_target="tpu_custom_call" | custom-call | flops 29491200 | bytes 9437184 | tf_op jit(solution)/shard_map/far_part_own/pallas_call | solution.py:644
  45.7 0.0 collective-permute-done.5.enter_ref
  45.7 0.0 copy-done.3
  45.7 5.3 %far_part_other.1 = (bf16[128,8192]{1,0:T(8,128)(2,1)}, f32[64,128,128]{2,1,0:T(8,128)S(1)}, f32[128,128]{1,0:T(8,128)S(1)}, bf16[128,8192]{1,0:T(8,128)(2,1)}) custom-call(f32[79,8,128]{2,1,0:T(8,128)S(1)} %get-tuple-element.34.masks.refs_0_, ...), custom_call_target="tpu_custom_call", output_to_operand_aliasing={{0}: (11, {}), {1}: (12, {}), {2}: (13, {})} | custom-call | flops 29491200 | bytes 9437184 | tf_op jit(solution)/shard_map/far_part_other/pallas_call | solution.py:644
Async XLA Ops:
  1.8 6.6 %copy-start = (bf16[128,8192]{1,0:T(8,128)(2,1)S(1)}, bf16[128,8192]{1,0:T(8,128)(2,1)}, u32[]{:S(2)}) copy-start(bf16[128,8192]{1,0:T(8,128)(2,1)} %key_ref.5) | copy-start | bytes 6291460
  1.8 6.6 %collective-permute-start = (bf16[3,2,8192]{2,1,0:T(2,128)(2,1)S(1)}, bf16[3,2,8192]{2,1,0:T(2,128)(2,1)S(1)}, u32[]{:S(2)}, u32[]{:S(2)}) collective-permute-start(bf16[3,2,8192]{2,1,0:T(2,128)(2,1)S(1)} %tails.1), channel_id=1, source_target_pairs={{0,1},{1,2},{2,3},{3,4},{4,5},{5,6},{6,7},{7,8},{8,9},{9,10},{10,1... | collective-permute-start | bytes 294920 | tf_op jit(solution)/shard_map/ppermute | solution.py:23
  8.4 1.6 %copy-start.1 = (bf16[128,8192]{1,0:T(8,128)(2,1)S(1)}, bf16[128,8192]{1,0:T(8,128)(2,1)}, u32[]{:S(2)}) copy-start(bf16[128,8192]{1,0:T(8,128)(2,1)} %value_ref.5) | copy-start | bytes 6291460
  14.5 6.5 %collective-permute-start.1 = (f32[16,4096]{1,0:T(8,128)S(1)}, f32[16,4096]{1,0:T(8,128)S(1)}, u32[]{:S(2)}, u32[]{:S(2)}) collective-permute-start(f32[16,4096]{1,0:T(8,128)S(1)} %get-tuple-element.39), channel_id=1, source_target_pairs={{0,1},{1,0},{2,3},{3,2},{4,5},{5,4},{6,7},{7,6},{8,9},{9,8},{10,11... | collective-permute-start | bytes 786440 | tf_op jit(solution)/shard_map/ppermute | solution.py:27
  16.5 9.2 %copy-start.4 = (f32[16,8192]{1,0:T(8,128)S(1)}, f32[16,8192]{1,0:T(8,128)}, u32[]{:S(2)}) copy-start(f32[16,8192]{1,0:T(8,128)} %refs_4_.1) | copy-start | bytes 1572868
  16.5 9.2 %copy-start.5 = (f32[16,8192]{1,0:T(8,128)S(1)}, f32[16,8192]{1,0:T(8,128)}, u32[]{:S(2)}) copy-start(f32[16,8192]{1,0:T(8,128)} %param.14) | copy-start | bytes 1572868
  21.2 7.9 %collective-permute-start.3 = (bf16[16,4096]{1,0:T(8,128)(2,1)S(1)}, bf16[16,4096]{1,0:T(8,128)(2,1)S(1)}, u32[]{:S(2)}, u32[]{:S(2)}) collective-permute-start(bf16[16,4096]{1,0:T(8,128)(2,1)S(1)} %pair_ends.1), channel_id=1, source_target_pairs={{0,4},{1,5},{2,6},{3,7},{4,8},{5,9},{6,10},{7,11},{8,12},{9,13},{1... | collective-permute-start | bytes 393224 | tf_op jit(solution)/shard_map/ppermute | solution.py:23
  23.5 8.5 %collective-permute-start.2 = (bf16[16,4096]{1,0:T(8,128)(2,1)S(1)}, bf16[16,4096]{1,0:T(8,128)(2,1)S(1)}, u32[]{:S(2)}, u32[]{:S(2)}) collective-permute-start(bf16[16,4096]{1,0:T(8,128)(2,1)S(1)} %pair_ends.1), channel_id=1, source_target_pairs={{0,2},{1,3},{2,4},{3,5},{4,6},{5,7},{6,8},{7,9},{8,10},{9,11},{10,... | collective-permute-start | bytes 393224 | tf_op jit(solution)/shard_map/ppermute | solution.py:23
  32.1 7.4 %collective-permute-start.4 = (bf16[16,4096]{1,0:T(8,128)(2,1)S(1)}, bf16[16,4096]{1,0:T(8,128)(2,1)S(1)}, u32[]{:S(2)}, u32[]{:S(2)}) collective-permute-start(bf16[16,4096]{1,0:T(8,128)(2,1)S(1)} %reach_0.1.near_ref), channel_id=1, source_target_pairs={{0,4},{1,5},{2,6},{3,7},{4,8},{5,9},{6,10},{7,11},{8,12},{9,13},{1... | collective-permute-start | bytes 393224 | tf_op jit(solution)/shard_map/ppermute | solution.py:23
  37.1 4.3 %copy-start.2 = (bf16[128,8192]{1,0:T(8,128)(2,1)S(1)}, bf16[128,8192]{1,0:T(8,128)(2,1)}, u32[]{:S(2)}) copy-start(bf16[128,8192]{1,0:T(8,128)(2,1)} %resid_ref.3) | copy-start | bytes 6291460
  39.7 6.0 %collective-permute-start.5 = (f32[16,4096]{1,0:T(8,128)S(1)}, f32[16,4096]{1,0:T(8,128)S(1)}, u32[]{:S(2)}, u32[]{:S(2)}) collective-permute-start(f32[16,4096]{1,0:T(8,128)S(1)} %get-tuple-element.53), channel_id=1, source_target_pairs={{0,1},{1,0},{2,3},{3,2},{4,5},{5,4},{6,7},{7,6},{8,9},{9,8},{10,11... | collective-permute-start | bytes 786440 | tf_op jit(solution)/shard_map/ppermute | solution.py:27
  41.3 4.4 %copy-start.3 = (f32[8192]{0:T(1024)S(1)}, f32[8192]{0:T(1024)}, u32[]{:S(2)}) copy-start(f32[8192]{0:T(1024)} %param.17) | copy-start | bytes 98308

commit v16 on v14

--- a/solution.py
+++ b/solution.py
@@ -23,8 +23,8 @@
     return lax.ppermute(shard, axis, pairs)
 
 
-def swap(shard, axis):
-    return lax.ppermute(shard, axis, [(i, i ^ 1) for i in range(lax.axis_size(axis))])
+def swap(shard, axis, bit=1):
+    return lax.ppermute(shard, axis, [(i, i ^ bit) for i in range(lax.axis_size(axis))])
 
 
 def doc_start_rows(len_ref, base, span):
@@ -201,13 +201,19 @@
         self.edges = self.passes + SUBS
         self.late = self.edges + 3
         self.early = self.late + 1
-        self.reach = self.late + 2
-
-    def count(self, reaches):
-        return self.reach + reaches
-
-
-def write_masks(base_ref, len_ref, masks, span, reaches):
+        self.levels = self.late + 2
+
+    def lead(self, level):
+        return self.levels + 2 * level
+
+    def later(self, level):
+        return self.levels + 2 * level + 1
+
+    def count(self, levels):
+        return self.levels + 2 * levels + 1
+
+
+def write_masks(base_ref, len_ref, masks, span, levels):
     at = Masks(span)
     rows, starts = doc_start_rows(len_ref, base_ref[0], span)
     for j in range(span):
@@ -226,9 +232,14 @@
     flags = [at.passes + b for b in range(SUBS)]
     ranges += [(pair_at + size, size), (pair_at, size)]
     flags += [at.late, at.early]
-    for m in range(reaches):
-        ranges.append((pair_at - (2 * size << m), 2 * size << m))
-        flags.append(at.reach + m)
+    for m in range(levels + 1):
+        group = 2 * size << m
+        group_at = base_ref[0] - lax.rem(base_ref[0], group)
+        ranges.append((group_at, pair_at - group_at))
+        flags.append(at.lead(m))
+        if m < levels:
+            ranges.append((group_at + group * (1 - lax.rem(lax.div(base_ref[0], group), 2)), group))
+            flags.append(at.later(m))
     for index, (first, count) in zip(flags, ranges):
         masks[index] = jnp.full((SUBS, LANES), unbroken(len_ref, first, count), f32)
 
@@ -272,8 +283,8 @@
     each_group(count // LANES, most, lambda lanes: group([pl.multiple_of(first + lane, LANES) for lane in lanes]))
 
 
-def query_kernel(*refs, span, most, chunk, reaches, first, count):
-    if reaches:
+def query_kernel(*refs, span, most, chunk, levels, first, count):
+    if not first:
         base_ref, len_ref, query_ref, taps_ref, value_in, short_ref, masks, value_ref, query_buf, sems, wide_q, value_sem = refs
         value_copy = pltpu.make_async_copy(value_in, value_ref, value_sem)
     else:
@@ -286,9 +297,9 @@
 
     for c in range(count // chunk):
         fetch(c).start()
-    if reaches:
+    if not first:
         value_copy.start()
-        write_masks(base_ref, len_ref, masks, span, reaches)
+        write_masks(base_ref, len_ref, masks, span, levels)
     at = Masks(span)
 
     def group(lanes):
@@ -304,7 +315,7 @@
                 short_ref[pl.ds(j * SUBS, SUBS), cols_of(pl.multiple_of(first + lane, LANES))] = convs[slot].step(j, keep_one, keep_two)
 
     each_chunk(count, chunk, lambda c: fetch(c).wait(), group, lambda c: None, most)
-    if reaches:
+    if not first:
         value_copy.wait()
 
 
@@ -322,24 +333,41 @@
     return jnp.exp(-float(rows) * rate) * masks[index][0:1, 0:1]
 
 
-def pair_kernel(masks, own_ref, got_ref, rate_ref, end_ref, *, rows, index):
+def pair_kernel(masks, own_ref, got_ref, rate_ref, total_ref, sent_ref, *, rows, index):
     parity, rate = pair_rates(rate_ref, own_ref.shape[1])
     early, late = early_late(parity, own_ref[...], got_ref[...])
-    end_ref[...] = (late + leap(masks, index, rate, rows) * early).astype(bf16)
-
-
-def reach_kernel(masks, near_ref, far_ref, rate_ref, enter_ref, *, rows, index):
-    _, rate = pair_rates(rate_ref, near_ref.shape[1])
-    enter_ref[...] = (near_ref[...].astype(f32) + leap(masks, index, rate, rows) * far_ref[...].astype(f32)).astype(bf16)
+    total = late + leap(masks, index, rate, rows) * early
+    total_ref[...] = total
+    sent_ref[...] = total.astype(bf16)
+
+
+def lead_leap(masks, index, rate, rows, bit):
+    me = lax.axis_index("ctx")
+    lead = (lax.rem(me, bit) - lax.rem(me, 2)) * rows
+    return jnp.exp(rate * -lead.astype(f32)) * masks[index][0:1, 0:1]
+
+
+def level_kernel(masks, total_ref, got_ref, rate_ref, *refs, rows, level, lead, later):
+    before_ref, (new_ref, sent_ref, enter_ref) = (refs[0] if level else None), refs[-3:]
+    _, rate = pair_rates(rate_ref, total_ref.shape[1])
+    bit = 2 << level
+    after = lax.rem(lax.div(lax.axis_index("ctx"), bit), 2)
+    got = got_ref[...].astype(f32)
+    early, late = early_late(after, total_ref[...], got)
+    total = late + leap(masks, later, rate, bit * rows) * early
+    new_ref[...] = total
+    sent_ref[...] = total.astype(bf16)
+    entering = jnp.where(jnp.full(got.shape, after, jnp.int32) == 1, got, 0.0) * lead_leap(masks, lead, rate, rows, bit)
+    enter_ref[...] = entering if before_ref is None else before_ref[...] + entering
 
 
 def enter_kernel(
-    masks, near_ref, far_ref, own_ref, got_ref, rate_ref, mine_ref, give_ref, *, rows, index, block, block_index
+    masks, before_ref, got_ref, own_ref, other_ref, rate_ref, mine_ref, give_ref, *, rows, bit, lead, early_index
 ):
     parity, rate = pair_rates(rate_ref, own_ref.shape[1])
-    first = near_ref[...].astype(f32) + leap(masks, index, rate, rows) * far_ref[...].astype(f32)
-    early, _ = early_late(parity, own_ref[...], got_ref[...])
-    second = early + leap(masks, block_index, rate, block) * first
+    first = before_ref[...] + lead_leap(masks, lead, rate, rows, bit) * got_ref[...].astype(f32)
+    early, _ = early_late(parity, own_ref[...], other_ref[...])
+    second = early + leap(masks, early_index, rate, rows) * first
     give, mine = early_late(parity, second, first)
     mine_ref[...] = mine
     give_ref[...] = give
@@ -481,8 +509,8 @@
         name="tails",
     )(far_off(query_in), far_off(key_in), far_off(value_in))
     rim_rows = from_behind(tails, "ctx", 1)
-    reaches = max(1, (blocks // 8).bit_length() - 1)
-    mask_shape = (Masks(span).count(reaches),) + tile_shape
+    levels = max(1, (blocks // 4).bit_length() - 2)
+    mask_shape = (Masks(span).count(levels),) + tile_shape
 
     def query_piece(part, masks, before):
         count = chans // 2
@@ -502,7 +530,7 @@
             in_specs = [vmem, hbm, vmem, vmem]
         return pl.pallas_call(
             functools.partial(
-                query_kernel, span=span, most=Q_TILES, chunk=chunk, reaches=0 if part else reaches,
+                query_kernel, span=span, most=Q_TILES, chunk=chunk, levels=levels,
                 first=part * count, count=count,
             ),
             in_specs=in_specs,
@@ -573,40 +601,49 @@
 
     at = Masks(span)
 
-    def pair_call(kernel, operands, out_shape, name, **static):
+    def pair_call(kernel, operands, out_shape, name, extra=(), **static):
         return pl.pallas_call(
             functools.partial(kernel, **static),
-            in_specs=[vmem] * (len(operands) + 2),
+            in_specs=[vmem] * (len(operands) + 2 + len(extra)),
             out_specs=[vmem] * len(out_shape),
             out_shape=out_shape,
             compiler_params=params,
             name=name,
-        )(near_by(masks), *[near_by(x) for x in operands], rates)
-
-    ends = pair_call(pair_kernel, [own, got], [sent], "pair_ends", rows=tok_rows, index=at.late)[0]
-    two_on = from_behind(ends, "ctx", 4)
-    near = near_piece(0, None)
-    ends, near = lax.optimization_barrier((ends, near))
-    one_on = from_behind(ends, "ctx", 2)
-    near = near_piece(1, near)
-    one_on, two_on, near = lax.optimization_barrier((one_on, two_on, near))
-    enter, on = one_on, two_on
-    for m in range(reaches - 1):
-        enter = pair_call(
-            reach_kernel, [enter, on], [sent], "reach_%d" % m, rows=2 * tok_rows << m, index=at.reach + m
-        )[0]
-        on = from_behind(enter, "ctx", 4 << m)
+        )(near_by(masks), *[near_by(x) for x in operands], rates, *[near_by(x) for x in extra])
+
+    total, ends = pair_call(pair_kernel, [own, got], [kept, sent], "pair_ends", rows=tok_rows, index=at.late)
+    entering, near = [], None
+    for m in range(levels):
+        met = swap(ends, "ctx", 2 << m)
+        if m < NEAR_PARTS:
+            near = near_piece(m, near)
+            met, near = lax.optimization_barrier((met, near))
+        total, ends, enter = pair_call(
+            level_kernel,
+            [total, met],
+            [kept, sent, kept],
+            "level_%d" % m,
+            extra=entering,
+            rows=tok_rows,
+            level=m,
+            lead=at.lead(m),
+            later=at.later(m),
+        )
+        entering = [enter]
+    on = from_behind(ends, "ctx", 2 << levels)
+    for m in range(levels, NEAR_PARTS):
+        near = near_piece(m, near)
     q_short = query_piece(1, masks, q_short)[0]
-    on, q_short = lax.optimization_barrier((on, q_short))
+    on, q_short, near = lax.optimization_barrier((on, q_short, near))
     mine, give_back = pair_call(
         enter_kernel,
-        [enter, on, own, got],
+        entering + [on, own, got],
         [kept, kept],
         "pair_enter",
-        rows=2 * tok_rows << (reaches - 1),
-        index=at.reach + reaches - 1,
-        block=tok_rows,
-        block_index=at.early,
+        rows=tok_rows,
+        bit=2 << levels,
+        lead=at.lead(levels),
+        early_index=at.early,
     )
     got_back = swap(give_back, "ctx")
 

time: 52.3 us -> 48.9 us (0.935)
  starting transfers between devices: 15.6 us -> 12.2 us
  waiting for transfers between devices: 5.33 us -> 4.39 us
  Pallas kernels: 30 us -> 30.9 us
    ppermute x4 -> x2, waiting for transfers between devices: 5.33 us -> 0.48 us  [from_behind(): return lax.ppermute(shard, axis, pairs)]
    ppermute x4 -> x2, starting transfers between devices: 11.3 us -> 6.87 us  [from_behind(): return lax.ppermute(shard, axis, pairs)]
    ppermute x2 -> x4, waiting for transfers between devices: 0.01 us -> 3.91 us  [swap(): lax.ppermute(shard, axis, [(i, i ^ bit) for i in range(lax.axis_size(axis...]
    ppermute x2 -> x4, starting transfers between devices: 4.27 us -> 5.33 us  [swap(): lax.ppermute(shard, axis, [(i, i ^ bit) for i in range(lax.axis_size(axis...]
    pallas_call x3 -> x4, Pallas kernels: 0.55 us -> 1.57 us  [pair_call(): pl.pallas_call(functools.partial(kernel, **static), in_specs=[vmem] * (le...]
  transfers between devices with their start and end apart: 6 -> 6, of which waited for: 2 -> 3; matrix products, arithmetic and copies ran while one was open for 1% -> 1% of each run, Pallas kernels for 35% -> 38%
where the time goes in v16:
time: 48.9 us; the launch traced here: 48.7 us
  Pallas kernels  30.9 us (63%)
  starting transfers between devices  12.2 us (25%)
  waiting for transfers between devices  4.39 us (9%)
  between operations  0.84 us (2%)
    pallas_call x2, Pallas kernels, finish(): pl.pallas_call(functools.partial(final_kernel, span=span, modes=modes, ch...  9.66 us
    pallas_call x2, Pallas kernels, states_of(): pl.pallas_call(functools.partial(state_kernel, span=span, modes=modes, mo...  9.05 us
    ppermute x2, starting transfers between devices, from_behind(): return lax.ppermute(shard, axis, pairs)  6.87 us
    ppermute x4, starting transfers between devices, swap(): lax.ppermute(shard, axis, [(i, i ^ bit) for i in range(lax.axis_size(axis...  5.33 us
    pallas_call x2, Pallas kernels, query_piece(): pl.pallas_call(functools.partial(query_kernel, span=span, most=Q_TILES, c...  4.78 us
    pallas_call x2, Pallas kernels, near_piece(): pl.pallas_call(functools.partial(near_kernel, span=span, modes=modes, mos...  4.69 us
    ppermute x4, waiting for transfers between devices, swap(): lax.ppermute(shard, axis, [(i, i ^ bit) for i in range(lax.axis_size(axis...  3.91 us
    pallas_call x4, Pallas kernels, pair_call(): pl.pallas_call(functools.partial(kernel, **static), in_specs=[vmem] * (le...  1.57 us
  transfers between devices with their start and end apart: 6, of which 3 were waited for; matrix products, arithmetic and copies ran while one was open for 1% of the time, Pallas kernels for 38%

profile of v16, /device:TPU:9, one launch (start us, length us, event | category | flops | bytes accessed | tf_op | source)
XLA Modules:
  0.0 48.7 jit_solution(13918355671535179233)
XLA Ops:
  0.6 0.0 copy-start.2
  0.6 1.2 %tails.1 = bf16[3,2,8192]{2,1,0:T(2,128)(2,1)S(1)} custom-call(bf16[128,8192]{1,0:T(8,128)(2,1)} %refs_1_.3, bf16[128,8192]{1,0:T(8,128)(2,1)} %key_ref.5, bf16[128,8192]{1,0:T(8,128)(2,1)} %value_ref.1), custom_call_target="tpu_custom_call" | custom-call | tf_op jit(solution)/shard_map/tails/pallas_call | solution.py:502
  1.8 3.7 %collective-permute-start = (bf16[3,2,8192]{2,1,0:T(2,128)(2,1)S(1)}, bf16[3,2,8192]{2,1,0:T(2,128)(2,1)S(1)}, u32[]{:S(2)}, u32[]{:S(2)}) collective-permute-start(bf16[3,2,8192]{2,1,0:T(2,128)(2,1)S(1)} %tails.1), channel_id=1, source_target_pairs={{0,1},{1,2},{2,3},{3,4},{4,5},{5,6},{6,7},{7,8},{8,9},{9,10},{10,1... | collective-permute-start | bytes 294920 | tf_op jit(solution)/shard_map/ppermute | solution.py:23
  5.5 0.0 copy-done.2
  5.5 0.0 copy-start
  5.6 0.0 copy-start.1
  5.6 2.8 %query_part_0.1 = (f32[128,8192]{1,0:T(8,128)S(1)}, f32[82,8,128]{2,1,0:T(8,128)S(1)}, bf16[128,8192]{1,0:T(8,128)(2,1)S(1)}) custom-call(s32[1]{0:T(128)} %bitcast.refs_0_, s32[16]{0:T(128)} %refs_1_.2, bf16[128,8192]{1,0:T(8,128)(2,1)} %refs_1_.3, f32[3,3,8192]{2,1,0:T(4,128)S(1)} %copy-done.2, bf16[128,8192]{1,0:T(8,128)(2,1)} %value_ref.1), custom_call_target="tpu_custom_call" | custom-call | flops 6553600 | bytes 3145728 | tf_op jit(solution)/shard_map/query_part_0/pallas_call | solution.py:531
  8.4 0.0 collective-permute-done.rim_ref
  8.4 0.0 copy-done
  8.4 0.0 copy-done.1
  8.4 4.5 %block_states_give.1 = (bf16[128,8192]{1,0:T(8,128)(2,1)S(1)}, f32[64,136,128]{2,1,0:T(8,128)S(1)}, f32[16,4096]{1,0:T(8,128)S(1)}) custom-call(f32[82,8,128]{2,1,0:T(8,128)S(1)} %get-tuple-element.42.masks.refs_0_, bf16[128,8192]{1,0:T(8,128)(2,1)S(1)} %copy-done.1, bf16[128,8192]{1,0:T(8,128)(2,1)S(1)} %get-tuple-element.45.value_ref, ...), custom_call_target="tpu_custom_call" | custom-call | flops 32768000 | bytes 6291456 | tf_op jit(solution)/shard_map/block_states_give/pallas_call | solution.py:554
  12.9 1.9 %collective-permute-start.1 = (f32[16,4096]{1,0:T(8,128)S(1)}, f32[16,4096]{1,0:T(8,128)S(1)}, u32[]{:S(2)}, u32[]{:S(2)}) collective-permute-start(f32[16,4096]{1,0:T(8,128)S(1)} %get-tuple-element.47), channel_id=1, source_target_pairs={{0,1},{1,0},{2,3},{3,2},{4,5},{5,4},{6,7},{7,6},{8,9},{9,8},{10,11... | collective-permute-start | bytes 786440 | tf_op jit(solution)/shard_map/ppermute | solution.py:27
  14.9 0.0 copy-start.5
  14.9 4.5 %block_states_own.1 = (bf16[128,8192]{1,0:T(8,128)(2,1)S(1)}, f32[64,136,128]{2,1,0:T(8,128)S(1)}, f32[16,4096]{1,0:T(8,128)S(1)}) custom-call(f32[82,8,128]{2,1,0:T(8,128)S(1)} %get-tuple-element.42.masks.refs_0_, bf16[128,8192]{1,0:T(8,128)(2,1)S(1)} %copy-done.1, ...), custom_call_target="tpu_custom_call", output_to_operand_aliasing={{0}: (6, {}), {1}: (7, {})} | custom-call | flops 32768000 | bytes 6291456 | tf_op jit(solution)/shard_map/block_states_own/pallas_call | solution.py:554
  19.4 0.0 collective-permute-done.1.got_ref.other_ref
  19.4 0.2 pair_ends.1
  19.6 0.1 collective-permute-start.2
  19.6 0.0 copy-done.5
  19.7 0.3 sqrt_multiply_fusion.weight_ref
  20.0 2.3 %near_part_0.1.refs_0_ = f32[128,8192]{1,0:T(8,128)S(1)} custom-call(f32[82,8,128]{2,1,0:T(8,128)S(1)} %get-tuple-element.42.masks.refs_0_, bf16[128,8192]{1,0:T(8,128)(2,1)S(1)} %get-tuple-element.57.gate_ref, f32[16,8192]{1,0:T(8,128)S(1)} %copy-done, f32[16,8192]{1,0:T(8,128)S(1)} %sqrt_multiply_fusion.weight_ref), custom_call_target="tpu_custom_call" | custom-call | flops 19660800 | bytes 3670016 | tf_op jit(solution)/shard_map/near_part_0/pallas_call | solution.py:583
  22.3 2.4 %collective-permute-done.2.got_ref = bf16[16,4096]{1,0:T(8,128)(2,1)S(1)} collective-permute-done((bf16[16,4096]{1,0:T(8,128)(2,1)S(1)}, bf16[16,4096]{1,0:T(8,128)(2,1)S(1)}, u32[]{:S(2)}, u32[]{:S(2)}) %collective-permute-start.2) | collective-permute-done | bytes 131104 | tf_op jit(solution)/shard_map/ppermute | solution.py:27
  24.7 0.2 level_0.1
  25.0 0.4 collective-permute-start.3
  25.4 2.3 %near_part_1.1.near_ref = f32[128,8192]{1,0:T(8,128)S(1)} custom-call(f32[82,8,128]{2,1,0:T(8,128)S(1)} %get-tuple-element.42.masks.refs_0_, bf16[128,8192]{1,0:T(8,128)(2,1)S(1)} %get-tuple-element.57.gate_ref, f32[16,8192]{1,0:T(8,128)S(1)} %copy-done, f32[16,8192]{1,0:T(8,128)S(1)} %sqrt_multiply_fusion.weight_ref, ...), custom_call_target="tpu_custom_call", output_to_operand_aliasing={{}: (4, {})} | custom-call | flops 19660800 | bytes 3670016 | tf_op jit(solution)/shard_map/near_part_1/pallas_call | solution.py:583
  27.7 1.5 %collective-permute-done.3.got_ref = bf16[16,4096]{1,0:T(8,128)(2,1)S(1)} collective-permute-done((bf16[16,4096]{1,0:T(8,128)(2,1)S(1)}, bf16[16,4096]{1,0:T(8,128)(2,1)S(1)}, u32[]{:S(2)}, u32[]{:S(2)}) %collective-permute-start.3) | collective-permute-done | bytes 131104 | tf_op jit(solution)/shard_map/ppermute | solution.py:27
  29.2 0.9 %level_1.1 = (f32[16,4096]{1,0:T(8,128)}, bf16[16,4096]{1,0:T(8,128)(2,1)S(1)}, f32[16,4096]{1,0:T(8,128)S(1)}) custom-call(f32[82,8,128]{2,1,0:T(8,128)S(1)} %get-tuple-element.42.masks.refs_0_, f32[16,4096]{1,0:T(8,128)S(1)} %get-tuple-element.59.total_ref, bf16[16,4096]{1,0:T(8,128)(2,1)S(1)} %collective-permute-done.3.got_ref, f32[16,8192]{1,0:T(8,128)S(1)} %copy-done, ...), custom_call_target="tpu_custom_call" | custom-call | tf_op jit(solution)/shard_map/level_1/pallas_call | solution.py:605
  30.1 3.2 %collective-permute-start.4 = (bf16[16,4096]{1,0:T(8,128)(2,1)S(1)}, bf16[16,4096]{1,0:T(8,128)(2,1)S(1)}, u32[]{:S(2)}, u32[]{:S(2)}) collective-permute-start(bf16[16,4096]{1,0:T(8,128)(2,1)S(1)} %get-tuple-element.65), channel_id=1, source_target_pairs={{0,8},{1,9},{2,10},{3,11},{4,12},{5,13},{6,14},{7,15},{8,16},{9,17... | collective-permute-start | bytes 393224 | tf_op jit(solution)/shard_map/ppermute | solution.py:23
  33.3 0.0 copy-start.3
  33.3 2.0 %query_part_1.1.short_ref = f32[128,8192]{1,0:T(8,128)S(1)} custom-call(f32[82,8,128]{2,1,0:T(8,128)S(1)} %get-tuple-element.42.masks.refs_0_, bf16[128,8192]{1,0:T(8,128)(2,1)} %refs_1_.3, f32[3,3,8192]{2,1,0:T(4,128)S(1)} %copy-done.2, f32[128,8192]{1,0:T(8,128)S(1)} %get-tuple-element.66.refs_3_), custom_call_target="tpu_custom_call", output_to_operand_aliasing={{}: (3, {})} | custom-call | flops 6553600 | bytes 3145728 | tf_op jit(solution)/shard_map/query_part_1/pallas_call | solution.py:531
  35.4 0.5 collective-permute-done.4.got_ref
  35.8 0.3 pair_enter.1
  36.1 2.9 %collective-permute-start.5 = (f32[16,4096]{1,0:T(8,128)S(1)}, f32[16,4096]{1,0:T(8,128)S(1)}, u32[]{:S(2)}, u32[]{:S(2)}) collective-permute-start(f32[16,4096]{1,0:T(8,128)S(1)} %get-tuple-element.69), channel_id=1, source_target_pairs={{0,1},{1,0},{2,3},{3,2},{4,5},{5,4},{6,7},{7,6},{8,9},{9,8},{10,11... | collective-permute-start | bytes 786440 | tf_op jit(solution)/shard_map/ppermute | solution.py:27
  39.0 0.0 copy-done.3
  39.0 0.0 copy-start.4
  39.0 4.4 %far_part_own.1 = (bf16[128,8192]{1,0:T(8,128)(2,1)}, f32[64,128,128]{2,1,0:T(8,128)S(1)}, f32[128,128]{1,0:T(8,128)S(1)}) custom-call(f32[82,8,128]{2,1,0:T(8,128)S(1)} %get-tuple-element.42.masks.refs_0_, f32[64,136,128]{2,1,0:T(8,128)S(1)} %get-tuple-element.53.state_ref, f32[16,4096]{1,0:T(8,128)S(1)} %get-tuple-element.70.enter_ref, ...), custom_call_target="tpu_custom_call" | custom-call | flops 29491200 | bytes 9437184 | tf_op jit(solution)/shard_map/far_part_own/pallas_call | solution.py:679
  43.4 0.0 collective-permute-done.5.enter_ref
  43.4 0.0 copy-done.4
  43.4 5.3 %far_part_other.1 = (bf16[128,8192]{1,0:T(8,128)(2,1)}, f32[64,128,128]{2,1,0:T(8,128)S(1)}, f32[128,128]{1,0:T(8,128)S(1)}, bf16[128,8192]{1,0:T(8,128)(2,1)}) custom-call(f32[82,8,128]{2,1,0:T(8,128)S(1)} %get-tuple-element.42.masks.refs_0_, ...), custom_call_target="tpu_custom_call", output_to_operand_aliasing={{0}: (11, {}), {1}: (12, {}), {2}: (13, {})} | custom-call | flops 29491200 | bytes 9437184 | tf_op jit(solution)/shard_map/far_part_other/pallas_call | solution.py:679
Async XLA Ops:
  0.6 4.9 %copy-start.2 = (f32[3,3,8192]{2,1,0:T(4,128)S(1)}, f32[3,3,8192]{2,1,0:T(4,128)}, u32[]{:S(2)}) copy-start(f32[3,3,8192]{2,1,0:T(4,128)} %taps_ref.7) | copy-start | bytes 884740
  1.8 6.5 %collective-permute-start = (bf16[3,2,8192]{2,1,0:T(2,128)(2,1)S(1)}, bf16[3,2,8192]{2,1,0:T(2,128)(2,1)S(1)}, u32[]{:S(2)}, u32[]{:S(2)}) collective-permute-start(bf16[3,2,8192]{2,1,0:T(2,128)(2,1)S(1)} %tails.1), channel_id=1, source_target_pairs={{0,1},{1,2},{2,3},{3,4},{4,5},{5,6},{6,7},{7,8},{8,9},{9,10},{10,1... | collective-permute-start | bytes 294920 | tf_op jit(solution)/shard_map/ppermute | solution.py:23
  5.5 2.8 %copy-start = (f32[16,8192]{1,0:T(8,128)S(1)}, f32[16,8192]{1,0:T(8,128)}, u32[]{:S(2)}) copy-start(f32[16,8192]{1,0:T(8,128)} %rate_ref.19) | copy-start | bytes 1572868
  5.6 2.8 %copy-start.1 = (bf16[128,8192]{1,0:T(8,128)(2,1)S(1)}, bf16[128,8192]{1,0:T(8,128)(2,1)}, u32[]{:S(2)}) copy-start(bf16[128,8192]{1,0:T(8,128)(2,1)} %key_ref.5) | copy-start | bytes 6291460
  12.9 6.5 %collective-permute-start.1 = (f32[16,4096]{1,0:T(8,128)S(1)}, f32[16,4096]{1,0:T(8,128)S(1)}, u32[]{:S(2)}, u32[]{:S(2)}) collective-permute-start(f32[16,4096]{1,0:T(8,128)S(1)} %get-tuple-element.47), channel_id=1, source_target_pairs={{0,1},{1,0},{2,3},{3,2},{4,5},{5,4},{6,7},{7,6},{8,9},{9,8},{10,11... | collective-permute-start | bytes 786440 | tf_op jit(solution)/shard_map/ppermute | solution.py:27
  14.9 4.8 %copy-start.5 = (f32[16,8192]{1,0:T(8,128)S(1)}, f32[16,8192]{1,0:T(8,128)}, u32[]{:S(2)}) copy-start(f32[16,8192]{1,0:T(8,128)} %param.14) | copy-start | bytes 1572868
  19.6 5.2 %collective-permute-start.2 = (bf16[16,4096]{1,0:T(8,128)(2,1)S(1)}, bf16[16,4096]{1,0:T(8,128)(2,1)S(1)}, u32[]{:S(2)}, u32[]{:S(2)}) collective-permute-start(bf16[16,4096]{1,0:T(8,128)(2,1)S(1)} %get-tuple-element.56), channel_id=1, source_target_pairs={{0,2},{1,3},{2,0},{3,1},{4,6},{5,7},{6,4},{7,5},{8,10},{9,11},{10,... | collective-permute-start | bytes 393224 | tf_op jit(solution)/shard_map/ppermute | solution.py:27
  25.0 4.3 %collective-permute-start.3 = (bf16[16,4096]{1,0:T(8,128)(2,1)S(1)}, bf16[16,4096]{1,0:T(8,128)(2,1)S(1)}, u32[]{:S(2)}, u32[]{:S(2)}) collective-permute-start(bf16[16,4096]{1,0:T(8,128)(2,1)S(1)} %get-tuple-element.60), channel_id=1, source_target_pairs={{0,4},{1,5},{2,6},{3,7},{4,0},{5,1},{6,2},{7,3},{8,12},{9,13},{10,... | collective-permute-start | bytes 393224 | tf_op jit(solution)/shard_map/ppermute | solution.py:27
  30.1 5.7 %collective-permute-start.4 = (bf16[16,4096]{1,0:T(8,128)(2,1)S(1)}, bf16[16,4096]{1,0:T(8,128)(2,1)S(1)}, u32[]{:S(2)}, u32[]{:S(2)}) collective-permute-start(bf16[16,4096]{1,0:T(8,128)(2,1)S(1)} %get-tuple-element.65), channel_id=1, source_target_pairs={{0,8},{1,9},{2,10},{3,11},{4,12},{5,13},{6,14},{7,15},{8,16},{9,17... | collective-permute-start | bytes 393224 | tf_op jit(solution)/shard_map/ppermute | solution.py:23
  33.3 5.7 %copy-start.3 = (bf16[128,8192]{1,0:T(8,128)(2,1)S(1)}, bf16[128,8192]{1,0:T(8,128)(2,1)}, u32[]{:S(2)}) copy-start(bf16[128,8192]{1,0:T(8,128)(2,1)} %resid_ref.3) | copy-start | bytes 6291460
  36.1 7.3 %collective-permute-start.5 = (f32[16,4096]{1,0:T(8,128)S(1)}, f32[16,4096]{1,0:T(8,128)S(1)}, u32[]{:S(2)}, u32[]{:S(2)}) collective-permute-start(f32[16,4096]{1,0:T(8,128)S(1)} %get-tuple-element.69), channel_id=1, source_target_pairs={{0,1},{1,0},{2,3},{3,2},{4,5},{5,4},{6,7},{7,6},{8,9},{9,8},{10,11... | collective-permute-start | bytes 786440 | tf_op jit(solution)/shard_map/ppermute | solution.py:27
  39.0 4.4 %copy-start.4 = (f32[8192]{0:T(1024)S(1)}, f32[8192]{0:T(1024)}, u32[]{:S(2)}) copy-start(f32[8192]{0:T(1024)} %param.17) | copy-start | bytes 98308

commit v17 on v16

--- a/solution.py
+++ b/solution.py
@@ -17,14 +17,14 @@
 bf16 = jnp.bfloat16
 
 
-def from_behind(shard, axis, by):
-    count = lax.axis_size(axis)
-    pairs = [(i, i + by) for i in range(count) if 0 <= i + by < count]
-    return lax.ppermute(shard, axis, pairs)
-
-
 def swap(shard, axis, bit=1):
     return lax.ppermute(shard, axis, [(i, i ^ bit) for i in range(lax.axis_size(axis))])
+
+
+def swap_across(shard, axis, size):
+    count = lax.axis_size(axis)
+    pairs = [(i, i + size) for i in range(count - size) if (i // size) % 2 == 1]
+    return lax.ppermute(shard, axis, pairs + [(j, i) for i, j in pairs])
 
 
 def doc_start_rows(len_ref, base, span):
@@ -94,7 +94,7 @@
         self.wide, self.span = wide, span
         self.taps = [jnp.broadcast_to(taps[m : m + 1], (SUBS, LANES)) for m in range(3)]
         top = lax.broadcasted_iota(jnp.int32, (SUBS, LANES), 0) == 0
-        ahead = [0.0, 0.0] if rim is None else [jnp.broadcast_to(rim[m : m + 1].astype(f32), (SUBS, LANES)) for m in range(2)]
+        ahead = [0.0, 0.0] if rim is None else [jnp.broadcast_to(rim[m : m + 1], (SUBS, LANES)) for m in range(2)]
         self.behind = [jnp.where(top, ahead[m], pltpu.roll(self.row(span - 2 + m), 1, 0)) for m in range(2)]
 
     def row(self, j):
@@ -107,6 +107,11 @@
         return self.taps[0] * here + (self.taps[1] * one) * keep_one + (self.taps[2] * two) * keep_two
 
 
+def rim_of(even_ref, odd_ref, index, cols):
+    odd = jnp.full((2, LANES), lax.rem(lax.axis_index("ctx"), 2), jnp.int32) == 1
+    return jnp.where(odd, odd_ref[index, :, cols].astype(f32), even_ref[index, :, cols].astype(f32))
+
+
 def half_start(chans, own):
     parity = lax.rem(lax.axis_index("ctx"), 2)
     return pl.multiple_of((parity if own else 1 - parity) * (chans // 2), LANES)
@@ -121,7 +126,7 @@
 
 
 def state_kernel(
-    masks, key_ref, value_ref, rim_ref, taps_ref, rate_ref, *refs, span, modes, most, own
+    masks, key_ref, value_ref, even_ref, odd_ref, taps_ref, rate_ref, *refs, span, modes, most, own
 ):
     gate_ref, state_ref, end_ref, wide_k, wide_v, tables, held = refs[-7:]
     half = key_ref.shape[1] // 2
@@ -136,7 +141,7 @@
             tables[slot] = jnp.exp(-rate)
         convs = [
             [
-                Conv(wide.at[slot], rim_ref[i, :, cols_of(lane)], taps_ref[i, :, cols_of(lane)], span)
+                Conv(wide.at[slot], rim_of(even_ref, odd_ref, i, cols_of(lane)), taps_ref[i, :, cols_of(lane)], span)
                 for i, wide in ((1, wide_k), (2, wide_v))
             ]
             for slot, lane in enumerate(lanes)
@@ -348,24 +353,29 @@
 
 
 def level_kernel(masks, total_ref, got_ref, rate_ref, *refs, rows, level, lead, later):
-    before_ref, (new_ref, sent_ref, enter_ref) = (refs[0] if level else None), refs[-3:]
+    before_ref = refs[0] if level else None
+    sent_ref, enter_ref, *new_ref = refs[1 if level else 0 :]
     _, rate = pair_rates(rate_ref, total_ref.shape[1])
     bit = 2 << level
     after = lax.rem(lax.div(lax.axis_index("ctx"), bit), 2)
     got = got_ref[...].astype(f32)
     early, late = early_late(after, total_ref[...], got)
     total = late + leap(masks, later, rate, bit * rows) * early
-    new_ref[...] = total
+    for ref in new_ref:
+        ref[...] = total
     sent_ref[...] = total.astype(bf16)
     entering = jnp.where(jnp.full(got.shape, after, jnp.int32) == 1, got, 0.0) * lead_leap(masks, lead, rate, rows, bit)
     enter_ref[...] = entering if before_ref is None else before_ref[...] + entering
 
 
 def enter_kernel(
-    masks, before_ref, got_ref, own_ref, other_ref, rate_ref, mine_ref, give_ref, *, rows, bit, lead, early_index
+    masks, before_ref, even_ref, odd_ref, own_ref, other_ref, rate_ref, mine_ref, give_ref, *, rows, bit, lead, early_index
 ):
     parity, rate = pair_rates(rate_ref, own_ref.shape[1])
-    first = before_ref[...] + lead_leap(masks, lead, rate, rows, bit) * got_ref[...].astype(f32)
+    group = jnp.full(own_ref.shape, lax.div(lax.axis_index("ctx"), bit), jnp.int32)
+    got = jnp.where(lax.rem(group, 2) == 1, odd_ref[...].astype(f32), even_ref[...].astype(f32))
+    got = jnp.where(group == 0, 0.0, got)
+    first = before_ref[...] + lead_leap(masks, lead, rate, rows, bit) * got
     early, _ = early_late(parity, own_ref[...], other_ref[...])
     second = early + leap(masks, early_index, rate, rows) * first
     give, mine = early_late(parity, second, first)
@@ -374,7 +384,7 @@
 
 
 def final_kernel(
-    masks, state_ref, enter_ref, near_ref, short_ref, resid_ref, rim_ref, taps_ref, rate_ref, weight_ref, *refs,
+    masks, state_ref, enter_ref, near_ref, short_ref, resid_ref, even_ref, odd_ref, taps_ref, rate_ref, weight_ref, *refs,
     span, modes, channels, most, chunk, own,
 ):
     if own:
@@ -413,7 +423,7 @@
         for slot, lane in enumerate(lanes):
             part = [starts_at[slot, pl.ds(n, SUBS, stride=modes + 1), :] for n in range(modes)]
             decay = [row_of(tables.at[slot], n) for n in range(modes)]
-            rim = rim_ref[0, :, cols_of(lane)].astype(f32)
+            rim = rim_of(even_ref, odd_ref, 0, cols_of(lane))
             tap = taps_ref[0, :, cols_of(lane)]
             edge = [
                 (tap[1:2] * rim[1:2]) * masks[at.edges] + (tap[2:3] * rim[0:1]) * masks[at.edges + 1],
@@ -508,7 +518,7 @@
         compiler_params=params,
         name="tails",
     )(far_off(query_in), far_off(key_in), far_off(value_in))
-    rim_rows = from_behind(tails, "ctx", 1)
+    rims = (swap_across(tails, "ctx", 1), swap(tails, "ctx"))
     levels = max(1, (blocks // 4).bit_length() - 2)
     mask_shape = (Masks(span).count(levels),) + tile_shape
 
@@ -544,8 +554,8 @@
         )(*operands)
 
     q_short, masks, values = query_piece(0, None, None)
-    rim_rows, q_short, values = lax.optimization_barrier((rim_rows, q_short, values))
-    rates, weights, taps, rims = near_by(decay_rate), near_by(weight), near_by(short_taps), near_by(rim_rows)
+    rims, q_short, values = lax.optimization_barrier((rims, q_short, values))
+    rates, weights, taps, rims = near_by(decay_rate), near_by(weight), near_by(short_taps), [near_by(x) for x in rims]
     kept = pltpu.VMEM((modes, chans // 2), f32)
     sent = pltpu.VMEM((modes, chans // 2), bf16)
     keys, values = near_by(key_in), near_by(values)
@@ -553,7 +563,7 @@
     def states_of(own, before):
         return pl.pallas_call(
             functools.partial(state_kernel, span=span, modes=modes, most=A_TILES, own=own),
-            in_specs=[vmem] * (6 + len(before)),
+            in_specs=[vmem] * (7 + len(before)),
             out_specs=[vmem] * 3,
             out_shape=[
                 pltpu.VMEM((tok_rows, chans), bf16),
@@ -566,11 +576,11 @@
                 pltpu.VMEM((A_TILES, modes, LANES), f32),
                 pltpu.VMEM((A_TILES, span) + tile_shape, f32),
             ],
-            input_output_aliases={6 + i: i for i in range(len(before))},
+            input_output_aliases={7 + i: i for i in range(len(before))},
             compiler_params=params,
             cost_estimate=cost(500, 6 * tok_rows * chans),
             name="block_states_own" if own else "block_states_give",
-        )(near_by(masks), keys, values, rims, taps, rates, *[near_by(x) for x in before])
+        )(near_by(masks), keys, values, *rims, taps, rates, *[near_by(x) for x in before])
 
     gates, states, give = states_of(False, [])
     got = swap(give, "ctx")
@@ -618,10 +628,10 @@
         if m < NEAR_PARTS:
             near = near_piece(m, near)
             met, near = lax.optimization_barrier((met, near))
-        total, ends, enter = pair_call(
+        ends, enter, *total = pair_call(
             level_kernel,
             [total, met],
-            [kept, sent, kept],
+            [sent, kept] + [kept] * (m < levels - 1),
             "level_%d" % m,
             extra=entering,
             rows=tok_rows,
@@ -630,14 +640,15 @@
             later=at.later(m),
         )
         entering = [enter]
-    on = from_behind(ends, "ctx", 2 << levels)
+        total = total[0] if total else None
+    on = (swap_across(ends, "ctx", 2 << levels), swap(ends, "ctx", 2 << levels))
     for m in range(levels, NEAR_PARTS):
         near = near_piece(m, near)
     q_short = query_piece(1, masks, q_short)[0]
     on, q_short, near = lax.optimization_barrier((on, q_short, near))
     mine, give_back = pair_call(
         enter_kernel,
-        entering + [on, own, got],
+        entering + [*on, own, got],
         [kept, kept],
         "pair_enter",
         rows=tok_rows,
@@ -665,7 +676,7 @@
             pltpu.VMEM((F_TILES, modes, LANES), f32),
             pltpu.VMEM((F_TILES, SUBS * (modes + 1), LANES), f32),
         ]
-        operands = [near_by(x) for x in (masks, states, enter, near, q_short)] + [resid, rims, taps, rates, weights]
+        operands = [near_by(x) for x in (masks, states, enter, near, q_short)] + [resid, *rims, taps, rates, weights]
         if last:
             operands.append(near_by(norm_gain.reshape(1, chans)))
             out_specs.append(hbm)

time: 48.9 us -> 50.4 us (1.031)
  starting transfers between devices: 12.2 us -> 14 us
    ppermute x4 -> x6, waiting for transfers between devices: 3.91 us -> 2.64 us  [swap(): lax.ppermute(shard, axis, [(i, i ^ bit) for i in range(lax.axis_size(axis...]
    ppermute x4 -> x6, starting transfers between devices: 5.33 us -> 6.46 us  [swap(): lax.ppermute(shard, axis, [(i, i ^ bit) for i in range(lax.axis_size(axis...]
    ppermute x2, waiting for transfers between devices: 0.48 us -> 1.43 us  [swap_across(): return lax.ppermute(shard, axis, pairs + [(j, i) for i, j in pairs])]
    ppermute x2, starting transfers between devices: 6.87 us -> 7.49 us  [swap_across(): return lax.ppermute(shard, axis, pairs + [(j, i) for i, j in pairs])]
    pallas_call x4, Pallas kernels: 1.57 us -> 0.98 us  [pair_call(): pl.pallas_call(functools.partial(kernel, **static), in_specs=[vmem] * (le...]
  transfers between devices with their start and end apart: 6 -> 8, of which waited for: 3 -> 4; matrix products, arithmetic and copies ran while one was open for 1% -> 1% of each run, Pallas kernels for 38% -> 37%
where the time goes in v17:
time: 50.4 us; the launch traced here: 49.7 us
  Pallas kernels  30.5 us (61%)
  starting transfers between devices  14 us (28%)
  waiting for transfers between devices  4.07 us (8%)
  between operations  0.83 us (2%)
    pallas_call x2, Pallas kernels, finish(): pl.pallas_call(functools.partial(final_kernel, span=span, modes=modes, ch...  9.74 us
    pallas_call x2, Pallas kernels, states_of(): pl.pallas_call(functools.partial(state_kernel, span=span, modes=modes, mo...  9.16 us
    ppermute x2, starting transfers between devices, swap_across(): return lax.ppermute(shard, axis, pairs + [(j, i) for i, j in pairs])  7.49 us
    ppermute x6, starting transfers between devices, swap(): lax.ppermute(shard, axis, [(i, i ^ bit) for i in range(lax.axis_size(axis...  6.46 us
    pallas_call x2, Pallas kernels, query_piece(): pl.pallas_call(functools.partial(query_kernel, span=span, most=Q_TILES, c...  4.78 us
    pallas_call x2, Pallas kernels, near_piece(): pl.pallas_call(functools.partial(near_kernel, span=span, modes=modes, mos...  4.69 us
    ppermute x6, waiting for transfers between devices, swap(): lax.ppermute(shard, axis, [(i, i ^ bit) for i in range(lax.axis_size(axis...  2.64 us
    ppermute x2, waiting for transfers between devices, swap_across(): return lax.ppermute(shard, axis, pairs + [(j, i) for i, j in pairs])  1.43 us
  transfers between devices with their start and end apart: 8, of which 4 were waited for; matrix products, arithmetic and copies ran while one was open for 1% of the time, Pallas kernels for 37%

profile of v17, /device:TPU:9, one launch (start us, length us, event | category | flops | bytes accessed | tf_op | source)
XLA Modules:
  0.0 49.7 jit_solution(4187741535566455706)
XLA Ops:
  0.6 0.0 copy-start.2
  0.6 1.2 %tails.1 = bf16[3,2,8192]{2,1,0:T(2,128)(2,1)S(1)} custom-call(bf16[128,8192]{1,0:T(8,128)(2,1)} %refs_1_.3, bf16[128,8192]{1,0:T(8,128)(2,1)} %key_ref.5, bf16[128,8192]{1,0:T(8,128)(2,1)} %value_ref.1), custom_call_target="tpu_custom_call" | custom-call | tf_op jit(solution)/shard_map/tails/pallas_call | solution.py:512
  1.8 0.7 %collective-permute-start.1 = (bf16[3,2,8192]{2,1,0:T(2,128)(2,1)S(1)}, bf16[3,2,8192]{2,1,0:T(2,128)(2,1)S(1)}, u32[]{:S(2)}, u32[]{:S(2)}) collective-permute-start(bf16[3,2,8192]{2,1,0:T(2,128)(2,1)S(1)} %tails.1), channel_id=1, source_target_pairs={{0,1},{1,0},{2,3},{3,2},{4,5},{5,4},{6,7},{7,6},{8,9},{9,8},{10,11... | collective-permute-start | bytes 294920 | tf_op jit(solution)/shard_map/ppermute | solution.py:21
  2.6 3.0 %collective-permute-start = (bf16[3,2,8192]{2,1,0:T(2,128)(2,1)S(1)}, bf16[3,2,8192]{2,1,0:T(2,128)(2,1)S(1)}, u32[]{:S(2)}, u32[]{:S(2)}) collective-permute-start(bf16[3,2,8192]{2,1,0:T(2,128)(2,1)S(1)} %tails.1), channel_id=1, source_target_pairs={{1,2},{3,4},{5,6},{7,8},{9,10},{11,12},{13,14},{15,16},{17,18},{19... | collective-permute-start | bytes 294920 | tf_op jit(solution)/shard_map/ppermute | solution.py:27
  5.6 0.0 copy-done.2
  5.6 0.0 copy-start
  5.6 0.0 copy-start.1
  5.7 2.8 %query_part_0.1 = (f32[128,8192]{1,0:T(8,128)S(1)}, f32[82,8,128]{2,1,0:T(8,128)S(1)}, bf16[128,8192]{1,0:T(8,128)(2,1)S(1)}) custom-call(s32[1]{0:T(128)} %bitcast.refs_0_, s32[16]{0:T(128)} %refs_1_.2, bf16[128,8192]{1,0:T(8,128)(2,1)} %refs_1_.3, f32[3,3,8192]{2,1,0:T(4,128)S(1)} %copy-done.2, bf16[128,8192]{1,0:T(8,128)(2,1)} %value_ref.1), custom_call_target="tpu_custom_call" | custom-call | flops 6553600 | bytes 3145728 | tf_op jit(solution)/shard_map/query_part_0/pallas_call | solution.py:541
  8.4 0.0 collective-permute-done.1.odd_ref
  8.4 1.1 %collective-permute-done.even_ref = bf16[3,2,8192]{2,1,0:T(2,128)(2,1)S(1)} collective-permute-done((bf16[3,2,8192]{2,1,0:T(2,128)(2,1)S(1)}, bf16[3,2,8192]{2,1,0:T(2,128)(2,1)S(1)}, u32[]{:S(2)}, u32[]{:S(2)}) %collective-permute-start) | collective-permute-done | bytes 98336 | tf_op jit(solution)/shard_map/ppermute | solution.py:27
  9.6 0.0 copy-done
  9.6 0.0 copy-done.1
  9.6 4.6 %block_states_give.1 = (bf16[128,8192]{1,0:T(8,128)(2,1)S(1)}, f32[64,136,128]{2,1,0:T(8,128)S(1)}, f32[16,4096]{1,0:T(8,128)S(1)}) custom-call(f32[82,8,128]{2,1,0:T(8,128)S(1)} %get-tuple-element.44.masks.refs_0_, bf16[128,8192]{1,0:T(8,128)(2,1)S(1)} %copy-done.1, bf16[128,8192]{1,0:T(8,128)(2,1)S(1)} %get-tuple-element.47.value_ref, ...), custom_call_target="tpu_custom_call" | custom-call | flops 32768000 | bytes 6291456 | tf_op jit(solution)/shard_map/block_states_give/pallas_call | solution.py:564
  14.2 0.9 %collective-permute-start.2 = (f32[16,4096]{1,0:T(8,128)S(1)}, f32[16,4096]{1,0:T(8,128)S(1)}, u32[]{:S(2)}, u32[]{:S(2)}) collective-permute-start(f32[16,4096]{1,0:T(8,128)S(1)} %get-tuple-element.50), channel_id=1, source_target_pairs={{0,1},{1,0},{2,3},{3,2},{4,5},{5,4},{6,7},{7,6},{8,9},{9,8},{10,11... | collective-permute-start | bytes 786440 | tf_op jit(solution)/shard_map/ppermute | solution.py:21
  15.1 0.0 copy-start.5
  15.1 4.6 %block_states_own.1 = (bf16[128,8192]{1,0:T(8,128)(2,1)S(1)}, f32[64,136,128]{2,1,0:T(8,128)S(1)}, f32[16,4096]{1,0:T(8,128)S(1)}) custom-call(f32[82,8,128]{2,1,0:T(8,128)S(1)} %get-tuple-element.44.masks.refs_0_, bf16[128,8192]{1,0:T(8,128)(2,1)S(1)} %copy-done.1, ...), custom_call_target="tpu_custom_call", output_to_operand_aliasing={{0}: (7, {}), {1}: (8, {})} | custom-call | flops 32768000 | bytes 6291456 | tf_op jit(solution)/shard_map/block_states_own/pallas_call | solution.py:564
  19.7 0.0 collective-permute-done.2.got_ref.other_ref
  19.7 0.2 pair_ends.1
  19.9 0.7 %collective-permute-start.3 = (bf16[16,4096]{1,0:T(8,128)(2,1)S(1)}, bf16[16,4096]{1,0:T(8,128)(2,1)S(1)}, u32[]{:S(2)}, u32[]{:S(2)}) collective-permute-start(bf16[16,4096]{1,0:T(8,128)(2,1)S(1)} %get-tuple-element.59), channel_id=1, source_target_pairs={{0,2},{1,3},{2,0},{3,1},{4,6},{5,7},{6,4},{7,5},{8,10},{9,11},{10,... | collective-permute-start | bytes 393224 | tf_op jit(solution)/shard_map/ppermute | solution.py:21
  20.6 0.0 copy-done.5
  20.6 0.3 sqrt_multiply_fusion.weight_ref
  20.9 2.3 %near_part_0.1.refs_0_ = f32[128,8192]{1,0:T(8,128)S(1)} custom-call(f32[82,8,128]{2,1,0:T(8,128)S(1)} %get-tuple-element.44.masks.refs_0_, bf16[128,8192]{1,0:T(8,128)(2,1)S(1)} %get-tuple-element.60.gate_ref, f32[16,8192]{1,0:T(8,128)S(1)} %copy-done, f32[16,8192]{1,0:T(8,128)S(1)} %sqrt_multiply_fusion.weight_ref), custom_call_target="tpu_custom_call" | custom-call | flops 19660800 | bytes 3670016 | tf_op jit(solution)/shard_map/near_part_0/pallas_call | solution.py:593
  23.3 1.8 %collective-permute-done.3.got_ref = bf16[16,4096]{1,0:T(8,128)(2,1)S(1)} collective-permute-done((bf16[16,4096]{1,0:T(8,128)(2,1)S(1)}, bf16[16,4096]{1,0:T(8,128)(2,1)S(1)}, u32[]{:S(2)}, u32[]{:S(2)}) %collective-permute-start.3) | collective-permute-done | bytes 131104 | tf_op jit(solution)/shard_map/ppermute | solution.py:21
  25.0 0.2 level_0.1
  25.3 1.0 %collective-permute-start.4 = (bf16[16,4096]{1,0:T(8,128)(2,1)S(1)}, bf16[16,4096]{1,0:T(8,128)(2,1)S(1)}, u32[]{:S(2)}, u32[]{:S(2)}) collective-permute-start(bf16[16,4096]{1,0:T(8,128)(2,1)S(1)} %get-tuple-element.63), channel_id=1, source_target_pairs={{0,4},{1,5},{2,6},{3,7},{4,0},{5,1},{6,2},{7,3},{8,12},{9,13},{10,... | collective-permute-start | bytes 393224 | tf_op jit(solution)/shard_map/ppermute | solution.py:21
  26.3 2.3 %near_part_1.1.near_ref = f32[128,8192]{1,0:T(8,128)S(1)} custom-call(f32[82,8,128]{2,1,0:T(8,128)S(1)} %get-tuple-element.44.masks.refs_0_, bf16[128,8192]{1,0:T(8,128)(2,1)S(1)} %get-tuple-element.60.gate_ref, f32[16,8192]{1,0:T(8,128)S(1)} %copy-done, f32[16,8192]{1,0:T(8,128)S(1)} %sqrt_multiply_fusion.weight_ref, ...), custom_call_target="tpu_custom_call", output_to_operand_aliasing={{}: (4, {})} | custom-call | flops 19660800 | bytes 3670016 | tf_op jit(solution)/shard_map/near_part_1/pallas_call | solution.py:593
  28.7 0.9 %collective-permute-done.4.got_ref = bf16[16,4096]{1,0:T(8,128)(2,1)S(1)} collective-permute-done((bf16[16,4096]{1,0:T(8,128)(2,1)S(1)}, bf16[16,4096]{1,0:T(8,128)(2,1)S(1)}, u32[]{:S(2)}, u32[]{:S(2)}) %collective-permute-start.4) | collective-permute-done | bytes 131104 | tf_op jit(solution)/shard_map/ppermute | solution.py:21
  29.5 0.3 level_1.1
  29.8 0.1 collective-permute-start.6
  29.9 4.5 %collective-permute-start.5 = (bf16[16,4096]{1,0:T(8,128)(2,1)S(1)}, bf16[16,4096]{1,0:T(8,128)(2,1)S(1)}, u32[]{:S(2)}, u32[]{:S(2)}) collective-permute-start(bf16[16,4096]{1,0:T(8,128)(2,1)S(1)} %get-tuple-element.68), channel_id=1, source_target_pairs={{8,16},{9,17},{10,18},{11,19},{12,20},{13,21},{14,22},{15,23},{16,... | collective-permute-start | bytes 393224 | tf_op jit(solution)/shard_map/ppermute | solution.py:27
  34.4 0.0 copy-start.3
  34.4 2.0 %query_part_1.1.short_ref = f32[128,8192]{1,0:T(8,128)S(1)} custom-call(f32[82,8,128]{2,1,0:T(8,128)S(1)} %get-tuple-element.44.masks.refs_0_, bf16[128,8192]{1,0:T(8,128)(2,1)} %refs_1_.3, f32[3,3,8192]{2,1,0:T(4,128)S(1)} %copy-done.2, f32[128,8192]{1,0:T(8,128)S(1)} %get-tuple-element.69.refs_3_), custom_call_target="tpu_custom_call", output_to_operand_aliasing={{}: (3, {})} | custom-call | flops 6553600 | bytes 3145728 | tf_op jit(solution)/shard_map/query_part_1/pallas_call | solution.py:541
  36.4 0.0 collective-permute-done.6.odd_ref
  36.4 0.3 collective-permute-done.5.even_ref
  36.7 0.3 pair_enter.1
  37.0 2.9 %collective-permute-start.7 = (f32[16,4096]{1,0:T(8,128)S(1)}, f32[16,4096]{1,0:T(8,128)S(1)}, u32[]{:S(2)}, u32[]{:S(2)}) collective-permute-start(f32[16,4096]{1,0:T(8,128)S(1)} %get-tuple-element.73), channel_id=1, source_target_pairs={{0,1},{1,0},{2,3},{3,2},{4,5},{5,4},{6,7},{7,6},{8,9},{9,8},{10,11... | collective-permute-start | bytes 786440 | tf_op jit(solution)/shard_map/ppermute | solution.py:21
  40.0 0.0 copy-done.3
  40.0 0.0 copy-start.4
  40.0 4.4 %far_part_own.1 = (bf16[128,8192]{1,0:T(8,128)(2,1)}, f32[64,128,128]{2,1,0:T(8,128)S(1)}, f32[128,128]{1,0:T(8,128)S(1)}) custom-call(f32[82,8,128]{2,1,0:T(8,128)S(1)} %get-tuple-element.44.masks.refs_0_, f32[64,136,128]{2,1,0:T(8,128)S(1)} %get-tuple-element.56.state_ref, f32[16,4096]{1,0:T(8,128)S(1)} %get-tuple-element.74.enter_ref, ...), custom_call_target="tpu_custom_call" | custom-call | flops 29491200 | bytes 9437184 | tf_op jit(solution)/shard_map/far_part_own/pallas_call | solution.py:690
  44.4 0.0 collective-permute-done.7.enter_ref
  44.4 0.0 copy-done.4
  44.4 5.3 %far_part_other.1 = (bf16[128,8192]{1,0:T(8,128)(2,1)}, f32[64,128,128]{2,1,0:T(8,128)S(1)}, f32[128,128]{1,0:T(8,128)S(1)}, bf16[128,8192]{1,0:T(8,128)(2,1)}) custom-call(f32[82,8,128]{2,1,0:T(8,128)S(1)} %get-tuple-element.44.masks.refs_0_, ...), custom_call_target="tpu_custom_call", output_to_operand_aliasing={{0}: (12, {}), {1}: (13, {}), {2}: (14, {})} | custom-call | flops 29491200 | bytes 9437184 | tf_op jit(solution)/shard_map/far_part_other/pallas_call | solution.py:690
Async XLA Ops:
  0.6 5.0 %copy-start.2 = (f32[3,3,8192]{2,1,0:T(4,128)S(1)}, f32[3,3,8192]{2,1,0:T(4,128)}, u32[]{:S(2)}) copy-start(f32[3,3,8192]{2,1,0:T(4,128)} %taps_ref.7) | copy-start | bytes 884740
  1.8 6.6 %collective-permute-start.1 = (bf16[3,2,8192]{2,1,0:T(2,128)(2,1)S(1)}, bf16[3,2,8192]{2,1,0:T(2,128)(2,1)S(1)}, u32[]{:S(2)}, u32[]{:S(2)}) collective-permute-start(bf16[3,2,8192]{2,1,0:T(2,128)(2,1)S(1)} %tails.1), channel_id=1, source_target_pairs={{0,1},{1,0},{2,3},{3,2},{4,5},{5,4},{6,7},{7,6},{8,9},{9,8},{10,11... | collective-permute-start | bytes 294920 | tf_op jit(solution)/shard_map/ppermute | solution.py:21
  2.6 7.0 %collective-permute-start = (bf16[3,2,8192]{2,1,0:T(2,128)(2,1)S(1)}, bf16[3,2,8192]{2,1,0:T(2,128)(2,1)S(1)}, u32[]{:S(2)}, u32[]{:S(2)}) collective-permute-start(bf16[3,2,8192]{2,1,0:T(2,128)(2,1)S(1)} %tails.1), channel_id=1, source_target_pairs={{1,2},{3,4},{5,6},{7,8},{9,10},{11,12},{13,14},{15,16},{17,18},{19... | collective-permute-start | bytes 294920 | tf_op jit(solution)/shard_map/ppermute | solution.py:27
  5.6 3.9 %copy-start = (f32[16,8192]{1,0:T(8,128)S(1)}, f32[16,8192]{1,0:T(8,128)}, u32[]{:S(2)}) copy-start(f32[16,8192]{1,0:T(8,128)} %rate_ref.19) | copy-start | bytes 1572868
  5.6 3.9 %copy-start.1 = (bf16[128,8192]{1,0:T(8,128)(2,1)S(1)}, bf16[128,8192]{1,0:T(8,128)(2,1)}, u32[]{:S(2)}) copy-start(bf16[128,8192]{1,0:T(8,128)(2,1)} %key_ref.5) | copy-start | bytes 6291460
  14.2 5.5 %collective-permute-start.2 = (f32[16,4096]{1,0:T(8,128)S(1)}, f32[16,4096]{1,0:T(8,128)S(1)}, u32[]{:S(2)}, u32[]{:S(2)}) collective-permute-start(f32[16,4096]{1,0:T(8,128)S(1)} %get-tuple-element.50), channel_id=1, source_target_pairs={{0,1},{1,0},{2,3},{3,2},{4,5},{5,4},{6,7},{7,6},{8,9},{9,8},{10,11... | collective-permute-start | bytes 786440 | tf_op jit(solution)/shard_map/ppermute | solution.py:21
  15.1 5.5 %copy-start.5 = (f32[16,8192]{1,0:T(8,128)S(1)}, f32[16,8192]{1,0:T(8,128)}, u32[]{:S(2)}) copy-start(f32[16,8192]{1,0:T(8,128)} %param.14) | copy-start | bytes 1572868
  19.9 5.2 %collective-permute-start.3 = (bf16[16,4096]{1,0:T(8,128)(2,1)S(1)}, bf16[16,4096]{1,0:T(8,128)(2,1)S(1)}, u32[]{:S(2)}, u32[]{:S(2)}) collective-permute-start(bf16[16,4096]{1,0:T(8,128)(2,1)S(1)} %get-tuple-element.59), channel_id=1, source_target_pairs={{0,2},{1,3},{2,0},{3,1},{4,6},{5,7},{6,4},{7,5},{8,10},{9,11},{10,... | collective-permute-start | bytes 393224 | tf_op jit(solution)/shard_map/ppermute | solution.py:21
  25.3 4.3 %collective-permute-start.4 = (bf16[16,4096]{1,0:T(8,128)(2,1)S(1)}, bf16[16,4096]{1,0:T(8,128)(2,1)S(1)}, u32[]{:S(2)}, u32[]{:S(2)}) collective-permute-start(bf16[16,4096]{1,0:T(8,128)(2,1)S(1)} %get-tuple-element.63), channel_id=1, source_target_pairs={{0,4},{1,5},{2,6},{3,7},{4,0},{5,1},{6,2},{7,3},{8,12},{9,13},{10,... | collective-permute-start | bytes 393224 | tf_op jit(solution)/shard_map/ppermute | solution.py:21
  29.8 6.6 %collective-permute-start.6 = (bf16[16,4096]{1,0:T(8,128)(2,1)S(1)}, bf16[16,4096]{1,0:T(8,128)(2,1)S(1)}, u32[]{:S(2)}, u32[]{:S(2)}) collective-permute-start(bf16[16,4096]{1,0:T(8,128)(2,1)S(1)} %get-tuple-element.68), channel_id=1, source_target_pairs={{0,8},{1,9},{2,10},{3,11},{4,12},{5,13},{6,14},{7,15},{8,0},{9,1},... | collective-permute-start | bytes 393224 | tf_op jit(solution)/shard_map/ppermute | solution.py:21
  29.9 6.8 %collective-permute-start.5 = (bf16[16,4096]{1,0:T(8,128)(2,1)S(1)}, bf16[16,4096]{1,0:T(8,128)(2,1)S(1)}, u32[]{:S(2)}, u32[]{:S(2)}) collective-permute-start(bf16[16,4096]{1,0:T(8,128)(2,1)S(1)} %get-tuple-element.68), channel_id=1, source_target_pairs={{8,16},{9,17},{10,18},{11,19},{12,20},{13,21},{14,22},{15,23},{16,... | collective-permute-start | bytes 393224 | tf_op jit(solution)/shard_map/ppermute | solution.py:27
  34.4 5.6 %copy-start.3 = (bf16[128,8192]{1,0:T(8,128)(2,1)S(1)}, bf16[128,8192]{1,0:T(8,128)(2,1)}, u32[]{:S(2)}) copy-start(bf16[128,8192]{1,0:T(8,128)(2,1)} %resid_ref.3) | copy-start | bytes 6291460
  37.0 7.4 %collective-permute-start.7 = (f32[16,4096]{1,0:T(8,128)S(1)}, f32[16,4096]{1,0:T(8,128)S(1)}, u32[]{:S(2)}, u32[]{:S(2)}) collective-permute-start(f32[16,4096]{1,0:T(8,128)S(1)} %get-tuple-element.73), channel_id=1, source_target_pairs={{0,1},{1,0},{2,3},{3,2},{4,5},{5,4},{6,7},{7,6},{8,9},{9,8},{10,11... | collective-permute-start | bytes 786440 | tf_op jit(solution)/shard_map/ppermute | solution.py:21
  40.0 4.4 %copy-start.4 = (f32[8192]{0:T(1024)S(1)}, f32[8192]{0:T(1024)}, u32[]{:S(2)}) copy-start(f32[8192]{0:T(1024)} %param.17) | copy-start | bytes 98308

commit v18 on v17

--- a/solution.py
+++ b/solution.py
@@ -15,6 +15,11 @@
 NEAR_PARTS = 2
 f32 = jnp.float32
 bf16 = jnp.bfloat16
+
+
+def from_behind(shard, axis, by):
+    count = lax.axis_size(axis)
+    return lax.ppermute(shard, axis, [(i, i + by) for i in range(count - by)])
 
 
 def swap(shard, axis, bit=1):
@@ -107,11 +112,6 @@
         return self.taps[0] * here + (self.taps[1] * one) * keep_one + (self.taps[2] * two) * keep_two
 
 
-def rim_of(even_ref, odd_ref, index, cols):
-    odd = jnp.full((2, LANES), lax.rem(lax.axis_index("ctx"), 2), jnp.int32) == 1
-    return jnp.where(odd, odd_ref[index, :, cols].astype(f32), even_ref[index, :, cols].astype(f32))
-
-
 def half_start(chans, own):
     parity = lax.rem(lax.axis_index("ctx"), 2)
     return pl.multiple_of((parity if own else 1 - parity) * (chans // 2), LANES)
@@ -125,23 +125,28 @@
     return state_ref[lax.div(lane, LANES), pl.ds(b * (modes + 1), modes), :]
 
 
-def state_kernel(
-    masks, key_ref, value_ref, even_ref, odd_ref, taps_ref, rate_ref, *refs, span, modes, most, own
-):
-    gate_ref, state_ref, end_ref, wide_k, wide_v, tables, held = refs[-7:]
-    half = key_ref.shape[1] // 2
+def state_kernel(masks, key_ref, value_ref, rim_ref, taps_ref, rate_ref, *refs, span, modes, most, own):
+    if own:
+        _, _, gate_ref, state_ref, end_ref, wide_k, wide_v, tables, held = refs
+    else:
+        key_in, value_in, gate_ref, state_ref, end_ref, key_own, value_own, wide_k, wide_v, tables, held, sems = refs
+    half = key_ref.shape[1]
     first = half_start(2 * half, own)
+    if not own:
+        fetches = half_copies(key_in, value_in, key_own, value_own, sems, True)
+        for copy in fetches:
+            copy.start()
     at = Masks(span)
 
     def group(lanes):
         for slot, lane in enumerate(lanes):
-            spread(key_ref[:, cols_of(lane)], wide_k.at[slot], span)
-            spread(value_ref[:, cols_of(lane)], wide_v.at[slot], span)
+            spread(key_ref[:, cols_of(pl.multiple_of(lane - first, LANES))], wide_k.at[slot], span)
+            spread(value_ref[:, cols_of(pl.multiple_of(lane - first, LANES))], wide_v.at[slot], span)
             rate = rate_ref[:, cols_of(lane)]
             tables[slot] = jnp.exp(-rate)
         convs = [
             [
-                Conv(wide.at[slot], rim_of(even_ref, odd_ref, i, cols_of(lane)), taps_ref[i, :, cols_of(lane)], span)
+                Conv(wide.at[slot], rim_ref[i, :, cols_of(lane)].astype(f32), taps_ref[i, :, cols_of(lane)], span)
                 for i, wide in ((1, wide_k), (2, wide_v))
             ]
             for slot, lane in enumerate(lanes)
@@ -175,6 +180,31 @@
             end_ref[:, cols_of(pl.multiple_of(lane - first, LANES))] = end
 
     each_group(half // LANES, most, lambda lanes: group([pl.multiple_of(first + lane, LANES) for lane in lanes]))
+    if not own:
+        for copy in fetches:
+            copy.wait()
+
+
+def half_copies(key_in, value_in, key_half, value_half, sems, own):
+    cols = pl.ds(half_start(key_in.shape[1], own), key_half.shape[1])
+    return [
+        pltpu.make_async_copy(key_in.at[:, cols], key_half, sems.at[0]),
+        pltpu.make_async_copy(value_in.at[:, cols], value_half, sems.at[1]),
+    ]
+
+
+def first_kernel(
+    base_ref, len_ref, key_in, value_in, taps_in, rate_in, masks, key_give, value_give, taps_ref, rate_ref, sems,
+    *, span, levels,
+):
+    copies = half_copies(key_in, value_in, key_give, value_give, sems, False)
+    copies.append(pltpu.make_async_copy(taps_in, taps_ref, sems.at[2]))
+    copies.append(pltpu.make_async_copy(rate_in, rate_ref, sems.at[3]))
+    for copy in copies:
+        copy.start()
+    write_masks(base_ref, len_ref, masks, span, levels)
+    for copy in copies:
+        copy.wait()
 
 
 def tail_kernel(query_ref, key_ref, value_ref, tail_ref, bufs, sems):
@@ -288,12 +318,8 @@
     each_group(count // LANES, most, lambda lanes: group([pl.multiple_of(first + lane, LANES) for lane in lanes]))
 
 
-def query_kernel(*refs, span, most, chunk, levels, first, count):
-    if not first:
-        base_ref, len_ref, query_ref, taps_ref, value_in, short_ref, masks, value_ref, query_buf, sems, wide_q, value_sem = refs
-        value_copy = pltpu.make_async_copy(value_in, value_ref, value_sem)
-    else:
-        masks, query_ref, taps_ref, _, short_ref, query_buf, sems, wide_q = refs
+def query_kernel(masks, query_ref, taps_ref, *refs, span, most, chunk, first, count):
+    short_ref, query_buf, sems, wide_q = refs[-4:]
 
     def fetch(c):
         there = pl.ds(first + c * chunk if isinstance(c, int) else pl.multiple_of(first + c * chunk, chunk), chunk)
@@ -302,9 +328,6 @@
 
     for c in range(count // chunk):
         fetch(c).start()
-    if not first:
-        value_copy.start()
-        write_masks(base_ref, len_ref, masks, span, levels)
     at = Masks(span)
 
     def group(lanes):
@@ -320,8 +343,6 @@
                 short_ref[pl.ds(j * SUBS, SUBS), cols_of(pl.multiple_of(first + lane, LANES))] = convs[slot].step(j, keep_one, keep_two)
 
     each_chunk(count, chunk, lambda c: fetch(c).wait(), group, lambda c: None, most)
-    if not first:
-        value_copy.wait()
 
 
 def pair_rates(rate_ref, count):
@@ -384,7 +405,7 @@
 
 
 def final_kernel(
-    masks, state_ref, enter_ref, near_ref, short_ref, resid_ref, even_ref, odd_ref, taps_ref, rate_ref, weight_ref, *refs,
+    masks, state_ref, enter_ref, near_ref, short_ref, resid_ref, rim_ref, taps_ref, rate_ref, weight_ref, *refs,
     span, modes, channels, most, chunk, own,
 ):
     if own:
@@ -423,7 +444,7 @@
         for slot, lane in enumerate(lanes):
             part = [starts_at[slot, pl.ds(n, SUBS, stride=modes + 1), :] for n in range(modes)]
             decay = [row_of(tables.at[slot], n) for n in range(modes)]
-            rim = rim_of(even_ref, odd_ref, 0, cols_of(lane))
+            rim = rim_ref[0, :, cols_of(lane)].astype(f32)
             tap = taps_ref[0, :, cols_of(lane)]
             edge = [
                 (tap[1:2] * rim[1:2]) * masks[at.edges] + (tap[2:3] * rim[0:1]) * masks[at.edges + 1],
@@ -518,7 +539,7 @@
         compiler_params=params,
         name="tails",
     )(far_off(query_in), far_off(key_in), far_off(value_in))
-    rims = (swap_across(tails, "ctx", 1), swap(tails, "ctx"))
+    rim_rows = from_behind(tails, "ctx", 1)
     levels = max(1, (blocks // 4).bit_length() - 2)
     mask_shape = (Masks(span).count(levels),) + tile_shape
 
@@ -529,23 +550,14 @@
             pltpu.SemaphoreType.DMA((count // chunk,)),
             pltpu.VMEM((Q_TILES, wide_rows, LANES), f32),
         ]
-        out_shape = [pltpu.VMEM((tok_rows, chans), f32)]
-        if part == 0:
-            operands = [base, lengths, far_off(query_in), near_by(short_taps), far_off(value_in)]
-            in_specs = [smem, smem, hbm, vmem, hbm]
-            out_shape += [pltpu.VMEM(mask_shape, f32), pltpu.VMEM((tok_rows, chans), bf16)]
-            scratch.append(pltpu.SemaphoreType.DMA(()))
-        else:
-            operands = [near_by(masks), far_off(query_in), near_by(short_taps), near_by(before)]
-            in_specs = [vmem, hbm, vmem, vmem]
+        operands = [near_by(masks), far_off(query_in), taps] + ([near_by(before)] if part else [])
         return pl.pallas_call(
             functools.partial(
-                query_kernel, span=span, most=Q_TILES, chunk=chunk, levels=levels,
-                first=part * count, count=count,
+                query_kernel, span=span, most=Q_TILES, chunk=chunk, first=part * count, count=count
             ),
-            in_specs=in_specs,
-            out_specs=[vmem] * len(out_shape),
-            out_shape=out_shape,
+            in_specs=[vmem, hbm, vmem] + [vmem] * (len(operands) - 3),
+            out_specs=vmem,
+            out_shape=pltpu.VMEM((tok_rows, chans), f32),
             scratch_shapes=scratch,
             input_output_aliases={3: 0} if part else {},
             compiler_params=params,
@@ -553,38 +565,61 @@
             name="query_part_%d" % part,
         )(*operands)
 
-    q_short, masks, values = query_piece(0, None, None)
-    rims, q_short, values = lax.optimization_barrier((rims, q_short, values))
-    rates, weights, taps, rims = near_by(decay_rate), near_by(weight), near_by(short_taps), [near_by(x) for x in rims]
+    key_half = pltpu.VMEM((tok_rows, chans // 2), bf16)
+    masks, key_give, value_give, taps, rates = pl.pallas_call(
+        functools.partial(first_kernel, span=span, levels=levels),
+        in_specs=[smem, smem, hbm, hbm, hbm, hbm],
+        out_specs=[vmem] * 5,
+        out_shape=[
+            pltpu.VMEM(mask_shape, f32), key_half, key_half,
+            pltpu.VMEM(short_taps.shape, f32), pltpu.VMEM(decay_rate.shape, f32),
+        ],
+        scratch_shapes=[pltpu.SemaphoreType.DMA((4,))],
+        compiler_params=params,
+        name="masks_and_fetch",
+    )(base, lengths, far_off(key_in), far_off(value_in), far_off(short_taps), far_off(decay_rate))
+    rim_rows, masks = lax.optimization_barrier((rim_rows, masks))
+    rates, weights, taps, rims = near_by(rates), near_by(weight), near_by(taps), near_by(rim_rows)
     kept = pltpu.VMEM((modes, chans // 2), f32)
     sent = pltpu.VMEM((modes, chans // 2), bf16)
-    keys, values = near_by(key_in), near_by(values)
-
-    def states_of(own, before):
+
+    def states_of(own, keys, values, before):
+        operands = [near_by(x) for x in (masks, keys, values)] + [rims, taps, rates]
+        in_specs = [vmem] * len(operands)
+        out_shape = [
+            pltpu.VMEM((tok_rows, chans), bf16),
+            pltpu.VMEM((chans // LANES, SUBS * (modes + 1), LANES), f32),
+            kept,
+        ]
+        scratch = [
+            pltpu.VMEM((A_TILES, wide_rows, LANES), f32),
+            pltpu.VMEM((A_TILES, wide_rows, LANES), f32),
+            pltpu.VMEM((A_TILES, modes, LANES), f32),
+            pltpu.VMEM((A_TILES, span) + tile_shape, f32),
+        ]
+        if own:
+            operands += [near_by(x) for x in before]
+            in_specs += [vmem] * len(before)
+        else:
+            operands += [far_off(key_in), far_off(value_in)]
+            in_specs += [hbm, hbm]
+            out_shape += [key_half, key_half]
+            scratch.append(pltpu.SemaphoreType.DMA((2,)))
         return pl.pallas_call(
             functools.partial(state_kernel, span=span, modes=modes, most=A_TILES, own=own),
-            in_specs=[vmem] * (7 + len(before)),
-            out_specs=[vmem] * 3,
-            out_shape=[
-                pltpu.VMEM((tok_rows, chans), bf16),
-                pltpu.VMEM((chans // LANES, SUBS * (modes + 1), LANES), f32),
-                kept,
-            ],
-            scratch_shapes=[
-                pltpu.VMEM((A_TILES, wide_rows, LANES), f32),
-                pltpu.VMEM((A_TILES, wide_rows, LANES), f32),
-                pltpu.VMEM((A_TILES, modes, LANES), f32),
-                pltpu.VMEM((A_TILES, span) + tile_shape, f32),
-            ],
-            input_output_aliases={7 + i: i for i in range(len(before))},
+            in_specs=in_specs,
+            out_specs=[vmem] * len(out_shape),
+            out_shape=out_shape,
+            scratch_shapes=scratch,
+            input_output_aliases={6: 0, 7: 1} if own else {},
             compiler_params=params,
             cost_estimate=cost(500, 6 * tok_rows * chans),
             name="block_states_own" if own else "block_states_give",
-        )(near_by(masks), keys, values, *rims, taps, rates, *[near_by(x) for x in before])
-
-    gates, states, give = states_of(False, [])
+        )(*operands)
+
+    gates, states, give, key_own, value_own = states_of(False, key_give, value_give, [])
     got = swap(give, "ctx")
-    gates, states, own = states_of(True, [gates, states])
+    gates, states, own = states_of(True, key_own, value_own, [gates, states])
     got, gates, states, own = lax.optimization_barrier((got, gates, states, own))
 
     def near_piece(part, near):
@@ -627,6 +662,9 @@
         met = swap(ends, "ctx", 2 << m)
         if m < NEAR_PARTS:
             near = near_piece(m, near)
+            if m == 0:
+                q_short = query_piece(0, masks, None)
+                met, q_short = lax.optimization_barrier((met, q_short))
             met, near = lax.optimization_barrier((met, near))
         ends, enter, *total = pair_call(
             level_kernel,
@@ -644,7 +682,7 @@
     on = (swap_across(ends, "ctx", 2 << levels), swap(ends, "ctx", 2 << levels))
     for m in range(levels, NEAR_PARTS):
         near = near_piece(m, near)
-    q_short = query_piece(1, masks, q_short)[0]
+    q_short = query_piece(1, masks, q_short)
     on, q_short, near = lax.optimization_barrier((on, q_short, near))
     mine, give_back = pair_call(
         enter_kernel,
@@ -676,7 +714,7 @@
             pltpu.VMEM((F_TILES, modes, LANES), f32),
             pltpu.VMEM((F_TILES, SUBS * (modes + 1), LANES), f32),
         ]
-        operands = [near_by(x) for x in (masks, states, enter, near, q_short)] + [resid, *rims, taps, rates, weights]
+        operands = [near_by(x) for x in (masks, states, enter, near, q_short)] + [resid, rims, taps, rates, weights]
         if last:
             operands.append(near_by(norm_gain.reshape(1, chans)))
             out_specs.append(hbm)

time: 50.4 us -> 50 us (level)
  waiting for transfers between devices: 4.07 us -> 2.33 us
  Pallas kernels: 30.5 us -> 32 us
    ppermute x0 -> x1, starting transfers between devices: none -> 3.68 us  [from_behind(): return lax.ppermute(shard, axis, [(i, i + by) for i in range(count - by)])]
    ppermute x2 -> x1, starting transfers between devices: 7.49 us -> 4.48 us  [swap_across(): return lax.ppermute(shard, axis, pairs + [(j, i) for i, j in pairs])]
    pallas_call x0 -> x1, Pallas kernels: none -> 2.5 us  [shards(): pl.pallas_call(functools.partial(first_kernel, span=span, levels=levels),...]
    ppermute x2 -> x1, waiting for transfers between devices: 1.43 us -> 0.31 us  [swap_across(): return lax.ppermute(shard, axis, pairs + [(j, i) for i, j in pairs])]
    pallas_call x2, Pallas kernels: 4.78 us -> 3.85 us  [query_piece(): pl.pallas_call(functools.partial(query_kernel, span=span, most=Q_TILES, c...]
    ppermute x6 -> x5, starting transfers between devices: 6.46 us -> 5.73 us  [swap(): lax.ppermute(shard, axis, [(i, i ^ bit) for i in range(lax.axis_size(axis...]
    ppermute x6 -> x5, waiting for transfers between devices: 2.64 us -> 2.02 us  [swap(): lax.ppermute(shard, axis, [(i, i ^ bit) for i in range(lax.axis_size(axis...]
  transfers between devices with their start and end apart: 8 -> 7, of which waited for: 4 -> 3; matrix products, arithmetic and copies ran while one was open for 1% -> 1% of each run, Pallas kernels for 37% -> 40%
where the time goes in v18:
time: 50 us; the launch traced here: 49.4 us
  Pallas kernels  32 us (64%)
  starting transfers between devices  13.9 us (28%)
  waiting for transfers between devices  2.33 us (5%)
  between operations  0.82 us (2%)
    pallas_call x2, Pallas kernels, finish(): pl.pallas_call(functools.partial(final_kernel, span=span, modes=modes, ch...  9.68 us
    pallas_call x2, Pallas kernels, states_of(): pl.pallas_call(functools.partial(state_kernel, span=span, modes=modes, mo...  9.13 us
    ppermute x5, starting transfers between devices, swap(): lax.ppermute(shard, axis, [(i, i ^ bit) for i in range(lax.axis_size(axis...  5.73 us
    pallas_call x2, Pallas kernels, near_piece(): pl.pallas_call(functools.partial(near_kernel, span=span, modes=modes, mos...  4.69 us
    ppermute x1, starting transfers between devices, swap_across(): return lax.ppermute(shard, axis, pairs + [(j, i) for i, j in pairs])  4.48 us
    pallas_call x2, Pallas kernels, query_piece(): pl.pallas_call(functools.partial(query_kernel, span=span, most=Q_TILES, c...  3.85 us
    ppermute x1, starting transfers between devices, from_behind(): return lax.ppermute(shard, axis, [(i, i + by) for i in range(count - by)])  3.68 us
    pallas_call x1, Pallas kernels, shards(): pl.pallas_call(functools.partial(first_kernel, span=span, levels=levels),...  2.5 us
  transfers between devices with their start and end apart: 7, of which 3 were waited for; matrix products, arithmetic and copies ran while one was open for 1% of the time, Pallas kernels for 40%

profile of v18, /device:TPU:9, one launch (start us, length us, event | category | flops | bytes accessed | tf_op | source)
XLA Modules:
  0.0 49.4 jit_solution(9486629586727567930)
XLA Ops:
  0.6 1.2 %tails.1 = bf16[3,2,8192]{2,1,0:T(2,128)(2,1)S(1)} custom-call(bf16[128,8192]{1,0:T(8,128)(2,1)} %query_ref.5, bf16[128,8192]{1,0:T(8,128)(2,1)} %refs_0_.1, bf16[128,8192]{1,0:T(8,128)(2,1)} %refs_1_.1), custom_call_target="tpu_custom_call" | custom-call | tf_op jit(solution)/shard_map/tails/pallas_call | solution.py:533
  1.8 3.7 %collective-permute-start = (bf16[3,2,8192]{2,1,0:T(2,128)(2,1)S(1)}, bf16[3,2,8192]{2,1,0:T(2,128)(2,1)S(1)}, u32[]{:S(2)}, u32[]{:S(2)}) collective-permute-start(bf16[3,2,8192]{2,1,0:T(2,128)(2,1)S(1)} %tails.1), channel_id=1, source_target_pairs={{0,1},{1,2},{2,3},{3,4},{4,5},{5,6},{6,7},{7,8},{8,9},{9,10},{10,1... | collective-permute-start | bytes 294920 | tf_op jit(solution)/shard_map/ppermute | solution.py:22
  5.5 2.5 %masks_and_fetch.1 = (f32[82,8,128]{2,1,0:T(8,128)S(1)}, bf16[128,4096]{1,0:T(8,128)(2,1)S(1)}, bf16[128,4096]{1,0:T(8,128)(2,1)S(1)}, f32[3,3,8192]{2,1,0:T(4,128)S(1)}, f32[16,8192]{1,0:T(8,128)S(1)}) custom-call(s32[1]{0:T(128)} %bitcast.base_ref, s32[16]{0:T(128)} %len_ref.1, bf16[128,8192]{1,0:T(8,128)(2,1)} %refs_0_.1, bf16[128,8192]{1,0:T(8,128)(2,1)} %refs_1_.1, ...), custom_call_target="tpu_custom_call" | custom-call | tf_op jit(solution)/shard_map/masks_and_fetch/pallas_call | solution.py:569
  8.0 0.0 collective-permute-done.rim_ref
  8.0 4.6 %block_states_give.1 = (bf16[128,8192]{1,0:T(8,128)(2,1)S(1)}, f32[64,136,128]{2,1,0:T(8,128)S(1)}, f32[16,4096]{1,0:T(8,128)S(1)}, bf16[128,4096]{1,0:T(8,128)(2,1)S(1)}, bf16[128,4096]{1,0:T(8,128)(2,1)S(1)}) custom-call(f32[82,8,128]{2,1,0:T(8,128)S(1)} %get-tuple-element.49.masks, bf16[128,4096]{1,0:T(8,128)(2,1)S(1)} %get-tuple-element.50.key_ref, ...), custom_call_target="tpu_custom_call" | custom-call | flops 32768000 | bytes 6291456 | tf_op jit(solution)/shard_map/block_states_give/pallas_call | solution.py:608
  12.6 2.2 %collective-permute-start.1 = (f32[16,4096]{1,0:T(8,128)S(1)}, f32[16,4096]{1,0:T(8,128)S(1)}, u32[]{:S(2)}, u32[]{:S(2)}) collective-permute-start(f32[16,4096]{1,0:T(8,128)S(1)} %get-tuple-element.55), channel_id=1, source_target_pairs={{0,1},{1,0},{2,3},{3,2},{4,5},{5,4},{6,7},{7,6},{8,9},{9,8},{10,11... | collective-permute-start | bytes 786440 | tf_op jit(solution)/shard_map/ppermute | solution.py:26
  14.8 0.0 copy-start.2
  14.8 0.0 copy-start.3
  14.8 4.5 %block_states_own.1 = (bf16[128,8192]{1,0:T(8,128)(2,1)S(1)}, f32[64,136,128]{2,1,0:T(8,128)S(1)}, f32[16,4096]{1,0:T(8,128)S(1)}) custom-call(f32[82,8,128]{2,1,0:T(8,128)S(1)} %get-tuple-element.49.masks, bf16[128,4096]{1,0:T(8,128)(2,1)S(1)} %get-tuple-element.56.key_ref, ...), custom_call_target="tpu_custom_call", output_to_operand_aliasing={{0}: (6, {}), {1}: (7, {})} | custom-call | flops 32768000 | bytes 6291456 | tf_op jit(solution)/shard_map/block_states_own/pallas_call | solution.py:608
  19.4 0.0 collective-permute-done.1.got_ref.other_ref
  19.4 0.2 pair_ends.1
  19.6 0.1 collective-permute-start.2
  19.7 0.0 copy-done.2
  19.7 0.0 copy-done.3
  19.7 0.3 sqrt_multiply_fusion.weight_ref
  20.0 1.9 %query_part_0.1.refs_0_ = f32[128,8192]{1,0:T(8,128)S(1)} custom-call(f32[82,8,128]{2,1,0:T(8,128)S(1)} %get-tuple-element.49.masks, bf16[128,8192]{1,0:T(8,128)(2,1)} %query_ref.5, f32[3,3,8192]{2,1,0:T(4,128)S(1)} %get-tuple-element.53.taps_ref), custom_call_target="tpu_custom_call" | custom-call | flops 6553600 | bytes 3145728 | tf_op jit(solution)/shard_map/query_part_0/pallas_call | solution.py:554
  21.9 2.3 %near_part_0.1.refs_0_ = f32[128,8192]{1,0:T(8,128)S(1)} custom-call(f32[82,8,128]{2,1,0:T(8,128)S(1)} %get-tuple-element.49.masks, bf16[128,8192]{1,0:T(8,128)(2,1)S(1)} %get-tuple-element.68.gate_ref, f32[16,8192]{1,0:T(8,128)S(1)} %get-tuple-element.54.rate_ref, f32[16,8192]{1,0:T(8,128)S(1)} %sqrt_multiply_fusion.weight_ref), custom_call_target="tpu_custom_call" | custom-call | flops 19660800 | bytes 3670016 | tf_op jit(solution)/shard_map/near_part_0/pallas_call | solution.py:628
  24.2 0.5 %collective-permute-done.2.got_ref = bf16[16,4096]{1,0:T(8,128)(2,1)S(1)} collective-permute-done((bf16[16,4096]{1,0:T(8,128)(2,1)S(1)}, bf16[16,4096]{1,0:T(8,128)(2,1)S(1)}, u32[]{:S(2)}, u32[]{:S(2)}) %collective-permute-start.2) | collective-permute-done | bytes 131104 | tf_op jit(solution)/shard_map/ppermute | solution.py:26
  24.7 0.2 level_0.1
  25.0 0.4 collective-permute-start.3
  25.4 2.3 %near_part_1.1.near_ref = f32[128,8192]{1,0:T(8,128)S(1)} custom-call(f32[82,8,128]{2,1,0:T(8,128)S(1)} %get-tuple-element.49.masks, bf16[128,8192]{1,0:T(8,128)(2,1)S(1)} %get-tuple-element.68.gate_ref, f32[16,8192]{1,0:T(8,128)S(1)} %get-tuple-element.54.rate_ref, f32[16,8192]{1,0:T(8,128)S(1)} %sqrt_multiply_fusion.weight_ref, ...), custom_call_target="tpu_custom_call", output_to_operand_aliasing={{}: (4, {})} | custom-call | flops 19660800 | bytes 3670016 | tf_op jit(solution)/shard_map/near_part_1/pallas_call | solution.py:628
  27.7 1.5 %collective-permute-done.3.got_ref = bf16[16,4096]{1,0:T(8,128)(2,1)S(1)} collective-permute-done((bf16[16,4096]{1,0:T(8,128)(2,1)S(1)}, bf16[16,4096]{1,0:T(8,128)(2,1)S(1)}, u32[]{:S(2)}, u32[]{:S(2)}) %collective-permute-start.3) | collective-permute-done | bytes 131104 | tf_op jit(solution)/shard_map/ppermute | solution.py:26
  29.2 0.3 level_1.1
  29.5 0.1 collective-permute-start.5
  29.6 4.5 %collective-permute-start.4 = (bf16[16,4096]{1,0:T(8,128)(2,1)S(1)}, bf16[16,4096]{1,0:T(8,128)(2,1)S(1)}, u32[]{:S(2)}, u32[]{:S(2)}) collective-permute-start(bf16[16,4096]{1,0:T(8,128)(2,1)S(1)} %get-tuple-element.76), channel_id=1, source_target_pairs={{8,16},{9,17},{10,18},{11,19},{12,20},{13,21},{14,22},{15,23},{16,... | collective-permute-start | bytes 393224 | tf_op jit(solution)/shard_map/ppermute | solution.py:32
  34.1 0.0 copy-start
  34.1 2.0 %query_part_1.1.short_ref = f32[128,8192]{1,0:T(8,128)S(1)} custom-call(f32[82,8,128]{2,1,0:T(8,128)S(1)} %get-tuple-element.49.masks, bf16[128,8192]{1,0:T(8,128)(2,1)} %query_ref.5, f32[3,3,8192]{2,1,0:T(4,128)S(1)} %get-tuple-element.53.taps_ref, f32[128,8192]{1,0:T(8,128)S(1)} %query_part_0.1.refs_0_), custom_call_target="tpu_custom_call", output_to_operand_aliasing={{}: (3, {})} | custom-call | flops 6553600 | bytes 3145728 | tf_op jit(solution)/shard_map/query_part_1/pallas_call | solution.py:554
  36.1 0.0 collective-permute-done.5.odd_ref
  36.1 0.3 collective-permute-done.4.even_ref
  36.4 0.3 pair_enter.1
  36.7 2.9 %collective-permute-start.6 = (f32[16,4096]{1,0:T(8,128)S(1)}, f32[16,4096]{1,0:T(8,128)S(1)}, u32[]{:S(2)}, u32[]{:S(2)}) collective-permute-start(f32[16,4096]{1,0:T(8,128)S(1)} %get-tuple-element.81), channel_id=1, source_target_pairs={{0,1},{1,0},{2,3},{3,2},{4,5},{5,4},{6,7},{7,6},{8,9},{9,8},{10,11... | collective-permute-start | bytes 786440 | tf_op jit(solution)/shard_map/ppermute | solution.py:26
  39.7 0.0 copy-done
  39.7 0.0 copy-start.1
  39.7 4.4 %far_part_own.1 = (bf16[128,8192]{1,0:T(8,128)(2,1)}, f32[64,128,128]{2,1,0:T(8,128)S(1)}, f32[128,128]{1,0:T(8,128)S(1)}) custom-call(f32[82,8,128]{2,1,0:T(8,128)S(1)} %get-tuple-element.49.masks, f32[64,136,128]{2,1,0:T(8,128)S(1)} %get-tuple-element.63.state_ref, f32[16,4096]{1,0:T(8,128)S(1)} %get-tuple-element.82.enter_ref, ...), custom_call_target="tpu_custom_call" | custom-call | flops 29491200 | bytes 9437184 | tf_op jit(solution)/shard_map/far_part_own/pallas_call | solution.py:728
  44.1 0.0 collective-permute-done.6.enter_ref
  44.1 0.0 copy-done.1
  44.1 5.3 %far_part_other.1 = (bf16[128,8192]{1,0:T(8,128)(2,1)}, f32[64,128,128]{2,1,0:T(8,128)S(1)}, f32[128,128]{1,0:T(8,128)S(1)}, bf16[128,8192]{1,0:T(8,128)(2,1)}) custom-call(f32[82,8,128]{2,1,0:T(8,128)S(1)} %get-tuple-element.49.masks, ...), custom_call_target="tpu_custom_call", output_to_operand_aliasing={{0}: (11, {}), {1}: (12, {}), {2}: (13, {})} | custom-call | flops 29491200 | bytes 9437184 | tf_op jit(solution)/shard_map/far_part_other/pallas_call | solution.py:728
Async XLA Ops:
  1.8 6.2 %collective-permute-start = (bf16[3,2,8192]{2,1,0:T(2,128)(2,1)S(1)}, bf16[3,2,8192]{2,1,0:T(2,128)(2,1)S(1)}, u32[]{:S(2)}, u32[]{:S(2)}) collective-permute-start(bf16[3,2,8192]{2,1,0:T(2,128)(2,1)S(1)} %tails.1), channel_id=1, source_target_pairs={{0,1},{1,2},{2,3},{3,4},{4,5},{5,6},{6,7},{7,8},{8,9},{9,10},{10,1... | collective-permute-start | bytes 294920 | tf_op jit(solution)/shard_map/ppermute | solution.py:22
  12.6 6.8 %collective-permute-start.1 = (f32[16,4096]{1,0:T(8,128)S(1)}, f32[16,4096]{1,0:T(8,128)S(1)}, u32[]{:S(2)}, u32[]{:S(2)}) collective-permute-start(f32[16,4096]{1,0:T(8,128)S(1)} %get-tuple-element.55), channel_id=1, source_target_pairs={{0,1},{1,0},{2,3},{3,2},{4,5},{5,4},{6,7},{7,6},{8,9},{9,8},{10,11... | collective-permute-start | bytes 786440 | tf_op jit(solution)/shard_map/ppermute | solution.py:26
  14.8 4.8 %copy-start.2 = (f32[16,8192]{1,0:T(8,128)S(1)}, f32[16,8192]{1,0:T(8,128)}, u32[]{:S(2)}) copy-start(f32[16,8192]{1,0:T(8,128)} %rate_in.1) | copy-start | bytes 1572868
  14.8 4.8 %copy-start.3 = (f32[16,8192]{1,0:T(8,128)S(1)}, f32[16,8192]{1,0:T(8,128)}, u32[]{:S(2)}) copy-start(f32[16,8192]{1,0:T(8,128)} %param.14) | copy-start | bytes 1572868
  19.6 5.1 %collective-permute-start.2 = (bf16[16,4096]{1,0:T(8,128)(2,1)S(1)}, bf16[16,4096]{1,0:T(8,128)(2,1)S(1)}, u32[]{:S(2)}, u32[]{:S(2)}) collective-permute-start(bf16[16,4096]{1,0:T(8,128)(2,1)S(1)} %get-tuple-element.66), channel_id=1, source_target_pairs={{0,2},{1,3},{2,0},{3,1},{4,6},{5,7},{6,4},{7,5},{8,10},{9,11},{10,... | collective-permute-start | bytes 393224 | tf_op jit(solution)/shard_map/ppermute | solution.py:26
  25.0 4.2 %collective-permute-start.3 = (bf16[16,4096]{1,0:T(8,128)(2,1)S(1)}, bf16[16,4096]{1,0:T(8,128)(2,1)S(1)}, u32[]{:S(2)}, u32[]{:S(2)}) collective-permute-start(bf16[16,4096]{1,0:T(8,128)(2,1)S(1)} %get-tuple-element.71), channel_id=1, source_target_pairs={{0,4},{1,5},{2,6},{3,7},{4,0},{5,1},{6,2},{7,3},{8,12},{9,13},{10,... | collective-permute-start | bytes 393224 | tf_op jit(solution)/shard_map/ppermute | solution.py:26
  29.5 6.6 %collective-permute-start.5 = (bf16[16,4096]{1,0:T(8,128)(2,1)S(1)}, bf16[16,4096]{1,0:T(8,128)(2,1)S(1)}, u32[]{:S(2)}, u32[]{:S(2)}) collective-permute-start(bf16[16,4096]{1,0:T(8,128)(2,1)S(1)} %get-tuple-element.76), channel_id=1, source_target_pairs={{0,8},{1,9},{2,10},{3,11},{4,12},{5,13},{6,14},{7,15},{8,0},{9,1},... | collective-permute-start | bytes 393224 | tf_op jit(solution)/shard_map/ppermute | solution.py:26
  29.6 6.8 %collective-permute-start.4 = (bf16[16,4096]{1,0:T(8,128)(2,1)S(1)}, bf16[16,4096]{1,0:T(8,128)(2,1)S(1)}, u32[]{:S(2)}, u32[]{:S(2)}) collective-permute-start(bf16[16,4096]{1,0:T(8,128)(2,1)S(1)} %get-tuple-element.76), channel_id=1, source_target_pairs={{8,16},{9,17},{10,18},{11,19},{12,20},{13,21},{14,22},{15,23},{16,... | collective-permute-start | bytes 393224 | tf_op jit(solution)/shard_map/ppermute | solution.py:32
  34.1 5.6 %copy-start = (bf16[128,8192]{1,0:T(8,128)(2,1)S(1)}, bf16[128,8192]{1,0:T(8,128)(2,1)}, u32[]{:S(2)}) copy-start(bf16[128,8192]{1,0:T(8,128)(2,1)} %resid_ref.3) | copy-start | bytes 6291460
  36.7 7.3 %collective-permute-start.6 = (f32[16,4096]{1,0:T(8,128)S(1)}, f32[16,4096]{1,0:T(8,128)S(1)}, u32[]{:S(2)}, u32[]{:S(2)}) collective-permute-start(f32[16,4096]{1,0:T(8,128)S(1)} %get-tuple-element.81), channel_id=1, source_target_pairs={{0,1},{1,0},{2,3},{3,2},{4,5},{5,4},{6,7},{7,6},{8,9},{9,8},{10,11... | collective-permute-start | bytes 786440 | tf_op jit(solution)/shard_map/ppermute | solution.py:26
  39.7 4.4 %copy-start.1 = (f32[8192]{0:T(1024)S(1)}, f32[8192]{0:T(1024)}, u32[]{:S(2)}) copy-start(f32[8192]{0:T(1024)} %param.17) | copy-start | bytes 98308

commit v19 on v16

--- a/solution.py
+++ b/solution.py
@@ -19,8 +19,7 @@
 
 def from_behind(shard, axis, by):
     count = lax.axis_size(axis)
-    pairs = [(i, i + by) for i in range(count) if 0 <= i + by < count]
-    return lax.ppermute(shard, axis, pairs)
+    return lax.ppermute(shard, axis, [(i, i + by) for i in range(count - by)])
 
 
 def swap(shard, axis, bit=1):
@@ -94,7 +93,7 @@
         self.wide, self.span = wide, span
         self.taps = [jnp.broadcast_to(taps[m : m + 1], (SUBS, LANES)) for m in range(3)]
         top = lax.broadcasted_iota(jnp.int32, (SUBS, LANES), 0) == 0
-        ahead = [0.0, 0.0] if rim is None else [jnp.broadcast_to(rim[m : m + 1].astype(f32), (SUBS, LANES)) for m in range(2)]
+        ahead = [0.0, 0.0] if rim is None else [jnp.broadcast_to(rim[m : m + 1], (SUBS, LANES)) for m in range(2)]
         self.behind = [jnp.where(top, ahead[m], pltpu.roll(self.row(span - 2 + m), 1, 0)) for m in range(2)]
 
     def row(self, j):
@@ -120,23 +119,44 @@
     return state_ref[lax.div(lane, LANES), pl.ds(b * (modes + 1), modes), :]
 
 
-def state_kernel(
-    masks, key_ref, value_ref, rim_ref, taps_ref, rate_ref, *refs, span, modes, most, own
-):
-    gate_ref, state_ref, end_ref, wide_k, wide_v, tables, held = refs[-7:]
-    half = key_ref.shape[1] // 2
+def state_kernel(masks, *refs, span, modes, most, own, chunk):
+    if own:
+        key_ref, value_ref, rim_ref, taps_ref, rate_ref, _, _, gate_ref, state_ref, end_ref, wide_k, wide_v, tables, held = refs
+    else:
+        (key_in, value_in, taps_ref, rate_ref, gate_ref, state_ref, end_ref, key_own, value_own, heads,
+         key_ref, value_ref, wide_k, wide_v, tables, held, sems) = refs
+    half = key_ref.shape[1]
     first = half_start(2 * half, own)
+    if not own:
+        def fetch(c):
+            there = pl.ds(pl.multiple_of(first + c * chunk, chunk), chunk)
+            here = pl.ds(pl.multiple_of(c * chunk, chunk), chunk)
+            return [
+                pltpu.make_async_copy(key_in.at[:, there], key_ref.at[:, here], sems.at[0, c]),
+                pltpu.make_async_copy(value_in.at[:, there], value_ref.at[:, here], sems.at[1, c]),
+            ]
+
+        cols = pl.ds(half_start(2 * half, True), half)
+        others = [
+            pltpu.make_async_copy(key_in.at[:, cols], key_own, sems.at[0, half // chunk]),
+            pltpu.make_async_copy(value_in.at[:, cols], value_own, sems.at[1, half // chunk]),
+        ]
+        for c in range(half // chunk):
+            for copy in fetch(c):
+                copy.start()
+        for copy in others:
+            copy.start()
     at = Masks(span)
 
     def group(lanes):
         for slot, lane in enumerate(lanes):
-            spread(key_ref[:, cols_of(lane)], wide_k.at[slot], span)
-            spread(value_ref[:, cols_of(lane)], wide_v.at[slot], span)
+            spread(key_ref[:, cols_of(pl.multiple_of(lane - first, LANES))], wide_k.at[slot], span)
+            spread(value_ref[:, cols_of(pl.multiple_of(lane - first, LANES))], wide_v.at[slot], span)
             rate = rate_ref[:, cols_of(lane)]
             tables[slot] = jnp.exp(-rate)
         convs = [
             [
-                Conv(wide.at[slot], rim_ref[i, :, cols_of(lane)], taps_ref[i, :, cols_of(lane)], span)
+                Conv(wide.at[slot], rim_ref[i, :, cols_of(lane)].astype(f32) if own else None, taps_ref[i, :, cols_of(lane)], span)
                 for i, wide in ((1, wide_k), (2, wide_v))
             ]
             for slot, lane in enumerate(lanes)
@@ -152,8 +172,9 @@
                 pair = jnp.concatenate([last[slot], k_short * v_short], axis=0).astype(bf16)
                 gate_ref[pl.ds((j - 1) * SUBS, 2 * SUBS), cols_of(lane)] = pair
                 pair = pair.astype(f32)
-                held[slot, j - 1] = pair[:SUBS] * masks[at.last + j - 1]
-                held[slot, j] = pair[SUBS:] * masks[at.last + j]
+                used = at.inner if j == 1 and not own else at.last + j - 1
+                held[slot, j - 1] = pair[:SUBS] * masks[used]
+                held[slot, j] = pair[SUBS:] * masks[used + 1]
         for slot, lane in enumerate(lanes):
             decay = [row_of(tables.at[slot], n) for n in range(modes)]
             state = [held[slot, 0]] * modes
@@ -169,10 +190,63 @@
                 end = (leap * twice(masks[at.passes + b], modes)) * end + sub_state(state_ref, lane, b, modes)
             end_ref[:, cols_of(pl.multiple_of(lane - first, LANES))] = end
 
-    each_group(half // LANES, most, lambda lanes: group([pl.multiple_of(first + lane, LANES) for lane in lanes]))
-
-
-def tail_kernel(query_ref, key_ref, value_ref, tail_ref, bufs, sems):
+    def shifted(lanes):
+        group([pl.multiple_of(first + lane, LANES) for lane in lanes])
+
+    if own:
+        each_group(half // LANES, most, shifted)
+    else:
+        def before(c):
+            for copy in fetch(c):
+                copy.wait()
+
+        each_chunk(half, chunk, before, shifted, lambda c: None, most)
+        heads[0] = key_ref[pl.ds(0, heads.shape[1]), :]
+        heads[1] = value_ref[pl.ds(0, heads.shape[1]), :]
+        for copy in others:
+            copy.wait()
+
+
+def patch_kernel(
+    masks, heads, rim_ref, taps_ref, rate_ref, gate_in, state_in, end_in, gate_ref, state_ref, end_ref, *, span, modes
+):
+    half = end_ref.shape[1]
+    first = half_start(2 * half, False)
+    at = Masks(span)
+    rows = lax.broadcasted_iota(jnp.int32, (2 * SUBS, LANES), 0)
+
+    def one(index):
+        return masks[index][0:1]
+
+    def group(lanes):
+        for lane in lanes:
+            there = cols_of(pl.multiple_of(first + lane, LANES))
+            shorts = []
+            for i in (1, 2):
+                here = heads[i - 1, :, cols_of(lane)].astype(f32)
+                rim = rim_ref[i, :, there].astype(f32)
+                tap = taps_ref[i, :, there]
+                shorts.append([
+                    tap[0:1] * here[0:1] + (tap[1:2] * rim[1:2]) * one(at.one) + (tap[2:3] * rim[0:1]) * one(at.two),
+                    tap[0:1] * here[1:2] + (tap[1:2] * here[0:1]) * one(at.one + 1) + (tap[2:3] * rim[1:2]) * one(at.two + 1),
+                ])
+            gates = [(k * v).astype(bf16).astype(f32) for k, v in zip(*shorts)]
+            old = gate_in[pl.ds(0, 2 * SUBS), there].astype(f32)
+            new = jnp.where(rows == 0, gates[0], jnp.where(rows == SUBS, gates[1], old))
+            gate_ref[pl.ds(0, 2 * SUBS), there] = new.astype(bf16)
+            rate = rate_ref[:, there]
+            added = jnp.exp(-float(span - 1) * rate) * (gates[0] * one(at.last)) + jnp.exp(-float(span - 2) * rate) * (
+                gates[1] * one(at.last + 1)
+            )
+            tile = lax.div(first + lane, LANES)
+            state_ref[tile, pl.ds(0, modes), :] = state_in[tile, pl.ds(0, modes), :] + added
+            reach = jnp.exp(-float((SUBS - 1) * span) * rate) * one(at.rest)
+            end_ref[:, cols_of(lane)] = end_in[:, cols_of(lane)] + reach * added
+
+    each_group(half // LANES, 4, group)
+
+
+def tail_kernel(base_ref, len_ref, query_ref, key_ref, value_ref, tail_ref, masks, bufs, sems, *, span, levels):
     rows, count = query_ref.shape[0], bufs.shape[1]
     copies = [
         pltpu.make_async_copy(ref.at[pl.ds(rows - count, count)], bufs.at[i], sems.at[i])
@@ -180,6 +254,7 @@
     ]
     for copy in copies:
         copy.start()
+    write_masks(base_ref, len_ref, masks, span, levels)
     for i, copy in enumerate(copies):
         copy.wait()
         tail_ref[i] = bufs[i].astype(f32)[count - 2 :].astype(bf16)
@@ -201,7 +276,9 @@
         self.edges = self.passes + SUBS
         self.late = self.edges + 3
         self.early = self.late + 1
-        self.levels = self.late + 2
+        self.rest = self.late + 2
+        self.inner = self.late + 3
+        self.levels = self.late + 5
 
     def lead(self, level):
         return self.levels + 2 * level
@@ -222,6 +299,8 @@
         masks[at.last + j] = flag(starts[span - 1] <= rows + j)
         masks[at.enter + j] = flag(starts[j] < rows)
     top = flag(lax.broadcasted_iota(jnp.int32, (SUBS, LANES), 0) == 0)
+    for j in range(2):
+        masks[at.inner + j] = (1.0 - top) * masks[at.last + j]
     masks[at.edges] = top * masks[at.one]
     masks[at.edges + 1] = top * masks[at.two]
     masks[at.edges + 2] = top * masks[at.two + 1]
@@ -230,8 +309,8 @@
     pair_at = base_ref[0] - parity * size
     ranges = [(base_ref[0] + b * span, span) for b in range(SUBS)]
     flags = [at.passes + b for b in range(SUBS)]
-    ranges += [(pair_at + size, size), (pair_at, size)]
-    flags += [at.late, at.early]
+    ranges += [(pair_at + size, size), (pair_at, size), (base_ref[0] + span, size - span)]
+    flags += [at.late, at.early, at.rest]
     for m in range(levels + 1):
         group = 2 * size << m
         group_at = base_ref[0] - lax.rem(base_ref[0], group)
@@ -283,12 +362,8 @@
     each_group(count // LANES, most, lambda lanes: group([pl.multiple_of(first + lane, LANES) for lane in lanes]))
 
 
-def query_kernel(*refs, span, most, chunk, levels, first, count):
-    if not first:
-        base_ref, len_ref, query_ref, taps_ref, value_in, short_ref, masks, value_ref, query_buf, sems, wide_q, value_sem = refs
-        value_copy = pltpu.make_async_copy(value_in, value_ref, value_sem)
-    else:
-        masks, query_ref, taps_ref, _, short_ref, query_buf, sems, wide_q = refs
+def query_kernel(masks, query_ref, taps_ref, *refs, span, most, chunk, first, count):
+    short_ref, query_buf, sems, wide_q = refs[-4:]
 
     def fetch(c):
         there = pl.ds(first + c * chunk if isinstance(c, int) else pl.multiple_of(first + c * chunk, chunk), chunk)
@@ -297,9 +372,6 @@
 
     for c in range(count // chunk):
         fetch(c).start()
-    if not first:
-        value_copy.start()
-        write_masks(base_ref, len_ref, masks, span, levels)
     at = Masks(span)
 
     def group(lanes):
@@ -315,8 +387,6 @@
                 short_ref[pl.ds(j * SUBS, SUBS), cols_of(pl.multiple_of(first + lane, LANES))] = convs[slot].step(j, keep_one, keep_two)
 
     each_chunk(count, chunk, lambda c: fetch(c).wait(), group, lambda c: None, most)
-    if not first:
-        value_copy.wait()
 
 
 def pair_rates(rate_ref, count):
@@ -348,14 +418,16 @@
 
 
 def level_kernel(masks, total_ref, got_ref, rate_ref, *refs, rows, level, lead, later):
-    before_ref, (new_ref, sent_ref, enter_ref) = (refs[0] if level else None), refs[-3:]
+    before_ref = refs[0] if level else None
+    sent_ref, enter_ref, *new_ref = refs[1 if level else 0 :]
     _, rate = pair_rates(rate_ref, total_ref.shape[1])
     bit = 2 << level
     after = lax.rem(lax.div(lax.axis_index("ctx"), bit), 2)
     got = got_ref[...].astype(f32)
     early, late = early_late(after, total_ref[...], got)
     total = late + leap(masks, later, rate, bit * rows) * early
-    new_ref[...] = total
+    for ref in new_ref:
+        ref[...] = total
     sent_ref[...] = total.astype(bf16)
     entering = jnp.where(jnp.full(got.shape, after, jnp.int32) == 1, got, 0.0) * lead_leap(masks, lead, rate, rows, bit)
     enter_ref[...] = entering if before_ref is None else before_ref[...] + entering
@@ -499,19 +571,18 @@
     def cost(per_tile, moved):
         return pl.CostEstimate(flops=per_tile * (chans // LANES) * SUBS * LANES, bytes_accessed=moved, transcendentals=0)
 
-    tails = pl.pallas_call(
-        tail_kernel,
-        in_specs=[hbm, hbm, hbm],
-        out_specs=vmem,
-        out_shape=pltpu.VMEM((3, 2, chans), bf16),
+    levels = max(1, (blocks // 4).bit_length() - 2)
+    mask_shape = (Masks(span).count(levels),) + tile_shape
+    tails, masks = pl.pallas_call(
+        functools.partial(tail_kernel, span=span, levels=levels),
+        in_specs=[smem, smem, hbm, hbm, hbm],
+        out_specs=[vmem, vmem],
+        out_shape=[pltpu.VMEM((3, 2, chans), bf16), pltpu.VMEM(mask_shape, f32)],
         scratch_shapes=[pltpu.VMEM((3, 16, chans), bf16), pltpu.SemaphoreType.DMA((3,))],
         compiler_params=params,
         name="tails",
-    )(far_off(query_in), far_off(key_in), far_off(value_in))
+    )(base, lengths, far_off(query_in), far_off(key_in), far_off(value_in))
     rim_rows = from_behind(tails, "ctx", 1)
-    levels = max(1, (blocks // 4).bit_length() - 2)
-    mask_shape = (Masks(span).count(levels),) + tile_shape
-
     def query_piece(part, masks, before):
         count = chans // 2
         scratch = [
@@ -519,23 +590,14 @@
             pltpu.SemaphoreType.DMA((count // chunk,)),
             pltpu.VMEM((Q_TILES, wide_rows, LANES), f32),
         ]
-        out_shape = [pltpu.VMEM((tok_rows, chans), f32)]
-        if part == 0:
-            operands = [base, lengths, far_off(query_in), near_by(short_taps), far_off(value_in)]
-            in_specs = [smem, smem, hbm, vmem, hbm]
-            out_shape += [pltpu.VMEM(mask_shape, f32), pltpu.VMEM((tok_rows, chans), bf16)]
-            scratch.append(pltpu.SemaphoreType.DMA(()))
-        else:
-            operands = [near_by(masks), far_off(query_in), near_by(short_taps), near_by(before)]
-            in_specs = [vmem, hbm, vmem, vmem]
+        operands = [near_by(masks), far_off(query_in), taps] + ([near_by(before)] if part else [])
         return pl.pallas_call(
             functools.partial(
-                query_kernel, span=span, most=Q_TILES, chunk=chunk, levels=levels,
-                first=part * count, count=count,
+                query_kernel, span=span, most=Q_TILES, chunk=chunk, first=part * count, count=count
             ),
-            in_specs=in_specs,
-            out_specs=[vmem] * len(out_shape),
-            out_shape=out_shape,
+            in_specs=[vmem, hbm, vmem] + [vmem] * (len(operands) - 3),
+            out_specs=vmem,
+            out_shape=pltpu.VMEM((tok_rows, chans), f32),
             scratch_shapes=scratch,
             input_output_aliases={3: 0} if part else {},
             compiler_params=params,
@@ -543,38 +605,65 @@
             name="query_part_%d" % part,
         )(*operands)
 
-    q_short, masks, values = query_piece(0, None, None)
-    rim_rows, q_short, values = lax.optimization_barrier((rim_rows, q_short, values))
+    key_half = pltpu.VMEM((tok_rows, chans // 2), bf16)
     rates, weights, taps, rims = near_by(decay_rate), near_by(weight), near_by(short_taps), near_by(rim_rows)
     kept = pltpu.VMEM((modes, chans // 2), f32)
     sent = pltpu.VMEM((modes, chans // 2), bf16)
-    keys, values = near_by(key_in), near_by(values)
-
-    def states_of(own, before):
+
+    small = min(chans // 2, 512)
+    gate_shape = pltpu.VMEM((tok_rows, chans), bf16)
+    state_shape = pltpu.VMEM((chans // LANES, SUBS * (modes + 1), LANES), f32)
+
+    def states_of(own, operands, in_specs, out_shape, scratch, aliases):
         return pl.pallas_call(
-            functools.partial(state_kernel, span=span, modes=modes, most=A_TILES, own=own),
-            in_specs=[vmem] * (6 + len(before)),
-            out_specs=[vmem] * 3,
-            out_shape=[
-                pltpu.VMEM((tok_rows, chans), bf16),
-                pltpu.VMEM((chans // LANES, SUBS * (modes + 1), LANES), f32),
-                kept,
-            ],
-            scratch_shapes=[
+            functools.partial(state_kernel, span=span, modes=modes, most=A_TILES, own=own, chunk=small),
+            in_specs=[vmem] + in_specs,
+            out_specs=[vmem] * (3 + len(out_shape)),
+            out_shape=[gate_shape, state_shape, kept] + out_shape,
+            scratch_shapes=scratch[:-1]
+            + [
                 pltpu.VMEM((A_TILES, wide_rows, LANES), f32),
                 pltpu.VMEM((A_TILES, wide_rows, LANES), f32),
                 pltpu.VMEM((A_TILES, modes, LANES), f32),
                 pltpu.VMEM((A_TILES, span) + tile_shape, f32),
-            ],
-            input_output_aliases={6 + i: i for i in range(len(before))},
+            ]
+            + scratch[-1:],
+            input_output_aliases=aliases,
             compiler_params=params,
             cost_estimate=cost(500, 6 * tok_rows * chans),
             name="block_states_own" if own else "block_states_give",
-        )(near_by(masks), keys, values, rims, taps, rates, *[near_by(x) for x in before])
-
-    gates, states, give = states_of(False, [])
+        )(near_by(masks), *operands)
+
+    gates, states, give, key_own, value_own, heads = states_of(
+        False,
+        [far_off(key_in), far_off(value_in), taps, rates],
+        [hbm, hbm, vmem, vmem],
+        [key_half, key_half, pltpu.VMEM((2, 16, chans // 2), bf16)],
+        [
+            pltpu.VMEM((tok_rows, chans // 2), bf16),
+            pltpu.VMEM((tok_rows, chans // 2), bf16),
+            pltpu.SemaphoreType.DMA((2, chans // 2 // small + 1)),
+        ],
+        {},
+    )
+    gates, states, give = pl.pallas_call(
+        functools.partial(patch_kernel, span=span, modes=modes),
+        in_specs=[vmem] * 8,
+        out_specs=[vmem] * 3,
+        out_shape=[gate_shape, state_shape, kept],
+        input_output_aliases={5: 0, 6: 1, 7: 2},
+        compiler_params=params,
+        name="first_rows",
+    )(near_by(masks), near_by(heads), rims, taps, rates, near_by(gates), near_by(states), near_by(give))
     got = swap(give, "ctx")
-    gates, states, own = states_of(True, [gates, states])
+    gates, states, own = states_of(
+        True,
+        [near_by(key_own), near_by(value_own), rims, taps, rates, near_by(gates), near_by(states)],
+        [vmem] * 7,
+        [],
+        [],
+        {6: 0, 7: 1},
+    )
     got, gates, states, own = lax.optimization_barrier((got, gates, states, own))
 
     def near_piece(part, near):
@@ -617,11 +706,14 @@
         met = swap(ends, "ctx", 2 << m)
         if m < NEAR_PARTS:
             near = near_piece(m, near)
+            if m == 0:
+                q_short = query_piece(0, masks, None)
+                met, q_short = lax.optimization_barrier((met, q_short))
             met, near = lax.optimization_barrier((met, near))
-        total, ends, enter = pair_call(
+        ends, enter, *total = pair_call(
             level_kernel,
             [total, met],
-            [kept, sent, kept],
+            [sent, kept] + [kept] * (m < levels - 1),
             "level_%d" % m,
             extra=entering,
             rows=tok_rows,
@@ -630,10 +722,11 @@
             later=at.later(m),
         )
         entering = [enter]
+        total = total[0] if total else None
     on = from_behind(ends, "ctx", 2 << levels)
     for m in range(levels, NEAR_PARTS):
         near = near_piece(m, near)
-    q_short = query_piece(1, masks, q_short)[0]
+    q_short = query_piece(1, masks, q_short)
     on, q_short, near = lax.optimization_barrier((on, q_short, near))
     mine, give_back = pair_call(
         enter_kernel,

time: 48.9 us -> 46.8 us (0.957)
  waiting for transfers between devices: 4.39 us -> 1.19 us
  Pallas kernels: 30.9 us -> 31.8 us
    ppermute x4, waiting for transfers between devices: 3.91 us -> 0.71 us  [swap(): lax.ppermute(shard, axis, [(i, i ^ bit) for i in range(lax.axis_size(axis...]
    pallas_call x1 -> x2, Pallas kernels: 1.2 us -> 2.47 us  [the longest x1 1.94 us: shards(): pl.pallas_call(functools.partial(tail_kernel, span=span, levels=levels),...]
    pallas_call x2, Pallas kernels: 9.05 us -> 10.2 us  [states_of(): pl.pallas_call(functools.partial(state_kernel, span=span, modes=modes, mo...]
    pallas_call x2, Pallas kernels: 4.78 us -> 3.85 us  [query_piece(): pl.pallas_call(functools.partial(query_kernel, span=span, most=Q_TILES, c...]
    pallas_call x4, Pallas kernels: 1.57 us -> 0.93 us  [pair_call(): pl.pallas_call(functools.partial(kernel, **static), in_specs=[vmem] * (le...]
  transfers between devices with their start and end apart: 6 -> 6, of which waited for: 3 -> 2; matrix products, arithmetic and copies ran while one was open for 1% -> 1% of each run, Pallas kernels for 38% -> 50%
where the time goes in v19:
time: 46.8 us; the launch traced here: 46.6 us
  Pallas kernels  31.8 us (68%)
  starting transfers between devices  12.4 us (26%)
  waiting for transfers between devices  1.19 us (3%)
  between operations  0.84 us (2%)
    pallas_call x2, Pallas kernels, states_of(): pl.pallas_call(functools.partial(state_kernel, span=span, modes=modes, mo...  10.2 us
    pallas_call x2, Pallas kernels, finish(): pl.pallas_call(functools.partial(final_kernel, span=span, modes=modes, ch...  9.67 us
    ppermute x2, starting transfers between devices, from_behind(): return lax.ppermute(shard, axis, [(i, i + by) for i in range(count - by)])  6.88 us
    ppermute x4, starting transfers between devices, swap(): lax.ppermute(shard, axis, [(i, i ^ bit) for i in range(lax.axis_size(axis...  5.5 us
    pallas_call x2, Pallas kernels, near_piece(): pl.pallas_call(functools.partial(near_kernel, span=span, modes=modes, mos...  4.67 us
    pallas_call x2, Pallas kernels, query_piece(): pl.pallas_call(functools.partial(query_kernel, span=span, most=Q_TILES, c...  3.85 us
    pallas_call x1, Pallas kernels, shards(): pl.pallas_call(functools.partial(tail_kernel, span=span, levels=levels),...  1.94 us
  transfers between devices with their start and end apart: 6, of which 2 were waited for; matrix products, arithmetic and copies ran while one was open for 1% of the time, Pallas kernels for 50%

profile of v19, /device:TPU:9, one launch (start us, length us, event | category | flops | bytes accessed | tf_op | source)
XLA Modules:
  0.0 46.6 jit_solution(5300465038520547301)
XLA Ops:
  0.6 0.0 copy-start
  0.6 0.0 copy-start.1
  0.7 1.9 %tails.1 = (bf16[3,2,8192]{2,1,0:T(2,128)(2,1)S(1)}, f32[85,8,128]{2,1,0:T(8,128)S(1)}) custom-call(s32[1]{0:T(128)} %bitcast.base_ref, s32[16]{0:T(128)} %len_ref.1, bf16[128,8192]{1,0:T(8,128)(2,1)} %query_ref.5, bf16[128,8192]{1,0:T(8,128)(2,1)} %refs_0_.1, bf16[128,8192]{1,0:T(8,128)(2,1)} %refs_1_.1), custom_call_target="tpu_custom_call" | custom-call | tf_op jit(solution)/shard_map/tails/pallas_call | solution.py:576
  2.6 3.7 %collective-permute-start = (bf16[3,2,8192]{2,1,0:T(2,128)(2,1)S(1)}, bf16[3,2,8192]{2,1,0:T(2,128)(2,1)S(1)}, u32[]{:S(2)}, u32[]{:S(2)}) collective-permute-start(bf16[3,2,8192]{2,1,0:T(2,128)(2,1)S(1)} %get-tuple-element.48), channel_id=1, source_target_pairs={{0,1},{1,2},{2,3},{3,4},{4,5},{5,6},{6,7},{7,8},{8,9},{9,10},{10,1... | collective-permute-start | bytes 294920 | tf_op jit(solution)/shard_map/ppermute | solution.py:22
  6.3 0.0 copy-done
  6.3 0.0 copy-done.1
  6.3 5.7 %block_states_give.1 = (bf16[128,8192]{1,0:T(8,128)(2,1)S(1)}, f32[64,136,128]{2,1,0:T(8,128)S(1)}, f32[16,4096]{1,0:T(8,128)S(1)}, bf16[128,4096]{1,0:T(8,128)(...) custom-call(f32[85,8,128]{2,1,0:T(8,128)S(1)} %get-tuple-element.46.masks, ...), custom_call_target="tpu_custom_call" | custom-call | flops 32768000 | bytes 6291456 | tf_op jit(solution)/shard_map/block_states_give/pallas_call | solution.py:618
  12.0 0.0 collective-permute-done.rim_ref.refs_2_
  12.0 0.5 %first_rows.1 = (bf16[128,8192]{1,0:T(8,128)(2,1)S(1)}, f32[64,136,128]{2,1,0:T(8,128)S(1)}, f32[16,4096]{1,0:T(8,128)S(1)}) custom-call(f32[85,8,128]{2,1,0:T(8,128)S(1)} %get-tuple-element.46.masks, bf16[2,16,4096]{2,1,0:T(8,128)(2,1)S(1)} %get-tuple-element.47.heads, ...), custom_call_target="tpu_custom_call", output_to_operand_aliasing={{0}: (5, {}), {1}: (6, {}), {2}: (7, {})} | custom-call | tf_op jit(solution)/shard_map/first_rows/pallas_call | solution.py:649
  12.6 0.1 collective-permute-start.1
  12.6 0.0 copy-start.4
  12.7 4.5 %block_states_own.1 = (bf16[128,8192]{1,0:T(8,128)(2,1)S(1)}, f32[64,136,128]{2,1,0:T(8,128)S(1)}, f32[16,4096]{1,0:T(8,128)S(1)}) custom-call(f32[85,8,128]{2,1,0:T(8,128)S(1)} %get-tuple-element.46.masks, bf16[128,4096]{1,0:T(8,128)(2,1)S(1)} %get-tuple-element.53.refs_0_, ...), custom_call_target="tpu_custom_call", output_to_operand_aliasing={{0}: (6, {}), {1}: (7, {})} | custom-call | flops 32768000 | bytes 6291456 | tf_op jit(solution)/shard_map/block_states_own/pallas_call | solution.py:618
  17.2 0.0 collective-permute-done.1.got_ref.other_ref
  17.2 0.2 pair_ends.1
  17.4 1.3 %collective-permute-start.2 = (bf16[16,4096]{1,0:T(8,128)(2,1)S(1)}, bf16[16,4096]{1,0:T(8,128)(2,1)S(1)}, u32[]{:S(2)}, u32[]{:S(2)}) collective-permute-start(bf16[16,4096]{1,0:T(8,128)(2,1)S(1)} %get-tuple-element.63), channel_id=1, source_target_pairs={{0,2},{1,3},{2,0},{3,1},{4,6},{5,7},{6,4},{7,5},{8,10},{9,11},{10,... | collective-permute-start | bytes 393224 | tf_op jit(solution)/shard_map/ppermute | solution.py:26
  18.7 0.0 copy-done.4
  18.7 0.3 sqrt_multiply_fusion.weight_ref
  19.0 1.9 %query_part_0.1.refs_0_ = f32[128,8192]{1,0:T(8,128)S(1)} custom-call(f32[85,8,128]{2,1,0:T(8,128)S(1)} %get-tuple-element.46.masks, bf16[128,8192]{1,0:T(8,128)(2,1)} %query_ref.5, f32[3,3,8192]{2,1,0:T(4,128)S(1)} %copy-done.1), custom_call_target="tpu_custom_call" | custom-call | flops 6553600 | bytes 3145728 | tf_op jit(solution)/shard_map/query_part_0/pallas_call | solution.py:594
  20.8 2.3 %near_part_0.1.refs_0_ = f32[128,8192]{1,0:T(8,128)S(1)} custom-call(f32[85,8,128]{2,1,0:T(8,128)S(1)} %get-tuple-element.46.masks, bf16[128,8192]{1,0:T(8,128)(2,1)S(1)} %get-tuple-element.65.gate_ref, f32[16,8192]{1,0:T(8,128)S(1)} %copy-done, f32[16,8192]{1,0:T(8,128)S(1)} %sqrt_multiply_fusion.weight_ref), custom_call_target="tpu_custom_call" | custom-call | flops 19660800 | bytes 3670016 | tf_op jit(solution)/shard_map/near_part_0/pallas_call | solution.py:672
  23.2 0.0 collective-permute-done.2.got_ref
  23.2 0.2 level_0.1
  23.5 1.3 %collective-permute-start.3 = (bf16[16,4096]{1,0:T(8,128)(2,1)S(1)}, bf16[16,4096]{1,0:T(8,128)(2,1)S(1)}, u32[]{:S(2)}, u32[]{:S(2)}) collective-permute-start(bf16[16,4096]{1,0:T(8,128)(2,1)S(1)} %get-tuple-element.68), channel_id=1, source_target_pairs={{0,4},{1,5},{2,6},{3,7},{4,0},{5,1},{6,2},{7,3},{8,12},{9,13},{10,... | collective-permute-start | bytes 393224 | tf_op jit(solution)/shard_map/ppermute | solution.py:26
  24.8 2.3 %near_part_1.1.near_ref = f32[128,8192]{1,0:T(8,128)S(1)} custom-call(f32[85,8,128]{2,1,0:T(8,128)S(1)} %get-tuple-element.46.masks, bf16[128,8192]{1,0:T(8,128)(2,1)S(1)} %get-tuple-element.65.gate_ref, f32[16,8192]{1,0:T(8,128)S(1)} %copy-done, f32[16,8192]{1,0:T(8,128)S(1)} %sqrt_multiply_fusion.weight_ref, ...), custom_call_target="tpu_custom_call", output_to_operand_aliasing={{}: (4, {})} | custom-call | flops 19660800 | bytes 3670016 | tf_op jit(solution)/shard_map/near_part_1/pallas_call | solution.py:672
  27.1 0.7 %collective-permute-done.3.got_ref = bf16[16,4096]{1,0:T(8,128)(2,1)S(1)} collective-permute-done((bf16[16,4096]{1,0:T(8,128)(2,1)S(1)}, bf16[16,4096]{1,0:T(8,128)(2,1)S(1)}, u32[]{:S(2)}, u32[]{:S(2)}) %collective-permute-start.3) | collective-permute-done | bytes 131104 | tf_op jit(solution)/shard_map/ppermute | solution.py:26
  27.8 0.2 level_1.1
  28.0 3.2 %collective-permute-start.4 = (bf16[16,4096]{1,0:T(8,128)(2,1)S(1)}, bf16[16,4096]{1,0:T(8,128)(2,1)S(1)}, u32[]{:S(2)}, u32[]{:S(2)}) collective-permute-start(bf16[16,4096]{1,0:T(8,128)(2,1)S(1)} %get-tuple-element.73), channel_id=1, source_target_pairs={{0,8},{1,9},{2,10},{3,11},{4,12},{5,13},{6,14},{7,15},{8,16},{9,17... | collective-permute-start | bytes 393224 | tf_op jit(solution)/shard_map/ppermute | solution.py:22
  31.3 0.0 copy-start.2
  31.3 2.0 %query_part_1.1.short_ref = f32[128,8192]{1,0:T(8,128)S(1)} custom-call(f32[85,8,128]{2,1,0:T(8,128)S(1)} %get-tuple-element.46.masks, bf16[128,8192]{1,0:T(8,128)(2,1)} %query_ref.5, f32[3,3,8192]{2,1,0:T(4,128)S(1)} %copy-done.1, f32[128,8192]{1,0:T(8,128)S(1)} %query_part_0.1.refs_0_), custom_call_target="tpu_custom_call", output_to_operand_aliasing={{}: (3, {})} | custom-call | flops 6553600 | bytes 3145728 | tf_op jit(solution)/shard_map/query_part_1/pallas_call | solution.py:594
  33.3 0.5 %collective-permute-done.4.got_ref = bf16[16,4096]{1,0:T(8,128)(2,1)S(1)} collective-permute-done((bf16[16,4096]{1,0:T(8,128)(2,1)S(1)}, bf16[16,4096]{1,0:T(8,128)(2,1)S(1)}, u32[]{:S(2)}, u32[]{:S(2)}) %collective-permute-start.4) | collective-permute-done | bytes 131104 | tf_op jit(solution)/shard_map/ppermute | solution.py:22
  33.8 0.3 pair_enter.1
  34.0 2.8 %collective-permute-start.5 = (f32[16,4096]{1,0:T(8,128)S(1)}, f32[16,4096]{1,0:T(8,128)S(1)}, u32[]{:S(2)}, u32[]{:S(2)}) collective-permute-start(f32[16,4096]{1,0:T(8,128)S(1)} %get-tuple-element.77), channel_id=1, source_target_pairs={{0,1},{1,0},{2,3},{3,2},{4,5},{5,4},{6,7},{7,6},{8,9},{9,8},{10,11... | collective-permute-start | bytes 786440 | tf_op jit(solution)/shard_map/ppermute | solution.py:26
  36.9 0.0 copy-done.2
  36.9 0.0 copy-start.3
  36.9 4.4 %far_part_own.1 = (bf16[128,8192]{1,0:T(8,128)(2,1)}, f32[64,128,128]{2,1,0:T(8,128)S(1)}, f32[128,128]{1,0:T(8,128)S(1)}) custom-call(f32[85,8,128]{2,1,0:T(8,128)S(1)} %get-tuple-element.46.masks, f32[64,136,128]{2,1,0:T(8,128)S(1)} %get-tuple-element.60.state_ref, f32[16,4096]{1,0:T(8,128)S(1)} %get-tuple-element.78.enter_ref, ...), custom_call_target="tpu_custom_call" | custom-call | flops 29491200 | bytes 9437184 | tf_op jit(solution)/shard_map/far_part_own/pallas_call | solution.py:772
  41.3 0.0 collective-permute-done.5.enter_ref
  41.3 0.0 copy-done.3
  41.3 5.3 %far_part_other.1 = (bf16[128,8192]{1,0:T(8,128)(2,1)}, f32[64,128,128]{2,1,0:T(8,128)S(1)}, f32[128,128]{1,0:T(8,128)S(1)}, bf16[128,8192]{1,0:T(8,128)(2,1)}) custom-call(f32[85,8,128]{2,1,0:T(8,128)S(1)} %get-tuple-element.46.masks, ...), custom_call_target="tpu_custom_call", output_to_operand_aliasing={{0}: (11, {}), {1}: (12, {}), {2}: (13, {})} | custom-call | flops 29491200 | bytes 9437184 | tf_op jit(solution)/shard_map/far_part_other/pallas_call | solution.py:772
Async XLA Ops:
  0.6 5.7 %copy-start = (f32[16,8192]{1,0:T(8,128)S(1)}, f32[16,8192]{1,0:T(8,128)}, u32[]{:S(2)}) copy-start(f32[16,8192]{1,0:T(8,128)} %rate_ref.17) | copy-start | bytes 1572868
  0.6 5.7 %copy-start.1 = (f32[3,3,8192]{2,1,0:T(4,128)S(1)}, f32[3,3,8192]{2,1,0:T(4,128)}, u32[]{:S(2)}) copy-start(f32[3,3,8192]{2,1,0:T(4,128)} %taps_ref.9) | copy-start | bytes 884740
  2.6 9.4 %collective-permute-start = (bf16[3,2,8192]{2,1,0:T(2,128)(2,1)S(1)}, bf16[3,2,8192]{2,1,0:T(2,128)(2,1)S(1)}, u32[]{:S(2)}, u32[]{:S(2)}) collective-permute-start(bf16[3,2,8192]{2,1,0:T(2,128)(2,1)S(1)} %get-tuple-element.48), channel_id=1, source_target_pairs={{0,1},{1,2},{2,3},{3,4},{4,5},{5,6},{6,7},{7,8},{8,9},{9,10},{10,1... | collective-permute-start | bytes 294920 | tf_op jit(solution)/shard_map/ppermute | solution.py:22
  12.6 4.6 %collective-permute-start.1 = (f32[16,4096]{1,0:T(8,128)S(1)}, f32[16,4096]{1,0:T(8,128)S(1)}, u32[]{:S(2)}, u32[]{:S(2)}) collective-permute-start(f32[16,4096]{1,0:T(8,128)S(1)} %get-tuple-element.52), channel_id=1, source_target_pairs={{0,1},{1,0},{2,3},{3,2},{4,5},{5,4},{6,7},{7,6},{8,9},{9,8},{10,11... | collective-permute-start | bytes 786440 | tf_op jit(solution)/shard_map/ppermute | solution.py:26
  12.6 6.0 %copy-start.4 = (f32[16,8192]{1,0:T(8,128)S(1)}, f32[16,8192]{1,0:T(8,128)}, u32[]{:S(2)}) copy-start(f32[16,8192]{1,0:T(8,128)} %param.14) | copy-start | bytes 1572868
  17.4 5.8 %collective-permute-start.2 = (bf16[16,4096]{1,0:T(8,128)(2,1)S(1)}, bf16[16,4096]{1,0:T(8,128)(2,1)S(1)}, u32[]{:S(2)}, u32[]{:S(2)}) collective-permute-start(bf16[16,4096]{1,0:T(8,128)(2,1)S(1)} %get-tuple-element.63), channel_id=1, source_target_pairs={{0,2},{1,3},{2,0},{3,1},{4,6},{5,7},{6,4},{7,5},{8,10},{9,11},{10,... | collective-permute-start | bytes 393224 | tf_op jit(solution)/shard_map/ppermute | solution.py:26
  23.5 4.3 %collective-permute-start.3 = (bf16[16,4096]{1,0:T(8,128)(2,1)S(1)}, bf16[16,4096]{1,0:T(8,128)(2,1)S(1)}, u32[]{:S(2)}, u32[]{:S(2)}) collective-permute-start(bf16[16,4096]{1,0:T(8,128)(2,1)S(1)} %get-tuple-element.68), channel_id=1, source_target_pairs={{0,4},{1,5},{2,6},{3,7},{4,0},{5,1},{6,2},{7,3},{8,12},{9,13},{10,... | collective-permute-start | bytes 393224 | tf_op jit(solution)/shard_map/ppermute | solution.py:26
  28.0 5.7 %collective-permute-start.4 = (bf16[16,4096]{1,0:T(8,128)(2,1)S(1)}, bf16[16,4096]{1,0:T(8,128)(2,1)S(1)}, u32[]{:S(2)}, u32[]{:S(2)}) collective-permute-start(bf16[16,4096]{1,0:T(8,128)(2,1)S(1)} %get-tuple-element.73), channel_id=1, source_target_pairs={{0,8},{1,9},{2,10},{3,11},{4,12},{5,13},{6,14},{7,15},{8,16},{9,17... | collective-permute-start | bytes 393224 | tf_op jit(solution)/shard_map/ppermute | solution.py:22
  31.3 5.6 %copy-start.2 = (bf16[128,8192]{1,0:T(8,128)(2,1)S(1)}, bf16[128,8192]{1,0:T(8,128)(2,1)}, u32[]{:S(2)}) copy-start(bf16[128,8192]{1,0:T(8,128)(2,1)} %resid_ref.3) | copy-start | bytes 6291460
  34.0 7.2 %collective-permute-start.5 = (f32[16,4096]{1,0:T(8,128)S(1)}, f32[16,4096]{1,0:T(8,128)S(1)}, u32[]{:S(2)}, u32[]{:S(2)}) collective-permute-start(f32[16,4096]{1,0:T(8,128)S(1)} %get-tuple-element.77), channel_id=1, source_target_pairs={{0,1},{1,0},{2,3},{3,2},{4,5},{5,4},{6,7},{7,6},{8,9},{9,8},{10,11... | collective-permute-start | bytes 786440 | tf_op jit(solution)/shard_map/ppermute | solution.py:26
  36.9 4.4 %copy-start.3 = (f32[8192]{0:T(1024)S(1)}, f32[8192]{0:T(1024)}, u32[]{:S(2)}) copy-start(f32[8192]{0:T(1024)} %param.17) | copy-start | bytes 98308

commit v20 on v19

--- a/solution.py
+++ b/solution.py
@@ -55,7 +55,7 @@
     lax.fori_loop(0, count // size, step, 0)
 
 
-def each_chunk(chans, chunk, before, group, after, most):
+def each_chunk(chans, chunk, before, group, after, most, start=0):
     def step(c, carry):
         before(c)
 
@@ -66,7 +66,7 @@
         after(c)
         return carry
 
-    lax.fori_loop(0, chans // chunk, step, 0)
+    lax.fori_loop(start, chans // chunk, step, 0)
 
 
 def cols_copy(src, dst, sem, c, chunk):
@@ -123,7 +123,7 @@
     if own:
         key_ref, value_ref, rim_ref, taps_ref, rate_ref, _, _, gate_ref, state_ref, end_ref, wide_k, wide_v, tables, held = refs
     else:
-        (key_in, value_in, taps_ref, rate_ref, gate_ref, state_ref, end_ref, key_own, value_own, heads,
+        (ahead_ref, key_in, value_in, taps_ref, rate_ref, gate_ref, state_ref, end_ref, key_own, value_own, heads,
          key_ref, value_ref, wide_k, wide_v, tables, held, sems) = refs
     half = key_ref.shape[1]
     first = half_start(2 * half, own)
@@ -141,17 +141,15 @@
             pltpu.make_async_copy(key_in.at[:, cols], key_own, sems.at[0, half // chunk]),
             pltpu.make_async_copy(value_in.at[:, cols], value_own, sems.at[1, half // chunk]),
         ]
-        for c in range(half // chunk):
+        for c in range(1, half // chunk):
             for copy in fetch(c):
                 copy.start()
-        for copy in others:
-            copy.start()
     at = Masks(span)
 
-    def group(lanes):
+    def group(lanes, keys=key_ref, values=value_ref):
         for slot, lane in enumerate(lanes):
-            spread(key_ref[:, cols_of(pl.multiple_of(lane - first, LANES))], wide_k.at[slot], span)
-            spread(value_ref[:, cols_of(pl.multiple_of(lane - first, LANES))], wide_v.at[slot], span)
+            spread(keys[:, cols_of(pl.multiple_of(lane - first, LANES))], wide_k.at[slot], span)
+            spread(values[:, cols_of(pl.multiple_of(lane - first, LANES))], wide_v.at[slot], span)
             rate = rate_ref[:, cols_of(lane)]
             tables[slot] = jnp.exp(-rate)
         convs = [
@@ -190,8 +188,8 @@
                 end = (leap * twice(masks[at.passes + b], modes)) * end + sub_state(state_ref, lane, b, modes)
             end_ref[:, cols_of(pl.multiple_of(lane - first, LANES))] = end
 
-    def shifted(lanes):
-        group([pl.multiple_of(first + lane, LANES) for lane in lanes])
+    def shifted(lanes, *sources):
+        group([pl.multiple_of(first + lane, LANES) for lane in lanes], *sources)
 
     if own:
         each_group(half // LANES, most, shifted)
@@ -200,9 +198,15 @@
             for copy in fetch(c):
                 copy.wait()
 
-        each_chunk(half, chunk, before, shifted, lambda c: None, most)
-        heads[0] = key_ref[pl.ds(0, heads.shape[1]), :]
-        heads[1] = value_ref[pl.ds(0, heads.shape[1]), :]
+        each_group(chunk // LANES, most, lambda lanes: shifted(lanes, ahead_ref.at[0], ahead_ref.at[1]))
+        for copy in others:
+            copy.start()
+        each_chunk(half, chunk, before, shifted, lambda c: None, most, 1)
+        rows = pl.ds(0, heads.shape[1])
+        for i, ref in enumerate((key_ref, value_ref)):
+            heads[i, :, pl.ds(0, chunk)] = ahead_ref[i, rows, :]
+            if half > chunk:
+                heads[i, :, pl.ds(chunk, half - chunk)] = ref[rows, pl.ds(chunk, half - chunk)]
         for copy in others:
             copy.wait()
 
@@ -246,18 +250,27 @@
     each_group(half // LANES, 4, group)
 
 
-def tail_kernel(base_ref, len_ref, query_ref, key_ref, value_ref, tail_ref, masks, bufs, sems, *, span, levels):
+def tail_kernel(
+    base_ref, len_ref, query_ref, key_ref, value_ref, tail_ref, masks, ahead_ref, bufs, rows_of, sems, *, span, levels
+):
     rows, count = query_ref.shape[0], bufs.shape[1]
     copies = [
         pltpu.make_async_copy(ref.at[pl.ds(rows - count, count)], bufs.at[i], sems.at[i])
         for i, ref in enumerate((query_ref, key_ref, value_ref))
     ]
-    for copy in copies:
+    cols = pl.ds(half_start(query_ref.shape[1], False), ahead_ref.shape[2])
+    aheads = [
+        pltpu.make_async_copy(ref.at[:, cols], ahead_ref.at[i], sems.at[3 + i])
+        for i, ref in enumerate((key_ref, value_ref))
+    ]
+    for copy in copies + aheads:
         copy.start()
-    write_masks(base_ref, len_ref, masks, span, levels)
+    write_masks(base_ref, len_ref, masks, rows_of, span, levels)
     for i, copy in enumerate(copies):
         copy.wait()
         tail_ref[i] = bufs[i].astype(f32)[count - 2 :].astype(bf16)
+    for copy in aheads:
+        copy.wait()
 
 
 def unbroken(len_ref, first, count):
@@ -290,7 +303,7 @@
         return self.levels + 2 * levels + 1
 
 
-def write_masks(base_ref, len_ref, masks, span, levels):
+def write_masks(base_ref, len_ref, masks, rows_of, span, levels):
     at = Masks(span)
     rows, starts = doc_start_rows(len_ref, base_ref[0], span)
     for j in range(span):
@@ -307,8 +320,11 @@
     size = SUBS * span
     parity = lax.rem(lax.div(base_ref[0], size), 2)
     pair_at = base_ref[0] - parity * size
-    ranges = [(base_ref[0] + b * span, span) for b in range(SUBS)]
-    flags = [at.passes + b for b in range(SUBS)]
+    rows_of[...] = flag(starts[span - 1] < rows)
+    for b in range(SUBS):
+        masks[at.passes + b] = row_of(rows_of, b)
+    ranges = []
+    flags = []
     ranges += [(pair_at + size, size), (pair_at, size), (base_ref[0] + span, size - span)]
     flags += [at.late, at.early, at.rest]
     for m in range(levels + 1):
@@ -544,7 +560,7 @@
     span = tok_rows // SUBS
     blocks = lax.axis_size("ctx")
     grp = lax.axis_size("grp")
-    chunk = min(chans // 2, 1024)
+    chunk = min(chans // 2, 512)
     pieces = chans // chunk
     ctx_index = lax.axis_index("ctx")
     base = (ctx_index * tok_rows).astype(jnp.int32).reshape(1)
@@ -573,12 +589,17 @@
 
     levels = max(1, (blocks // 4).bit_length() - 2)
     mask_shape = (Masks(span).count(levels),) + tile_shape
-    tails, masks = pl.pallas_call(
+    small = min(chans // 2, 512)
+    tails, masks, ahead = pl.pallas_call(
         functools.partial(tail_kernel, span=span, levels=levels),
         in_specs=[smem, smem, hbm, hbm, hbm],
-        out_specs=[vmem, vmem],
-        out_shape=[pltpu.VMEM((3, 2, chans), bf16), pltpu.VMEM(mask_shape, f32)],
-        scratch_shapes=[pltpu.VMEM((3, 16, chans), bf16), pltpu.SemaphoreType.DMA((3,))],
+        out_specs=[vmem, vmem, vmem],
+        out_shape=[
+            pltpu.VMEM((3, 2, chans), bf16), pltpu.VMEM(mask_shape, f32), pltpu.VMEM((2, tok_rows, small), bf16)
+        ],
+        scratch_shapes=[
+            pltpu.VMEM((3, 16, chans), bf16), pltpu.VMEM(tile_shape, f32), pltpu.SemaphoreType.DMA((5,))
+        ],
         compiler_params=params,
         name="tails",
     )(base, lengths, far_off(query_in), far_off(key_in), far_off(value_in))
@@ -610,7 +631,6 @@
     kept = pltpu.VMEM((modes, chans // 2), f32)
     sent = pltpu.VMEM((modes, chans // 2), bf16)
 
-    small = min(chans // 2, 512)
     gate_shape = pltpu.VMEM((tok_rows, chans), bf16)
     state_shape = pltpu.VMEM((chans // LANES, SUBS * (modes + 1), LANES), f32)
 
@@ -636,8 +656,8 @@
 
     gates, states, give, key_own, value_own, heads = states_of(
         False,
-        [far_off(key_in), far_off(value_in), taps, rates],
-        [hbm, hbm, vmem, vmem],
+        [near_by(ahead), far_off(key_in), far_off(value_in), taps, rates],
+        [vmem, hbm, hbm, vmem, vmem],
         [key_half, key_half, pltpu.VMEM((2, 16, chans // 2), bf16)],
         [
             pltpu.VMEM((tok_rows, chans // 2), bf16),

time: 46.8 us -> 46.4 us (level)
    pallas_call x2, Pallas kernels: 10.2 us -> 9.72 us  [states_of(): pl.pallas_call(functools.partial(state_kernel, span=span, modes=modes, mo...]
  transfers between devices with their start and end apart: 6 -> 6, of which waited for: 2 -> 2; matrix products, arithmetic and copies ran while one was open for 1% -> 1% of each run, Pallas kernels for 50% -> 49%
where the time goes in v20:
time: 46.4 us; the launch traced here: 46.2 us
  Pallas kernels  31.4 us (68%)
  starting transfers between devices  12.4 us (27%)
  waiting for transfers between devices  1.21 us (3%)
  between operations  0.84 us (2%)
    pallas_call x2, Pallas kernels, states_of(): pl.pallas_call(functools.partial(state_kernel, span=span, modes=modes, mo...  9.72 us
    pallas_call x2, Pallas kernels, finish(): pl.pallas_call(functools.partial(final_kernel, span=span, modes=modes, ch...  9.7 us
    ppermute x2, starting transfers between devices, from_behind(): return lax.ppermute(shard, axis, [(i, i + by) for i in range(count - by)])  6.88 us
    ppermute x4, starting transfers between devices, swap(): lax.ppermute(shard, axis, [(i, i ^ bit) for i in range(lax.axis_size(axis...  5.5 us
    pallas_call x2, Pallas kernels, near_piece(): pl.pallas_call(functools.partial(near_kernel, span=span, modes=modes, mos...  4.67 us
    pallas_call x2, Pallas kernels, query_piece(): pl.pallas_call(functools.partial(query_kernel, span=span, most=Q_TILES, c...  3.82 us
    pallas_call x1, Pallas kernels, shards(): pl.pallas_call(functools.partial(tail_kernel, span=span, levels=levels),...  2.02 us
  transfers between devices with their start and end apart: 6, of which 2 were waited for; matrix products, arithmetic and copies ran while one was open for 1% of the time, Pallas kernels for 49%

profile of v20, /device:TPU:9, one launch (start us, length us, event | category | flops | bytes accessed | tf_op | source)
XLA Modules:
  0.0 46.2 jit_solution(3675847709155749172)
XLA Ops:
  0.6 0.0 copy-start
  0.6 0.0 copy-start.1
  0.7 2.0 %tails.1 = (bf16[3,2,8192]{2,1,0:T(2,128)(2,1)S(1)}, f32[85,8,128]{2,1,0:T(8,128)S(1)}, bf16[2,128,512]{2,1,0:T(8,128)(2,1)S(1)}) custom-call(s32[1]{0:T(128)} %bitcast.base_ref, s32[16]{0:T(128)} %len_ref.1, bf16[128,8192]{1,0:T(8,128)(2,1)} %query_ref.5, bf16[128,8192]{1,0:T(8,128)(2,1)} %refs_1_.1, bf16[128,8192]{1,0:T(8,128)(2,1)} %refs_2_.1), custom_call_target="tpu_custom_call" | custom-call | tf_op jit(solution)/shard_map/tails/pallas_call | solution.py:593
  2.7 3.7 %collective-permute-start = (bf16[3,2,8192]{2,1,0:T(2,128)(2,1)S(1)}, bf16[3,2,8192]{2,1,0:T(2,128)(2,1)S(1)}, u32[]{:S(2)}, u32[]{:S(2)}) collective-permute-start(bf16[3,2,8192]{2,1,0:T(2,128)(2,1)S(1)} %get-tuple-element.50), channel_id=1, source_target_pairs={{0,1},{1,2},{2,3},{3,4},{4,5},{5,6},{6,7},{7,8},{8,9},{9,10},{10,1... | collective-permute-start | bytes 294920 | tf_op jit(solution)/shard_map/ppermute | solution.py:22
  6.4 0.0 copy-done
  6.4 0.0 copy-done.1
  6.4 5.2 %block_states_give.1 = (bf16[128,8192]{1,0:T(8,128)(2,1)S(1)}, f32[64,136,128]{2,1,0:T(8,128)S(1)}, f32[16,4096]{1,0:T(8,128)S(1)}, bf16[128,4096]{1,0:T(8,128)(...) custom-call(f32[85,8,128]{2,1,0:T(8,128)S(1)} %get-tuple-element.47.masks, ...), custom_call_target="tpu_custom_call" | custom-call | flops 32768000 | bytes 6291456 | tf_op jit(solution)/shard_map/block_states_give/pallas_call | solution.py:638
  11.6 0.0 collective-permute-done.rim_ref.refs_2_
  11.6 0.5 %first_rows.1 = (bf16[128,8192]{1,0:T(8,128)(2,1)S(1)}, f32[64,136,128]{2,1,0:T(8,128)S(1)}, f32[16,4096]{1,0:T(8,128)S(1)}) custom-call(f32[85,8,128]{2,1,0:T(8,128)S(1)} %get-tuple-element.47.masks, bf16[2,16,4096]{2,1,0:T(8,128)(2,1)S(1)} %get-tuple-element.49.heads, ...), custom_call_target="tpu_custom_call", output_to_operand_aliasing={{0}: (5, {}), {1}: (6, {}), {2}: (7, {})} | custom-call | tf_op jit(solution)/shard_map/first_rows/pallas_call | solution.py:669
  12.1 0.1 collective-permute-start.1
  12.2 0.0 copy-start.4
  12.2 4.5 %block_states_own.1 = (bf16[128,8192]{1,0:T(8,128)(2,1)S(1)}, f32[64,136,128]{2,1,0:T(8,128)S(1)}, f32[16,4096]{1,0:T(8,128)S(1)}) custom-call(f32[85,8,128]{2,1,0:T(8,128)S(1)} %get-tuple-element.47.masks, bf16[128,4096]{1,0:T(8,128)(2,1)S(1)} %get-tuple-element.55.refs_0_, ...), custom_call_target="tpu_custom_call", output_to_operand_aliasing={{0}: (6, {}), {1}: (7, {})} | custom-call | flops 32768000 | bytes 6291456 | tf_op jit(solution)/shard_map/block_states_own/pallas_call | solution.py:638
  16.8 0.0 collective-permute-done.1.got_ref.other_ref
  16.8 0.2 pair_ends.1
  16.9 1.3 %collective-permute-start.2 = (bf16[16,4096]{1,0:T(8,128)(2,1)S(1)}, bf16[16,4096]{1,0:T(8,128)(2,1)S(1)}, u32[]{:S(2)}, u32[]{:S(2)}) collective-permute-start(bf16[16,4096]{1,0:T(8,128)(2,1)S(1)} %get-tuple-element.65), channel_id=1, source_target_pairs={{0,2},{1,3},{2,0},{3,1},{4,6},{5,7},{6,4},{7,5},{8,10},{9,11},{10,... | collective-permute-start | bytes 393224 | tf_op jit(solution)/shard_map/ppermute | solution.py:26
  18.2 0.0 copy-done.4
  18.2 0.3 sqrt_multiply_fusion.weight_ref
  18.5 1.8 %query_part_0.1.refs_0_ = f32[128,8192]{1,0:T(8,128)S(1)} custom-call(f32[85,8,128]{2,1,0:T(8,128)S(1)} %get-tuple-element.47.masks, bf16[128,8192]{1,0:T(8,128)(2,1)} %query_ref.5, f32[3,3,8192]{2,1,0:T(4,128)S(1)} %copy-done.1), custom_call_target="tpu_custom_call" | custom-call | flops 6553600 | bytes 3145728 | tf_op jit(solution)/shard_map/query_part_0/pallas_call | solution.py:615
  20.4 2.3 %near_part_0.1.refs_0_ = f32[128,8192]{1,0:T(8,128)S(1)} custom-call(f32[85,8,128]{2,1,0:T(8,128)S(1)} %get-tuple-element.47.masks, bf16[128,8192]{1,0:T(8,128)(2,1)S(1)} %get-tuple-element.67.gate_ref, f32[16,8192]{1,0:T(8,128)S(1)} %copy-done, f32[16,8192]{1,0:T(8,128)S(1)} %sqrt_multiply_fusion.weight_ref), custom_call_target="tpu_custom_call" | custom-call | flops 19660800 | bytes 3670016 | tf_op jit(solution)/shard_map/near_part_0/pallas_call | solution.py:692
  22.7 0.0 collective-permute-done.2.got_ref
  22.7 0.2 level_0.1
  23.0 1.3 %collective-permute-start.3 = (bf16[16,4096]{1,0:T(8,128)(2,1)S(1)}, bf16[16,4096]{1,0:T(8,128)(2,1)S(1)}, u32[]{:S(2)}, u32[]{:S(2)}) collective-permute-start(bf16[16,4096]{1,0:T(8,128)(2,1)S(1)} %get-tuple-element.70), channel_id=1, source_target_pairs={{0,4},{1,5},{2,6},{3,7},{4,0},{5,1},{6,2},{7,3},{8,12},{9,13},{10,... | collective-permute-start | bytes 393224 | tf_op jit(solution)/shard_map/ppermute | solution.py:26
  24.3 2.3 %near_part_1.1.near_ref = f32[128,8192]{1,0:T(8,128)S(1)} custom-call(f32[85,8,128]{2,1,0:T(8,128)S(1)} %get-tuple-element.47.masks, bf16[128,8192]{1,0:T(8,128)(2,1)S(1)} %get-tuple-element.67.gate_ref, f32[16,8192]{1,0:T(8,128)S(1)} %copy-done, f32[16,8192]{1,0:T(8,128)S(1)} %sqrt_multiply_fusion.weight_ref, ...), custom_call_target="tpu_custom_call", output_to_operand_aliasing={{}: (4, {})} | custom-call | flops 19660800 | bytes 3670016 | tf_op jit(solution)/shard_map/near_part_1/pallas_call | solution.py:692
  26.6 0.7 %collective-permute-done.3.got_ref = bf16[16,4096]{1,0:T(8,128)(2,1)S(1)} collective-permute-done((bf16[16,4096]{1,0:T(8,128)(2,1)S(1)}, bf16[16,4096]{1,0:T(8,128)(2,1)S(1)}, u32[]{:S(2)}, u32[]{:S(2)}) %collective-permute-start.3) | collective-permute-done | bytes 131104 | tf_op jit(solution)/shard_map/ppermute | solution.py:26
  27.3 0.2 level_1.1
  27.6 3.2 %collective-permute-start.4 = (bf16[16,4096]{1,0:T(8,128)(2,1)S(1)}, bf16[16,4096]{1,0:T(8,128)(2,1)S(1)}, u32[]{:S(2)}, u32[]{:S(2)}) collective-permute-start(bf16[16,4096]{1,0:T(8,128)(2,1)S(1)} %get-tuple-element.75), channel_id=1, source_target_pairs={{0,8},{1,9},{2,10},{3,11},{4,12},{5,13},{6,14},{7,15},{8,16},{9,17... | collective-permute-start | bytes 393224 | tf_op jit(solution)/shard_map/ppermute | solution.py:22
  30.8 0.0 copy-start.2
  30.8 2.0 %query_part_1.1.short_ref = f32[128,8192]{1,0:T(8,128)S(1)} custom-call(f32[85,8,128]{2,1,0:T(8,128)S(1)} %get-tuple-element.47.masks, bf16[128,8192]{1,0:T(8,128)(2,1)} %query_ref.5, f32[3,3,8192]{2,1,0:T(4,128)S(1)} %copy-done.1, f32[128,8192]{1,0:T(8,128)S(1)} %query_part_0.1.refs_0_), custom_call_target="tpu_custom_call", output_to_operand_aliasing={{}: (3, {})} | custom-call | flops 6553600 | bytes 3145728 | tf_op jit(solution)/shard_map/query_part_1/pallas_call | solution.py:615
  32.8 0.5 %collective-permute-done.4.got_ref = bf16[16,4096]{1,0:T(8,128)(2,1)S(1)} collective-permute-done((bf16[16,4096]{1,0:T(8,128)(2,1)S(1)}, bf16[16,4096]{1,0:T(8,128)(2,1)S(1)}, u32[]{:S(2)}, u32[]{:S(2)}) %collective-permute-start.4) | collective-permute-done | bytes 131104 | tf_op jit(solution)/shard_map/ppermute | solution.py:22
  33.3 0.3 pair_enter.1
  33.6 2.8 %collective-permute-start.5 = (f32[16,4096]{1,0:T(8,128)S(1)}, f32[16,4096]{1,0:T(8,128)S(1)}, u32[]{:S(2)}, u32[]{:S(2)}) collective-permute-start(f32[16,4096]{1,0:T(8,128)S(1)} %get-tuple-element.79), channel_id=1, source_target_pairs={{0,1},{1,0},{2,3},{3,2},{4,5},{5,4},{6,7},{7,6},{8,9},{9,8},{10,11... | collective-permute-start | bytes 786440 | tf_op jit(solution)/shard_map/ppermute | solution.py:26
  36.4 0.0 copy-done.2
  36.4 0.0 copy-start.3
  36.4 4.4 %far_part_own.1 = (bf16[128,8192]{1,0:T(8,128)(2,1)}, f32[64,128,128]{2,1,0:T(8,128)S(1)}, f32[128,128]{1,0:T(8,128)S(1)}) custom-call(f32[85,8,128]{2,1,0:T(8,128)S(1)} %get-tuple-element.47.masks, f32[64,136,128]{2,1,0:T(8,128)S(1)} %get-tuple-element.62.state_ref, f32[16,4096]{1,0:T(8,128)S(1)} %get-tuple-element.80.enter_ref, ...), custom_call_target="tpu_custom_call" | custom-call | flops 29491200 | bytes 9437184 | tf_op jit(solution)/shard_map/far_part_own/pallas_call | solution.py:792
  40.9 0.0 collective-permute-done.5.enter_ref
  40.9 0.0 copy-done.3
  40.9 5.3 %far_part_other.1 = (bf16[128,8192]{1,0:T(8,128)(2,1)}, f32[64,128,128]{2,1,0:T(8,128)S(1)}, f32[128,128]{1,0:T(8,128)S(1)}, bf16[128,8192]{1,0:T(8,128)(2,1)}) custom-call(f32[85,8,128]{2,1,0:T(8,128)S(1)} %get-tuple-element.47.masks, ...), custom_call_target="tpu_custom_call", output_to_operand_aliasing={{0}: (11, {}), {1}: (12, {}), {2}: (13, {})} | custom-call | flops 29491200 | bytes 9437184 | tf_op jit(solution)/shard_map/far_part_other/pallas_call | solution.py:792
Async XLA Ops:
  0.6 5.7 %copy-start = (f32[16,8192]{1,0:T(8,128)S(1)}, f32[16,8192]{1,0:T(8,128)}, u32[]{:S(2)}) copy-start(f32[16,8192]{1,0:T(8,128)} %rate_ref.17) | copy-start | bytes 1572868
  0.6 5.7 %copy-start.1 = (f32[3,3,8192]{2,1,0:T(4,128)S(1)}, f32[3,3,8192]{2,1,0:T(4,128)}, u32[]{:S(2)}) copy-start(f32[3,3,8192]{2,1,0:T(4,128)} %taps_ref.9) | copy-start | bytes 884740
  2.7 8.9 %collective-permute-start = (bf16[3,2,8192]{2,1,0:T(2,128)(2,1)S(1)}, bf16[3,2,8192]{2,1,0:T(2,128)(2,1)S(1)}, u32[]{:S(2)}, u32[]{:S(2)}) collective-permute-start(bf16[3,2,8192]{2,1,0:T(2,128)(2,1)S(1)} %get-tuple-element.50), channel_id=1, source_target_pairs={{0,1},{1,2},{2,3},{3,4},{4,5},{5,6},{6,7},{7,8},{8,9},{9,10},{10,1... | collective-permute-start | bytes 294920 | tf_op jit(solution)/shard_map/ppermute | solution.py:22
  12.1 4.6 %collective-permute-start.1 = (f32[16,4096]{1,0:T(8,128)S(1)}, f32[16,4096]{1,0:T(8,128)S(1)}, u32[]{:S(2)}, u32[]{:S(2)}) collective-permute-start(f32[16,4096]{1,0:T(8,128)S(1)} %get-tuple-element.54), channel_id=1, source_target_pairs={{0,1},{1,0},{2,3},{3,2},{4,5},{5,4},{6,7},{7,6},{8,9},{9,8},{10,11... | collective-permute-start | bytes 786440 | tf_op jit(solution)/shard_map/ppermute | solution.py:26
  12.2 6.0 %copy-start.4 = (f32[16,8192]{1,0:T(8,128)S(1)}, f32[16,8192]{1,0:T(8,128)}, u32[]{:S(2)}) copy-start(f32[16,8192]{1,0:T(8,128)} %param.14) | copy-start | bytes 1572868
  16.9 5.8 %collective-permute-start.2 = (bf16[16,4096]{1,0:T(8,128)(2,1)S(1)}, bf16[16,4096]{1,0:T(8,128)(2,1)S(1)}, u32[]{:S(2)}, u32[]{:S(2)}) collective-permute-start(bf16[16,4096]{1,0:T(8,128)(2,1)S(1)} %get-tuple-element.65), channel_id=1, source_target_pairs={{0,2},{1,3},{2,0},{3,1},{4,6},{5,7},{6,4},{7,5},{8,10},{9,11},{10,... | collective-permute-start | bytes 393224 | tf_op jit(solution)/shard_map/ppermute | solution.py:26
  23.0 4.3 %collective-permute-start.3 = (bf16[16,4096]{1,0:T(8,128)(2,1)S(1)}, bf16[16,4096]{1,0:T(8,128)(2,1)S(1)}, u32[]{:S(2)}, u32[]{:S(2)}) collective-permute-start(bf16[16,4096]{1,0:T(8,128)(2,1)S(1)} %get-tuple-element.70), channel_id=1, source_target_pairs={{0,4},{1,5},{2,6},{3,7},{4,0},{5,1},{6,2},{7,3},{8,12},{9,13},{10,... | collective-permute-start | bytes 393224 | tf_op jit(solution)/shard_map/ppermute | solution.py:26
  27.6 5.7 %collective-permute-start.4 = (bf16[16,4096]{1,0:T(8,128)(2,1)S(1)}, bf16[16,4096]{1,0:T(8,128)(2,1)S(1)}, u32[]{:S(2)}, u32[]{:S(2)}) collective-permute-start(bf16[16,4096]{1,0:T(8,128)(2,1)S(1)} %get-tuple-element.75), channel_id=1, source_target_pairs={{0,8},{1,9},{2,10},{3,11},{4,12},{5,13},{6,14},{7,15},{8,16},{9,17... | collective-permute-start | bytes 393224 | tf_op jit(solution)/shard_map/ppermute | solution.py:22
  30.8 5.6 %copy-start.2 = (bf16[128,8192]{1,0:T(8,128)(2,1)S(1)}, bf16[128,8192]{1,0:T(8,128)(2,1)}, u32[]{:S(2)}) copy-start(bf16[128,8192]{1,0:T(8,128)(2,1)} %resid_ref.3) | copy-start | bytes 6291460
  33.6 7.3 %collective-permute-start.5 = (f32[16,4096]{1,0:T(8,128)S(1)}, f32[16,4096]{1,0:T(8,128)S(1)}, u32[]{:S(2)}, u32[]{:S(2)}) collective-permute-start(f32[16,4096]{1,0:T(8,128)S(1)} %get-tuple-element.79), channel_id=1, source_target_pairs={{0,1},{1,0},{2,3},{3,2},{4,5},{5,4},{6,7},{7,6},{8,9},{9,8},{10,11... | collective-permute-start | bytes 786440 | tf_op jit(solution)/shard_map/ppermute | solution.py:26
  36.4 4.4 %copy-start.3 = (f32[8192]{0:T(1024)S(1)}, f32[8192]{0:T(1024)}, u32[]{:S(2)}) copy-start(f32[8192]{0:T(1024)} %param.17) | copy-start | bytes 98308

commit v21 on v20

--- a/solution.py
+++ b/solution.py
@@ -119,12 +119,13 @@
     return state_ref[lax.div(lane, LANES), pl.ds(b * (modes + 1), modes), :]
 
 
-def state_kernel(masks, *refs, span, modes, most, own, chunk):
+def state_kernel(*refs, span, modes, most, own, chunk, levels):
     if own:
-        key_ref, value_ref, rim_ref, taps_ref, rate_ref, _, _, gate_ref, state_ref, end_ref, wide_k, wide_v, tables, held = refs
+        masks, key_ref, value_ref, rim_ref, taps_ref, rate_ref, _, _, gate_ref, state_ref, end_ref, wide_k, wide_v, tables, held = refs
     else:
-        (ahead_ref, key_in, value_in, taps_ref, rate_ref, gate_ref, state_ref, end_ref, key_own, value_own, heads,
-         key_ref, value_ref, wide_k, wide_v, tables, held, sems) = refs
+        (base_ref, len_ref, ahead_ref, key_in, value_in, taps_ref, rate_ref,
+         gate_ref, state_ref, end_ref, masks, key_own, value_own, heads,
+         key_ref, value_ref, rows_of, wide_k, wide_v, tables, held, sems) = refs
     half = key_ref.shape[1]
     first = half_start(2 * half, own)
     if not own:
@@ -144,6 +145,7 @@
         for c in range(1, half // chunk):
             for copy in fetch(c):
                 copy.start()
+        write_masks(base_ref, len_ref, masks, rows_of, span, levels)
     at = Masks(span)
 
     def group(lanes, keys=key_ref, values=value_ref):
@@ -251,7 +253,7 @@
 
 
 def tail_kernel(
-    base_ref, len_ref, query_ref, key_ref, value_ref, tail_ref, masks, ahead_ref, bufs, rows_of, sems, *, span, levels
+    query_ref, key_ref, value_ref, tail_ref, ahead_ref, bufs, sems
 ):
     rows, count = query_ref.shape[0], bufs.shape[1]
     copies = [
@@ -265,7 +267,6 @@
     ]
     for copy in copies + aheads:
         copy.start()
-    write_masks(base_ref, len_ref, masks, rows_of, span, levels)
     for i, copy in enumerate(copies):
         copy.wait()
         tail_ref[i] = bufs[i].astype(f32)[count - 2 :].astype(bf16)
@@ -590,19 +591,15 @@
     levels = max(1, (blocks // 4).bit_length() - 2)
     mask_shape = (Masks(span).count(levels),) + tile_shape
     small = min(chans // 2, 512)
-    tails, masks, ahead = pl.pallas_call(
-        functools.partial(tail_kernel, span=span, levels=levels),
-        in_specs=[smem, smem, hbm, hbm, hbm],
-        out_specs=[vmem, vmem, vmem],
-        out_shape=[
-            pltpu.VMEM((3, 2, chans), bf16), pltpu.VMEM(mask_shape, f32), pltpu.VMEM((2, tok_rows, small), bf16)
-        ],
-        scratch_shapes=[
-            pltpu.VMEM((3, 16, chans), bf16), pltpu.VMEM(tile_shape, f32), pltpu.SemaphoreType.DMA((5,))
-        ],
+    tails, ahead = pl.pallas_call(
+        tail_kernel,
+        in_specs=[hbm, hbm, hbm],
+        out_specs=[vmem, vmem],
+        out_shape=[pltpu.VMEM((3, 2, chans), bf16), pltpu.VMEM((2, tok_rows, small), bf16)],
+        scratch_shapes=[pltpu.VMEM((3, 16, chans), bf16), pltpu.SemaphoreType.DMA((5,))],
         compiler_params=params,
         name="tails",
-    )(base, lengths, far_off(query_in), far_off(key_in), far_off(value_in))
+    )(far_off(query_in), far_off(key_in), far_off(value_in))
     rim_rows = from_behind(tails, "ctx", 1)
     def query_piece(part, masks, before):
         count = chans // 2
@@ -636,8 +633,10 @@
 
     def states_of(own, operands, in_specs, out_shape, scratch, aliases):
         return pl.pallas_call(
-            functools.partial(state_kernel, span=span, modes=modes, most=A_TILES, own=own, chunk=small),
-            in_specs=[vmem] + in_specs,
+            functools.partial(
+                state_kernel, span=span, modes=modes, most=A_TILES, own=own, chunk=small, levels=levels
+            ),
+            in_specs=in_specs,
             out_specs=[vmem] * (3 + len(out_shape)),
             out_shape=[gate_shape, state_shape, kept] + out_shape,
             scratch_shapes=scratch[:-1]
@@ -652,16 +651,17 @@
             compiler_params=params,
             cost_estimate=cost(500, 6 * tok_rows * chans),
             name="block_states_own" if own else "block_states_give",
-        )(near_by(masks), *operands)
-
-    gates, states, give, key_own, value_own, heads = states_of(
+        )(*operands)
+
+    gates, states, give, masks, key_own, value_own, heads = states_of(
         False,
-        [near_by(ahead), far_off(key_in), far_off(value_in), taps, rates],
-        [vmem, hbm, hbm, vmem, vmem],
-        [key_half, key_half, pltpu.VMEM((2, 16, chans // 2), bf16)],
+        [base, lengths, near_by(ahead), far_off(key_in), far_off(value_in), taps, rates],
+        [smem, smem, vmem, hbm, hbm, vmem, vmem],
+        [pltpu.VMEM(mask_shape, f32), key_half, key_half, pltpu.VMEM((2, 16, chans // 2), bf16)],
         [
             pltpu.VMEM((tok_rows, chans // 2), bf16),
             pltpu.VMEM((tok_rows, chans // 2), bf16),
+            pltpu.VMEM(tile_shape, f32),
             pltpu.SemaphoreType.DMA((2, chans // 2 // small + 1)),
         ],
         {},
@@ -678,8 +678,8 @@
     got = swap(give, "ctx")
     gates, states, own = states_of(
         True,
-        [near_by(key_own), near_by(value_own), rims, taps, rates, near_by(gates), near_by(states)],
-        [vmem] * 7,
+        [near_by(masks), near_by(key_own), near_by(value_own), rims, taps, rates, near_by(gates), near_by(states)],
+        [vmem] * 8,
         [],
         [],
         {6: 0, 7: 1},

time: 46.4 us -> 46.3 us (level)
    pallas_call x1, Pallas kernels: 2.02 us -> 1.31 us  [shards(): pl.pallas_call(tail_kernel, in_specs=[hbm, hbm, hbm], out_specs=[vmem, vm...]
    pallas_call x2, Pallas kernels: 9.72 us -> 10.4 us  [states_of(): pl.pallas_call(functools.partial(state_kernel, span=span, modes=modes, mo...]
  transfers between devices with their start and end apart: 6 -> 6, of which waited for: 2 -> 2; matrix products, arithmetic and copies ran while one was open for 1% -> 1% of each run, Pallas kernels for 49% -> 51%
where the time goes in v21:
time: 46.3 us; the launch traced here: 46.1 us
  Pallas kernels  31.3 us (68%)
  starting transfers between devices  12.4 us (27%)
  waiting for transfers between devices  1.2 us (3%)
  between operations  0.84 us (2%)
    pallas_call x2, Pallas kernels, states_of(): pl.pallas_call(functools.partial(state_kernel, span=span, modes=modes, mo...  10.4 us
    pallas_call x2, Pallas kernels, finish(): pl.pallas_call(functools.partial(final_kernel, span=span, modes=modes, ch...  9.7 us
    ppermute x2, starting transfers between devices, from_behind(): return lax.ppermute(shard, axis, [(i, i + by) for i in range(count - by)])  6.88 us
    ppermute x4, starting transfers between devices, swap(): lax.ppermute(shard, axis, [(i, i ^ bit) for i in range(lax.axis_size(axis...  5.5 us
    pallas_call x2, Pallas kernels, near_piece(): pl.pallas_call(functools.partial(near_kernel, span=span, modes=modes, mos...  4.67 us
    pallas_call x2, Pallas kernels, query_piece(): pl.pallas_call(functools.partial(query_kernel, span=span, most=Q_TILES, c...  3.83 us
    pallas_call x1, Pallas kernels, shards(): pl.pallas_call(tail_kernel, in_specs=[hbm, hbm, hbm], out_specs=[vmem, vm...  1.31 us
    pallas_call x4, Pallas kernels, pair_call(): pl.pallas_call(functools.partial(kernel, **static), in_specs=[vmem] * (le...  0.93 us
  transfers between devices with their start and end apart: 6, of which 2 were waited for; matrix products, arithmetic and copies ran while one was open for 1% of the time, Pallas kernels for 51%

profile of v21, /device:TPU:9, one launch (start us, length us, event | category | flops | bytes accessed | tf_op | source)
XLA Modules:
  0.0 46.1 jit_solution(11130965775101545388)
XLA Ops:
  0.6 0.0 copy-start
  0.6 0.0 copy-start.1
  0.6 1.3 %tails.1 = (bf16[3,2,8192]{2,1,0:T(2,128)(2,1)S(1)}, bf16[2,128,512]{2,1,0:T(8,128)(2,1)S(1)}) custom-call(bf16[128,8192]{1,0:T(8,128)(2,1)} %query_ref.5, bf16[128,8192]{1,0:T(8,128)(2,1)} %refs_3_.1, bf16[128,8192]{1,0:T(8,128)(2,1)} %refs_4_.2), custom_call_target="tpu_custom_call" | custom-call | tf_op jit(solution)/shard_map/tails/pallas_call | solution.py:594
  2.0 3.7 %collective-permute-start = (bf16[3,2,8192]{2,1,0:T(2,128)(2,1)S(1)}, bf16[3,2,8192]{2,1,0:T(2,128)(2,1)S(1)}, u32[]{:S(2)}, u32[]{:S(2)}) collective-permute-start(bf16[3,2,8192]{2,1,0:T(2,128)(2,1)S(1)} %get-tuple-element.50), channel_id=1, source_target_pairs={{0,1},{1,2},{2,3},{3,4},{4,5},{5,6},{6,7},{7,8},{8,9},{9,10},{10,1... | collective-permute-start | bytes 294920 | tf_op jit(solution)/shard_map/ppermute | solution.py:22
  5.7 0.0 copy-done
  5.7 0.0 copy-done.1
  5.7 5.8 %block_states_give.1 = (bf16[128,8192]{1,0:T(8,128)(2,1)S(1)}, f32[64,136,128]{2,1,0:T(8,128)S(1)}, f32[16,4096]{1,0:T(8,128)S(1)}, f32[85,8,128]{2,1,0:T(8,128)...) custom-call(s32[1]{0:T(128)} %bitcast.refs_0_, s32[16]{0:T(128)} %refs_1_.1, ...), custom_call_target="tpu_custom_call" | custom-call | flops 32768000 | bytes 6291456 | tf_op jit(solution)/shard_map/block_states_give/pallas_call | solution.py:635
  11.5 0.0 collective-permute-done.rim_ref.refs_3_
  11.5 0.5 %first_rows.1 = (bf16[128,8192]{1,0:T(8,128)(2,1)S(1)}, f32[64,136,128]{2,1,0:T(8,128)S(1)}, f32[16,4096]{1,0:T(8,128)S(1)}) custom-call(f32[85,8,128]{2,1,0:T(8,128)S(1)} %get-tuple-element.48.masks.refs_0_, bf16[2,16,4096]{2,1,0:T(8,128)(2,1)S(1)} %get-tuple-element.49.heads, ...), custom_call_target="tpu_custom_call", output_to_operand_aliasing={{0}: (5, {}), {1}: (6, {}), {2}: (7, {})} | custom-call | tf_op jit(solution)/shard_map/first_rows/pallas_call | solution.py:669
  12.1 0.1 collective-permute-start.1
  12.1 0.0 copy-start.4
  12.1 4.5 %block_states_own.1 = (bf16[128,8192]{1,0:T(8,128)(2,1)S(1)}, f32[64,136,128]{2,1,0:T(8,128)S(1)}, f32[16,4096]{1,0:T(8,128)S(1)}) custom-call(f32[85,8,128]{2,1,0:T(8,128)S(1)} %get-tuple-element.48.masks.refs_0_, bf16[128,4096]{1,0:T(8,128)(2,1)S(1)} %get-tuple-element.55.refs_1_, ...), custom_call_target="tpu_custom_call", output_to_operand_aliasing={{0}: (6, {}), {1}: (7, {})} | custom-call | flops 32768000 | bytes 6291456 | tf_op jit(solution)/shard_map/block_states_own/pallas_call | solution.py:635
  16.7 0.0 collective-permute-done.1.got_ref.other_ref
  16.7 0.2 pair_ends.1
  16.9 1.3 %collective-permute-start.2 = (bf16[16,4096]{1,0:T(8,128)(2,1)S(1)}, bf16[16,4096]{1,0:T(8,128)(2,1)S(1)}, u32[]{:S(2)}, u32[]{:S(2)}) collective-permute-start(bf16[16,4096]{1,0:T(8,128)(2,1)S(1)} %get-tuple-element.65), channel_id=1, source_target_pairs={{0,2},{1,3},{2,0},{3,1},{4,6},{5,7},{6,4},{7,5},{8,10},{9,11},{10,... | collective-permute-start | bytes 393224 | tf_op jit(solution)/shard_map/ppermute | solution.py:26
  18.1 0.0 copy-done.4
  18.2 0.3 sqrt_multiply_fusion.weight_ref
  18.5 1.8 %query_part_0.1.refs_0_ = f32[128,8192]{1,0:T(8,128)S(1)} custom-call(f32[85,8,128]{2,1,0:T(8,128)S(1)} %get-tuple-element.48.masks.refs_0_, bf16[128,8192]{1,0:T(8,128)(2,1)} %query_ref.5, f32[3,3,8192]{2,1,0:T(4,128)S(1)} %copy-done.1), custom_call_target="tpu_custom_call" | custom-call | flops 6553600 | bytes 3145728 | tf_op jit(solution)/shard_map/query_part_0/pallas_call | solution.py:612
  20.3 2.3 %near_part_0.1.refs_0_ = f32[128,8192]{1,0:T(8,128)S(1)} custom-call(f32[85,8,128]{2,1,0:T(8,128)S(1)} %get-tuple-element.48.masks.refs_0_, bf16[128,8192]{1,0:T(8,128)(2,1)S(1)} %get-tuple-element.67.gate_ref, f32[16,8192]{1,0:T(8,128)S(1)} %copy-done, f32[16,8192]{1,0:T(8,128)S(1)} %sqrt_multiply_fusion.weight_ref), custom_call_target="tpu_custom_call" | custom-call | flops 19660800 | bytes 3670016 | tf_op jit(solution)/shard_map/near_part_0/pallas_call | solution.py:692
  22.7 0.0 collective-permute-done.2.got_ref
  22.7 0.2 level_0.1
  22.9 1.3 %collective-permute-start.3 = (bf16[16,4096]{1,0:T(8,128)(2,1)S(1)}, bf16[16,4096]{1,0:T(8,128)(2,1)S(1)}, u32[]{:S(2)}, u32[]{:S(2)}) collective-permute-start(bf16[16,4096]{1,0:T(8,128)(2,1)S(1)} %get-tuple-element.70), channel_id=1, source_target_pairs={{0,4},{1,5},{2,6},{3,7},{4,0},{5,1},{6,2},{7,3},{8,12},{9,13},{10,... | collective-permute-start | bytes 393224 | tf_op jit(solution)/shard_map/ppermute | solution.py:26
  24.2 2.3 %near_part_1.1.near_ref = f32[128,8192]{1,0:T(8,128)S(1)} custom-call(f32[85,8,128]{2,1,0:T(8,128)S(1)} %get-tuple-element.48.masks.refs_0_, bf16[128,8192]{1,0:T(8,128)(2,1)S(1)} %get-tuple-element.67.gate_ref, f32[16,8192]{1,0:T(8,128)S(1)} %copy-done, f32[16,8192]{1,0:T(8,128)S(1)} %sqrt_multiply_fusion.weight_ref, ...), custom_call_target="tpu_custom_call", output_to_operand_aliasing={{}: (4, {})} | custom-call | flops 19660800 | bytes 3670016 | tf_op jit(solution)/shard_map/near_part_1/pallas_call | solution.py:692
  26.6 0.7 %collective-permute-done.3.got_ref = bf16[16,4096]{1,0:T(8,128)(2,1)S(1)} collective-permute-done((bf16[16,4096]{1,0:T(8,128)(2,1)S(1)}, bf16[16,4096]{1,0:T(8,128)(2,1)S(1)}, u32[]{:S(2)}, u32[]{:S(2)}) %collective-permute-start.3) | collective-permute-done | bytes 131104 | tf_op jit(solution)/shard_map/ppermute | solution.py:26
  27.3 0.2 level_1.1
  27.5 3.2 %collective-permute-start.4 = (bf16[16,4096]{1,0:T(8,128)(2,1)S(1)}, bf16[16,4096]{1,0:T(8,128)(2,1)S(1)}, u32[]{:S(2)}, u32[]{:S(2)}) collective-permute-start(bf16[16,4096]{1,0:T(8,128)(2,1)S(1)} %get-tuple-element.75), channel_id=1, source_target_pairs={{0,8},{1,9},{2,10},{3,11},{4,12},{5,13},{6,14},{7,15},{8,16},{9,17... | collective-permute-start | bytes 393224 | tf_op jit(solution)/shard_map/ppermute | solution.py:22
  30.7 0.0 copy-start.2
  30.7 2.0 %query_part_1.1.short_ref = f32[128,8192]{1,0:T(8,128)S(1)} custom-call(f32[85,8,128]{2,1,0:T(8,128)S(1)} %get-tuple-element.48.masks.refs_0_, bf16[128,8192]{1,0:T(8,128)(2,1)} %query_ref.5, f32[3,3,8192]{2,1,0:T(4,128)S(1)} %copy-done.1, f32[128,8192]{1,0:T(8,128)S(1)} %query_part_0.1.refs_0_), custom_call_target="tpu_custom_call", output_to_operand_aliasing={{}: (3, {})} | custom-call | flops 6553600 | bytes 3145728 | tf_op jit(solution)/shard_map/query_part_1/pallas_call | solution.py:612
  32.7 0.5 %collective-permute-done.4.got_ref = bf16[16,4096]{1,0:T(8,128)(2,1)S(1)} collective-permute-done((bf16[16,4096]{1,0:T(8,128)(2,1)S(1)}, bf16[16,4096]{1,0:T(8,128)(2,1)S(1)}, u32[]{:S(2)}, u32[]{:S(2)}) %collective-permute-start.4) | collective-permute-done | bytes 131104 | tf_op jit(solution)/shard_map/ppermute | solution.py:22
  33.2 0.3 pair_enter.1
  33.5 2.8 %collective-permute-start.5 = (f32[16,4096]{1,0:T(8,128)S(1)}, f32[16,4096]{1,0:T(8,128)S(1)}, u32[]{:S(2)}, u32[]{:S(2)}) collective-permute-start(f32[16,4096]{1,0:T(8,128)S(1)} %get-tuple-element.79), channel_id=1, source_target_pairs={{0,1},{1,0},{2,3},{3,2},{4,5},{5,4},{6,7},{7,6},{8,9},{9,8},{10,11... | collective-permute-start | bytes 786440 | tf_op jit(solution)/shard_map/ppermute | solution.py:26
  36.4 0.0 copy-done.2
  36.4 0.0 copy-start.3
  36.4 4.4 %far_part_own.1 = (bf16[128,8192]{1,0:T(8,128)(2,1)}, f32[64,128,128]{2,1,0:T(8,128)S(1)}, f32[128,128]{1,0:T(8,128)S(1)}) custom-call(f32[85,8,128]{2,1,0:T(8,128)S(1)} %get-tuple-element.48.masks.refs_0_, f32[64,136,128]{2,1,0:T(8,128)S(1)} %get-tuple-element.62.state_ref, f32[16,4096]{1,0:T(8,128)S(1)} %get-tuple-element.80.enter_ref, ...), custom_call_target="tpu_custom_call" | custom-call | flops 29491200 | bytes 9437184 | tf_op jit(solution)/shard_map/far_part_own/pallas_call | solution.py:792
  40.8 0.0 collective-permute-done.5.enter_ref
  40.8 0.0 copy-done.3
  40.8 5.3 %far_part_other.1 = (bf16[128,8192]{1,0:T(8,128)(2,1)}, f32[64,128,128]{2,1,0:T(8,128)S(1)}, f32[128,128]{1,0:T(8,128)S(1)}, bf16[128,8192]{1,0:T(8,128)(2,1)}) custom-call(f32[85,8,128]{2,1,0:T(8,128)S(1)} %get-tuple-element.48.masks.refs_0_, ...), custom_call_target="tpu_custom_call", output_to_operand_aliasing={{0}: (11, {}), {1}: (12, {}), {2}: (13, {})} | custom-call | flops 29491200 | bytes 9437184 | tf_op jit(solution)/shard_map/far_part_other/pallas_call | solution.py:792
Async XLA Ops:
  0.6 5.0 %copy-start = (f32[16,8192]{1,0:T(8,128)S(1)}, f32[16,8192]{1,0:T(8,128)}, u32[]{:S(2)}) copy-start(f32[16,8192]{1,0:T(8,128)} %rate_ref.17) | copy-start | bytes 1572868
  0.6 5.0 %copy-start.1 = (f32[3,3,8192]{2,1,0:T(4,128)S(1)}, f32[3,3,8192]{2,1,0:T(4,128)}, u32[]{:S(2)}) copy-start(f32[3,3,8192]{2,1,0:T(4,128)} %taps_ref.9) | copy-start | bytes 884740
  2.0 9.6 %collective-permute-start = (bf16[3,2,8192]{2,1,0:T(2,128)(2,1)S(1)}, bf16[3,2,8192]{2,1,0:T(2,128)(2,1)S(1)}, u32[]{:S(2)}, u32[]{:S(2)}) collective-permute-start(bf16[3,2,8192]{2,1,0:T(2,128)(2,1)S(1)} %get-tuple-element.50), channel_id=1, source_target_pairs={{0,1},{1,2},{2,3},{3,4},{4,5},{5,6},{6,7},{7,8},{8,9},{9,10},{10,1... | collective-permute-start | bytes 294920 | tf_op jit(solution)/shard_map/ppermute | solution.py:22
  12.1 4.6 %collective-permute-start.1 = (f32[16,4096]{1,0:T(8,128)S(1)}, f32[16,4096]{1,0:T(8,128)S(1)}, u32[]{:S(2)}, u32[]{:S(2)}) collective-permute-start(f32[16,4096]{1,0:T(8,128)S(1)} %get-tuple-element.54), channel_id=1, source_target_pairs={{0,1},{1,0},{2,3},{3,2},{4,5},{5,4},{6,7},{7,6},{8,9},{9,8},{10,11... | collective-permute-start | bytes 786440 | tf_op jit(solution)/shard_map/ppermute | solution.py:26
  12.1 6.0 %copy-start.4 = (f32[16,8192]{1,0:T(8,128)S(1)}, f32[16,8192]{1,0:T(8,128)}, u32[]{:S(2)}) copy-start(f32[16,8192]{1,0:T(8,128)} %param.14) | copy-start | bytes 1572868
  16.9 5.8 %collective-permute-start.2 = (bf16[16,4096]{1,0:T(8,128)(2,1)S(1)}, bf16[16,4096]{1,0:T(8,128)(2,1)S(1)}, u32[]{:S(2)}, u32[]{:S(2)}) collective-permute-start(bf16[16,4096]{1,0:T(8,128)(2,1)S(1)} %get-tuple-element.65), channel_id=1, source_target_pairs={{0,2},{1,3},{2,0},{3,1},{4,6},{5,7},{6,4},{7,5},{8,10},{9,11},{10,... | collective-permute-start | bytes 393224 | tf_op jit(solution)/shard_map/ppermute | solution.py:26
  22.9 4.3 %collective-permute-start.3 = (bf16[16,4096]{1,0:T(8,128)(2,1)S(1)}, bf16[16,4096]{1,0:T(8,128)(2,1)S(1)}, u32[]{:S(2)}, u32[]{:S(2)}) collective-permute-start(bf16[16,4096]{1,0:T(8,128)(2,1)S(1)} %get-tuple-element.70), channel_id=1, source_target_pairs={{0,4},{1,5},{2,6},{3,7},{4,0},{5,1},{6,2},{7,3},{8,12},{9,13},{10,... | collective-permute-start | bytes 393224 | tf_op jit(solution)/shard_map/ppermute | solution.py:26
  27.5 5.7 %collective-permute-start.4 = (bf16[16,4096]{1,0:T(8,128)(2,1)S(1)}, bf16[16,4096]{1,0:T(8,128)(2,1)S(1)}, u32[]{:S(2)}, u32[]{:S(2)}) collective-permute-start(bf16[16,4096]{1,0:T(8,128)(2,1)S(1)} %get-tuple-element.75), channel_id=1, source_target_pairs={{0,8},{1,9},{2,10},{3,11},{4,12},{5,13},{6,14},{7,15},{8,16},{9,17... | collective-permute-start | bytes 393224 | tf_op jit(solution)/shard_map/ppermute | solution.py:22
  30.7 5.6 %copy-start.2 = (bf16[128,8192]{1,0:T(8,128)(2,1)S(1)}, bf16[128,8192]{1,0:T(8,128)(2,1)}, u32[]{:S(2)}) copy-start(bf16[128,8192]{1,0:T(8,128)(2,1)} %resid_ref.3) | copy-start | bytes 6291460
  33.5 7.3 %collective-permute-start.5 = (f32[16,4096]{1,0:T(8,128)S(1)}, f32[16,4096]{1,0:T(8,128)S(1)}, u32[]{:S(2)}, u32[]{:S(2)}) collective-permute-start(f32[16,4096]{1,0:T(8,128)S(1)} %get-tuple-element.79), channel_id=1, source_target_pairs={{0,1},{1,0},{2,3},{3,2},{4,5},{5,4},{6,7},{7,6},{8,9},{9,8},{10,11... | collective-permute-start | bytes 786440 | tf_op jit(solution)/shard_map/ppermute | solution.py:26
  36.4 4.4 %copy-start.3 = (f32[8192]{0:T(1024)S(1)}, f32[8192]{0:T(1024)}, u32[]{:S(2)}) copy-start(f32[8192]{0:T(1024)} %param.17) | copy-start | bytes 98308

commit v22 on v21

--- a/solution.py
+++ b/solution.py
@@ -11,7 +11,7 @@
 SUBS = 8
 LANES = 128
 MIB = 1024 * 1024
-A_TILES, N_TILES, Q_TILES, F_TILES = 2, 2, 4, 4
+A_TILES, N_TILES, Q_TILES, F_TILES = 1, 1, 2, 2
 NEAR_PARTS = 2
 f32 = jnp.float32
 bf16 = jnp.bfloat16

time: 46.3 us -> 48.2 us (1.041)
  Pallas kernels: 31.3 us -> 33.8 us
  waiting for transfers between devices: 1.2 us -> 0.68 us
    pallas_call x2, Pallas kernels: 4.67 us -> 5.54 us  [near_piece(): pl.pallas_call(functools.partial(near_kernel, span=span, modes=modes, mos...]
    pallas_call x2, Pallas kernels: 10.4 us -> 11.2 us  [states_of(): pl.pallas_call(functools.partial(state_kernel, span=span, modes=modes, mo...]
    pallas_call x2, Pallas kernels: 9.7 us -> 10.3 us  [finish(): pl.pallas_call(functools.partial(final_kernel, span=span, modes=modes, ch...]
  transfers between devices with their start and end apart: 6 -> 6, of which waited for: 2 -> 2; matrix products, arithmetic and copies ran while one was open for 1% -> 1% of each run, Pallas kernels for 51% -> 53%
where the time goes in v22:
time: 48.2 us; the launch traced here: 48 us
  Pallas kernels  33.8 us (70%)
  starting transfers between devices  12.4 us (26%)
  between operations  0.84 us (2%)
  waiting for transfers between devices  0.68 us (1%)
    pallas_call x2, Pallas kernels, states_of(): pl.pallas_call(functools.partial(state_kernel, span=span, modes=modes, mo...  11.2 us
    pallas_call x2, Pallas kernels, finish(): pl.pallas_call(functools.partial(final_kernel, span=span, modes=modes, ch...  10.3 us
    ppermute x2, starting transfers between devices, from_behind(): return lax.ppermute(shard, axis, [(i, i + by) for i in range(count - by)])  6.88 us
    pallas_call x2, Pallas kernels, near_piece(): pl.pallas_call(functools.partial(near_kernel, span=span, modes=modes, mos...  5.54 us
    ppermute x4, starting transfers between devices, swap(): lax.ppermute(shard, axis, [(i, i ^ bit) for i in range(lax.axis_size(axis...  5.51 us
    pallas_call x2, Pallas kernels, query_piece(): pl.pallas_call(functools.partial(query_kernel, span=span, most=Q_TILES, c...  4.01 us
    pallas_call x1, Pallas kernels, shards(): pl.pallas_call(tail_kernel, in_specs=[hbm, hbm, hbm], out_specs=[vmem, vm...  1.31 us
  transfers between devices with their start and end apart: 6, of which 2 were waited for; matrix products, arithmetic and copies ran while one was open for 1% of the time, Pallas kernels for 53%

profile of v22, /device:TPU:9, one launch (start us, length us, event | category | flops | bytes accessed | tf_op | source)
XLA Modules:
  0.0 48.0 jit_solution(6803693665961989828)
XLA Ops:
  0.6 0.0 copy-start
  0.6 0.0 copy-start.1
  0.6 1.3 %tails.1 = (bf16[3,2,8192]{2,1,0:T(2,128)(2,1)S(1)}, bf16[2,128,512]{2,1,0:T(8,128)(2,1)S(1)}) custom-call(bf16[128,8192]{1,0:T(8,128)(2,1)} %query_ref.5, bf16[128,8192]{1,0:T(8,128)(2,1)} %refs_3_.1, bf16[128,8192]{1,0:T(8,128)(2,1)} %refs_4_.2), custom_call_target="tpu_custom_call" | custom-call | tf_op jit(solution)/shard_map/tails/pallas_call | solution.py:594
  2.0 3.7 %collective-permute-start = (bf16[3,2,8192]{2,1,0:T(2,128)(2,1)S(1)}, bf16[3,2,8192]{2,1,0:T(2,128)(2,1)S(1)}, u32[]{:S(2)}, u32[]{:S(2)}) collective-permute-start(bf16[3,2,8192]{2,1,0:T(2,128)(2,1)S(1)} %get-tuple-element.50), channel_id=1, source_target_pairs={{0,1},{1,2},{2,3},{3,4},{4,5},{5,6},{6,7},{7,8},{8,9},{9,10},{10,1... | collective-permute-start | bytes 294920 | tf_op jit(solution)/shard_map/ppermute | solution.py:22
  5.7 0.0 copy-done
  5.7 0.0 copy-done.1
  5.7 6.2 %block_states_give.1 = (bf16[128,8192]{1,0:T(8,128)(2,1)S(1)}, f32[64,136,128]{2,1,0:T(8,128)S(1)}, f32[16,4096]{1,0:T(8,128)S(1)}, f32[85,8,128]{2,1,0:T(8,128)...) custom-call(s32[1]{0:T(128)} %bitcast.refs_0_, s32[16]{0:T(128)} %refs_1_.1, ...), custom_call_target="tpu_custom_call" | custom-call | flops 32768000 | bytes 6291456 | tf_op jit(solution)/shard_map/block_states_give/pallas_call | solution.py:635
  11.9 0.0 collective-permute-done.rim_ref.refs_3_
  11.9 0.5 %first_rows.1 = (bf16[128,8192]{1,0:T(8,128)(2,1)S(1)}, f32[64,136,128]{2,1,0:T(8,128)S(1)}, f32[16,4096]{1,0:T(8,128)S(1)}) custom-call(f32[85,8,128]{2,1,0:T(8,128)S(1)} %get-tuple-element.48.masks.refs_0_, bf16[2,16,4096]{2,1,0:T(8,128)(2,1)S(1)} %get-tuple-element.49.heads, ...), custom_call_target="tpu_custom_call", output_to_operand_aliasing={{0}: (5, {}), {1}: (6, {}), {2}: (7, {})} | custom-call | tf_op jit(solution)/shard_map/first_rows/pallas_call | solution.py:669
  12.4 0.1 collective-permute-start.1
  12.5 0.0 copy-start.4
  12.5 5.0 %block_states_own.1 = (bf16[128,8192]{1,0:T(8,128)(2,1)S(1)}, f32[64,136,128]{2,1,0:T(8,128)S(1)}, f32[16,4096]{1,0:T(8,128)S(1)}) custom-call(f32[85,8,128]{2,1,0:T(8,128)S(1)} %get-tuple-element.48.masks.refs_0_, bf16[128,4096]{1,0:T(8,128)(2,1)S(1)} %get-tuple-element.55.refs_1_, ...), custom_call_target="tpu_custom_call", output_to_operand_aliasing={{0}: (6, {}), {1}: (7, {})} | custom-call | flops 32768000 | bytes 6291456 | tf_op jit(solution)/shard_map/block_states_own/pallas_call | solution.py:635
  17.5 0.0 collective-permute-done.1.got_ref.other_ref
  17.5 0.2 pair_ends.1
  17.7 1.3 %collective-permute-start.2 = (bf16[16,4096]{1,0:T(8,128)(2,1)S(1)}, bf16[16,4096]{1,0:T(8,128)(2,1)S(1)}, u32[]{:S(2)}, u32[]{:S(2)}) collective-permute-start(bf16[16,4096]{1,0:T(8,128)(2,1)S(1)} %get-tuple-element.65), channel_id=1, source_target_pairs={{0,2},{1,3},{2,0},{3,1},{4,6},{5,7},{6,4},{7,5},{8,10},{9,11},{10,... | collective-permute-start | bytes 393224 | tf_op jit(solution)/shard_map/ppermute | solution.py:26
  19.0 0.0 copy-done.4
  19.0 0.3 sqrt_multiply_fusion.weight_ref
  19.3 1.9 %query_part_0.1.refs_0_ = f32[128,8192]{1,0:T(8,128)S(1)} custom-call(f32[85,8,128]{2,1,0:T(8,128)S(1)} %get-tuple-element.48.masks.refs_0_, bf16[128,8192]{1,0:T(8,128)(2,1)} %query_ref.5, f32[3,3,8192]{2,1,0:T(4,128)S(1)} %copy-done.1), custom_call_target="tpu_custom_call" | custom-call | flops 6553600 | bytes 3145728 | tf_op jit(solution)/shard_map/query_part_0/pallas_call | solution.py:612
  21.2 2.8 %near_part_0.1.refs_0_ = f32[128,8192]{1,0:T(8,128)S(1)} custom-call(f32[85,8,128]{2,1,0:T(8,128)S(1)} %get-tuple-element.48.masks.refs_0_, bf16[128,8192]{1,0:T(8,128)(2,1)S(1)} %get-tuple-element.67.gate_ref, f32[16,8192]{1,0:T(8,128)S(1)} %copy-done, f32[16,8192]{1,0:T(8,128)S(1)} %sqrt_multiply_fusion.weight_ref), custom_call_target="tpu_custom_call" | custom-call | flops 19660800 | bytes 3670016 | tf_op jit(solution)/shard_map/near_part_0/pallas_call | solution.py:692
  24.0 0.0 collective-permute-done.2.got_ref
  24.0 0.2 level_0.1
  24.3 1.3 %collective-permute-start.3 = (bf16[16,4096]{1,0:T(8,128)(2,1)S(1)}, bf16[16,4096]{1,0:T(8,128)(2,1)S(1)}, u32[]{:S(2)}, u32[]{:S(2)}) collective-permute-start(bf16[16,4096]{1,0:T(8,128)(2,1)S(1)} %get-tuple-element.70), channel_id=1, source_target_pairs={{0,4},{1,5},{2,6},{3,7},{4,0},{5,1},{6,2},{7,3},{8,12},{9,13},{10,... | collective-permute-start | bytes 393224 | tf_op jit(solution)/shard_map/ppermute | solution.py:26
  25.6 2.8 %near_part_1.1.near_ref = f32[128,8192]{1,0:T(8,128)S(1)} custom-call(f32[85,8,128]{2,1,0:T(8,128)S(1)} %get-tuple-element.48.masks.refs_0_, bf16[128,8192]{1,0:T(8,128)(2,1)S(1)} %get-tuple-element.67.gate_ref, f32[16,8192]{1,0:T(8,128)S(1)} %copy-done, f32[16,8192]{1,0:T(8,128)S(1)} %sqrt_multiply_fusion.weight_ref, ...), custom_call_target="tpu_custom_call", output_to_operand_aliasing={{}: (4, {})} | custom-call | flops 19660800 | bytes 3670016 | tf_op jit(solution)/shard_map/near_part_1/pallas_call | solution.py:692
  28.4 0.3 collective-permute-done.3.got_ref
  28.6 0.2 level_1.1
  28.9 3.2 %collective-permute-start.4 = (bf16[16,4096]{1,0:T(8,128)(2,1)S(1)}, bf16[16,4096]{1,0:T(8,128)(2,1)S(1)}, u32[]{:S(2)}, u32[]{:S(2)}) collective-permute-start(bf16[16,4096]{1,0:T(8,128)(2,1)S(1)} %get-tuple-element.75), channel_id=1, source_target_pairs={{0,8},{1,9},{2,10},{3,11},{4,12},{5,13},{6,14},{7,15},{8,16},{9,17... | collective-permute-start | bytes 393224 | tf_op jit(solution)/shard_map/ppermute | solution.py:22
  32.1 0.0 copy-start.2
  32.1 2.1 %query_part_1.1.short_ref = f32[128,8192]{1,0:T(8,128)S(1)} custom-call(f32[85,8,128]{2,1,0:T(8,128)S(1)} %get-tuple-element.48.masks.refs_0_, bf16[128,8192]{1,0:T(8,128)(2,1)} %query_ref.5, f32[3,3,8192]{2,1,0:T(4,128)S(1)} %copy-done.1, f32[128,8192]{1,0:T(8,128)S(1)} %query_part_0.1.refs_0_), custom_call_target="tpu_custom_call", output_to_operand_aliasing={{}: (3, {})} | custom-call | flops 6553600 | bytes 3145728 | tf_op jit(solution)/shard_map/query_part_1/pallas_call | solution.py:612
  34.2 0.4 collective-permute-done.4.got_ref
  34.6 0.3 pair_enter.1
  34.9 2.9 %collective-permute-start.5 = (f32[16,4096]{1,0:T(8,128)S(1)}, f32[16,4096]{1,0:T(8,128)S(1)}, u32[]{:S(2)}, u32[]{:S(2)}) collective-permute-start(f32[16,4096]{1,0:T(8,128)S(1)} %get-tuple-element.79), channel_id=1, source_target_pairs={{0,1},{1,0},{2,3},{3,2},{4,5},{5,4},{6,7},{7,6},{8,9},{9,8},{10,11... | collective-permute-start | bytes 786440 | tf_op jit(solution)/shard_map/ppermute | solution.py:26
  37.7 0.0 copy-done.2
  37.7 0.0 copy-start.3
  37.7 4.7 %far_part_own.1 = (bf16[128,8192]{1,0:T(8,128)(2,1)}, f32[64,128,128]{2,1,0:T(8,128)S(1)}, f32[128,128]{1,0:T(8,128)S(1)}) custom-call(f32[85,8,128]{2,1,0:T(8,128)S(1)} %get-tuple-element.48.masks.refs_0_, f32[64,136,128]{2,1,0:T(8,128)S(1)} %get-tuple-element.62.state_ref, f32[16,4096]{1,0:T(8,128)S(1)} %get-tuple-element.80.enter_ref, ...), custom_call_target="tpu_custom_call" | custom-call | flops 29491200 | bytes 9437184 | tf_op jit(solution)/shard_map/far_part_own/pallas_call | solution.py:792
  42.4 0.0 collective-permute-done.5.enter_ref
  42.5 0.0 copy-done.3
  42.5 5.6 %far_part_other.1 = (bf16[128,8192]{1,0:T(8,128)(2,1)}, f32[64,128,128]{2,1,0:T(8,128)S(1)}, f32[128,128]{1,0:T(8,128)S(1)}, bf16[128,8192]{1,0:T(8,128)(2,1)}) custom-call(f32[85,8,128]{2,1,0:T(8,128)S(1)} %get-tuple-element.48.masks.refs_0_, ...), custom_call_target="tpu_custom_call", output_to_operand_aliasing={{0}: (11, {}), {1}: (12, {}), {2}: (13, {})} | custom-call | flops 29491200 | bytes 9437184 | tf_op jit(solution)/shard_map/far_part_other/pallas_call | solution.py:792
Async XLA Ops:
  0.6 5.0 %copy-start = (f32[16,8192]{1,0:T(8,128)S(1)}, f32[16,8192]{1,0:T(8,128)}, u32[]{:S(2)}) copy-start(f32[16,8192]{1,0:T(8,128)} %rate_ref.17) | copy-start | bytes 1572868
  0.6 5.0 %copy-start.1 = (f32[3,3,8192]{2,1,0:T(4,128)S(1)}, f32[3,3,8192]{2,1,0:T(4,128)}, u32[]{:S(2)}) copy-start(f32[3,3,8192]{2,1,0:T(4,128)} %taps_ref.9) | copy-start | bytes 884740
  2.0 9.9 %collective-permute-start = (bf16[3,2,8192]{2,1,0:T(2,128)(2,1)S(1)}, bf16[3,2,8192]{2,1,0:T(2,128)(2,1)S(1)}, u32[]{:S(2)}, u32[]{:S(2)}) collective-permute-start(bf16[3,2,8192]{2,1,0:T(2,128)(2,1)S(1)} %get-tuple-element.50), channel_id=1, source_target_pairs={{0,1},{1,2},{2,3},{3,4},{4,5},{5,6},{6,7},{7,8},{8,9},{9,10},{10,1... | collective-permute-start | bytes 294920 | tf_op jit(solution)/shard_map/ppermute | solution.py:22
  12.4 5.1 %collective-permute-start.1 = (f32[16,4096]{1,0:T(8,128)S(1)}, f32[16,4096]{1,0:T(8,128)S(1)}, u32[]{:S(2)}, u32[]{:S(2)}) collective-permute-start(f32[16,4096]{1,0:T(8,128)S(1)} %get-tuple-element.54), channel_id=1, source_target_pairs={{0,1},{1,0},{2,3},{3,2},{4,5},{5,4},{6,7},{7,6},{8,9},{9,8},{10,11... | collective-permute-start | bytes 786440 | tf_op jit(solution)/shard_map/ppermute | solution.py:26
  12.5 6.5 %copy-start.4 = (f32[16,8192]{1,0:T(8,128)S(1)}, f32[16,8192]{1,0:T(8,128)}, u32[]{:S(2)}) copy-start(f32[16,8192]{1,0:T(8,128)} %param.14) | copy-start | bytes 1572868
  17.7 6.3 %collective-permute-start.2 = (bf16[16,4096]{1,0:T(8,128)(2,1)S(1)}, bf16[16,4096]{1,0:T(8,128)(2,1)S(1)}, u32[]{:S(2)}, u32[]{:S(2)}) collective-permute-start(bf16[16,4096]{1,0:T(8,128)(2,1)S(1)} %get-tuple-element.65), channel_id=1, source_target_pairs={{0,2},{1,3},{2,0},{3,1},{4,6},{5,7},{6,4},{7,5},{8,10},{9,11},{10,... | collective-permute-start | bytes 393224 | tf_op jit(solution)/shard_map/ppermute | solution.py:26
  24.3 4.3 %collective-permute-start.3 = (bf16[16,4096]{1,0:T(8,128)(2,1)S(1)}, bf16[16,4096]{1,0:T(8,128)(2,1)S(1)}, u32[]{:S(2)}, u32[]{:S(2)}) collective-permute-start(bf16[16,4096]{1,0:T(8,128)(2,1)S(1)} %get-tuple-element.70), channel_id=1, source_target_pairs={{0,4},{1,5},{2,6},{3,7},{4,0},{5,1},{6,2},{7,3},{8,12},{9,13},{10,... | collective-permute-start | bytes 393224 | tf_op jit(solution)/shard_map/ppermute | solution.py:26
  28.9 5.7 %collective-permute-start.4 = (bf16[16,4096]{1,0:T(8,128)(2,1)S(1)}, bf16[16,4096]{1,0:T(8,128)(2,1)S(1)}, u32[]{:S(2)}, u32[]{:S(2)}) collective-permute-start(bf16[16,4096]{1,0:T(8,128)(2,1)S(1)} %get-tuple-element.75), channel_id=1, source_target_pairs={{0,8},{1,9},{2,10},{3,11},{4,12},{5,13},{6,14},{7,15},{8,16},{9,17... | collective-permute-start | bytes 393224 | tf_op jit(solution)/shard_map/ppermute | solution.py:22
  32.1 5.6 %copy-start.2 = (bf16[128,8192]{1,0:T(8,128)(2,1)S(1)}, bf16[128,8192]{1,0:T(8,128)(2,1)}, u32[]{:S(2)}) copy-start(bf16[128,8192]{1,0:T(8,128)(2,1)} %resid_ref.3) | copy-start | bytes 6291460
  34.9 7.6 %collective-permute-start.5 = (f32[16,4096]{1,0:T(8,128)S(1)}, f32[16,4096]{1,0:T(8,128)S(1)}, u32[]{:S(2)}, u32[]{:S(2)}) collective-permute-start(f32[16,4096]{1,0:T(8,128)S(1)} %get-tuple-element.79), channel_id=1, source_target_pairs={{0,1},{1,0},{2,3},{3,2},{4,5},{5,4},{6,7},{7,6},{8,9},{9,8},{10,11... | collective-permute-start | bytes 786440 | tf_op jit(solution)/shard_map/ppermute | solution.py:26
  37.7 4.7 %copy-start.3 = (f32[8192]{0:T(1024)S(1)}, f32[8192]{0:T(1024)}, u32[]{:S(2)}) copy-start(f32[8192]{0:T(1024)} %param.17) | copy-start | bytes 98308

commit v23 on v22

--- a/solution.py
+++ b/solution.py
@@ -11,7 +11,7 @@
 SUBS = 8
 LANES = 128
 MIB = 1024 * 1024
-A_TILES, N_TILES, Q_TILES, F_TILES = 1, 1, 2, 2
+A_TILES, N_TILES, Q_TILES, F_TILES = 4, 4, 8, 8
 NEAR_PARTS = 2
 f32 = jnp.float32
 bf16 = jnp.bfloat16
@@ -561,7 +561,7 @@
     span = tok_rows // SUBS
     blocks = lax.axis_size("ctx")
     grp = lax.axis_size("grp")
-    chunk = min(chans // 2, 512)
+    chunk = min(chans // 2, 1024)
     pieces = chans // chunk
     ctx_index = lax.axis_index("ctx")
     base = (ctx_index * tok_rows).astype(jnp.int32).reshape(1)

time: 48.2 us -> 45.4 us (0.942)
  Pallas kernels: 33.8 us -> 30.2 us
  waiting for transfers between devices: 0.68 us -> 1.4 us
    pallas_call x2, Pallas kernels: 5.54 us -> 4.33 us  [near_piece(): pl.pallas_call(functools.partial(near_kernel, span=span, modes=modes, mos...]
    pallas_call x2, Pallas kernels: 11.2 us -> 10.1 us  [states_of(): pl.pallas_call(functools.partial(state_kernel, span=span, modes=modes, mo...]
    pallas_call x2, Pallas kernels: 10.3 us -> 9.28 us  [finish(): pl.pallas_call(functools.partial(final_kernel, span=span, modes=modes, ch...]
    ppermute x4, waiting for transfers between devices: 0.27 us -> 0.88 us  [swap(): lax.ppermute(shard, axis, [(i, i ^ bit) for i in range(lax.axis_size(axis...]
  transfers between devices with their start and end apart: 6 -> 6, of which waited for: 2 -> 2; matrix products, arithmetic and copies ran while one was open for 1% -> 1% of each run, Pallas kernels for 53% -> 49%
where the time goes in v23:
time: 45.4 us; the launch traced here: 45.2 us
  Pallas kernels  30.2 us (67%)
  starting transfers between devices  12.4 us (27%)
  waiting for transfers between devices  1.4 us (3%)
  between operations  0.84 us (2%)
    pallas_call x2, Pallas kernels, states_of(): pl.pallas_call(functools.partial(state_kernel, span=span, modes=modes, mo...  10.1 us
    pallas_call x2, Pallas kernels, finish(): pl.pallas_call(functools.partial(final_kernel, span=span, modes=modes, ch...  9.28 us
    ppermute x2, starting transfers between devices, from_behind(): return lax.ppermute(shard, axis, [(i, i + by) for i in range(count - by)])  6.88 us
    ppermute x4, starting transfers between devices, swap(): lax.ppermute(shard, axis, [(i, i ^ bit) for i in range(lax.axis_size(axis...  5.5 us
    pallas_call x2, Pallas kernels, near_piece(): pl.pallas_call(functools.partial(near_kernel, span=span, modes=modes, mos...  4.33 us
    pallas_call x2, Pallas kernels, query_piece(): pl.pallas_call(functools.partial(query_kernel, span=span, most=Q_TILES, c...  3.76 us
    pallas_call x1, Pallas kernels, shards(): pl.pallas_call(tail_kernel, in_specs=[hbm, hbm, hbm], out_specs=[vmem, vm...  1.31 us
    pallas_call x4, Pallas kernels, pair_call(): pl.pallas_call(functools.partial(kernel, **static), in_specs=[vmem] * (le...  0.93 us
  transfers between devices with their start and end apart: 6, of which 2 were waited for; matrix products, arithmetic and copies ran while one was open for 1% of the time, Pallas kernels for 49%

profile of v23, /device:TPU:9, one launch (start us, length us, event | category | flops | bytes accessed | tf_op | source)
XLA Modules:
  0.0 45.2 jit_solution(4895900149922441450)
XLA Ops:
  0.6 0.0 copy-start
  0.6 0.0 copy-start.1
  0.6 1.3 %tails.1 = (bf16[3,2,8192]{2,1,0:T(2,128)(2,1)S(1)}, bf16[2,128,512]{2,1,0:T(8,128)(2,1)S(1)}) custom-call(bf16[128,8192]{1,0:T(8,128)(2,1)} %query_ref.5, bf16[128,8192]{1,0:T(8,128)(2,1)} %refs_3_.1, bf16[128,8192]{1,0:T(8,128)(2,1)} %refs_4_.2), custom_call_target="tpu_custom_call" | custom-call | tf_op jit(solution)/shard_map/tails/pallas_call | solution.py:594
  2.0 3.7 %collective-permute-start = (bf16[3,2,8192]{2,1,0:T(2,128)(2,1)S(1)}, bf16[3,2,8192]{2,1,0:T(2,128)(2,1)S(1)}, u32[]{:S(2)}, u32[]{:S(2)}) collective-permute-start(bf16[3,2,8192]{2,1,0:T(2,128)(2,1)S(1)} %get-tuple-element.50), channel_id=1, source_target_pairs={{0,1},{1,2},{2,3},{3,4},{4,5},{5,6},{6,7},{7,8},{8,9},{9,10},{10,1... | collective-permute-start | bytes 294920 | tf_op jit(solution)/shard_map/ppermute | solution.py:22
  5.7 0.0 copy-done
  5.7 0.0 copy-done.1
  5.7 5.7 %block_states_give.1 = (bf16[128,8192]{1,0:T(8,128)(2,1)S(1)}, f32[64,136,128]{2,1,0:T(8,128)S(1)}, f32[16,4096]{1,0:T(8,128)S(1)}, f32[85,8,128]{2,1,0:T(8,128)...) custom-call(s32[1]{0:T(128)} %bitcast.refs_0_, s32[16]{0:T(128)} %refs_1_.1, ...), custom_call_target="tpu_custom_call" | custom-call | flops 32768000 | bytes 6291456 | tf_op jit(solution)/shard_map/block_states_give/pallas_call | solution.py:635
  11.4 0.0 collective-permute-done.rim_ref.refs_3_
  11.4 0.5 %first_rows.1 = (bf16[128,8192]{1,0:T(8,128)(2,1)S(1)}, f32[64,136,128]{2,1,0:T(8,128)S(1)}, f32[16,4096]{1,0:T(8,128)S(1)}) custom-call(f32[85,8,128]{2,1,0:T(8,128)S(1)} %get-tuple-element.48.masks.refs_0_, bf16[2,16,4096]{2,1,0:T(8,128)(2,1)S(1)} %get-tuple-element.49.heads, ...), custom_call_target="tpu_custom_call", output_to_operand_aliasing={{0}: (5, {}), {1}: (6, {}), {2}: (7, {})} | custom-call | tf_op jit(solution)/shard_map/first_rows/pallas_call | solution.py:669
  11.9 0.1 collective-permute-start.1
  12.0 0.0 copy-start.4
  12.0 4.4 %block_states_own.1 = (bf16[128,8192]{1,0:T(8,128)(2,1)S(1)}, f32[64,136,128]{2,1,0:T(8,128)S(1)}, f32[16,4096]{1,0:T(8,128)S(1)}) custom-call(f32[85,8,128]{2,1,0:T(8,128)S(1)} %get-tuple-element.48.masks.refs_0_, bf16[128,4096]{1,0:T(8,128)(2,1)S(1)} %get-tuple-element.55.refs_1_, ...), custom_call_target="tpu_custom_call", output_to_operand_aliasing={{0}: (6, {}), {1}: (7, {})} | custom-call | flops 32768000 | bytes 6291456 | tf_op jit(solution)/shard_map/block_states_own/pallas_call | solution.py:635
  16.4 0.0 collective-permute-done.1.got_ref.other_ref
  16.4 0.2 pair_ends.1
  16.6 1.3 %collective-permute-start.2 = (bf16[16,4096]{1,0:T(8,128)(2,1)S(1)}, bf16[16,4096]{1,0:T(8,128)(2,1)S(1)}, u32[]{:S(2)}, u32[]{:S(2)}) collective-permute-start(bf16[16,4096]{1,0:T(8,128)(2,1)S(1)} %get-tuple-element.65), channel_id=1, source_target_pairs={{0,2},{1,3},{2,0},{3,1},{4,6},{5,7},{6,4},{7,5},{8,10},{9,11},{10,... | collective-permute-start | bytes 393224 | tf_op jit(solution)/shard_map/ppermute | solution.py:26
  17.9 0.0 copy-done.4
  17.9 0.3 sqrt_multiply_fusion.weight_ref
  18.2 1.8 %query_part_0.1.refs_0_ = f32[128,8192]{1,0:T(8,128)S(1)} custom-call(f32[85,8,128]{2,1,0:T(8,128)S(1)} %get-tuple-element.48.masks.refs_0_, bf16[128,8192]{1,0:T(8,128)(2,1)} %query_ref.5, f32[3,3,8192]{2,1,0:T(4,128)S(1)} %copy-done.1), custom_call_target="tpu_custom_call" | custom-call | flops 6553600 | bytes 3145728 | tf_op jit(solution)/shard_map/query_part_0/pallas_call | solution.py:612
  20.0 2.2 %near_part_0.1.refs_0_ = f32[128,8192]{1,0:T(8,128)S(1)} custom-call(f32[85,8,128]{2,1,0:T(8,128)S(1)} %get-tuple-element.48.masks.refs_0_, bf16[128,8192]{1,0:T(8,128)(2,1)S(1)} %get-tuple-element.67.gate_ref, f32[16,8192]{1,0:T(8,128)S(1)} %copy-done, f32[16,8192]{1,0:T(8,128)S(1)} %sqrt_multiply_fusion.weight_ref), custom_call_target="tpu_custom_call" | custom-call | flops 19660800 | bytes 3670016 | tf_op jit(solution)/shard_map/near_part_0/pallas_call | solution.py:692
  22.2 0.0 collective-permute-done.2.got_ref
  22.2 0.2 level_0.1
  22.4 1.3 %collective-permute-start.3 = (bf16[16,4096]{1,0:T(8,128)(2,1)S(1)}, bf16[16,4096]{1,0:T(8,128)(2,1)S(1)}, u32[]{:S(2)}, u32[]{:S(2)}) collective-permute-start(bf16[16,4096]{1,0:T(8,128)(2,1)S(1)} %get-tuple-element.70), channel_id=1, source_target_pairs={{0,4},{1,5},{2,6},{3,7},{4,0},{5,1},{6,2},{7,3},{8,12},{9,13},{10,... | collective-permute-start | bytes 393224 | tf_op jit(solution)/shard_map/ppermute | solution.py:26
  23.8 2.2 %near_part_1.1.near_ref = f32[128,8192]{1,0:T(8,128)S(1)} custom-call(f32[85,8,128]{2,1,0:T(8,128)S(1)} %get-tuple-element.48.masks.refs_0_, bf16[128,8192]{1,0:T(8,128)(2,1)S(1)} %get-tuple-element.67.gate_ref, f32[16,8192]{1,0:T(8,128)S(1)} %copy-done, f32[16,8192]{1,0:T(8,128)S(1)} %sqrt_multiply_fusion.weight_ref, ...), custom_call_target="tpu_custom_call", output_to_operand_aliasing={{}: (4, {})} | custom-call | flops 19660800 | bytes 3670016 | tf_op jit(solution)/shard_map/near_part_1/pallas_call | solution.py:692
  25.9 0.9 %collective-permute-done.3.got_ref = bf16[16,4096]{1,0:T(8,128)(2,1)S(1)} collective-permute-done((bf16[16,4096]{1,0:T(8,128)(2,1)S(1)}, bf16[16,4096]{1,0:T(8,128)(2,1)S(1)}, u32[]{:S(2)}, u32[]{:S(2)}) %collective-permute-start.3) | collective-permute-done | bytes 131104 | tf_op jit(solution)/shard_map/ppermute | solution.py:26
  26.8 0.2 level_1.1
  27.0 3.2 %collective-permute-start.4 = (bf16[16,4096]{1,0:T(8,128)(2,1)S(1)}, bf16[16,4096]{1,0:T(8,128)(2,1)S(1)}, u32[]{:S(2)}, u32[]{:S(2)}) collective-permute-start(bf16[16,4096]{1,0:T(8,128)(2,1)S(1)} %get-tuple-element.75), channel_id=1, source_target_pairs={{0,8},{1,9},{2,10},{3,11},{4,12},{5,13},{6,14},{7,15},{8,16},{9,17... | collective-permute-start | bytes 393224 | tf_op jit(solution)/shard_map/ppermute | solution.py:22
  30.3 0.0 copy-start.2
  30.3 2.0 %query_part_1.1.short_ref = f32[128,8192]{1,0:T(8,128)S(1)} custom-call(f32[85,8,128]{2,1,0:T(8,128)S(1)} %get-tuple-element.48.masks.refs_0_, bf16[128,8192]{1,0:T(8,128)(2,1)} %query_ref.5, f32[3,3,8192]{2,1,0:T(4,128)S(1)} %copy-done.1, f32[128,8192]{1,0:T(8,128)S(1)} %query_part_0.1.refs_0_), custom_call_target="tpu_custom_call", output_to_operand_aliasing={{}: (3, {})} | custom-call | flops 6553600 | bytes 3145728 | tf_op jit(solution)/shard_map/query_part_1/pallas_call | solution.py:612
  32.2 0.5 %collective-permute-done.4.got_ref = bf16[16,4096]{1,0:T(8,128)(2,1)S(1)} collective-permute-done((bf16[16,4096]{1,0:T(8,128)(2,1)S(1)}, bf16[16,4096]{1,0:T(8,128)(2,1)S(1)}, u32[]{:S(2)}, u32[]{:S(2)}) %collective-permute-start.4) | collective-permute-done | bytes 131104 | tf_op jit(solution)/shard_map/ppermute | solution.py:22
  32.8 0.3 pair_enter.1
  33.0 2.8 %collective-permute-start.5 = (f32[16,4096]{1,0:T(8,128)S(1)}, f32[16,4096]{1,0:T(8,128)S(1)}, u32[]{:S(2)}, u32[]{:S(2)}) collective-permute-start(f32[16,4096]{1,0:T(8,128)S(1)} %get-tuple-element.79), channel_id=1, source_target_pairs={{0,1},{1,0},{2,3},{3,2},{4,5},{5,4},{6,7},{7,6},{8,9},{9,8},{10,11... | collective-permute-start | bytes 786440 | tf_op jit(solution)/shard_map/ppermute | solution.py:26
  35.9 0.0 copy-done.2
  35.9 0.0 copy-start.3
  35.9 4.2 %far_part_own.1 = (bf16[128,8192]{1,0:T(8,128)(2,1)}, f32[64,128,128]{2,1,0:T(8,128)S(1)}, f32[128,128]{1,0:T(8,128)S(1)}) custom-call(f32[85,8,128]{2,1,0:T(8,128)S(1)} %get-tuple-element.48.masks.refs_0_, f32[64,136,128]{2,1,0:T(8,128)S(1)} %get-tuple-element.62.state_ref, f32[16,4096]{1,0:T(8,128)S(1)} %get-tuple-element.80.enter_ref, ...), custom_call_target="tpu_custom_call" | custom-call | flops 29491200 | bytes 9437184 | tf_op jit(solution)/shard_map/far_part_own/pallas_call | solution.py:792
  40.1 0.0 collective-permute-done.5.enter_ref
  40.1 0.0 copy-done.3
  40.1 5.1 %far_part_other.1 = (bf16[128,8192]{1,0:T(8,128)(2,1)}, f32[64,128,128]{2,1,0:T(8,128)S(1)}, f32[128,128]{1,0:T(8,128)S(1)}, bf16[128,8192]{1,0:T(8,128)(2,1)}) custom-call(f32[85,8,128]{2,1,0:T(8,128)S(1)} %get-tuple-element.48.masks.refs_0_, ...), custom_call_target="tpu_custom_call", output_to_operand_aliasing={{0}: (11, {}), {1}: (12, {}), {2}: (13, {})} | custom-call | flops 29491200 | bytes 9437184 | tf_op jit(solution)/shard_map/far_part_other/pallas_call | solution.py:792
Async XLA Ops:
  0.6 5.0 %copy-start = (f32[16,8192]{1,0:T(8,128)S(1)}, f32[16,8192]{1,0:T(8,128)}, u32[]{:S(2)}) copy-start(f32[16,8192]{1,0:T(8,128)} %rate_ref.17) | copy-start | bytes 1572868
  0.6 5.0 %copy-start.1 = (f32[3,3,8192]{2,1,0:T(4,128)S(1)}, f32[3,3,8192]{2,1,0:T(4,128)}, u32[]{:S(2)}) copy-start(f32[3,3,8192]{2,1,0:T(4,128)} %taps_ref.9) | copy-start | bytes 884740
  2.0 9.4 %collective-permute-start = (bf16[3,2,8192]{2,1,0:T(2,128)(2,1)S(1)}, bf16[3,2,8192]{2,1,0:T(2,128)(2,1)S(1)}, u32[]{:S(2)}, u32[]{:S(2)}) collective-permute-start(bf16[3,2,8192]{2,1,0:T(2,128)(2,1)S(1)} %get-tuple-element.50), channel_id=1, source_target_pairs={{0,1},{1,2},{2,3},{3,4},{4,5},{5,6},{6,7},{7,8},{8,9},{9,10},{10,1... | collective-permute-start | bytes 294920 | tf_op jit(solution)/shard_map/ppermute | solution.py:22
  11.9 4.5 %collective-permute-start.1 = (f32[16,4096]{1,0:T(8,128)S(1)}, f32[16,4096]{1,0:T(8,128)S(1)}, u32[]{:S(2)}, u32[]{:S(2)}) collective-permute-start(f32[16,4096]{1,0:T(8,128)S(1)} %get-tuple-element.54), channel_id=1, source_target_pairs={{0,1},{1,0},{2,3},{3,2},{4,5},{5,4},{6,7},{7,6},{8,9},{9,8},{10,11... | collective-permute-start | bytes 786440 | tf_op jit(solution)/shard_map/ppermute | solution.py:26
  12.0 5.9 %copy-start.4 = (f32[16,8192]{1,0:T(8,128)S(1)}, f32[16,8192]{1,0:T(8,128)}, u32[]{:S(2)}) copy-start(f32[16,8192]{1,0:T(8,128)} %param.14) | copy-start | bytes 1572868
  16.6 5.6 %collective-permute-start.2 = (bf16[16,4096]{1,0:T(8,128)(2,1)S(1)}, bf16[16,4096]{1,0:T(8,128)(2,1)S(1)}, u32[]{:S(2)}, u32[]{:S(2)}) collective-permute-start(bf16[16,4096]{1,0:T(8,128)(2,1)S(1)} %get-tuple-element.65), channel_id=1, source_target_pairs={{0,2},{1,3},{2,0},{3,1},{4,6},{5,7},{6,4},{7,5},{8,10},{9,11},{10,... | collective-permute-start | bytes 393224 | tf_op jit(solution)/shard_map/ppermute | solution.py:26
  22.4 4.3 %collective-permute-start.3 = (bf16[16,4096]{1,0:T(8,128)(2,1)S(1)}, bf16[16,4096]{1,0:T(8,128)(2,1)S(1)}, u32[]{:S(2)}, u32[]{:S(2)}) collective-permute-start(bf16[16,4096]{1,0:T(8,128)(2,1)S(1)} %get-tuple-element.70), channel_id=1, source_target_pairs={{0,4},{1,5},{2,6},{3,7},{4,0},{5,1},{6,2},{7,3},{8,12},{9,13},{10,... | collective-permute-start | bytes 393224 | tf_op jit(solution)/shard_map/ppermute | solution.py:26
  27.0 5.7 %collective-permute-start.4 = (bf16[16,4096]{1,0:T(8,128)(2,1)S(1)}, bf16[16,4096]{1,0:T(8,128)(2,1)S(1)}, u32[]{:S(2)}, u32[]{:S(2)}) collective-permute-start(bf16[16,4096]{1,0:T(8,128)(2,1)S(1)} %get-tuple-element.75), channel_id=1, source_target_pairs={{0,8},{1,9},{2,10},{3,11},{4,12},{5,13},{6,14},{7,15},{8,16},{9,17... | collective-permute-start | bytes 393224 | tf_op jit(solution)/shard_map/ppermute | solution.py:22
  30.3 5.6 %copy-start.2 = (bf16[128,8192]{1,0:T(8,128)(2,1)S(1)}, bf16[128,8192]{1,0:T(8,128)(2,1)}, u32[]{:S(2)}) copy-start(bf16[128,8192]{1,0:T(8,128)(2,1)} %resid_ref.3) | copy-start | bytes 6291460
  33.0 7.0 %collective-permute-start.5 = (f32[16,4096]{1,0:T(8,128)S(1)}, f32[16,4096]{1,0:T(8,128)S(1)}, u32[]{:S(2)}, u32[]{:S(2)}) collective-permute-start(f32[16,4096]{1,0:T(8,128)S(1)} %get-tuple-element.79), channel_id=1, source_target_pairs={{0,1},{1,0},{2,3},{3,2},{4,5},{5,4},{6,7},{7,6},{8,9},{9,8},{10,11... | collective-permute-start | bytes 786440 | tf_op jit(solution)/shard_map/ppermute | solution.py:26
  35.9 4.2 %copy-start.3 = (f32[8192]{0:T(1024)S(1)}, f32[8192]{0:T(1024)}, u32[]{:S(2)}) copy-start(f32[8192]{0:T(1024)} %param.17) | copy-start | bytes 98308

commit v24 on v23

--- a/solution.py
+++ b/solution.py
@@ -11,7 +11,7 @@
 SUBS = 8
 LANES = 128
 MIB = 1024 * 1024
-A_TILES, N_TILES, Q_TILES, F_TILES = 4, 4, 8, 8
+A_TILES, N_TILES, Q_TILES, F_TILES = 4, 8, 8, 8
 NEAR_PARTS = 2
 f32 = jnp.float32
 bf16 = jnp.bfloat16
@@ -153,7 +153,7 @@
             spread(keys[:, cols_of(pl.multiple_of(lane - first, LANES))], wide_k.at[slot], span)
             spread(values[:, cols_of(pl.multiple_of(lane - first, LANES))], wide_v.at[slot], span)
             rate = rate_ref[:, cols_of(lane)]
-            tables[slot] = jnp.exp(-rate)
+            tables[slot, pl.ds(0, modes), :] = jnp.exp(-rate)
         convs = [
             [
                 Conv(wide.at[slot], rim_ref[i, :, cols_of(lane)].astype(f32) if own else None, taps_ref[i, :, cols_of(lane)], span)
@@ -321,7 +321,7 @@
     size = SUBS * span
     parity = lax.rem(lax.div(base_ref[0], size), 2)
     pair_at = base_ref[0] - parity * size
-    rows_of[...] = flag(starts[span - 1] < rows)
+    rows_of[pl.ds(0, SUBS), :] = flag(starts[span - 1] < rows)
     for b in range(SUBS):
         masks[at.passes + b] = row_of(rows_of, b)
     ranges = []
@@ -493,7 +493,7 @@
             state = enter_ref[:, cols_of(pl.multiple_of(lane - first, LANES))]
             rate = rate_ref[:, cols_of(lane)]
             weight = weight_ref[:, cols_of(lane)]
-            tables[slot] = jnp.exp(-rate)
+            tables[slot, pl.ds(0, modes), :] = jnp.exp(-rate)
             leap = jnp.exp(-float(span) * rate)
             for b in range(SUBS):
                 starts_at[slot, pl.ds(b * (modes + 1), modes), :] = weight * state
@@ -571,7 +571,7 @@
     vmem = pl.BlockSpec(memory_space=pltpu.VMEM)
     hbm = pl.BlockSpec(memory_space=pltpu.HBM)
     tile_shape = (SUBS, LANES)
-    wide_rows = SUBS * (span + 1)
+    wide_rows = SUBS * (span + 3)
     params = pltpu.CompilerParams(vmem_limit_bytes=16 * MIB)
 
     lengths = pltpu.with_memory_space_constraint(doc_lengths, pltpu.HBM)
@@ -629,7 +629,7 @@
     sent = pltpu.VMEM((modes, chans // 2), bf16)
 
     gate_shape = pltpu.VMEM((tok_rows, chans), bf16)
-    state_shape = pltpu.VMEM((chans // LANES, SUBS * (modes + 1), LANES), f32)
+    state_shape = pltpu.VMEM((chans // LANES, SUBS * (modes + 3), LANES), f32)
 
     def states_of(own, operands, in_specs, out_shape, scratch, aliases):
         return pl.pallas_call(
@@ -643,7 +643,7 @@
             + [
                 pltpu.VMEM((A_TILES, wide_rows, LANES), f32),
                 pltpu.VMEM((A_TILES, wide_rows, LANES), f32),
-                pltpu.VMEM((A_TILES, modes, LANES), f32),
+                pltpu.VMEM((A_TILES, modes + SUBS, LANES), f32),
                 pltpu.VMEM((A_TILES, span) + tile_shape, f32),
             ]
             + scratch[-1:],
@@ -661,7 +661,7 @@
         [
             pltpu.VMEM((tok_rows, chans // 2), bf16),
             pltpu.VMEM((tok_rows, chans // 2), bf16),
-            pltpu.VMEM(tile_shape, f32),
+            pltpu.VMEM((2 * SUBS, LANES), f32),
             pltpu.SemaphoreType.DMA((2, chans // 2 // small + 1)),
         ],
         {},
@@ -697,8 +697,8 @@
             out_specs=vmem,
             out_shape=pltpu.VMEM((tok_rows, chans), f32),
             scratch_shapes=[
-                pltpu.VMEM((N_TILES, span * (SUBS + 1), LANES), f32),
-                pltpu.VMEM((N_TILES, span, LANES), f32),
+                pltpu.VMEM((N_TILES, span * (SUBS + 2), LANES), f32),
+                pltpu.VMEM((N_TILES, span + SUBS, LANES), f32),
             ],
             compiler_params=params,
             input_output_aliases={4: 0} if before else {},
@@ -775,8 +775,8 @@
             pltpu.VMEM((tok_rows, chans // 2), bf16),
             copies(2),
             pltpu.VMEM((F_TILES, wide_rows, LANES), f32),
-            pltpu.VMEM((F_TILES, modes, LANES), f32),
-            pltpu.VMEM((F_TILES, SUBS * (modes + 1), LANES), f32),
+            pltpu.VMEM((F_TILES, modes + SUBS, LANES), f32),
+            pltpu.VMEM((F_TILES, SUBS * (modes + 3), LANES), f32),
         ]
         operands = [near_by(x) for x in (masks, states, enter, near, q_short)] + [resid, rims, taps, rates, weights]
         if last:

time: 45.4 us -> 45.2 us (level)
  no operation moved by 1% of the time
where the time goes in v24:
time: 45.2 us; the launch traced here: 45 us
  Pallas kernels  29.9 us (66%)
  starting transfers between devices  12.4 us (27%)
  waiting for transfers between devices  1.53 us (3%)
  between operations  0.83 us (2%)
    pallas_call x2, Pallas kernels, states_of(): pl.pallas_call(functools.partial(state_kernel, span=span, modes=modes, mo...  10 us
    pallas_call x2, Pallas kernels, finish(): pl.pallas_call(functools.partial(final_kernel, span=span, modes=modes, ch...  9.26 us
    ppermute x2, starting transfers between devices, from_behind(): return lax.ppermute(shard, axis, [(i, i + by) for i in range(count - by)])  6.88 us
    ppermute x4, starting transfers between devices, swap(): lax.ppermute(shard, axis, [(i, i ^ bit) for i in range(lax.axis_size(axis...  5.5 us
    pallas_call x2, Pallas kernels, near_piece(): pl.pallas_call(functools.partial(near_kernel, span=span, modes=modes, mos...  4.07 us
    pallas_call x2, Pallas kernels, query_piece(): pl.pallas_call(functools.partial(query_kernel, span=span, most=Q_TILES, c...  3.77 us
    pallas_call x1, Pallas kernels, shards(): pl.pallas_call(tail_kernel, in_specs=[hbm, hbm, hbm], out_specs=[vmem, vm...  1.31 us
    ppermute x4, waiting for transfers between devices, swap(): lax.ppermute(shard, axis, [(i, i ^ bit) for i in range(lax.axis_size(axis...  1.01 us
  transfers between devices with their start and end apart: 6, of which 2 were waited for; matrix products, arithmetic and copies ran while one was open for 1% of the time, Pallas kernels for 49%

profile of v24, /device:TPU:9, one launch (start us, length us, event | category | flops | bytes accessed | tf_op | source)
XLA Modules:
  0.0 45.0 jit_solution(11604310169390111794)
XLA Ops:
  0.6 0.0 copy-start
  0.6 0.0 copy-start.1
  0.6 1.3 %tails.1 = (bf16[3,2,8192]{2,1,0:T(2,128)(2,1)S(1)}, bf16[2,128,512]{2,1,0:T(8,128)(2,1)S(1)}) custom-call(bf16[128,8192]{1,0:T(8,128)(2,1)} %query_ref.5, bf16[128,8192]{1,0:T(8,128)(2,1)} %refs_3_.1, bf16[128,8192]{1,0:T(8,128)(2,1)} %refs_4_.2), custom_call_target="tpu_custom_call" | custom-call | tf_op jit(solution)/shard_map/tails/pallas_call | solution.py:594
  2.0 3.7 %collective-permute-start = (bf16[3,2,8192]{2,1,0:T(2,128)(2,1)S(1)}, bf16[3,2,8192]{2,1,0:T(2,128)(2,1)S(1)}, u32[]{:S(2)}, u32[]{:S(2)}) collective-permute-start(bf16[3,2,8192]{2,1,0:T(2,128)(2,1)S(1)} %get-tuple-element.50), channel_id=1, source_target_pairs={{0,1},{1,2},{2,3},{3,4},{4,5},{5,6},{6,7},{7,8},{8,9},{9,10},{10,1... | collective-permute-start | bytes 294920 | tf_op jit(solution)/shard_map/ppermute | solution.py:22
  5.7 0.0 copy-done
  5.7 0.0 copy-done.1
  5.7 5.7 %block_states_give.1 = (bf16[128,8192]{1,0:T(8,128)(2,1)S(1)}, f32[64,152,128]{2,1,0:T(8,128)S(1)}, f32[16,4096]{1,0:T(8,128)S(1)}, f32[85,8,128]{2,1,0:T(8,128)...) custom-call(s32[1]{0:T(128)} %bitcast.refs_0_, s32[16]{0:T(128)} %refs_1_.1, ...), custom_call_target="tpu_custom_call" | custom-call | flops 32768000 | bytes 6291456 | tf_op jit(solution)/shard_map/block_states_give/pallas_call | solution.py:635
  11.3 0.0 collective-permute-done.rim_ref.refs_3_
  11.3 0.5 %first_rows.1 = (bf16[128,8192]{1,0:T(8,128)(2,1)S(1)}, f32[64,152,128]{2,1,0:T(8,128)S(1)}, f32[16,4096]{1,0:T(8,128)S(1)}) custom-call(f32[85,8,128]{2,1,0:T(8,128)S(1)} %get-tuple-element.48.masks.refs_0_, bf16[2,16,4096]{2,1,0:T(8,128)(2,1)S(1)} %get-tuple-element.49.heads, ...), custom_call_target="tpu_custom_call", output_to_operand_aliasing={{0}: (5, {}), {1}: (6, {}), {2}: (7, {})} | custom-call | tf_op jit(solution)/shard_map/first_rows/pallas_call | solution.py:669
  11.9 0.1 collective-permute-start.1
  12.0 0.0 copy-start.4
  12.0 4.4 %block_states_own.1 = (bf16[128,8192]{1,0:T(8,128)(2,1)S(1)}, f32[64,152,128]{2,1,0:T(8,128)S(1)}, f32[16,4096]{1,0:T(8,128)S(1)}) custom-call(f32[85,8,128]{2,1,0:T(8,128)S(1)} %get-tuple-element.48.masks.refs_0_, bf16[128,4096]{1,0:T(8,128)(2,1)S(1)} %get-tuple-element.55.refs_1_, ...), custom_call_target="tpu_custom_call", output_to_operand_aliasing={{0}: (6, {}), {1}: (7, {})} | custom-call | flops 32768000 | bytes 6291456 | tf_op jit(solution)/shard_map/block_states_own/pallas_call | solution.py:635
  16.4 0.0 collective-permute-done.1.got_ref.other_ref
  16.4 0.2 pair_ends.1
  16.5 1.3 %collective-permute-start.2 = (bf16[16,4096]{1,0:T(8,128)(2,1)S(1)}, bf16[16,4096]{1,0:T(8,128)(2,1)S(1)}, u32[]{:S(2)}, u32[]{:S(2)}) collective-permute-start(bf16[16,4096]{1,0:T(8,128)(2,1)S(1)} %get-tuple-element.65), channel_id=1, source_target_pairs={{0,2},{1,3},{2,0},{3,1},{4,6},{5,7},{6,4},{7,5},{8,10},{9,11},{10,... | collective-permute-start | bytes 393224 | tf_op jit(solution)/shard_map/ppermute | solution.py:26
  17.8 0.0 copy-done.4
  17.8 0.3 sqrt_multiply_fusion.weight_ref
  18.1 1.8 %query_part_0.1.refs_0_ = f32[128,8192]{1,0:T(8,128)S(1)} custom-call(f32[85,8,128]{2,1,0:T(8,128)S(1)} %get-tuple-element.48.masks.refs_0_, bf16[128,8192]{1,0:T(8,128)(2,1)} %query_ref.5, f32[3,3,8192]{2,1,0:T(4,128)S(1)} %copy-done.1), custom_call_target="tpu_custom_call" | custom-call | flops 6553600 | bytes 3145728 | tf_op jit(solution)/shard_map/query_part_0/pallas_call | solution.py:612
  20.0 2.0 %near_part_0.1.refs_0_ = f32[128,8192]{1,0:T(8,128)S(1)} custom-call(f32[85,8,128]{2,1,0:T(8,128)S(1)} %get-tuple-element.48.masks.refs_0_, bf16[128,8192]{1,0:T(8,128)(2,1)S(1)} %get-tuple-element.67.gate_ref, f32[16,8192]{1,0:T(8,128)S(1)} %copy-done, f32[16,8192]{1,0:T(8,128)S(1)} %sqrt_multiply_fusion.weight_ref), custom_call_target="tpu_custom_call" | custom-call | flops 19660800 | bytes 3670016 | tf_op jit(solution)/shard_map/near_part_0/pallas_call | solution.py:692
  22.0 0.0 collective-permute-done.2.got_ref
  22.0 0.2 level_0.1
  22.3 1.3 %collective-permute-start.3 = (bf16[16,4096]{1,0:T(8,128)(2,1)S(1)}, bf16[16,4096]{1,0:T(8,128)(2,1)S(1)}, u32[]{:S(2)}, u32[]{:S(2)}) collective-permute-start(bf16[16,4096]{1,0:T(8,128)(2,1)S(1)} %get-tuple-element.70), channel_id=1, source_target_pairs={{0,4},{1,5},{2,6},{3,7},{4,0},{5,1},{6,2},{7,3},{8,12},{9,13},{10,... | collective-permute-start | bytes 393224 | tf_op jit(solution)/shard_map/ppermute | solution.py:26
  23.6 2.0 %near_part_1.1.near_ref = f32[128,8192]{1,0:T(8,128)S(1)} custom-call(f32[85,8,128]{2,1,0:T(8,128)S(1)} %get-tuple-element.48.masks.refs_0_, bf16[128,8192]{1,0:T(8,128)(2,1)S(1)} %get-tuple-element.67.gate_ref, f32[16,8192]{1,0:T(8,128)S(1)} %copy-done, f32[16,8192]{1,0:T(8,128)S(1)} %sqrt_multiply_fusion.weight_ref, ...), custom_call_target="tpu_custom_call", output_to_operand_aliasing={{}: (4, {})} | custom-call | flops 19660800 | bytes 3670016 | tf_op jit(solution)/shard_map/near_part_1/pallas_call | solution.py:692
  25.6 1.0 %collective-permute-done.3.got_ref = bf16[16,4096]{1,0:T(8,128)(2,1)S(1)} collective-permute-done((bf16[16,4096]{1,0:T(8,128)(2,1)S(1)}, bf16[16,4096]{1,0:T(8,128)(2,1)S(1)}, u32[]{:S(2)}, u32[]{:S(2)}) %collective-permute-start.3) | collective-permute-done | bytes 131104 | tf_op jit(solution)/shard_map/ppermute | solution.py:26
  26.6 0.2 level_1.1
  26.9 3.2 %collective-permute-start.4 = (bf16[16,4096]{1,0:T(8,128)(2,1)S(1)}, bf16[16,4096]{1,0:T(8,128)(2,1)S(1)}, u32[]{:S(2)}, u32[]{:S(2)}) collective-permute-start(bf16[16,4096]{1,0:T(8,128)(2,1)S(1)} %get-tuple-element.75), channel_id=1, source_target_pairs={{0,8},{1,9},{2,10},{3,11},{4,12},{5,13},{6,14},{7,15},{8,16},{9,17... | collective-permute-start | bytes 393224 | tf_op jit(solution)/shard_map/ppermute | solution.py:22
  30.1 0.0 copy-start.2
  30.1 2.0 %query_part_1.1.short_ref = f32[128,8192]{1,0:T(8,128)S(1)} custom-call(f32[85,8,128]{2,1,0:T(8,128)S(1)} %get-tuple-element.48.masks.refs_0_, bf16[128,8192]{1,0:T(8,128)(2,1)} %query_ref.5, f32[3,3,8192]{2,1,0:T(4,128)S(1)} %copy-done.1, f32[128,8192]{1,0:T(8,128)S(1)} %query_part_0.1.refs_0_), custom_call_target="tpu_custom_call", output_to_operand_aliasing={{}: (3, {})} | custom-call | flops 6553600 | bytes 3145728 | tf_op jit(solution)/shard_map/query_part_1/pallas_call | solution.py:612
  32.1 0.5 %collective-permute-done.4.got_ref = bf16[16,4096]{1,0:T(8,128)(2,1)S(1)} collective-permute-done((bf16[16,4096]{1,0:T(8,128)(2,1)S(1)}, bf16[16,4096]{1,0:T(8,128)(2,1)S(1)}, u32[]{:S(2)}, u32[]{:S(2)}) %collective-permute-start.4) | collective-permute-done | bytes 131104 | tf_op jit(solution)/shard_map/ppermute | solution.py:22
  32.6 0.3 pair_enter.1
  32.9 2.8 %collective-permute-start.5 = (f32[16,4096]{1,0:T(8,128)S(1)}, f32[16,4096]{1,0:T(8,128)S(1)}, u32[]{:S(2)}, u32[]{:S(2)}) collective-permute-start(f32[16,4096]{1,0:T(8,128)S(1)} %get-tuple-element.79), channel_id=1, source_target_pairs={{0,1},{1,0},{2,3},{3,2},{4,5},{5,4},{6,7},{7,6},{8,9},{9,8},{10,11... | collective-permute-start | bytes 786440 | tf_op jit(solution)/shard_map/ppermute | solution.py:26
  35.7 0.0 copy-done.2
  35.7 0.0 copy-start.3
  35.7 4.2 %far_part_own.1 = (bf16[128,8192]{1,0:T(8,128)(2,1)}, f32[64,128,128]{2,1,0:T(8,128)S(1)}, f32[128,128]{1,0:T(8,128)S(1)}) custom-call(f32[85,8,128]{2,1,0:T(8,128)S(1)} %get-tuple-element.48.masks.refs_0_, f32[64,152,128]{2,1,0:T(8,128)S(1)} %get-tuple-element.62.state_ref, f32[16,4096]{1,0:T(8,128)S(1)} %get-tuple-element.80.enter_ref, ...), custom_call_target="tpu_custom_call" | custom-call | flops 29491200 | bytes 9437184 | tf_op jit(solution)/shard_map/far_part_own/pallas_call | solution.py:792
  39.9 0.0 collective-permute-done.5.enter_ref
  39.9 0.0 copy-done.3
  39.9 5.1 %far_part_other.1 = (bf16[128,8192]{1,0:T(8,128)(2,1)}, f32[64,128,128]{2,1,0:T(8,128)S(1)}, f32[128,128]{1,0:T(8,128)S(1)}, bf16[128,8192]{1,0:T(8,128)(2,1)}) custom-call(f32[85,8,128]{2,1,0:T(8,128)S(1)} %get-tuple-element.48.masks.refs_0_, ...), custom_call_target="tpu_custom_call", output_to_operand_aliasing={{0}: (11, {}), {1}: (12, {}), {2}: (13, {})} | custom-call | flops 29491200 | bytes 9437184 | tf_op jit(solution)/shard_map/far_part_other/pallas_call | solution.py:792
Async XLA Ops:
  0.6 5.0 %copy-start = (f32[16,8192]{1,0:T(8,128)S(1)}, f32[16,8192]{1,0:T(8,128)}, u32[]{:S(2)}) copy-start(f32[16,8192]{1,0:T(8,128)} %rate_ref.17) | copy-start | bytes 1572868
  0.6 5.0 %copy-start.1 = (f32[3,3,8192]{2,1,0:T(4,128)S(1)}, f32[3,3,8192]{2,1,0:T(4,128)}, u32[]{:S(2)}) copy-start(f32[3,3,8192]{2,1,0:T(4,128)} %taps_ref.9) | copy-start | bytes 884740
  2.0 9.4 %collective-permute-start = (bf16[3,2,8192]{2,1,0:T(2,128)(2,1)S(1)}, bf16[3,2,8192]{2,1,0:T(2,128)(2,1)S(1)}, u32[]{:S(2)}, u32[]{:S(2)}) collective-permute-start(bf16[3,2,8192]{2,1,0:T(2,128)(2,1)S(1)} %get-tuple-element.50), channel_id=1, source_target_pairs={{0,1},{1,2},{2,3},{3,4},{4,5},{5,6},{6,7},{7,8},{8,9},{9,10},{10,1... | collective-permute-start | bytes 294920 | tf_op jit(solution)/shard_map/ppermute | solution.py:22
  11.9 4.5 %collective-permute-start.1 = (f32[16,4096]{1,0:T(8,128)S(1)}, f32[16,4096]{1,0:T(8,128)S(1)}, u32[]{:S(2)}, u32[]{:S(2)}) collective-permute-start(f32[16,4096]{1,0:T(8,128)S(1)} %get-tuple-element.54), channel_id=1, source_target_pairs={{0,1},{1,0},{2,3},{3,2},{4,5},{5,4},{6,7},{7,6},{8,9},{9,8},{10,11... | collective-permute-start | bytes 786440 | tf_op jit(solution)/shard_map/ppermute | solution.py:26
  12.0 5.9 %copy-start.4 = (f32[16,8192]{1,0:T(8,128)S(1)}, f32[16,8192]{1,0:T(8,128)}, u32[]{:S(2)}) copy-start(f32[16,8192]{1,0:T(8,128)} %param.14) | copy-start | bytes 1572868
  16.5 5.5 %collective-permute-start.2 = (bf16[16,4096]{1,0:T(8,128)(2,1)S(1)}, bf16[16,4096]{1,0:T(8,128)(2,1)S(1)}, u32[]{:S(2)}, u32[]{:S(2)}) collective-permute-start(bf16[16,4096]{1,0:T(8,128)(2,1)S(1)} %get-tuple-element.65), channel_id=1, source_target_pairs={{0,2},{1,3},{2,0},{3,1},{4,6},{5,7},{6,4},{7,5},{8,10},{9,11},{10,... | collective-permute-start | bytes 393224 | tf_op jit(solution)/shard_map/ppermute | solution.py:26
  22.3 4.3 %collective-permute-start.3 = (bf16[16,4096]{1,0:T(8,128)(2,1)S(1)}, bf16[16,4096]{1,0:T(8,128)(2,1)S(1)}, u32[]{:S(2)}, u32[]{:S(2)}) collective-permute-start(bf16[16,4096]{1,0:T(8,128)(2,1)S(1)} %get-tuple-element.70), channel_id=1, source_target_pairs={{0,4},{1,5},{2,6},{3,7},{4,0},{5,1},{6,2},{7,3},{8,12},{9,13},{10,... | collective-permute-start | bytes 393224 | tf_op jit(solution)/shard_map/ppermute | solution.py:26
  26.9 5.7 %collective-permute-start.4 = (bf16[16,4096]{1,0:T(8,128)(2,1)S(1)}, bf16[16,4096]{1,0:T(8,128)(2,1)S(1)}, u32[]{:S(2)}, u32[]{:S(2)}) collective-permute-start(bf16[16,4096]{1,0:T(8,128)(2,1)S(1)} %get-tuple-element.75), channel_id=1, source_target_pairs={{0,8},{1,9},{2,10},{3,11},{4,12},{5,13},{6,14},{7,15},{8,16},{9,17... | collective-permute-start | bytes 393224 | tf_op jit(solution)/shard_map/ppermute | solution.py:22
  30.1 5.6 %copy-start.2 = (bf16[128,8192]{1,0:T(8,128)(2,1)S(1)}, bf16[128,8192]{1,0:T(8,128)(2,1)}, u32[]{:S(2)}) copy-start(bf16[128,8192]{1,0:T(8,128)(2,1)} %resid_ref.3) | copy-start | bytes 6291460
  32.9 7.0 %collective-permute-start.5 = (f32[16,4096]{1,0:T(8,128)S(1)}, f32[16,4096]{1,0:T(8,128)S(1)}, u32[]{:S(2)}, u32[]{:S(2)}) collective-permute-start(f32[16,4096]{1,0:T(8,128)S(1)} %get-tuple-element.79), channel_id=1, source_target_pairs={{0,1},{1,0},{2,3},{3,2},{4,5},{5,4},{6,7},{7,6},{8,9},{9,8},{10,11... | collective-permute-start | bytes 786440 | tf_op jit(solution)/shard_map/ppermute | solution.py:26
  35.7 4.2 %copy-start.3 = (f32[8192]{0:T(1024)S(1)}, f32[8192]{0:T(1024)}, u32[]{:S(2)}) copy-start(f32[8192]{0:T(1024)} %param.17) | copy-start | bytes 98308
